TPU v7x, 1024 devices: a whole 8x8x8 slice. The times are simulated.
1024 devices in a mesh: row: 32 (over x, z_lo), col: 32 (over z_hi, y, core).
Axes of the slice: x: 8, y: 8, z: 8 (z_hi: 2, z_lo: 4; z = z_hi * 4 + z_lo), core: 2. Of those that a mesh axis runs over, the one named last changes fastest.
Arguments:
- left_blocks: bfloat16 [128, 4096, 128], P('row', 'col'), may hold values from -6 to 6
- right_blocks: bfloat16 [64, 4096, 128], P('col', 'row'), may hold values from -0.078125 to 0.078125
- pair_lists: int32 [1024, 256, 3], P(('row', 'col')), may hold values from 0 to 3, as said below
- pair_count: int32 [1024, 32], P(('row', 'col')), may hold values from 1 to 8, as said below
Outputs:
- product_blocks: bfloat16 [2048, 128, 128], P(('row', 'col'))
Inputs may be any that keep to these rules, and one draw needn't show every extreme that they name: `pair_lists`: Columns: a stored left block below 4, a stored right block below 2, a stored product block below 2; the live slots of one list are distinct triples. `pair_count`: live slots per list; some list is full.
All inputs are finite; a program needn't handle non-finite values.
Results may differ from a plain program's by a relative error of at most 0.001.
Values may be sent and summed in bfloat16 or wider, within the bound.
No kernel may reach another device: no remote copies, remote signals or barrier semaphores. Data moves between devices by JAX's collectives and lax.ppermute only.
A program may use at most 32 MiB of HBM per device.

v0:
```python
import jax
import jax.numpy as jnp
from jax import lax
from jax.sharding import PartitionSpec as P

NC = 2
NT = 8


def per_device(left_blocks, right_blocks, pair_lists, pair_count):
    row_size = lax.axis_size("row")
    col_size = lax.axis_size("col")
    my_row = lax.axis_index("row")
    my_col = lax.axis_index("col")
    owned = pair_lists.shape[0]
    stored_left = left_blocks.shape[0]
    stored_right = right_blocks.shape[0]
    block_size = left_blocks.shape[1]
    lists = pair_lists.reshape(owned, col_size, NT, 3)
    slot_index = jnp.arange(NT, dtype=jnp.int32)
    target_index = jnp.arange(owned * NC, dtype=jnp.int32)
    initial = jnp.zeros((owned * NC, block_size, block_size), jnp.float32)

    def tile_terms(left_tiles, right_tiles, seat, inner):
        pairs_now = lists[seat, inner]
        live = slot_index[None, :] < pair_count[seat, inner][:, None]
        left_pick = jnp.take_along_axis(left_tiles, pairs_now[..., 0][..., None, None], axis=1)
        right_pick = jnp.take_along_axis(right_tiles, pairs_now[..., 1][..., None, None], axis=1)
        products = jnp.einsum(
            "gtrx,gtxc->gtrc", left_pick, right_pick, preferred_element_type=jnp.float32
        )
        target = seat[:, None] * NC + pairs_now[..., 2]
        weight = ((target[..., None] == target_index) & live[..., None]).astype(jnp.float32)
        return jnp.einsum("gtrc,gtw->wrc", products, weight, precision=lax.Precision.HIGHEST)

    left_all = lax.all_gather(left_blocks, "col", axis=0, tiled=True)
    left_all = left_all.reshape(col_size, stored_left, block_size, block_size)
    piece = lax.all_gather(right_blocks, "row", axis=0, tiled=True)
    tile_number = piece.shape[0] // stored_right
    bundle = [size for size in (8, 4, 2, 1) if tile_number % size == 0][0]
    tiles = piece.reshape(tile_number // bundle, bundle, stored_right, block_size, block_size)

    def step(turn, accum):
        right_now = tiles[turn]
        source = turn * bundle + jnp.arange(bundle, dtype=jnp.int32)
        seat_code = (source + my_col) % row_size
        inner = seat_code % col_size
        seat = seat_code // col_size
        left_now = left_all[(inner - my_row) % col_size]
        return accum + tile_terms(left_now, right_now, seat, inner)

    summed = lax.fori_loop(0, tile_number // bundle, step, initial)
    return summed.astype(jnp.bfloat16)


def solution(mesh):
    return jax.shard_map(
        per_device,
        mesh=mesh,
        in_specs=(
            P("row", "col", None),
            P("col", "row", None),
            P(("row", "col"), None, None),
            P(("row", "col"), None),
        ),
        out_specs=P(("row", "col"), None, None),
        check_vma=False,
    )
```

profile of v0, /device:TPU:1, one launch (start us, length us, event | category | flops | bytes accessed | tf_op | source)
XLA Modules:
  0.0 385.6 jit_solution(4012568287187245904)
XLA Ops:
  6.5 0.7 all-gather.5.cloned.1.call-update
  7.3 0.7 all-gather.3.cloned.1.call-update
  8.0 0.7 reduce.2
  8.7 0.1 reshape.274
  8.9 150.0 %all-gather.5.cloned.1.call-done = bf16[64,128,128]{2,1,0:T(8,128)(2,1)} async-done(((bf16[2,128,128]{2,1,0:T(8,128)(2,1)}), bf16[64,128,128]{2,1,0:T(8,128)(2,1)}) %all-gather.5.cloned.1.call-update) | async-done | bytes 2097168 | tf_op jit(solution)/shard_map/all_gather | solution.py:38
  158.9 141.2 %all-gather.3.cloned.1.call-done = bf16[128,128,128]{2,1,0:T(8,128)(2,1)} async-done(((bf16[4,128,128]{2,1,0:T(8,128)(2,1)}), bf16[128,128,128]{2,1,0:T(8,128)(2,1)}) %all-gather.3.cloned.1.call-update) | async-done | bytes 4194320 | tf_op jit(solution)/shard_map/all_gather | solution.py:36
  300.1 78.1 %while.16 = (s32[]{:T(128)}, f32[2,128,128]{2,0,1:T(2,128)S(1)}, s32[]{:T(128)}, s32[1,32,8,3]{2,3,1,0:T(4,128)S(1)}, s32[1,32]{1,0:T(1,128)}, /*index=5*/s32[]{...) while((s32[]{:T(128)}, f32[2,128,128]{2,0,1:T(2,128)S(1)}, ...), condition=%wide.region_1.2_spmd.clone, body=%wide.region_0.1_spmd.clone.sunk | while | flops 295767744 | bytes 24391124 | solution.py:52
  300.1 0.6 gather_fusion
  300.7 0.1 or_reduce_fusion.3
  300.8 0.1 reshape.363
  300.9 2.9 gather_fusion.2
  303.8 1.0 gather_fusion.3
  304.8 0.1 reshape.362
  304.9 1.1 dynamic-slice_bitcast_fusion.2
  306.0 2.1 gather_fusion.1
  308.1 4.4 %fusion.50 = f32[8,8,128,128]{3,2,1,0:T(8,128)} fusion(bf16[8,8,128,128]{3,2,1,0:T(8,128)(2,1)} %bitcast.46, bf16[8,8,128,128]{3,2,1,0:T(8,128)(2,1)S(1)} %bitcast.45, pred[8,8]{1,0:T(8,128)(4,1)S(1)} %bitcast.50, pred[8,8]{1,0:T(8,128)(4,1)S(1)} %bitcast.51), kind=kOutput, calls=%fused_computation.9.clone.1 | convolution fusion | flops 270532608 | bytes 8388736 | tf_op jit(solution)/shard_map/while/body/eval_jaxpr/gtrx,gtxc->gtrc/dot_general | solution.py:29
  312.5 0.6 gather_fusion.4
  313.2 6.3 %fusion.51 = f32[2,128,128]{2,0,1:T(2,128)S(1)} fusion(f32[8,8,128,128]{3,2,1,0:T(8,128)} %fusion.50, f32[2,128,128]{2,0,1:T(2,128)S(1)} %get-tuple-element.404, pred[]{:T(512)S(6)} %compare.54, pred[8,8]{1,0:T(8,128)(4,1)S(1)} %iota_compare_fusion.2, s32[8,8]{1,0:T(8,128)S(1)} %bitcast.49), kind=kOutput, calls=%fused_computation.15.clone.1 | convolution fusion | flops 25231616 | bytes 4456769 | tf_op jit(solution)/shard_map/while/body/eval_jaxpr/gtrc,gtw->wrc/dot_general | solution.py:34
  319.6 0.6 gather_fusion
  320.2 0.1 or_reduce_fusion.3
  320.3 0.1 reshape.363
  320.4 2.9 gather_fusion.2
  323.3 1.0 gather_fusion.3
  324.3 0.1 reshape.362
  324.4 1.1 dynamic-slice_bitcast_fusion.2
  325.5 2.1 gather_fusion.1
  327.7 4.4 %fusion.50 = f32[8,8,128,128]{3,2,1,0:T(8,128)} fusion(bf16[8,8,128,128]{3,2,1,0:T(8,128)(2,1)} %bitcast.46, bf16[8,8,128,128]{3,2,1,0:T(8,128)(2,1)S(1)} %bitcast.45, pred[8,8]{1,0:T(8,128)(4,1)S(1)} %bitcast.50, pred[8,8]{1,0:T(8,128)(4,1)S(1)} %bitcast.51), kind=kOutput, calls=%fused_computation.9.clone.1 | convolution fusion | flops 270532608 | bytes 8388736 | tf_op jit(solution)/shard_map/while/body/eval_jaxpr/gtrx,gtxc->gtrc/dot_general | solution.py:29
  332.1 0.6 gather_fusion.4
  332.8 6.3 %fusion.51 = f32[2,128,128]{2,0,1:T(2,128)S(1)} fusion(f32[8,8,128,128]{3,2,1,0:T(8,128)} %fusion.50, f32[2,128,128]{2,0,1:T(2,128)S(1)} %get-tuple-element.404, pred[]{:T(512)S(6)} %compare.54, pred[8,8]{1,0:T(8,128)(4,1)S(1)} %iota_compare_fusion.2, s32[8,8]{1,0:T(8,128)S(1)} %bitcast.49), kind=kOutput, calls=%fused_computation.15.clone.1 | convolution fusion | flops 25231616 | bytes 4456769 | tf_op jit(solution)/shard_map/while/body/eval_jaxpr/gtrc,gtw->wrc/dot_general | solution.py:34
  339.2 0.6 gather_fusion
  339.9 2.9 gather_fusion.2
  342.9 1.0 gather_fusion.3
  343.8 0.1 reshape.362
  343.9 1.1 dynamic-slice_bitcast_fusion.2
  345.0 2.1 gather_fusion.1
  347.2 4.4 %fusion.50 = f32[8,8,128,128]{3,2,1,0:T(8,128)} fusion(bf16[8,8,128,128]{3,2,1,0:T(8,128)(2,1)} %bitcast.46, bf16[8,8,128,128]{3,2,1,0:T(8,128)(2,1)S(1)} %bitcast.45, pred[8,8]{1,0:T(8,128)(4,1)S(1)} %bitcast.50, pred[8,8]{1,0:T(8,128)(4,1)S(1)} %bitcast.51), kind=kOutput, calls=%fused_computation.9.clone.1 | convolution fusion | flops 270532608 | bytes 8388736 | tf_op jit(solution)/shard_map/while/body/eval_jaxpr/gtrx,gtxc->gtrc/dot_general | solution.py:29
  351.6 0.6 gather_fusion.4
  352.3 6.3 %fusion.51 = f32[2,128,128]{2,0,1:T(2,128)S(1)} fusion(f32[8,8,128,128]{3,2,1,0:T(8,128)} %fusion.50, f32[2,128,128]{2,0,1:T(2,128)S(1)} %get-tuple-element.404, pred[]{:T(512)S(6)} %compare.54, pred[8,8]{1,0:T(8,128)(4,1)S(1)} %iota_compare_fusion.2, s32[8,8]{1,0:T(8,128)S(1)} %bitcast.49), kind=kOutput, calls=%fused_computation.15.clone.1 | convolution fusion | flops 25231616 | bytes 4456769 | tf_op jit(solution)/shard_map/while/body/eval_jaxpr/gtrc,gtw->wrc/dot_general | solution.py:34
  358.7 0.6 gather_fusion
  359.4 2.9 gather_fusion.2
  362.4 1.0 gather_fusion.3
  363.4 0.1 reshape.362
  363.4 1.1 dynamic-slice_bitcast_fusion.2
  364.5 2.1 gather_fusion.1
  366.7 4.4 %fusion.50 = f32[8,8,128,128]{3,2,1,0:T(8,128)} fusion(bf16[8,8,128,128]{3,2,1,0:T(8,128)(2,1)} %bitcast.46, bf16[8,8,128,128]{3,2,1,0:T(8,128)(2,1)S(1)} %bitcast.45, pred[8,8]{1,0:T(8,128)(4,1)S(1)} %bitcast.50, pred[8,8]{1,0:T(8,128)(4,1)S(1)} %bitcast.51), kind=kOutput, calls=%fused_computation.9.clone.1 | convolution fusion | flops 270532608 | bytes 8388736 | tf_op jit(solution)/shard_map/while/body/eval_jaxpr/gtrx,gtxc->gtrc/dot_general | solution.py:29
  371.1 0.6 gather_fusion.4
  371.8 6.3 %fusion.51 = f32[2,128,128]{2,0,1:T(2,128)S(1)} fusion(f32[8,8,128,128]{3,2,1,0:T(8,128)} %fusion.50, f32[2,128,128]{2,0,1:T(2,128)S(1)} %get-tuple-element.404, pred[]{:T(512)S(6)} %compare.54, pred[8,8]{1,0:T(8,128)(4,1)S(1)} %iota_compare_fusion.2, s32[8,8]{1,0:T(8,128)S(1)} %bitcast.49), kind=kOutput, calls=%fused_computation.15.clone.1 | convolution fusion | flops 25231616 | bytes 4456769 | tf_op jit(solution)/shard_map/while/body/eval_jaxpr/gtrc,gtw->wrc/dot_general | solution.py:34
  378.2 0.6 copy.26
  (44 shorter events, 1.1 us)
Async XLA Ops:
  6.5 152.4 %all-gather.5.cloned.1.call-start = ((), (), s32[]{:S(2)}) async-start(), calls=%async_computation.1 | async-start | bytes 2162688 | tf_op jit(solution)/shard_map/all_gather | solution.py:38
  7.3 292.8 %all-gather.3.cloned.1.call-start = ((), (), s32[]{:S(2)}) async-start(), calls=%async_computation | async-start | bytes 4325376 | tf_op jit(solution)/shard_map/all_gather | solution.py:36
  308.1 4.4 %copy-start = (s32[1,32]{1,0:T(1,128)S(1)}, s32[1,32]{1,0:T(1,128)}, u32[]{:S(2)}) copy-start(s32[1,32]{1,0:T(1,128)} %get-tuple-element.418) | copy-start | bytes 388 | tf_op jit(solution)/shard_map/while
  327.7 4.4 %copy-start = (s32[1,32]{1,0:T(1,128)S(1)}, s32[1,32]{1,0:T(1,128)}, u32[]{:S(2)}) copy-start(s32[1,32]{1,0:T(1,128)} %get-tuple-element.418) | copy-start | bytes 388 | tf_op jit(solution)/shard_map/while
  347.2 4.4 %copy-start = (s32[1,32]{1,0:T(1,128)S(1)}, s32[1,32]{1,0:T(1,128)}, u32[]{:S(2)}) copy-start(s32[1,32]{1,0:T(1,128)} %get-tuple-element.418) | copy-start | bytes 388 | tf_op jit(solution)/shard_map/while
  366.7 4.4 %copy-start = (s32[1,32]{1,0:T(1,128)S(1)}, s32[1,32]{1,0:T(1,128)}, u32[]{:S(2)}) copy-start(s32[1,32]{1,0:T(1,128)} %get-tuple-element.418) | copy-start | bytes 388 | tf_op jit(solution)/shard_map/while
Sparse Core Ops, SparseCore 0:
  10.0 148.8 all-gather.4
  163.4 136.6 all-gather.2
where the time goes:
time: 386 us
  waiting for transfers between devices  293 us (76%)
  matrix products  42.9 us (11%)
  local copies, waits for them, and re-layouts  34.7 us (9%)
  between operations  13.4 us (3%)
    all_gather x1, waiting for transfers between devices, per_device(): piece = lax.all_gather(right_blocks, 'row', axis=0, tiled=True)  150 us
    all_gather x1, waiting for transfers between devices, per_device(): left_all = lax.all_gather(left_blocks, 'col', axis=0, tiled=True)  141 us
    dot_general x4, matrix products, tile_terms(): jnp.einsum('gtrc,gtw->wrc', products, weight, precision=lax.Precision.HIG...  25.4 us
    dot_general x4, matrix products, tile_terms(): jnp.einsum('gtrx,gtxc->gtrc', left_pick, right_pick, preferred_element_ty...  17.5 us
    gather x4, local copies, waits for them, and re-layouts, step(): left_now = left_all[(inner - my_row) % col_size]  11.7 us
    gather x8, local copies, waits for them, and re-layouts, tile_terms(): jnp.take_along_axis(right_tiles, pairs_now[..., 1][..., None, None], axis=1)  8.81 us
  transfers between devices with their start and end apart: 2, of which 2 were waited for; matrix products, arithmetic and copies ran while one was open for 0% of the time, Pallas kernels for 0%

commit v1 on v0

v1 whole, which is shorter than its diff:
```python
import jax
import jax.numpy as jnp
from jax import lax
from jax.experimental import pallas as pl
from jax.experimental.pallas import tpu as pltpu
from jax.sharding import Mesh
from jax.sharding import PartitionSpec as P

NX, NZL, NZH, NY, NCORE = 8, 4, 2, 8, 2
NK = 32
NA, NB, NC, NT = 4, 2, 2, 8
BS = 128
GROUP = 8
ZERO = NK * NB


def rot(size, shift):
    return [(s, (s + shift) % size) for s in range(size)]


def slot_lists(pair_lists, pair_count, row, col, zh, y, c):
    pairs = pair_lists.reshape(NK * NT, 3)
    flat = jnp.arange(NK * NT, dtype=jnp.int32)
    k = flat // NT
    live = flat % NT < jnp.repeat(pair_count.reshape(NK), NT)
    source = (k - row) % NK
    from_zh, from_y, from_c = source // (NY * NCORE), source // NCORE % NY, source % NCORE
    place = jnp.where(from_c == c, 0, NY) + (from_y - y) % NY
    place = place * 2 + jnp.where(from_zh == zh, 0, 1)
    left = place * NA + pairs[:, 0]
    right = (k - col) % NK * NB + pairs[:, 1]
    code = left * 128 + right
    target = jnp.arange(NC, dtype=jnp.int32)[:, None]
    mine = live[None] & (pairs[:, 2][None] == target)
    seat = jnp.sum(mine[:, None, :] & (flat[None, None, :] < flat[None, :, None]), axis=-1)
    hit = mine[:, :, None] & (seat[:, :, None] == flat[None, None, :])
    listed = jnp.sum(jnp.where(hit, code[None, :, None] - ZERO, 0), axis=1) + ZERO
    return listed.astype(jnp.int32), jnp.sum(mine, axis=1).astype(jnp.int32)


def product_kernel(plan, codes, counts, *refs):
    pieces, (out, left, right, sems) = refs[: len(refs) - 4], refs[len(refs) - 4 :]
    copies = []
    for piece, (which, start, size, at) in plan:
        target = right if which else left
        copies.append(
            pltpu.make_async_copy(
                pieces[piece].at[pl.ds(start, size)],
                target.at[pl.ds(at, size)],
                sems.at[len(copies)],
            )
        )
    for copy in copies:
        copy.start()
    right[ZERO] = jnp.zeros((BS, BS), jnp.bfloat16)
    for copy in copies:
        copy.wait()

    def part(n, step):
        first, second = [], []
        for g in range(GROUP):
            code = codes[n, step * GROUP + g]
            first.append(left[code // 128])
            second.append(right[code % 128])
        return jnp.dot(
            jnp.concatenate(first, axis=1),
            jnp.concatenate(second, axis=0),
            preferred_element_type=jnp.float32,
        )

    steps = (jnp.maximum(counts[0], counts[1]) + GROUP - 1) // GROUP
    zero = jnp.zeros((BS, BS), jnp.float32)

    def step(turn, total):
        return total[0] + part(0, turn), total[1] + part(1, turn)

    total = lax.fori_loop(0, steps, step, (zero, zero))
    out[0] = total[0].astype(jnp.bfloat16)
    out[1] = total[1].astype(jnp.bfloat16)


def per_device(left_blocks, right_blocks, pair_lists, pair_count):
    zh, y, c = lax.axis_index("zh"), lax.axis_index("y"), lax.axis_index("c")
    row = lax.axis_index("x") * NZL + lax.axis_index("zl")
    col = (zh * NY + y) * NCORE + c

    other = lax.ppermute(left_blocks, "zh", rot(NZH, 1))
    spread = jnp.broadcast_to(right_blocks[None], (NZL,) + right_blocks.shape)
    right_z = lax.all_to_all(spread.reshape(NZL * NB, BS, BS), "zl", 0, 0, tiled=True)
    right_all = lax.all_gather(right_z, "x", axis=0, tiled=True)

    base = jnp.concatenate([left_blocks, other], axis=0)
    up, down = [base], [base]
    for _ in range(3):
        up.append(lax.ppermute(up[-1], "y", rot(NY, 1)))
        down.append(lax.ppermute(down[-1], "y", rot(NY, -1)))
    up.append(lax.ppermute(up[3][:NA], "y", rot(NY, 1)))
    down.append(lax.ppermute(down[3][NA:], "y", rot(NY, -1)))

    near = jnp.concatenate([base, up[1], down[1], up[2], down[2]], axis=0)
    far = jnp.concatenate([up[3], down[3], up[4], down[4]], axis=0)
    near_swap = lax.ppermute(near, "c", rot(NCORE, 1))
    far_swap = lax.ppermute(far, "c", rot(NCORE, 1))

    codes, counts = slot_lists(pair_lists, pair_count, row, col, zh, y, c)

    tile = 2 * NA
    plan = []
    for half, (near_piece, far_piece) in enumerate(((0, 1), (2, 3))):
        for at, distance in enumerate((0, -1, 1, -2, 2)):
            plan.append((near_piece, (0, at * tile, tile, (half * NY + distance % NY) * tile)))
        for at, distance in enumerate((-3, 3, 4)):
            plan.append((far_piece, (0, at * tile, tile, (half * NY + distance % NY) * tile)))
    plan.append((4, (1, 0, ZERO, 0)))

    def kernel(*refs):
        product_kernel(plan, *refs)

    return pl.pallas_call(
        kernel,
        out_shape=jax.ShapeDtypeStruct((NC, BS, BS), jnp.bfloat16),
        in_specs=[pl.BlockSpec(memory_space=pltpu.SMEM)] * 2
        + [pl.BlockSpec(memory_space=pl.ANY)] * 5,
        out_specs=pl.BlockSpec(memory_space=pltpu.VMEM),
        scratch_shapes=[
            pltpu.VMEM((2 * NY * tile, BS, BS), jnp.bfloat16),
            pltpu.VMEM((ZERO + 1, BS, BS), jnp.bfloat16),
            pltpu.SemaphoreType.DMA((len(plan),)),
        ],
        compiler_params=pltpu.CompilerParams(vmem_limit_bytes=16 * 1024 * 1024),
        cost_estimate=pl.CostEstimate(
            flops=2 * 128 * BS**3, bytes_accessed=6 * 1024 * 1024, transcendentals=0
        ),
        name="block_products",
    )(codes, counts, near, far, near_swap, far_swap, right_all)


def solution(mesh):
    parts = Mesh(mesh.devices.reshape(NX, NZL, NZH, NY, NCORE), ("x", "zl", "zh", "y", "c"))
    row, col = ("x", "zl"), ("zh", "y", "c")
    return jax.shard_map(
        per_device,
        mesh=parts,
        in_specs=(P(row, col, None), P(col, row, None), P(row + col, None, None), P(row + col, None)),
        out_specs=P(row + col, None, None),
        check_vma=False,
    )
```

time: 386 us -> 110 us (0.28)
  the two profiles are of different devices: /device:TPU:1 before, /device:TPU:140 now
where the time goes in v1:
time: 110 us
  starting transfers between devices  45.9 us (42%)
  waiting for transfers between devices  18.5 us (17%)
  blocking collectives  15.7 us (14%)
  between operations  13.7 us (12%)
  local copies, waits for them, and re-layouts  9.49 us (9%)
  Pallas kernels  5.57 us (5%)
    ppermute x3, starting transfers between devices, per_device(): down.append(lax.ppermute(down[-1], 'y', rot(NY, -1)))  17.5 us
    all_to_all x1, blocking collectives, per_device(): lax.all_to_all(spread.reshape(NZL * NB, BS, BS), 'zl', 0, 0, tiled=True)  15.7 us
    ppermute x1, starting transfers between devices, per_device(): other = lax.ppermute(left_blocks, 'zh', rot(NZH, 1))  11.9 us
    unnamed x22, local copies, waits for them, and re-layouts  7.34 us
    ppermute x3, waiting for transfers between devices, per_device(): down.append(lax.ppermute(down[-1], 'y', rot(NY, -1)))  5.84 us
    ppermute x3, starting transfers between devices, per_device(): up.append(lax.ppermute(up[-1], 'y', rot(NY, 1)))  5.74 us
    pallas_call x1, Pallas kernels, per_device(): pl.pallas_call(kernel, out_shape=jax.ShapeDtypeStruct((NC, BS, BS), jnp.b...  5.57 us
    ppermute x1, starting transfers between devices, per_device(): down.append(lax.ppermute(down[3][NA:], 'y', rot(NY, -1)))  5.13 us
  transfers between devices with their start and end apart: 12, of which 7 were waited for; matrix products, arithmetic and copies ran while one was open for 4% of the time, Pallas kernels for 0%

profile of v1, /device:TPU:140, one launch (start us, length us, event | category | flops | bytes accessed | tf_op | source)
XLA Modules:
  0.0 109.5 jit_solution(3310266105025398070)
XLA Ops:
  6.5 0.0 copy-start.5
  6.5 0.0 copy-start.6
  6.5 0.0 all-gather.2.cloned.1.call-start
  6.5 0.9 broadcast_in_dim.21
  7.4 15.7 %all_to_all.5 = bf16[8,128,128]{2,1,0:T(8,128)(2,1)} all-to-all(bf16[8,128,128]{2,1,0:T(8,128)(2,1)S(1)} %bitcast.8), channel_id=1, replica_groups=mesh['x'=8,'zl'=4,'zh'=2,'y'=8,'c'=2] {'zl'}, dimensions={0} | all-to-all | bytes 524288 | tf_op jit(solution)/shard_map/all_to_all | solution.py:89
  23.1 0.0 all-gather.2.cloned.1.call-update
  23.2 11.9 %collective-permute-start = (bf16[4,128,128]{2,1,0:T(8,128)(2,1)}, bf16[4,128,128]{2,1,0:T(8,128)(2,1)S(1)}, u32[]{:S(2)}, u32[]{:S(2)}) collective-permute-start(bf16[4,128,128]{2,1,0:T(8,128)(2,1)} %param.4), channel_id=1, source_target_pairs={{0,16},{16,0},{1,17},{17,1},{2,18},{18,2},{3,19},{19,3},{4,20},{20... | collective-permute-start | bytes 393224 | tf_op jit(solution)/shard_map/ppermute | solution.py:87
  35.0 0.9 constant_dynamic-update-slice_fusion.1
  36.0 5.0 %collective-permute-done = bf16[4,128,128]{2,1,0:T(8,128)(2,1)S(1)} collective-permute-done((bf16[4,128,128]{2,1,0:T(8,128)(2,1)}, bf16[4,128,128]{2,1,0:T(8,128)(2,1)S(1)}, u32[]{:S(2)}, u32[]{:S(2)}) %collective-permute-start) | collective-permute-done | bytes 131104 | tf_op jit(solution)/shard_map/ppermute | solution.py:87
  41.0 0.1 constant_dynamic-update-slice_fusion
  41.0 6.2 %collective-permute-start.2 = (bf16[8,128,128]{2,1,0:T(8,128)(2,1)S(1)}, bf16[8,128,128]{2,1,0:T(8,128)(2,1)S(1)}, u32[]{:S(2)}, u32[]{:S(2)}) collective-permute-start(bf16[8,128,128]{2,1,0:T(8,128)(2,1)S(1)} %get-tuple-element.7), channel_id=1, source_target_pairs={{0,14},{2,0},{4,2},{6,4},{8,6},{10,8},{12,10},{14,12},{1,15},{3,1}... | collective-permute-start | bytes 786440 | tf_op jit(solution)/shard_map/ppermute | solution.py:96
  47.2 1.9 %collective-permute-start.1 = (bf16[8,128,128]{2,1,0:T(8,128)(2,1)S(1)}, bf16[8,128,128]{2,1,0:T(8,128)(2,1)S(1)}, u32[]{:S(2)}, u32[]{:S(2)}) collective-permute-start(bf16[8,128,128]{2,1,0:T(8,128)(2,1)S(1)} %get-tuple-element.7), channel_id=1, source_target_pairs={{0,2},{2,4},{4,6},{6,8},{8,10},{10,12},{12,14},{14,0},{1,3},{3,5},... | collective-permute-start | bytes 786440 | tf_op jit(solution)/shard_map/ppermute | solution.py:95
  49.1 0.0 copy-done.5
  49.1 0.0 copy-done.6
  49.2 0.1 broadcast_in_dim.18
  49.2 0.1 reshape.227
  49.3 2.6 %collective-permute-done.2 = bf16[8,128,128]{2,1,0:T(8,128)(2,1)S(1)} collective-permute-done((bf16[8,128,128]{2,1,0:T(8,128)(2,1)S(1)}, bf16[8,128,128]{2,1,0:T(8,128)(2,1)S(1)}, u32[]{:S(2)}, u32[]{:S(2)}) %collective-permute-start.2) | collective-permute-done | bytes 262176 | tf_op jit(solution)/shard_map/ppermute | solution.py:96
  51.9 5.6 %collective-permute-start.4 = (bf16[8,128,128]{2,1,0:T(8,128)(2,1)S(1)}, bf16[8,128,128]{2,1,0:T(8,128)(2,1)}, u32[]{:S(2)}, u32[]{:S(2)}) collective-permute-start(bf16[8,128,128]{2,1,0:T(8,128)(2,1)S(1)} %collective-permute-done.2), channel_id=1, source_target_pairs={{0,14},{2,0},{4,2},{6,4},{8,6},{10,8},{12,10},{14,12},{1,15},{3,1}... | collective-permute-start | bytes 786440 | tf_op jit(solution)/shard_map/ppermute | solution.py:96
  57.5 0.3 collective-permute-done.1
  57.8 1.9 %collective-permute-start.3 = (bf16[8,128,128]{2,1,0:T(8,128)(2,1)S(1)}, bf16[8,128,128]{2,1,0:T(8,128)(2,1)S(1)}, u32[]{:S(2)}, u32[]{:S(2)}) collective-permute-start(bf16[8,128,128]{2,1,0:T(8,128)(2,1)S(1)} %collective-permute-done.1), channel_id=1, source_target_pairs={{0,2},{2,4},{4,6},{6,8},{8,10},{10,12},{12,14},{14,0},{1,3},{3,5},... | collective-permute-start | bytes 786440 | tf_op jit(solution)/shard_map/ppermute | solution.py:95
  59.8 3.2 %collective-permute-done.4 = bf16[8,128,128]{2,1,0:T(8,128)(2,1)} collective-permute-done((bf16[8,128,128]{2,1,0:T(8,128)(2,1)S(1)}, bf16[8,128,128]{2,1,0:T(8,128)(2,1)}, u32[]{:S(2)}, u32[]{:S(2)}) %collective-permute-start.4) | collective-permute-done | bytes 262176 | tf_op jit(solution)/shard_map/ppermute | solution.py:96
  63.1 5.7 %collective-permute-start.6 = (bf16[8,128,128]{2,1,0:T(8,128)(2,1)}, bf16[8,128,128]{2,1,0:T(8,128)(2,1)S(1)}, u32[]{:S(2)}, u32[]{:S(2)}) collective-permute-start(bf16[8,128,128]{2,1,0:T(8,128)(2,1)} %collective-permute-done.4), channel_id=1, source_target_pairs={{0,14},{2,0},{4,2},{6,4},{8,6},{10,8},{12,10},{14,12},{1,15},{3,1}... | collective-permute-start | bytes 786440 | tf_op jit(solution)/shard_map/ppermute | solution.py:96
  68.8 0.8 collective-permute-done.3
  69.6 1.9 %collective-permute-start.5 = (bf16[8,128,128]{2,1,0:T(8,128)(2,1)S(1)}, bf16[8,128,128]{2,1,0:T(8,128)(2,1)S(1)}, u32[]{:S(2)}, u32[]{:S(2)}) collective-permute-start(bf16[8,128,128]{2,1,0:T(8,128)(2,1)S(1)} %collective-permute-done.3), channel_id=1, source_target_pairs={{0,2},{2,4},{4,6},{6,8},{8,10},{10,12},{12,14},{14,0},{1,3},{3,5},... | collective-permute-start | bytes 786440 | tf_op jit(solution)/shard_map/ppermute | solution.py:95
  71.6 1.0 constant_dynamic-update-slice_fusion.2.refs_2_
  72.6 1.9 %collective-permute-start.9 = (bf16[40,128,128]{2,1,0:T(8,128)(2,1)S(1)}, bf16[40,128,128]{2,1,0:T(8,128)(2,1)S(1)}, u32[]{:S(2)}, u32[]{:S(2)}) collective-permute-start(bf16[40,128,128]{2,1,0:T(8,128)(2,1)S(1)} %constant_dynamic-update-slice_fusion.2.refs_2_), channel_id=1, source_target_pairs={{0,1},{1,0},{2,3},{3,2},{4,5},{5,4},{6,7},{7,6},{8,9},{9,8},{10,11... | collective-permute-start | bytes 3932168 | tf_op jit(solution)/shard_map/ppermute | solution.py:102
  74.5 0.1 convert_reduce_fusion.1
  74.6 0.0 collective-permute-done.6
  74.6 0.0 copy-start.3
  74.7 5.1 %collective-permute-start.8 = (bf16[4,128,128]{2,1,0:T(8,128)(2,1)S(1)}, bf16[4,128,128]{2,1,0:T(8,128)(2,1)S(1)}, u32[]{:S(2)}, u32[]{:S(2)}) collective-permute-start(bf16[4,128,128]{2,1,0:T(8,128)(2,1)S(1)} %slice.24), channel_id=1, source_target_pairs={{0,14},{2,0},{4,2},{6,4},{8,6},{10,8},{12,10},{14,12},{1,15},{3,1}... | collective-permute-start | bytes 393224 | tf_op jit(solution)/shard_map/ppermute | solution.py:98
  79.8 0.0 collective-permute-done.5
  79.8 0.0 copy-start.4
  79.8 0.0 copy-done.3
  79.8 0.7 copy-done.4
  80.5 1.9 %collective-permute-start.7 = (bf16[4,128,128]{2,1,0:T(8,128)(2,1)S(1)}, bf16[4,128,128]{2,1,0:T(8,128)(2,1)S(1)}, u32[]{:S(2)}, u32[]{:S(2)}) collective-permute-start(bf16[4,128,128]{2,1,0:T(8,128)(2,1)S(1)} %slice.23), channel_id=1, source_target_pairs={{0,2},{2,4},{4,6},{6,8},{8,10},{10,12},{12,14},{14,0},{1,3},{3,5},... | collective-permute-start | bytes 393224 | tf_op jit(solution)/shard_map/ppermute | solution.py:97
  82.4 1.0 constant_dynamic-update-slice_fusion.11
  83.4 1.0 constant_dynamic-update-slice_fusion.10
  84.4 4.8 %collective-permute-done.7 = bf16[4,128,128]{2,1,0:T(8,128)(2,1)S(1)} collective-permute-done((bf16[4,128,128]{2,1,0:T(8,128)(2,1)S(1)}, bf16[4,128,128]{2,1,0:T(8,128)(2,1)S(1)}, u32[]{:S(2)}, u32[]{:S(2)}) %collective-permute-start.7) | collective-permute-done | bytes 131104 | tf_op jit(solution)/shard_map/ppermute | solution.py:97
  89.3 0.0 collective-permute-done.8
  89.3 1.9 %collective-permute-start.10 = (bf16[24,128,128]{2,1,0:T(8,128)(2,1)S(1)}, bf16[24,128,128]{2,1,0:T(8,128)(2,1)S(1)}, u32[]{:S(2)}, u32[]{:S(2)}) collective-permute-start(bf16[24,128,128]{2,1,0:T(8,128)(2,1)S(1)} %constant_dynamic-update-slice_fusion.8.refs_3_), channel_id=1, source_target_pairs={{0,1},{1,0},{2,3},{3,2},{4,5},{5,4},{6,7},{7,6},{8,9},{9,8},{10,11... | collective-permute-start | bytes 2359304 | tf_op jit(solution)/shard_map/ppermute | solution.py:103
  91.3 0.1 convert_reduce_fusion
  91.5 0.3 select_reduce_fusion
  91.7 1.8 %collective-permute-done.10.refs_5_ = bf16[24,128,128]{2,1,0:T(8,128)(2,1)S(1)} collective-permute-done((bf16[24,128,128]{2,1,0:T(8,128)(2,1)S(1)}, bf16[24,128,128]{2,1,0:T(8,128)(2,1)S(1)}, u32[]{:S(2)}, u32[]{:S(2)}) %collective-permute-start.10) | collective-permute-done | bytes 786464 | tf_op jit(solution)/shard_map/ppermute | solution.py:103
  93.5 0.9 copy-done.1
  94.4 0.0 collective-permute-done.9.refs_4_
  94.4 1.6 %copy-done = bf16[64,128,128]{2,1,0:T(8,128)(2,1)S(1)} copy-done((bf16[64,128,128]{2,1,0:T(8,128)(2,1)S(1)}, bf16[64,128,128]{2,1,0:T(8,128)(2,1)}, u32[]{:S(2)}) %copy-start) | copy-done | bytes 2097176
  96.0 1.1 %copy-done.2 = bf16[24,128,128]{2,1,0:T(8,128)(2,1)S(1)} copy-done((bf16[24,128,128]{2,1,0:T(8,128)(2,1)S(1)}, bf16[24,128,128]{2,1,0:T(8,128)(2,1)}, u32[]{:S(2)}) %copy-start.2) | copy-done | bytes 786456
  97.1 5.6 %block_products.1 = bf16[2,128,128]{2,1,0:T(8,128)(2,1)} custom-call(s32[2,256]{1,0:T(2,128)S(1)} %broadcast_add_fusion.refs_0_, s32[2]{0:T(128)S(1)} %get-tuple-element.5.refs_1_, bf16[40,128,128]{2,1,0:T(8,128)(2,1)S(1)} %constant_dynamic-update-slice_fusion.2.refs_2_, bf16[24,128,128]{2,1,0:T(8,128)(2,1)S(1)} %constant_dynamic-update-slice_fusion.8.refs_3_, ...), custom_call_target="tpu_custom_call" | custom-call | flops 536870912 | bytes 6291456 | tf_op jit(solution)/shard_map/block_products/pallas_call | solution.py:119
  (17 shorter events, 0.3 us)
Async XLA Ops:
  6.5 42.6 %copy-start.5 = (s32[1,256,3]{1,0,2:T(1,128)S(1)}, s32[1,256,3]{1,0,2:T(1,128)}, u32[]{:S(2)}) copy-start(s32[1,256,3]{1,0,2:T(1,128)} %param.6) | copy-start | bytes 9220
  6.5 42.6 %copy-start.6 = (s32[1,32]{1,0:T(1,128)S(1)}, s32[1,32]{1,0:T(1,128)}, u32[]{:S(2)}) copy-start(s32[1,32]{1,0:T(1,128)} %param.7) | copy-start | bytes 388
  6.5 87.8 %all-gather.2.cloned.1.call-start = ((), (), s32[]{:S(2)}) async-start(), calls=%async_computation.1 | async-start | bytes 2359296 | tf_op jit(solution)/shard_map/all_gather | solution.py:90
  23.2 17.8 %collective-permute-start = (bf16[4,128,128]{2,1,0:T(8,128)(2,1)}, bf16[4,128,128]{2,1,0:T(8,128)(2,1)S(1)}, u32[]{:S(2)}, u32[]{:S(2)}) collective-permute-start(bf16[4,128,128]{2,1,0:T(8,128)(2,1)} %param.4), channel_id=1, source_target_pairs={{0,16},{16,0},{1,17},{17,1},{2,18},{18,2},{3,19},{19,3},{4,20},{20... | collective-permute-start | bytes 393224 | tf_op jit(solution)/shard_map/ppermute | solution.py:87
  41.0 10.9 %collective-permute-start.2 = (bf16[8,128,128]{2,1,0:T(8,128)(2,1)S(1)}, bf16[8,128,128]{2,1,0:T(8,128)(2,1)S(1)}, u32[]{:S(2)}, u32[]{:S(2)}) collective-permute-start(bf16[8,128,128]{2,1,0:T(8,128)(2,1)S(1)} %get-tuple-element.7), channel_id=1, source_target_pairs={{0,14},{2,0},{4,2},{6,4},{8,6},{10,8},{12,10},{14,12},{1,15},{3,1}... | collective-permute-start | bytes 786440 | tf_op jit(solution)/shard_map/ppermute | solution.py:96
  47.2 10.6 %collective-permute-start.1 = (bf16[8,128,128]{2,1,0:T(8,128)(2,1)S(1)}, bf16[8,128,128]{2,1,0:T(8,128)(2,1)S(1)}, u32[]{:S(2)}, u32[]{:S(2)}) collective-permute-start(bf16[8,128,128]{2,1,0:T(8,128)(2,1)S(1)} %get-tuple-element.7), channel_id=1, source_target_pairs={{0,2},{2,4},{4,6},{6,8},{8,10},{10,12},{12,14},{14,0},{1,3},{3,5},... | collective-permute-start | bytes 786440 | tf_op jit(solution)/shard_map/ppermute | solution.py:95
  51.9 11.1 %collective-permute-start.4 = (bf16[8,128,128]{2,1,0:T(8,128)(2,1)S(1)}, bf16[8,128,128]{2,1,0:T(8,128)(2,1)}, u32[]{:S(2)}, u32[]{:S(2)}) collective-permute-start(bf16[8,128,128]{2,1,0:T(8,128)(2,1)S(1)} %collective-permute-done.2), channel_id=1, source_target_pairs={{0,14},{2,0},{4,2},{6,4},{8,6},{10,8},{12,10},{14,12},{1,15},{3,1}... | collective-permute-start | bytes 786440 | tf_op jit(solution)/shard_map/ppermute | solution.py:96
  57.8 11.8 %collective-permute-start.3 = (bf16[8,128,128]{2,1,0:T(8,128)(2,1)S(1)}, bf16[8,128,128]{2,1,0:T(8,128)(2,1)S(1)}, u32[]{:S(2)}, u32[]{:S(2)}) collective-permute-start(bf16[8,128,128]{2,1,0:T(8,128)(2,1)S(1)} %collective-permute-done.1), channel_id=1, source_target_pairs={{0,2},{2,4},{4,6},{6,8},{8,10},{10,12},{12,14},{14,0},{1,3},{3,5},... | collective-permute-start | bytes 786440 | tf_op jit(solution)/shard_map/ppermute | solution.py:95
  63.1 11.6 %collective-permute-start.6 = (bf16[8,128,128]{2,1,0:T(8,128)(2,1)}, bf16[8,128,128]{2,1,0:T(8,128)(2,1)S(1)}, u32[]{:S(2)}, u32[]{:S(2)}) collective-permute-start(bf16[8,128,128]{2,1,0:T(8,128)(2,1)} %collective-permute-done.4), channel_id=1, source_target_pairs={{0,14},{2,0},{4,2},{6,4},{8,6},{10,8},{12,10},{14,12},{1,15},{3,1}... | collective-permute-start | bytes 786440 | tf_op jit(solution)/shard_map/ppermute | solution.py:96
  69.6 10.2 %collective-permute-start.5 = (bf16[8,128,128]{2,1,0:T(8,128)(2,1)S(1)}, bf16[8,128,128]{2,1,0:T(8,128)(2,1)S(1)}, u32[]{:S(2)}, u32[]{:S(2)}) collective-permute-start(bf16[8,128,128]{2,1,0:T(8,128)(2,1)S(1)} %collective-permute-done.3), channel_id=1, source_target_pairs={{0,2},{2,4},{4,6},{6,8},{8,10},{10,12},{12,14},{14,0},{1,3},{3,5},... | collective-permute-start | bytes 786440 | tf_op jit(solution)/shard_map/ppermute | solution.py:95
  72.6 21.8 %collective-permute-start.9 = (bf16[40,128,128]{2,1,0:T(8,128)(2,1)S(1)}, bf16[40,128,128]{2,1,0:T(8,128)(2,1)S(1)}, u32[]{:S(2)}, u32[]{:S(2)}) collective-permute-start(bf16[40,128,128]{2,1,0:T(8,128)(2,1)S(1)} %constant_dynamic-update-slice_fusion.2.refs_2_), channel_id=1, source_target_pairs={{0,1},{1,0},{2,3},{3,2},{4,5},{5,4},{6,7},{7,6},{8,9},{9,8},{10,11... | collective-permute-start | bytes 3932168 | tf_op jit(solution)/shard_map/ppermute | solution.py:102
  74.6 5.2 %copy-start.3 = (bf16[8,128,128]{2,1,0:T(8,128)(2,1)}, bf16[8,128,128]{2,1,0:T(8,128)(2,1)S(1)}, u32[]{:S(2)}) copy-start(bf16[8,128,128]{2,1,0:T(8,128)(2,1)S(1)} %collective-permute-done.6) | copy-start | bytes 786436
  74.7 14.6 %collective-permute-start.8 = (bf16[4,128,128]{2,1,0:T(8,128)(2,1)S(1)}, bf16[4,128,128]{2,1,0:T(8,128)(2,1)S(1)}, u32[]{:S(2)}, u32[]{:S(2)}) collective-permute-start(bf16[4,128,128]{2,1,0:T(8,128)(2,1)S(1)} %slice.24), channel_id=1, source_target_pairs={{0,14},{2,0},{4,2},{6,4},{8,6},{10,8},{12,10},{14,12},{1,15},{3,1}... | collective-permute-start | bytes 393224 | tf_op jit(solution)/shard_map/ppermute | solution.py:98
  79.8 0.7 copy-start.4
  80.5 8.7 %collective-permute-start.7 = (bf16[4,128,128]{2,1,0:T(8,128)(2,1)S(1)}, bf16[4,128,128]{2,1,0:T(8,128)(2,1)S(1)}, u32[]{:S(2)}, u32[]{:S(2)}) collective-permute-start(bf16[4,128,128]{2,1,0:T(8,128)(2,1)S(1)} %slice.23), channel_id=1, source_target_pairs={{0,2},{2,4},{4,6},{6,8},{8,10},{10,12},{12,14},{14,0},{1,3},{3,5},... | collective-permute-start | bytes 393224 | tf_op jit(solution)/shard_map/ppermute | solution.py:97
  89.3 4.2 %collective-permute-start.10 = (bf16[24,128,128]{2,1,0:T(8,128)(2,1)S(1)}, bf16[24,128,128]{2,1,0:T(8,128)(2,1)S(1)}, u32[]{:S(2)}, u32[]{:S(2)}) collective-permute-start(bf16[24,128,128]{2,1,0:T(8,128)(2,1)S(1)} %constant_dynamic-update-slice_fusion.8.refs_3_), channel_id=1, source_target_pairs={{0,1},{1,0},{2,3},{3,2},{4,5},{5,4},{6,7},{7,6},{8,9},{9,8},{10,11... | collective-permute-start | bytes 2359304 | tf_op jit(solution)/shard_map/ppermute | solution.py:103
  93.5 0.9 copy-start.1
  94.4 1.6 %copy-start = (bf16[64,128,128]{2,1,0:T(8,128)(2,1)S(1)}, bf16[64,128,128]{2,1,0:T(8,128)(2,1)}, u32[]{:S(2)}) copy-start(bf16[64,128,128]{2,1,0:T(8,128)(2,1)} %all-gather.2.cloned.1.call-done.refs_6_) | copy-start | bytes 6291460
  96.0 1.1 %copy-start.2 = (bf16[24,128,128]{2,1,0:T(8,128)(2,1)S(1)}, bf16[24,128,128]{2,1,0:T(8,128)(2,1)}, u32[]{:S(2)}) copy-start(bf16[24,128,128]{2,1,0:T(8,128)(2,1)} %copy-done.1) | copy-start | bytes 2359300
Sparse Core Ops, SparseCore 0:
  23.3 51.8 all-gather.1

commit v2 on v1

v2 whole, which is shorter than its diff:
```python
import jax
import jax.numpy as jnp
from jax import lax
from jax.experimental import pallas as pl
from jax.experimental.pallas import tpu as pltpu
from jax.sharding import Mesh
from jax.sharding import PartitionSpec as P

NX, NZL, NZH, NY, NCORE = 8, 4, 2, 8, 2
NK = 32
NA, NB, NC, NT = 4, 2, 2, 8
BS = 128
GROUP = 8
TILE = 16
ZERO = 2 * NY * TILE


def rot(size, shift):
    return [(s, (s + shift) % size) for s in range(size)]


def slot_lists(pair_lists, pair_count, x, zl, zh, y, c):
    pairs = pair_lists.reshape(NK * NT, 3)
    flat = jnp.arange(NK * NT, dtype=jnp.int32)
    k = flat // NT
    live = flat % NT < jnp.repeat(pair_count.reshape(NK), NT)
    row, col = x * NZL + zl, (zh * NY + y) * NCORE + c
    source = (k - row) % NK
    from_zh, from_y, from_c = source // (NY * NCORE), source // NCORE % NY, source % NCORE
    near = from_zh == zh
    part = jnp.where(from_c == 0, jnp.where(near, 0, 1), jnp.where(near, 3, 2))
    left = (jnp.where(c == 1, 0, NY) + (from_y - y) % NY) * TILE + part * NA + pairs[:, 0]
    holder = (k - col) % NK
    part = (zl - holder % NZL) % NZL
    right = (jnp.where(c == 0, 0, NY) + (holder // NZL - x) % NX) * TILE
    right = right + (part * NCORE + c) * NB + pairs[:, 1]
    code = left * 512 + right
    target = jnp.arange(NC, dtype=jnp.int32)[:, None]
    mine = live[None] & (pairs[:, 2][None] == target)
    seat = jnp.sum(mine[:, None, :] & (flat[None, None, :] < flat[None, :, None]), axis=-1)
    hit = mine[:, :, None] & (seat[:, :, None] == flat[None, None, :])
    listed = jnp.sum(jnp.where(hit, code[None, :, None] - ZERO, 0), axis=1) + ZERO
    return listed.astype(jnp.int32), jnp.sum(mine, axis=1).astype(jnp.int32)


def product_kernel(plan, codes, counts, *refs):
    pieces, (out, held, sems) = refs[:-3], refs[-3:]
    copies = []
    for piece, (size, at) in zip(pieces, plan, strict=True):
        copies.append(
            pltpu.make_async_copy(piece, held.at[pl.ds(at, size)], sems.at[len(copies)])
        )
    for copy in copies:
        copy.start()
    held[ZERO] = jnp.zeros((BS, BS), jnp.bfloat16)
    for copy in copies:
        copy.wait()

    def part(n, step):
        first, second = [], []
        for g in range(GROUP):
            code = codes[n, step * GROUP + g]
            first.append(held[code // 512])
            second.append(held[code % 512])
        return jnp.dot(
            jnp.concatenate(first, axis=1),
            jnp.concatenate(second, axis=0),
            preferred_element_type=jnp.float32,
        )

    steps = (jnp.maximum(counts[0], counts[1]) + GROUP - 1) // GROUP
    zero = jnp.zeros((BS, BS), jnp.float32)

    def step(turn, total):
        return total[0] + part(0, turn), total[1] + part(1, turn)

    total = lax.fori_loop(0, steps, step, (zero, zero))
    out[0] = total[0].astype(jnp.bfloat16)
    out[1] = total[1].astype(jnp.bfloat16)


def along_plane(value, shift):
    pairs = []
    for x in range(NX):
        for y in range(NY):
            place = (x * NY + y) * NCORE
            pairs.append((place, ((x + shift) % NX * NY + y) * NCORE))
            pairs.append((place + 1, (x * NY + (y + shift) % NY) * NCORE + 1))
    return lax.ppermute(value, ("x", "y", "c"), pairs)


def along_z(value, shift, swap):
    pairs = []
    for zl in range(NZL):
        for zh in range(NZH):
            place = (zl * NZH + zh) * NCORE
            pairs.append((place, ((zl + shift) % NZL * NZH + zh) * NCORE))
            pairs.append((place + 1, (zl * NZH + (zh + swap) % NZH) * NCORE + 1))
    return lax.ppermute(value, ("zl", "zh", "c"), pairs)


def to_partner(value):
    return lax.ppermute(value, "c", rot(NCORE, 1))


def per_device(left_blocks, right_blocks, pair_lists, pair_count):
    x, zl, zh, y, c = (lax.axis_index(name) for name in ("x", "zl", "zh", "y", "c"))

    got = to_partner(jnp.where(c == 0, left_blocks, jnp.concatenate([right_blocks] * 2)))
    rights = jnp.concatenate([right_blocks, got[:NB]])
    first, second = jnp.where(c == 0, rights, got), jnp.where(c == 0, rights, left_blocks)
    own = jnp.concatenate(
        [first, along_z(first, 1, 1), along_z(second, 2, 1), along_z(second, 3, 0)]
    )
    up, down = [own], [own]
    for _ in range(3):
        up.append(along_plane(up[-1], 1))
        down.append(along_plane(down[-1], -1))
    up.append(along_plane(up[2][: TILE // 2], 2))
    down.append(along_plane(down[2][TILE // 2 :], -2))

    pieces, plan = [own], [(TILE, 0)]
    for distance in range(1, 4):
        pieces += [up[distance], down[distance]]
        plan += [(TILE, (NY - distance) * TILE), (TILE, distance * TILE)]
    pieces += [up[4], down[4]]
    plan += [(TILE // 2, 4 * TILE), (TILE // 2, 4 * TILE + TILE // 2)]
    pieces += [to_partner(piece) for piece in pieces]
    plan += [(size, NY * TILE + at) for size, at in plan]

    codes, counts = slot_lists(pair_lists, pair_count, x, zl, zh, y, c)

    def kernel(*refs):
        product_kernel(plan, *refs)

    return pl.pallas_call(
        kernel,
        out_shape=jax.ShapeDtypeStruct((NC, BS, BS), jnp.bfloat16),
        in_specs=[pl.BlockSpec(memory_space=pltpu.SMEM)] * 2
        + [pl.BlockSpec(memory_space=pl.ANY)] * len(pieces),
        out_specs=pl.BlockSpec(memory_space=pltpu.VMEM),
        scratch_shapes=[
            pltpu.VMEM((ZERO + 1, BS, BS), jnp.bfloat16),
            pltpu.SemaphoreType.DMA((len(plan),)),
        ],
        compiler_params=pltpu.CompilerParams(vmem_limit_bytes=16 * 1024 * 1024),
        cost_estimate=pl.CostEstimate(
            flops=2 * 128 * BS**3, bytes_accessed=6 * 1024 * 1024, transcendentals=0
        ),
        name="block_products",
    )(codes, counts, *pieces)


def solution(mesh):
    parts = Mesh(mesh.devices.reshape(NX, NZL, NZH, NY, NCORE), ("x", "zl", "zh", "y", "c"))
    row, col = ("x", "zl"), ("zh", "y", "c")
    return jax.shard_map(
        per_device,
        mesh=parts,
        in_specs=(P(row, col, None), P(col, row, None), P(row + col, None, None), P(row + col, None)),
        out_specs=P(row + col, None, None),
        check_vma=False,
    )
```

time: 110 us -> 103 us (0.936)
  the two profiles are of different devices: /device:TPU:140 before, /device:TPU:14 now
where the time goes in v2:
time: 103 us
  starting transfers between devices  68.4 us (66%)
  waiting for transfers between devices  22.7 us (22%)
  Pallas kernels  7.16 us (7%)
  local copies, waits for them, and re-layouts  2.24 us (2%)
  other arithmetic  1.7 us (2%)
    ppermute x8, starting transfers between devices, along_plane(): return lax.ppermute(value, ('x', 'y', 'c'), pairs)  29 us
    ppermute x10, starting transfers between devices, to_partner(): return lax.ppermute(value, 'c', rot(NCORE, 1))  24.4 us
    ppermute x3, starting transfers between devices, along_z(): return lax.ppermute(value, ('zl', 'zh', 'c'), pairs)  15 us
    ppermute x8, waiting for transfers between devices, along_plane(): return lax.ppermute(value, ('x', 'y', 'c'), pairs)  12.3 us
    ppermute x3, waiting for transfers between devices, along_z(): return lax.ppermute(value, ('zl', 'zh', 'c'), pairs)  8.16 us
    pallas_call x1, Pallas kernels, per_device(): pl.pallas_call(kernel, out_shape=jax.ShapeDtypeStruct((NC, BS, BS), jnp.b...  7.16 us
    ppermute x10, waiting for transfers between devices, to_partner(): return lax.ppermute(value, 'c', rot(NCORE, 1))  2.2 us
  transfers between devices with their start and end apart: 21, of which 6 were waited for; matrix products, arithmetic and copies ran while one was open for 1% of the time, Pallas kernels for 0%

profile of v2, /device:TPU:14, one launch (start us, length us, event | category | flops | bytes accessed | tf_op | source)
XLA Modules:
  0.0 102.5 jit_solution(704059294643122839)
XLA Ops:
  0.0 1.0 fusion.1
  1.0 0.0 copy-start
  1.0 2.1 %collective-permute-start = (bf16[4,128,128]{2,1,0:T(8,128)(2,1)S(1)}, bf16[4,128,128]{2,1,0:T(8,128)(2,1)S(1)}, u32[]{:S(2)}, u32[]{:S(2)}) collective-permute-start(bf16[4,128,128]{2,1,0:T(8,128)(2,1)S(1)} %fusion.1), channel_id=1, source_target_pairs={{0,1},{1,0},{2,3},{3,2},{4,5},{5,4},{6,7},{7,6},{8,9},{9,8},{10,11... | collective-permute-start | bytes 393224 | tf_op jit(solution)/shard_map/ppermute | solution.py:103
  3.1 1.3 %collective-permute-done = bf16[4,128,128]{2,1,0:T(8,128)(2,1)S(1)} collective-permute-done((bf16[4,128,128]{2,1,0:T(8,128)(2,1)S(1)}, bf16[4,128,128]{2,1,0:T(8,128)(2,1)S(1)}, u32[]{:S(2)}, u32[]{:S(2)}) %collective-permute-start) | collective-permute-done | bytes 131104 | tf_op jit(solution)/shard_map/ppermute | solution.py:103
  4.5 5.2 %collective-permute-start.1 = (bf16[4,128,128]{2,1,0:T(8,128)(2,1)S(1)}, bf16[4,128,128]{2,1,0:T(8,128)(2,1)S(1)}, u32[]{:S(2)}, u32[]{:S(2)}) collective-permute-start(bf16[4,128,128]{2,1,0:T(8,128)(2,1)S(1)} %get-tuple-element.7), channel_id=1, source_target_pairs={{0,32},{1,17},{16,48},{17,1},{32,64},{33,49},{48,80},{49,33},{64,9... | collective-permute-start | bytes 393224 | tf_op jit(solution)/shard_map/ppermute | solution.py:99
  9.7 7.4 %collective-permute-start.3 = (bf16[4,128,128]{2,1,0:T(8,128)(2,1)S(1)}, bf16[4,128,128]{2,1,0:T(8,128)(2,1)S(1)}, u32[]{:S(2)}, u32[]{:S(2)}) collective-permute-start(bf16[4,128,128]{2,1,0:T(8,128)(2,1)S(1)} %get-tuple-element.8), channel_id=1, source_target_pairs={{0,96},{1,1},{16,112},{17,17},{32,0},{33,33},{48,16},{49,49},{64,3... | collective-permute-start | bytes 393224 | tf_op jit(solution)/shard_map/ppermute | solution.py:99
  17.0 2.5 %collective-permute-start.2 = (bf16[4,128,128]{2,1,0:T(8,128)(2,1)S(1)}, bf16[4,128,128]{2,1,0:T(8,128)(2,1)S(1)}, u32[]{:S(2)}, u32[]{:S(2)}) collective-permute-start(bf16[4,128,128]{2,1,0:T(8,128)(2,1)S(1)} %get-tuple-element.8), channel_id=1, source_target_pairs={{0,64},{1,17},{16,80},{17,1},{32,96},{33,49},{48,112},{49,33},{64,... | collective-permute-start | bytes 393224 | tf_op jit(solution)/shard_map/ppermute | solution.py:99
  19.5 0.0 collective-permute-done.1
  19.5 0.2 collective-permute-done.3
  19.7 8.0 %collective-permute-done.2 = bf16[4,128,128]{2,1,0:T(8,128)(2,1)S(1)} collective-permute-done((bf16[4,128,128]{2,1,0:T(8,128)(2,1)S(1)}, bf16[4,128,128]{2,1,0:T(8,128)(2,1)S(1)}, u32[]{:S(2)}, u32[]{:S(2)}) %collective-permute-start.2) | collective-permute-done | bytes 131104 | tf_op jit(solution)/shard_map/ppermute | solution.py:99
  27.7 0.1 pad_maximum_fusion.refs_2_
  27.7 3.3 %collective-permute-start.5 = (bf16[16,128,128]{2,1,0:T(8,128)(2,1)S(1)}, bf16[16,128,128]{2,1,0:T(8,128)(2,1)S(1)}, u32[]{:S(2)}, u32[]{:S(2)}) collective-permute-start(bf16[16,128,128]{2,1,0:T(8,128)(2,1)S(1)} %pad_maximum_fusion.refs_2_), channel_id=1, source_target_pairs={{0,896},{1,15},{2,898},{3,1},{4,900},{5,3},{6,902},{7,5},{8,904},{... | collective-permute-start | bytes 1572872 | tf_op jit(solution)/shard_map/ppermute | solution.py:89
  31.1 7.4 %collective-permute-start.4 = (bf16[16,128,128]{2,1,0:T(8,128)(2,1)S(1)}, bf16[16,128,128]{2,1,0:T(8,128)(2,1)S(1)}, u32[]{:S(2)}, u32[]{:S(2)}) collective-permute-start(bf16[16,128,128]{2,1,0:T(8,128)(2,1)S(1)} %pad_maximum_fusion.refs_2_), channel_id=1, source_target_pairs={{0,128},{1,3},{2,130},{3,5},{4,132},{5,7},{6,134},{7,9},{8,136},{9... | collective-permute-start | bytes 1572872 | tf_op jit(solution)/shard_map/ppermute | solution.py:89
  38.5 5.2 %collective-permute-done.5.refs_4_ = bf16[16,128,128]{2,1,0:T(8,128)(2,1)S(1)} collective-permute-done((bf16[16,128,128]{2,1,0:T(8,128)(2,1)S(1)}, bf16[16,128,128]{2,1,0:T(8,128)(2,1)S(1)}, u32[]{:S(2)}, u32[]{:S(2)}) %collective-permute-start.5) | collective-permute-done | bytes 524320 | tf_op jit(solution)/shard_map/ppermute | solution.py:89
  43.7 1.9 %collective-permute-start.7 = (bf16[16,128,128]{2,1,0:T(8,128)(2,1)S(1)}, bf16[16,128,128]{2,1,0:T(8,128)(2,1)S(1)}, u32[]{:S(2)}, u32[]{:S(2)}) collective-permute-start(bf16[16,128,128]{2,1,0:T(8,128)(2,1)S(1)} %collective-permute-done.5.refs_4_), channel_id=1, source_target_pairs={{0,896},{1,15},{2,898},{3,1},{4,900},{5,3},{6,902},{7,5},{8,904},{... | collective-permute-start | bytes 1572872 | tf_op jit(solution)/shard_map/ppermute | solution.py:89
  45.6 5.1 %collective-permute-start.12 = (bf16[16,128,128]{2,1,0:T(8,128)(2,1)S(1)}, bf16[16,128,128]{2,1,0:T(8,128)(2,1)S(1)}, u32[]{:S(2)}, u32[]{:S(2)}) collective-permute-start(bf16[16,128,128]{2,1,0:T(8,128)(2,1)S(1)} %pad_maximum_fusion.refs_2_), channel_id=1, source_target_pairs={{0,1},{1,0},{2,3},{3,2},{4,5},{5,4},{6,7},{7,6},{8,9},{9,8},{10,11... | collective-permute-start | bytes 1572872 | tf_op jit(solution)/shard_map/ppermute | solution.py:103
  50.7 2.6 %collective-permute-start.6 = (bf16[16,128,128]{2,1,0:T(8,128)(2,1)S(1)}, bf16[16,128,128]{2,1,0:T(8,128)(2,1)S(1)}, u32[]{:S(2)}, u32[]{:S(2)}) collective-permute-start(bf16[16,128,128]{2,1,0:T(8,128)(2,1)S(1)} %collective-permute-done.4.refs_3_), channel_id=1, source_target_pairs={{0,128},{1,3},{2,130},{3,5},{4,132},{5,7},{6,134},{7,9},{8,136},{9... | collective-permute-start | bytes 1572872 | tf_op jit(solution)/shard_map/ppermute | solution.py:89
  53.3 1.9 %collective-permute-start.14 = (bf16[16,128,128]{2,1,0:T(8,128)(2,1)S(1)}, bf16[16,128,128]{2,1,0:T(8,128)(2,1)}, u32[]{:S(2)}, u32[]{:S(2)}) collective-permute-start(bf16[16,128,128]{2,1,0:T(8,128)(2,1)S(1)} %collective-permute-done.5.refs_4_), channel_id=1, source_target_pairs={{0,1},{1,0},{2,3},{3,2},{4,5},{5,4},{6,7},{7,6},{8,9},{9,8},{10,11... | collective-permute-start | bytes 1572872 | tf_op jit(solution)/shard_map/ppermute | solution.py:103
  55.2 0.0 copy-start.2
  55.2 0.7 copy-done.2
  55.9 2.4 %collective-permute-start.13 = (bf16[16,128,128]{2,1,0:T(8,128)(2,1)S(1)}, bf16[16,128,128]{2,1,0:T(8,128)(2,1)}, u32[]{:S(2)}, u32[]{:S(2)}) collective-permute-start(bf16[16,128,128]{2,1,0:T(8,128)(2,1)S(1)} %collective-permute-done.4.refs_3_), channel_id=1, source_target_pairs={{0,1},{1,0},{2,3},{3,2},{4,5},{5,4},{6,7},{7,6},{8,9},{9,8},{10,11... | collective-permute-start | bytes 1572872 | tf_op jit(solution)/shard_map/ppermute | solution.py:103
  58.3 0.0 collective-permute-done.7.refs_6_
  58.3 0.7 slice.29
  59.0 4.1 %collective-permute-start.11 = (bf16[8,128,128]{2,1,0:T(8,128)(2,1)}, bf16[8,128,128]{2,1,0:T(8,128)(2,1)S(1)}, u32[]{:S(2)}, u32[]{:S(2)}) collective-permute-start(bf16[8,128,128]{2,1,0:T(8,128)(2,1)} %slice.29), channel_id=1, source_target_pairs={{0,768},{1,13},{2,770},{3,15},{4,772},{5,1},{6,774},{7,3},{8,776},... | collective-permute-start | bytes 786440 | tf_op jit(solution)/shard_map/ppermute | solution.py:89
  63.2 0.0 collective-permute-done.12.refs_11_
  63.2 3.3 %collective-permute-start.9 = (bf16[16,128,128]{2,1,0:T(8,128)(2,1)S(1)}, bf16[16,128,128]{2,1,0:T(8,128)(2,1)}, u32[]{:S(2)}, u32[]{:S(2)}) collective-permute-start(bf16[16,128,128]{2,1,0:T(8,128)(2,1)S(1)} %collective-permute-done.7.refs_6_), channel_id=1, source_target_pairs={{0,896},{1,15},{2,898},{3,1},{4,900},{5,3},{6,902},{7,5},{8,904},{... | collective-permute-start | bytes 1572872 | tf_op jit(solution)/shard_map/ppermute | solution.py:89
  66.5 0.0 collective-permute-done.6.refs_5_
  66.6 3.7 %collective-permute-start.8 = (bf16[16,128,128]{2,1,0:T(8,128)(2,1)S(1)}, bf16[16,128,128]{2,1,0:T(8,128)(2,1)}, u32[]{:S(2)}, u32[]{:S(2)}) collective-permute-start(bf16[16,128,128]{2,1,0:T(8,128)(2,1)S(1)} %collective-permute-done.6.refs_5_), channel_id=1, source_target_pairs={{0,128},{1,3},{2,130},{3,5},{4,132},{5,7},{6,134},{7,9},{8,136},{9... | collective-permute-start | bytes 1572872 | tf_op jit(solution)/shard_map/ppermute | solution.py:89
  70.3 0.0 copy-start.3
  70.3 0.6 copy-done.3
  71.0 0.1 broadcast_in_dim.16
  71.1 0.1 reshape.279
  71.2 0.0 collective-permute-done.14.refs_13_
  71.2 2.6 %collective-permute-start.10 = (bf16[8,128,128]{2,1,0:T(8,128)(2,1)S(1)}, bf16[8,128,128]{2,1,0:T(8,128)(2,1)S(1)}, u32[]{:S(2)}, u32[]{:S(2)}) collective-permute-start(bf16[8,128,128]{2,1,0:T(8,128)(2,1)S(1)} %slice.28), channel_id=1, source_target_pairs={{0,256},{1,5},{2,258},{3,7},{4,260},{5,9},{6,262},{7,11},{8,264},{... | collective-permute-start | bytes 786440 | tf_op jit(solution)/shard_map/ppermute | solution.py:89
  73.8 0.0 collective-permute-done.11.refs_10_
  73.8 1.9 %collective-permute-start.20 = (bf16[8,128,128]{2,1,0:T(8,128)(2,1)S(1)}, bf16[8,128,128]{2,1,0:T(8,128)(2,1)S(1)}, u32[]{:S(2)}, u32[]{:S(2)}) collective-permute-start(bf16[8,128,128]{2,1,0:T(8,128)(2,1)S(1)} %collective-permute-done.11.refs_10_), channel_id=1, source_target_pairs={{0,1},{1,0},{2,3},{3,2},{4,5},{5,4},{6,7},{7,6},{8,9},{9,8},{10,11... | collective-permute-start | bytes 786440 | tf_op jit(solution)/shard_map/ppermute | solution.py:103
  75.7 0.1 convert_reduce_fusion.1
  75.9 2.4 %collective-permute-start.16 = (bf16[16,128,128]{2,1,0:T(8,128)(2,1)S(1)}, bf16[16,128,128]{2,1,0:T(8,128)(2,1)S(1)}, u32[]{:S(2)}, u32[]{:S(2)}) collective-permute-start(bf16[16,128,128]{2,1,0:T(8,128)(2,1)S(1)} %collective-permute-done.7.refs_6_), channel_id=1, source_target_pairs={{0,1},{1,0},{2,3},{3,2},{4,5},{5,4},{6,7},{7,6},{8,9},{9,8},{10,11... | collective-permute-start | bytes 1572872 | tf_op jit(solution)/shard_map/ppermute | solution.py:103
  78.3 7.1 %collective-permute-done.10.refs_9_ = bf16[8,128,128]{2,1,0:T(8,128)(2,1)S(1)} collective-permute-done((bf16[8,128,128]{2,1,0:T(8,128)(2,1)S(1)}, bf16[8,128,128]{2,1,0:T(8,128)(2,1)S(1)}, u32[]{:S(2)}, u32[]{:S(2)}) %collective-permute-start.10) | collective-permute-done | bytes 262176 | tf_op jit(solution)/shard_map/ppermute | solution.py:89
  85.3 1.9 %collective-permute-start.15 = (bf16[16,128,128]{2,1,0:T(8,128)(2,1)S(1)}, bf16[16,128,128]{2,1,0:T(8,128)(2,1)S(1)}, u32[]{:S(2)}, u32[]{:S(2)}) collective-permute-start(bf16[16,128,128]{2,1,0:T(8,128)(2,1)S(1)} %collective-permute-done.6.refs_5_), channel_id=1, source_target_pairs={{0,1},{1,0},{2,3},{3,2},{4,5},{5,4},{6,7},{7,6},{8,9},{9,8},{10,11... | collective-permute-start | bytes 1572872 | tf_op jit(solution)/shard_map/ppermute | solution.py:103
  87.3 2.4 %collective-permute-start.18 = (bf16[16,128,128]{2,1,0:T(8,128)(2,1)}, bf16[16,128,128]{2,1,0:T(8,128)(2,1)S(1)}, u32[]{:S(2)}, u32[]{:S(2)}) collective-permute-start(bf16[16,128,128]{2,1,0:T(8,128)(2,1)} %collective-permute-done.9.refs_8_), channel_id=1, source_target_pairs={{0,1},{1,0},{2,3},{3,2},{4,5},{5,4},{6,7},{7,6},{8,9},{9,8},{10,11... | collective-permute-start | bytes 1572872 | tf_op jit(solution)/shard_map/ppermute | solution.py:103
  89.7 0.0 collective-permute-done.8.refs_7_
  89.7 1.9 %collective-permute-start.17 = (bf16[16,128,128]{2,1,0:T(8,128)(2,1)}, bf16[16,128,128]{2,1,0:T(8,128)(2,1)S(1)}, u32[]{:S(2)}, u32[]{:S(2)}) collective-permute-start(bf16[16,128,128]{2,1,0:T(8,128)(2,1)} %collective-permute-done.8.refs_7_), channel_id=1, source_target_pairs={{0,1},{1,0},{2,3},{3,2},{4,5},{5,4},{6,7},{7,6},{8,9},{9,8},{10,11... | collective-permute-start | bytes 1572872 | tf_op jit(solution)/shard_map/ppermute | solution.py:103
  91.6 0.1 convert_reduce_fusion
  91.8 2.4 %collective-permute-start.19 = (bf16[8,128,128]{2,1,0:T(8,128)(2,1)S(1)}, bf16[8,128,128]{2,1,0:T(8,128)(2,1)S(1)}, u32[]{:S(2)}, u32[]{:S(2)}) collective-permute-start(bf16[8,128,128]{2,1,0:T(8,128)(2,1)S(1)} %collective-permute-done.10.refs_9_), channel_id=1, source_target_pairs={{0,1},{1,0},{2,3},{3,2},{4,5},{5,4},{6,7},{7,6},{8,9},{9,8},{10,11... | collective-permute-start | bytes 786440 | tf_op jit(solution)/shard_map/ppermute | solution.py:103
  94.2 0.2 select_reduce_fusion
  94.5 0.9 collective-permute-done.19.refs_18_
  95.4 7.2 %block_products.1 = bf16[2,128,128]{2,1,0:T(8,128)(2,1)} custom-call(s32[2,256]{1,0:T(2,128)S(1)} %broadcast_add_fusion.refs_0_, s32[2]{0:T(128)S(1)} %get-tuple-element.5.refs_1_, bf16[16,128,128]{2,1,0:T(8,128)(2,1)S(1)} %pad_maximum_fusion.refs_2_, bf16[16,128,128]{2,1,0:T(8,128)(2,1)S(1)} %collective-permute-done.4.refs_3_, ...), custom_call_target="tpu_custom_call" | custom-call | flops 536870912 | bytes 6291456 | tf_op jit(solution)/shard_map/block_products/pallas_call | solution.py:136
  (20 shorter events, 0.2 us)
Async XLA Ops:
  0.0 4.4 %copy-start.1 = (bf16[2,128,128]{2,1,0:T(8,128)(2,1)S(1)}, bf16[2,128,128]{2,1,0:T(8,128)(2,1)}, u32[]{:S(2)}) copy-start(bf16[2,128,128]{2,1,0:T(8,128)(2,1)} %param.5) | copy-start | bytes 196612
  1.0 3.4 %copy-start = (bf16[4,128,128]{2,1,0:T(8,128)(2,1)S(1)}, bf16[4,128,128]{2,1,0:T(8,128)(2,1)}, u32[]{:S(2)}) copy-start(bf16[4,128,128]{2,1,0:T(8,128)(2,1)} %param.4) | copy-start | bytes 393220
  1.0 3.4 %collective-permute-start = (bf16[4,128,128]{2,1,0:T(8,128)(2,1)S(1)}, bf16[4,128,128]{2,1,0:T(8,128)(2,1)S(1)}, u32[]{:S(2)}, u32[]{:S(2)}) collective-permute-start(bf16[4,128,128]{2,1,0:T(8,128)(2,1)S(1)} %fusion.1), channel_id=1, source_target_pairs={{0,1},{1,0},{2,3},{3,2},{4,5},{5,4},{6,7},{7,6},{8,9},{9,8},{10,11... | collective-permute-start | bytes 393224 | tf_op jit(solution)/shard_map/ppermute | solution.py:103
  4.5 15.0 %collective-permute-start.1 = (bf16[4,128,128]{2,1,0:T(8,128)(2,1)S(1)}, bf16[4,128,128]{2,1,0:T(8,128)(2,1)S(1)}, u32[]{:S(2)}, u32[]{:S(2)}) collective-permute-start(bf16[4,128,128]{2,1,0:T(8,128)(2,1)S(1)} %get-tuple-element.7), channel_id=1, source_target_pairs={{0,32},{1,17},{16,48},{17,1},{32,64},{33,49},{48,80},{49,33},{64,9... | collective-permute-start | bytes 393224 | tf_op jit(solution)/shard_map/ppermute | solution.py:99
  9.7 10.0 %collective-permute-start.3 = (bf16[4,128,128]{2,1,0:T(8,128)(2,1)S(1)}, bf16[4,128,128]{2,1,0:T(8,128)(2,1)S(1)}, u32[]{:S(2)}, u32[]{:S(2)}) collective-permute-start(bf16[4,128,128]{2,1,0:T(8,128)(2,1)S(1)} %get-tuple-element.8), channel_id=1, source_target_pairs={{0,96},{1,1},{16,112},{17,17},{32,0},{33,33},{48,16},{49,49},{64,3... | collective-permute-start | bytes 393224 | tf_op jit(solution)/shard_map/ppermute | solution.py:99
  17.0 10.7 %collective-permute-start.2 = (bf16[4,128,128]{2,1,0:T(8,128)(2,1)S(1)}, bf16[4,128,128]{2,1,0:T(8,128)(2,1)S(1)}, u32[]{:S(2)}, u32[]{:S(2)}) collective-permute-start(bf16[4,128,128]{2,1,0:T(8,128)(2,1)S(1)} %get-tuple-element.8), channel_id=1, source_target_pairs={{0,64},{1,17},{16,80},{17,1},{32,96},{33,49},{48,112},{49,33},{64,... | collective-permute-start | bytes 393224 | tf_op jit(solution)/shard_map/ppermute | solution.py:99
  27.7 15.9 %collective-permute-start.5 = (bf16[16,128,128]{2,1,0:T(8,128)(2,1)S(1)}, bf16[16,128,128]{2,1,0:T(8,128)(2,1)S(1)}, u32[]{:S(2)}, u32[]{:S(2)}) collective-permute-start(bf16[16,128,128]{2,1,0:T(8,128)(2,1)S(1)} %pad_maximum_fusion.refs_2_), channel_id=1, source_target_pairs={{0,896},{1,15},{2,898},{3,1},{4,900},{5,3},{6,902},{7,5},{8,904},{... | collective-permute-start | bytes 1572872 | tf_op jit(solution)/shard_map/ppermute | solution.py:89
  31.1 19.6 %collective-permute-start.4 = (bf16[16,128,128]{2,1,0:T(8,128)(2,1)S(1)}, bf16[16,128,128]{2,1,0:T(8,128)(2,1)S(1)}, u32[]{:S(2)}, u32[]{:S(2)}) collective-permute-start(bf16[16,128,128]{2,1,0:T(8,128)(2,1)S(1)} %pad_maximum_fusion.refs_2_), channel_id=1, source_target_pairs={{0,128},{1,3},{2,130},{3,5},{4,132},{5,7},{6,134},{7,9},{8,136},{9... | collective-permute-start | bytes 1572872 | tf_op jit(solution)/shard_map/ppermute | solution.py:89
  43.7 14.6 %collective-permute-start.7 = (bf16[16,128,128]{2,1,0:T(8,128)(2,1)S(1)}, bf16[16,128,128]{2,1,0:T(8,128)(2,1)S(1)}, u32[]{:S(2)}, u32[]{:S(2)}) collective-permute-start(bf16[16,128,128]{2,1,0:T(8,128)(2,1)S(1)} %collective-permute-done.5.refs_4_), channel_id=1, source_target_pairs={{0,896},{1,15},{2,898},{3,1},{4,900},{5,3},{6,902},{7,5},{8,904},{... | collective-permute-start | bytes 1572872 | tf_op jit(solution)/shard_map/ppermute | solution.py:89
  45.6 17.6 %collective-permute-start.12 = (bf16[16,128,128]{2,1,0:T(8,128)(2,1)S(1)}, bf16[16,128,128]{2,1,0:T(8,128)(2,1)S(1)}, u32[]{:S(2)}, u32[]{:S(2)}) collective-permute-start(bf16[16,128,128]{2,1,0:T(8,128)(2,1)S(1)} %pad_maximum_fusion.refs_2_), channel_id=1, source_target_pairs={{0,1},{1,0},{2,3},{3,2},{4,5},{5,4},{6,7},{7,6},{8,9},{9,8},{10,11... | collective-permute-start | bytes 1572872 | tf_op jit(solution)/shard_map/ppermute | solution.py:103
  50.7 15.9 %collective-permute-start.6 = (bf16[16,128,128]{2,1,0:T(8,128)(2,1)S(1)}, bf16[16,128,128]{2,1,0:T(8,128)(2,1)S(1)}, u32[]{:S(2)}, u32[]{:S(2)}) collective-permute-start(bf16[16,128,128]{2,1,0:T(8,128)(2,1)S(1)} %collective-permute-done.4.refs_3_), channel_id=1, source_target_pairs={{0,128},{1,3},{2,130},{3,5},{4,132},{5,7},{6,134},{7,9},{8,136},{9... | collective-permute-start | bytes 1572872 | tf_op jit(solution)/shard_map/ppermute | solution.py:89
  53.3 17.9 %collective-permute-start.14 = (bf16[16,128,128]{2,1,0:T(8,128)(2,1)S(1)}, bf16[16,128,128]{2,1,0:T(8,128)(2,1)}, u32[]{:S(2)}, u32[]{:S(2)}) collective-permute-start(bf16[16,128,128]{2,1,0:T(8,128)(2,1)S(1)} %collective-permute-done.5.refs_4_), channel_id=1, source_target_pairs={{0,1},{1,0},{2,3},{3,2},{4,5},{5,4},{6,7},{7,6},{8,9},{9,8},{10,11... | collective-permute-start | bytes 1572872 | tf_op jit(solution)/shard_map/ppermute | solution.py:103
  55.2 0.7 copy-start.2
  55.9 19.9 %collective-permute-start.13 = (bf16[16,128,128]{2,1,0:T(8,128)(2,1)S(1)}, bf16[16,128,128]{2,1,0:T(8,128)(2,1)}, u32[]{:S(2)}, u32[]{:S(2)}) collective-permute-start(bf16[16,128,128]{2,1,0:T(8,128)(2,1)S(1)} %collective-permute-done.4.refs_3_), channel_id=1, source_target_pairs={{0,1},{1,0},{2,3},{3,2},{4,5},{5,4},{6,7},{7,6},{8,9},{9,8},{10,11... | collective-permute-start | bytes 1572872 | tf_op jit(solution)/shard_map/ppermute | solution.py:103
  59.0 14.8 %collective-permute-start.11 = (bf16[8,128,128]{2,1,0:T(8,128)(2,1)}, bf16[8,128,128]{2,1,0:T(8,128)(2,1)S(1)}, u32[]{:S(2)}, u32[]{:S(2)}) collective-permute-start(bf16[8,128,128]{2,1,0:T(8,128)(2,1)} %slice.29), channel_id=1, source_target_pairs={{0,768},{1,13},{2,770},{3,15},{4,772},{5,1},{6,774},{7,3},{8,776},... | collective-permute-start | bytes 786440 | tf_op jit(solution)/shard_map/ppermute | solution.py:89
  63.2 24.1 %collective-permute-start.9 = (bf16[16,128,128]{2,1,0:T(8,128)(2,1)S(1)}, bf16[16,128,128]{2,1,0:T(8,128)(2,1)}, u32[]{:S(2)}, u32[]{:S(2)}) collective-permute-start(bf16[16,128,128]{2,1,0:T(8,128)(2,1)S(1)} %collective-permute-done.7.refs_6_), channel_id=1, source_target_pairs={{0,896},{1,15},{2,898},{3,1},{4,900},{5,3},{6,902},{7,5},{8,904},{... | collective-permute-start | bytes 1572872 | tf_op jit(solution)/shard_map/ppermute | solution.py:89
  66.6 23.1 %collective-permute-start.8 = (bf16[16,128,128]{2,1,0:T(8,128)(2,1)S(1)}, bf16[16,128,128]{2,1,0:T(8,128)(2,1)}, u32[]{:S(2)}, u32[]{:S(2)}) collective-permute-start(bf16[16,128,128]{2,1,0:T(8,128)(2,1)S(1)} %collective-permute-done.6.refs_5_), channel_id=1, source_target_pairs={{0,128},{1,3},{2,130},{3,5},{4,132},{5,7},{6,134},{7,9},{8,136},{9... | collective-permute-start | bytes 1572872 | tf_op jit(solution)/shard_map/ppermute | solution.py:89
  70.3 0.7 copy-start.3
  71.2 14.2 %collective-permute-start.10 = (bf16[8,128,128]{2,1,0:T(8,128)(2,1)S(1)}, bf16[8,128,128]{2,1,0:T(8,128)(2,1)S(1)}, u32[]{:S(2)}, u32[]{:S(2)}) collective-permute-start(bf16[8,128,128]{2,1,0:T(8,128)(2,1)S(1)} %slice.28), channel_id=1, source_target_pairs={{0,256},{1,5},{2,258},{3,7},{4,260},{5,9},{6,262},{7,11},{8,264},{... | collective-permute-start | bytes 786440 | tf_op jit(solution)/shard_map/ppermute | solution.py:89
  73.8 18.0 %collective-permute-start.20 = (bf16[8,128,128]{2,1,0:T(8,128)(2,1)S(1)}, bf16[8,128,128]{2,1,0:T(8,128)(2,1)S(1)}, u32[]{:S(2)}, u32[]{:S(2)}) collective-permute-start(bf16[8,128,128]{2,1,0:T(8,128)(2,1)S(1)} %collective-permute-done.11.refs_10_), channel_id=1, source_target_pairs={{0,1},{1,0},{2,3},{3,2},{4,5},{5,4},{6,7},{7,6},{8,9},{9,8},{10,11... | collective-permute-start | bytes 786440 | tf_op jit(solution)/shard_map/ppermute | solution.py:103
  75.9 18.6 %collective-permute-start.16 = (bf16[16,128,128]{2,1,0:T(8,128)(2,1)S(1)}, bf16[16,128,128]{2,1,0:T(8,128)(2,1)S(1)}, u32[]{:S(2)}, u32[]{:S(2)}) collective-permute-start(bf16[16,128,128]{2,1,0:T(8,128)(2,1)S(1)} %collective-permute-done.7.refs_6_), channel_id=1, source_target_pairs={{0,1},{1,0},{2,3},{3,2},{4,5},{5,4},{6,7},{7,6},{8,9},{9,8},{10,11... | collective-permute-start | bytes 1572872 | tf_op jit(solution)/shard_map/ppermute | solution.py:103
  85.3 10.0 %collective-permute-start.15 = (bf16[16,128,128]{2,1,0:T(8,128)(2,1)S(1)}, bf16[16,128,128]{2,1,0:T(8,128)(2,1)S(1)}, u32[]{:S(2)}, u32[]{:S(2)}) collective-permute-start(bf16[16,128,128]{2,1,0:T(8,128)(2,1)S(1)} %collective-permute-done.6.refs_5_), channel_id=1, source_target_pairs={{0,1},{1,0},{2,3},{3,2},{4,5},{5,4},{6,7},{7,6},{8,9},{9,8},{10,11... | collective-permute-start | bytes 1572872 | tf_op jit(solution)/shard_map/ppermute | solution.py:103
  87.3 8.1 %collective-permute-start.18 = (bf16[16,128,128]{2,1,0:T(8,128)(2,1)}, bf16[16,128,128]{2,1,0:T(8,128)(2,1)S(1)}, u32[]{:S(2)}, u32[]{:S(2)}) collective-permute-start(bf16[16,128,128]{2,1,0:T(8,128)(2,1)} %collective-permute-done.9.refs_8_), channel_id=1, source_target_pairs={{0,1},{1,0},{2,3},{3,2},{4,5},{5,4},{6,7},{7,6},{8,9},{9,8},{10,11... | collective-permute-start | bytes 1572872 | tf_op jit(solution)/shard_map/ppermute | solution.py:103
  89.7 5.7 %collective-permute-start.17 = (bf16[16,128,128]{2,1,0:T(8,128)(2,1)}, bf16[16,128,128]{2,1,0:T(8,128)(2,1)S(1)}, u32[]{:S(2)}, u32[]{:S(2)}) collective-permute-start(bf16[16,128,128]{2,1,0:T(8,128)(2,1)} %collective-permute-done.8.refs_7_), channel_id=1, source_target_pairs={{0,1},{1,0},{2,3},{3,2},{4,5},{5,4},{6,7},{7,6},{8,9},{9,8},{10,11... | collective-permute-start | bytes 1572872 | tf_op jit(solution)/shard_map/ppermute | solution.py:103
  91.8 3.6 %collective-permute-start.19 = (bf16[8,128,128]{2,1,0:T(8,128)(2,1)S(1)}, bf16[8,128,128]{2,1,0:T(8,128)(2,1)S(1)}, u32[]{:S(2)}, u32[]{:S(2)}) collective-permute-start(bf16[8,128,128]{2,1,0:T(8,128)(2,1)S(1)} %collective-permute-done.10.refs_9_), channel_id=1, source_target_pairs={{0,1},{1,0},{2,3},{3,2},{4,5},{5,4},{6,7},{7,6},{8,9},{9,8},{10,11... | collective-permute-start | bytes 786440 | tf_op jit(solution)/shard_map/ppermute | solution.py:103

commit v3 on v2

--- a/solution.py
+++ b/solution.py
@@ -13,10 +13,16 @@
 GROUP = 8
 TILE = 16
 ZERO = 2 * NY * TILE
+SEATS = (0, 6, 3, 5, 1, 7, 2, 4)
 
 
 def rot(size, shift):
     return [(s, (s + shift) % size) for s in range(size)]
+
+
+def seat_of(distance):
+    hit = distance[:, None] % NY == jnp.arange(NY, dtype=jnp.int32)
+    return jnp.sum(jnp.where(hit, jnp.array(SEATS, jnp.int32), 0), axis=1)
 
 
 def slot_lists(pair_lists, pair_count, x, zl, zh, y, c):
@@ -29,10 +35,10 @@
     from_zh, from_y, from_c = source // (NY * NCORE), source // NCORE % NY, source % NCORE
     near = from_zh == zh
     part = jnp.where(from_c == 0, jnp.where(near, 0, 1), jnp.where(near, 3, 2))
-    left = (jnp.where(c == 1, 0, NY) + (from_y - y) % NY) * TILE + part * NA + pairs[:, 0]
+    left = (jnp.where(c == 1, 0, NY) + seat_of(from_y - y)) * TILE + part * NA + pairs[:, 0]
     holder = (k - col) % NK
     part = (zl - holder % NZL) % NZL
-    right = (jnp.where(c == 0, 0, NY) + (holder // NZL - x) % NX) * TILE
+    right = (jnp.where(c == 0, 0, NY) + seat_of(holder // NZL - x)) * TILE
     right = right + (part * NCORE + c) * NB + pairs[:, 1]
     code = left * 512 + right
     target = jnp.arange(NC, dtype=jnp.int32)[:, None]
@@ -112,21 +118,14 @@
     own = jnp.concatenate(
         [first, along_z(first, 1, 1), along_z(second, 2, 1), along_z(second, 3, 0)]
     )
-    up, down = [own], [own]
-    for _ in range(3):
-        up.append(along_plane(up[-1], 1))
-        down.append(along_plane(down[-1], -1))
-    up.append(along_plane(up[2][: TILE // 2], 2))
-    down.append(along_plane(down[2][TILE // 2 :], -2))
-
-    pieces, plan = [own], [(TILE, 0)]
-    for distance in range(1, 4):
-        pieces += [up[distance], down[distance]]
-        plan += [(TILE, (NY - distance) * TILE), (TILE, distance * TILE)]
-    pieces += [up[4], down[4]]
-    plan += [(TILE // 2, 4 * TILE), (TILE // 2, 4 * TILE + TILE // 2)]
+    pair = jnp.concatenate([own, along_plane(own, NY // 2)])
+    pieces = [pair, along_plane(own, 2), along_plane(own, -2)]
+    pieces += [along_plane(pair, 1), along_plane(pair, -1)]
     pieces += [to_partner(piece) for piece in pieces]
-    plan += [(size, NY * TILE + at) for size, at in plan]
+    plan, at = [], 0
+    for piece in pieces:
+        plan.append((piece.shape[0], at))
+        at += piece.shape[0]
 
     codes, counts = slot_lists(pair_lists, pair_count, x, zl, zh, y, c)
 

time: 103 us -> 95.6 us (0.928)
  the two profiles are of different devices: /device:TPU:14 before, /device:TPU:29 now
where the time goes in v3:
time: 95.6 us; the launch traced here: 95 us
  starting transfers between devices  51.6 us (54%)
  waiting for transfers between devices  33.5 us (35%)
  Pallas kernels  6.1 us (6%)
  other arithmetic  1.85 us (2%)
  local copies, waits for them, and re-layouts  1.65 us (2%)
    ppermute x5, waiting for transfers between devices, along_plane(): return lax.ppermute(value, ('x', 'y', 'c'), pairs)  20.8 us
    ppermute x5, starting transfers between devices, along_plane(): return lax.ppermute(value, ('x', 'y', 'c'), pairs)  20.7 us
    ppermute x3, starting transfers between devices, along_z(): return lax.ppermute(value, ('zl', 'zh', 'c'), pairs)  16.9 us
    ppermute x6, starting transfers between devices, to_partner(): return lax.ppermute(value, 'c', rot(NCORE, 1))  14 us
    ppermute x3, waiting for transfers between devices, along_z(): return lax.ppermute(value, ('zl', 'zh', 'c'), pairs)  10.2 us
    pallas_call x1, Pallas kernels, per_device(): pl.pallas_call(kernel, out_shape=jax.ShapeDtypeStruct((NC, BS, BS), jnp.b...  6.1 us
    ppermute x6, waiting for transfers between devices, to_partner(): return lax.ppermute(value, 'c', rot(NCORE, 1))  2.6 us
  transfers between devices with their start and end apart: 14, of which 7 were waited for; matrix products, arithmetic and copies ran while one was open for 1% of the time, Pallas kernels for 0%

profile of v3, /device:TPU:29, one launch (start us, length us, event | category | flops | bytes accessed | tf_op | source)
XLA Modules:
  0.0 95.0 jit_solution(1473812235826094251)
XLA Ops:
  0.0 1.0 %fusion.1 = bf16[4,128,128]{2,1,0:T(8,128)(2,1)S(1)} fusion(bf16[4,128,128]{2,1,0:T(8,128)(2,1)} %param.6, bf16[2,128,128]{2,1,0:T(8,128)(2,1)} %param.7, pred[]{:T(512)S(6)} %eq.114), kind=kLoop, calls=%fused_computation.8 | loop fusion | flops 131072 | bytes 327681 | tf_op jit(solution)/shard_map/jit(_where)/select_n | solution.py:115
  1.0 0.0 copy-start.1
  1.0 2.8 %collective-permute-start = (bf16[4,128,128]{2,1,0:T(8,128)(2,1)S(1)}, bf16[4,128,128]{2,1,0:T(8,128)(2,1)S(1)}, u32[]{:S(2)}, u32[]{:S(2)}) collective-permute-start(bf16[4,128,128]{2,1,0:T(8,128)(2,1)S(1)} %fusion.1), channel_id=1, source_target_pairs={{0,1},{1,0},{2,3},{3,2},{4,5},{5,4},{6,7},{7,6},{8,9},{9,8},{10,11... | collective-permute-start | bytes 393224 | tf_op jit(solution)/shard_map/ppermute | solution.py:109
  3.7 1.0 %collective-permute-done = bf16[4,128,128]{2,1,0:T(8,128)(2,1)S(1)} collective-permute-done((bf16[4,128,128]{2,1,0:T(8,128)(2,1)S(1)}, bf16[4,128,128]{2,1,0:T(8,128)(2,1)S(1)}, u32[]{:S(2)}, u32[]{:S(2)}) %collective-permute-start) | collective-permute-done | bytes 131104 | tf_op jit(solution)/shard_map/ppermute | solution.py:109
  4.7 0.0 copy-done.2
  4.7 0.0 copy-done.1
  4.7 0.1 constant_dynamic-update-slice_fusion.4
  4.8 14.3 %collective-permute-start.1 = (bf16[4,128,128]{2,1,0:T(8,128)(2,1)S(1)}, bf16[4,128,128]{2,1,0:T(8,128)(2,1)S(1)}, u32[]{:S(2)}, u32[]{:S(2)}) collective-permute-start(bf16[4,128,128]{2,1,0:T(8,128)(2,1)S(1)} %get-tuple-element.8), channel_id=1, source_target_pairs={{0,32},{1,17},{16,48},{17,1},{32,64},{33,49},{48,80},{49,33},{64,9... | collective-permute-start | bytes 393224 | tf_op jit(solution)/shard_map/ppermute | solution.py:105
  19.1 0.7 collective-permute-start.3
  19.8 1.9 %collective-permute-start.2 = (bf16[4,128,128]{2,1,0:T(8,128)(2,1)S(1)}, bf16[4,128,128]{2,1,0:T(8,128)(2,1)S(1)}, u32[]{:S(2)}, u32[]{:S(2)}) collective-permute-start(bf16[4,128,128]{2,1,0:T(8,128)(2,1)S(1)} %get-tuple-element.11), channel_id=1, source_target_pairs={{0,64},{1,17},{16,80},{17,1},{32,96},{33,49},{48,112},{49,33},{64,... | collective-permute-start | bytes 393224 | tf_op jit(solution)/shard_map/ppermute | solution.py:105
  21.7 0.0 collective-permute-done.1
  21.7 0.0 collective-permute-done.3
  21.7 10.2 %collective-permute-done.2 = bf16[4,128,128]{2,1,0:T(8,128)(2,1)S(1)} collective-permute-done((bf16[4,128,128]{2,1,0:T(8,128)(2,1)S(1)}, bf16[4,128,128]{2,1,0:T(8,128)(2,1)S(1)}, u32[]{:S(2)}, u32[]{:S(2)}) %collective-permute-start.2) | collective-permute-done | bytes 131104 | tf_op jit(solution)/shard_map/ppermute | solution.py:105
  31.9 0.1 pad_maximum_fusion
  32.0 0.0 copy-start
  32.0 7.0 %collective-permute-start.4 = (bf16[16,128,128]{2,1,0:T(8,128)(2,1)S(1)}, bf16[16,128,128]{2,1,0:T(8,128)(2,1)S(1)}, u32[]{:S(2)}, u32[]{:S(2)}) collective-permute-start(bf16[16,128,128]{2,1,0:T(8,128)(2,1)S(1)} %pad_maximum_fusion), channel_id=1, source_target_pairs={{0,512},{1,9},{2,514},{3,11},{4,516},{5,13},{6,518},{7,15},{8,520}... | collective-permute-start | bytes 1572872 | tf_op jit(solution)/shard_map/ppermute | solution.py:95
  39.1 12.4 %collective-permute-done.4 = bf16[16,128,128]{2,1,0:T(8,128)(2,1)S(1)} collective-permute-done((bf16[16,128,128]{2,1,0:T(8,128)(2,1)S(1)}, bf16[16,128,128]{2,1,0:T(8,128)(2,1)S(1)}, u32[]{:S(2)}, u32[]{:S(2)}) %collective-permute-start.4) | collective-permute-done | bytes 524320 | tf_op jit(solution)/shard_map/ppermute | solution.py:95
  51.4 0.0 copy-done
  51.4 0.1 constant_dynamic-update-slice_fusion.refs_2_
  51.5 1.9 %collective-permute-start.8 = (bf16[32,128,128]{2,1,0:T(8,128)(2,1)S(1)}, bf16[32,128,128]{2,1,0:T(8,128)(2,1)S(1)}, u32[]{:S(2)}, u32[]{:S(2)}) collective-permute-start(bf16[32,128,128]{2,1,0:T(8,128)(2,1)S(1)} %constant_dynamic-update-slice_fusion.refs_2_), channel_id=1, source_target_pairs={{0,896},{1,15},{2,898},{3,1},{4,900},{5,3},{6,902},{7,5},{8,904},{... | collective-permute-start | bytes 3145736 | tf_op jit(solution)/shard_map/ppermute | solution.py:95
  53.4 3.5 %collective-permute-start.7 = (bf16[32,128,128]{2,1,0:T(8,128)(2,1)S(1)}, bf16[32,128,128]{2,1,0:T(8,128)(2,1)S(1)}, u32[]{:S(2)}, u32[]{:S(2)}) collective-permute-start(bf16[32,128,128]{2,1,0:T(8,128)(2,1)S(1)} %constant_dynamic-update-slice_fusion.refs_2_), channel_id=1, source_target_pairs={{0,128},{1,3},{2,130},{3,5},{4,132},{5,7},{6,134},{7,9},{8,136},{9... | collective-permute-start | bytes 3145736 | tf_op jit(solution)/shard_map/ppermute | solution.py:95
  57.0 0.0 copy-start.3
  57.0 0.7 copy-done.3
  57.7 0.7 copy-done.4
  58.3 0.1 broadcast_in_dim.46
  58.4 0.1 reshape.339
  58.5 0.0 copy-start.5
  58.6 6.3 %collective-permute-start.6 = (bf16[16,128,128]{2,1,0:T(8,128)(2,1)}, bf16[16,128,128]{2,1,0:T(8,128)(2,1)}, u32[]{:S(2)}, u32[]{:S(2)}) collective-permute-start(bf16[16,128,128]{2,1,0:T(8,128)(2,1)} %copy-done), channel_id=1, source_target_pairs={{0,768},{1,13},{2,770},{3,15},{4,772},{5,1},{6,774},{7,3},{8,776},... | collective-permute-start | bytes 1572872 | tf_op jit(solution)/shard_map/ppermute | solution.py:95
  64.9 1.9 %collective-permute-start.5 = (bf16[16,128,128]{2,1,0:T(8,128)(2,1)}, bf16[16,128,128]{2,1,0:T(8,128)(2,1)}, u32[]{:S(2)}, u32[]{:S(2)}) collective-permute-start(bf16[16,128,128]{2,1,0:T(8,128)(2,1)} %copy-done), channel_id=1, source_target_pairs={{0,256},{1,5},{2,258},{3,7},{4,260},{5,9},{6,262},{7,11},{8,264},{... | collective-permute-start | bytes 1572872 | tf_op jit(solution)/shard_map/ppermute | solution.py:95
  66.9 1.9 %collective-permute-start.9 = (bf16[32,128,128]{2,1,0:T(8,128)(2,1)S(1)}, bf16[32,128,128]{2,1,0:T(8,128)(2,1)}, u32[]{:S(2)}, u32[]{:S(2)}) collective-permute-start(bf16[32,128,128]{2,1,0:T(8,128)(2,1)S(1)} %constant_dynamic-update-slice_fusion.refs_2_), channel_id=1, source_target_pairs={{0,1},{1,0},{2,3},{3,2},{4,5},{5,4},{6,7},{7,6},{8,9},{9,8},{10,11... | collective-permute-start | bytes 3145736 | tf_op jit(solution)/shard_map/ppermute | solution.py:109
  68.8 0.0 collective-permute-done.8.refs_6_
  68.8 2.4 %collective-permute-start.13 = (bf16[32,128,128]{2,1,0:T(8,128)(2,1)S(1)}, bf16[32,128,128]{2,1,0:T(8,128)(2,1)}, u32[]{:S(2)}, u32[]{:S(2)}) collective-permute-start(bf16[32,128,128]{2,1,0:T(8,128)(2,1)S(1)} %collective-permute-done.8.refs_6_), channel_id=1, source_target_pairs={{0,1},{1,0},{2,3},{3,2},{4,5},{5,4},{6,7},{7,6},{8,9},{9,8},{10,11... | collective-permute-start | bytes 3145736 | tf_op jit(solution)/shard_map/ppermute | solution.py:109
  71.2 0.4 collective-permute-done.7.refs_5_
  71.6 1.9 %collective-permute-start.12 = (bf16[32,128,128]{2,1,0:T(8,128)(2,1)S(1)}, bf16[32,128,128]{2,1,0:T(8,128)(2,1)}, u32[]{:S(2)}, u32[]{:S(2)}) collective-permute-start(bf16[32,128,128]{2,1,0:T(8,128)(2,1)S(1)} %collective-permute-done.7.refs_5_), channel_id=1, source_target_pairs={{0,1},{1,0},{2,3},{3,2},{4,5},{5,4},{6,7},{7,6},{8,9},{9,8},{10,11... | collective-permute-start | bytes 3145736 | tf_op jit(solution)/shard_map/ppermute | solution.py:109
  73.5 0.1 select_reduce_fusion.1
  73.6 0.1 convert_reduce_fusion.1
  73.7 2.2 %collective-permute-done.6.refs_4_ = bf16[16,128,128]{2,1,0:T(8,128)(2,1)} collective-permute-done((bf16[16,128,128]{2,1,0:T(8,128)(2,1)}, bf16[16,128,128]{2,1,0:T(8,128)(2,1)}, u32[]{:S(2)}, u32[]{:S(2)}) %collective-permute-start.6) | collective-permute-done | bytes 524320 | tf_op jit(solution)/shard_map/ppermute | solution.py:95
  75.9 3.1 %collective-permute-start.11 = (bf16[16,128,128]{2,1,0:T(8,128)(2,1)}, bf16[16,128,128]{2,1,0:T(8,128)(2,1)S(1)}, u32[]{:S(2)}, u32[]{:S(2)}) collective-permute-start(bf16[16,128,128]{2,1,0:T(8,128)(2,1)} %collective-permute-done.6.refs_4_), channel_id=1, source_target_pairs={{0,1},{1,0},{2,3},{3,2},{4,5},{5,4},{6,7},{7,6},{8,9},{9,8},{10,11... | collective-permute-start | bytes 1572872 | tf_op jit(solution)/shard_map/ppermute | solution.py:109
  79.0 5.9 %collective-permute-done.5.refs_3_ = bf16[16,128,128]{2,1,0:T(8,128)(2,1)} collective-permute-done((bf16[16,128,128]{2,1,0:T(8,128)(2,1)}, bf16[16,128,128]{2,1,0:T(8,128)(2,1)}, u32[]{:S(2)}, u32[]{:S(2)}) %collective-permute-start.5) | collective-permute-done | bytes 524320 | tf_op jit(solution)/shard_map/ppermute | solution.py:95
  84.9 1.9 %collective-permute-start.10 = (bf16[16,128,128]{2,1,0:T(8,128)(2,1)}, bf16[16,128,128]{2,1,0:T(8,128)(2,1)S(1)}, u32[]{:S(2)}, u32[]{:S(2)}) collective-permute-start(bf16[16,128,128]{2,1,0:T(8,128)(2,1)} %collective-permute-done.5.refs_3_), channel_id=1, source_target_pairs={{0,1},{1,0},{2,3},{3,2},{4,5},{5,4},{6,7},{7,6},{8,9},{9,8},{10,11... | collective-permute-start | bytes 1572872 | tf_op jit(solution)/shard_map/ppermute | solution.py:109
  86.8 0.1 convert_reduce_fusion
  87.0 0.3 select_reduce_fusion
  87.3 0.0 collective-permute-done.11.refs_9_
  87.3 1.6 %collective-permute-done.10.refs_8_ = bf16[16,128,128]{2,1,0:T(8,128)(2,1)S(1)} collective-permute-done((bf16[16,128,128]{2,1,0:T(8,128)(2,1)}, bf16[16,128,128]{2,1,0:T(8,128)(2,1)S(1)}, u32[]{:S(2)}, u32[]{:S(2)}) %collective-permute-start.10) | collective-permute-done | bytes 524320 | tf_op jit(solution)/shard_map/ppermute | solution.py:109
  88.9 0.0 collective-permute-done.9.refs_7_
  88.9 0.0 collective-permute-done.13.refs_11_
  88.9 0.0 collective-permute-done.12.refs_10_
  88.9 6.1 %block_products.1 = bf16[2,128,128]{2,1,0:T(8,128)(2,1)} custom-call(s32[2,256]{1,0:T(2,128)S(1)} %broadcast_add_fusion.refs_0_, s32[2]{0:T(128)S(1)} %get-tuple-element.9.refs_1_, bf16[32,128,128]{2,1,0:T(8,128)(2,1)S(1)} %constant_dynamic-update-slice_fusion.refs_2_, bf16[16,128,128]{2,1,0:T(8,128)(2,1)} %collective-permute-done.5.refs_3_, ...), custom_call_target="tpu_custom_call" | custom-call | flops 536870912 | bytes 6291456 | tf_op jit(solution)/shard_map/block_products/pallas_call | solution.py:135
  (15 shorter events, 0.2 us)
Async XLA Ops:
  0.0 4.7 %copy-start.2 = (bf16[2,128,128]{2,1,0:T(8,128)(2,1)S(1)}, bf16[2,128,128]{2,1,0:T(8,128)(2,1)}, u32[]{:S(2)}) copy-start(bf16[2,128,128]{2,1,0:T(8,128)(2,1)} %param.7) | copy-start | bytes 196612
  1.0 3.7 %copy-start.1 = (bf16[4,128,128]{2,1,0:T(8,128)(2,1)S(1)}, bf16[4,128,128]{2,1,0:T(8,128)(2,1)}, u32[]{:S(2)}) copy-start(bf16[4,128,128]{2,1,0:T(8,128)(2,1)} %param.6) | copy-start | bytes 393220
  1.0 3.7 %collective-permute-start = (bf16[4,128,128]{2,1,0:T(8,128)(2,1)S(1)}, bf16[4,128,128]{2,1,0:T(8,128)(2,1)S(1)}, u32[]{:S(2)}, u32[]{:S(2)}) collective-permute-start(bf16[4,128,128]{2,1,0:T(8,128)(2,1)S(1)} %fusion.1), channel_id=1, source_target_pairs={{0,1},{1,0},{2,3},{3,2},{4,5},{5,4},{6,7},{7,6},{8,9},{9,8},{10,11... | collective-permute-start | bytes 393224 | tf_op jit(solution)/shard_map/ppermute | solution.py:109
  4.8 16.9 %collective-permute-start.1 = (bf16[4,128,128]{2,1,0:T(8,128)(2,1)S(1)}, bf16[4,128,128]{2,1,0:T(8,128)(2,1)S(1)}, u32[]{:S(2)}, u32[]{:S(2)}) collective-permute-start(bf16[4,128,128]{2,1,0:T(8,128)(2,1)S(1)} %get-tuple-element.8), channel_id=1, source_target_pairs={{0,32},{1,17},{16,48},{17,1},{32,64},{33,49},{48,80},{49,33},{64,9... | collective-permute-start | bytes 393224 | tf_op jit(solution)/shard_map/ppermute | solution.py:105
  19.1 2.6 %collective-permute-start.3 = (bf16[4,128,128]{2,1,0:T(8,128)(2,1)S(1)}, bf16[4,128,128]{2,1,0:T(8,128)(2,1)S(1)}, u32[]{:S(2)}, u32[]{:S(2)}) collective-permute-start(bf16[4,128,128]{2,1,0:T(8,128)(2,1)S(1)} %get-tuple-element.11), channel_id=1, source_target_pairs={{0,96},{1,1},{16,112},{17,17},{32,0},{33,33},{48,16},{49,49},{64,3... | collective-permute-start | bytes 393224 | tf_op jit(solution)/shard_map/ppermute | solution.py:105
  19.8 12.1 %collective-permute-start.2 = (bf16[4,128,128]{2,1,0:T(8,128)(2,1)S(1)}, bf16[4,128,128]{2,1,0:T(8,128)(2,1)S(1)}, u32[]{:S(2)}, u32[]{:S(2)}) collective-permute-start(bf16[4,128,128]{2,1,0:T(8,128)(2,1)S(1)} %get-tuple-element.11), channel_id=1, source_target_pairs={{0,64},{1,17},{16,80},{17,1},{32,96},{33,49},{48,112},{49,33},{64,... | collective-permute-start | bytes 393224 | tf_op jit(solution)/shard_map/ppermute | solution.py:105
  32.0 19.5 %copy-start = (bf16[16,128,128]{2,1,0:T(8,128)(2,1)}, bf16[16,128,128]{2,1,0:T(8,128)(2,1)S(1)}, u32[]{:S(2)}) copy-start(bf16[16,128,128]{2,1,0:T(8,128)(2,1)S(1)} %pad_maximum_fusion) | copy-start | bytes 1572868
  32.0 19.5 %collective-permute-start.4 = (bf16[16,128,128]{2,1,0:T(8,128)(2,1)S(1)}, bf16[16,128,128]{2,1,0:T(8,128)(2,1)S(1)}, u32[]{:S(2)}, u32[]{:S(2)}) collective-permute-start(bf16[16,128,128]{2,1,0:T(8,128)(2,1)S(1)} %pad_maximum_fusion), channel_id=1, source_target_pairs={{0,512},{1,9},{2,514},{3,11},{4,516},{5,13},{6,518},{7,15},{8,520}... | collective-permute-start | bytes 1572872 | tf_op jit(solution)/shard_map/ppermute | solution.py:95
  51.5 17.3 %collective-permute-start.8 = (bf16[32,128,128]{2,1,0:T(8,128)(2,1)S(1)}, bf16[32,128,128]{2,1,0:T(8,128)(2,1)S(1)}, u32[]{:S(2)}, u32[]{:S(2)}) collective-permute-start(bf16[32,128,128]{2,1,0:T(8,128)(2,1)S(1)} %constant_dynamic-update-slice_fusion.refs_2_), channel_id=1, source_target_pairs={{0,896},{1,15},{2,898},{3,1},{4,900},{5,3},{6,902},{7,5},{8,904},{... | collective-permute-start | bytes 3145736 | tf_op jit(solution)/shard_map/ppermute | solution.py:95
  53.4 18.1 %collective-permute-start.7 = (bf16[32,128,128]{2,1,0:T(8,128)(2,1)S(1)}, bf16[32,128,128]{2,1,0:T(8,128)(2,1)S(1)}, u32[]{:S(2)}, u32[]{:S(2)}) collective-permute-start(bf16[32,128,128]{2,1,0:T(8,128)(2,1)S(1)} %constant_dynamic-update-slice_fusion.refs_2_), channel_id=1, source_target_pairs={{0,128},{1,3},{2,130},{3,5},{4,132},{5,7},{6,134},{7,9},{8,136},{9... | collective-permute-start | bytes 3145736 | tf_op jit(solution)/shard_map/ppermute | solution.py:95
  57.0 0.7 copy-start.3
  57.7 0.7 copy-start.4
  58.5 14.9 %copy-start.5 = (s32[8]{0:T(128)S(1)}, s32[8]{0:T(128)}, u32[]{:S(2)}) copy-start(s32[8]{0:T(128)} %constant.162.clone) | copy-start | bytes 100
  58.6 17.3 %collective-permute-start.6 = (bf16[16,128,128]{2,1,0:T(8,128)(2,1)}, bf16[16,128,128]{2,1,0:T(8,128)(2,1)}, u32[]{:S(2)}, u32[]{:S(2)}) collective-permute-start(bf16[16,128,128]{2,1,0:T(8,128)(2,1)} %copy-done), channel_id=1, source_target_pairs={{0,768},{1,13},{2,770},{3,15},{4,772},{5,1},{6,774},{7,3},{8,776},... | collective-permute-start | bytes 1572872 | tf_op jit(solution)/shard_map/ppermute | solution.py:95
  64.9 20.0 %collective-permute-start.5 = (bf16[16,128,128]{2,1,0:T(8,128)(2,1)}, bf16[16,128,128]{2,1,0:T(8,128)(2,1)}, u32[]{:S(2)}, u32[]{:S(2)}) collective-permute-start(bf16[16,128,128]{2,1,0:T(8,128)(2,1)} %copy-done), channel_id=1, source_target_pairs={{0,256},{1,5},{2,258},{3,7},{4,260},{5,9},{6,262},{7,11},{8,264},{... | collective-permute-start | bytes 1572872 | tf_op jit(solution)/shard_map/ppermute | solution.py:95
  66.9 22.0 %collective-permute-start.9 = (bf16[32,128,128]{2,1,0:T(8,128)(2,1)S(1)}, bf16[32,128,128]{2,1,0:T(8,128)(2,1)}, u32[]{:S(2)}, u32[]{:S(2)}) collective-permute-start(bf16[32,128,128]{2,1,0:T(8,128)(2,1)S(1)} %constant_dynamic-update-slice_fusion.refs_2_), channel_id=1, source_target_pairs={{0,1},{1,0},{2,3},{3,2},{4,5},{5,4},{6,7},{7,6},{8,9},{9,8},{10,11... | collective-permute-start | bytes 3145736 | tf_op jit(solution)/shard_map/ppermute | solution.py:109
  68.8 20.1 %collective-permute-start.13 = (bf16[32,128,128]{2,1,0:T(8,128)(2,1)S(1)}, bf16[32,128,128]{2,1,0:T(8,128)(2,1)}, u32[]{:S(2)}, u32[]{:S(2)}) collective-permute-start(bf16[32,128,128]{2,1,0:T(8,128)(2,1)S(1)} %collective-permute-done.8.refs_6_), channel_id=1, source_target_pairs={{0,1},{1,0},{2,3},{3,2},{4,5},{5,4},{6,7},{7,6},{8,9},{9,8},{10,11... | collective-permute-start | bytes 3145736 | tf_op jit(solution)/shard_map/ppermute | solution.py:109
  71.6 17.3 %collective-permute-start.12 = (bf16[32,128,128]{2,1,0:T(8,128)(2,1)S(1)}, bf16[32,128,128]{2,1,0:T(8,128)(2,1)}, u32[]{:S(2)}, u32[]{:S(2)}) collective-permute-start(bf16[32,128,128]{2,1,0:T(8,128)(2,1)S(1)} %collective-permute-done.7.refs_5_), channel_id=1, source_target_pairs={{0,1},{1,0},{2,3},{3,2},{4,5},{5,4},{6,7},{7,6},{8,9},{9,8},{10,11... | collective-permute-start | bytes 3145736 | tf_op jit(solution)/shard_map/ppermute | solution.py:109
  75.9 11.4 %collective-permute-start.11 = (bf16[16,128,128]{2,1,0:T(8,128)(2,1)}, bf16[16,128,128]{2,1,0:T(8,128)(2,1)S(1)}, u32[]{:S(2)}, u32[]{:S(2)}) collective-permute-start(bf16[16,128,128]{2,1,0:T(8,128)(2,1)} %collective-permute-done.6.refs_4_), channel_id=1, source_target_pairs={{0,1},{1,0},{2,3},{3,2},{4,5},{5,4},{6,7},{7,6},{8,9},{9,8},{10,11... | collective-permute-start | bytes 1572872 | tf_op jit(solution)/shard_map/ppermute | solution.py:109
  84.9 4.0 %collective-permute-start.10 = (bf16[16,128,128]{2,1,0:T(8,128)(2,1)}, bf16[16,128,128]{2,1,0:T(8,128)(2,1)S(1)}, u32[]{:S(2)}, u32[]{:S(2)}) collective-permute-start(bf16[16,128,128]{2,1,0:T(8,128)(2,1)} %collective-permute-done.5.refs_3_), channel_id=1, source_target_pairs={{0,1},{1,0},{2,3},{3,2},{4,5},{5,4},{6,7},{7,6},{8,9},{9,8},{10,11... | collective-permute-start | bytes 1572872 | tf_op jit(solution)/shard_map/ppermute | solution.py:109

commit v4 on v3

--- a/solution.py
+++ b/solution.py
@@ -10,10 +10,10 @@
 NK = 32
 NA, NB, NC, NT = 4, 2, 2, 8
 BS = 128
-GROUP = 8
+GROUP = 16
 TILE = 16
 ZERO = 2 * NY * TILE
-SEATS = (0, 6, 3, 5, 1, 7, 2, 4)
+SEATS = (1, 5, 2, 6, 7, 3, 0, 4)
 
 
 def rot(size, shift):
@@ -118,9 +118,12 @@
     own = jnp.concatenate(
         [first, along_z(first, 1, 1), along_z(second, 2, 1), along_z(second, 3, 0)]
     )
-    pair = jnp.concatenate([own, along_plane(own, NY // 2)])
-    pieces = [pair, along_plane(own, 2), along_plane(own, -2)]
-    pieces += [along_plane(pair, 1), along_plane(pair, -1)]
+    half = TILE // 2
+    behind, ahead = along_plane(own, 2), along_plane(own, -2)
+    near = jnp.concatenate([behind, own, ahead])
+    pieces = [near, along_plane(near[: 2 * TILE], 1), along_plane(near[TILE:], -1)]
+    far = [along_plane(behind[:half], 2), along_plane(ahead[half:], -2)]
+    pieces.append(jnp.concatenate(far))
     pieces += [to_partner(piece) for piece in pieces]
     plan, at = [], 0
     for piece in pieces:

time: 95.6 us -> 92.4 us (0.967)
  the two profiles are of different devices: /device:TPU:29 before, /device:TPU:1 now
where the time goes in v4:
time: 92.4 us; the launch traced here: 91.2 us
  starting transfers between devices  57.2 us (62%)
  waiting for transfers between devices  19.3 us (21%)
  local copies, waits for them, and re-layouts  6.46 us (7%)
  Pallas kernels  4.52 us (5%)
  other arithmetic  3.42 us (4%)
    ppermute x5, starting transfers between devices, to_partner(): return lax.ppermute(value, 'c', rot(NCORE, 1))  27.3 us
    ppermute x6, starting transfers between devices, along_plane(): return lax.ppermute(value, ('x', 'y', 'c'), pairs)  20.1 us
    ppermute x6, waiting for transfers between devices, along_plane(): return lax.ppermute(value, ('x', 'y', 'c'), pairs)  12.3 us
    ppermute x3, starting transfers between devices, along_z(): return lax.ppermute(value, ('zl', 'zh', 'c'), pairs)  9.85 us
    ppermute x3, waiting for transfers between devices, along_z(): return lax.ppermute(value, ('zl', 'zh', 'c'), pairs)  5 us
    pallas_call x1, Pallas kernels, per_device(): pl.pallas_call(kernel, out_shape=jax.ShapeDtypeStruct((NC, BS, BS), jnp.b...  4.52 us
    unnamed x15, local copies, waits for them, and re-layouts  4.17 us
    ppermute x5, waiting for transfers between devices, to_partner(): return lax.ppermute(value, 'c', rot(NCORE, 1))  2.03 us
  transfers between devices with their start and end apart: 14, of which 7 were waited for; matrix products, arithmetic and copies ran while one was open for 7% of the time, Pallas kernels for 0%

profile of v4, /device:TPU:1, one launch (start us, length us, event | category | flops | bytes accessed | tf_op | source)
XLA Modules:
  0.0 91.2 jit_solution(10870175871402587771)
XLA Ops:
  0.0 0.9 %fusion.1 = bf16[4,128,128]{2,1,0:T(8,128)(2,1)S(1)} fusion(bf16[4,128,128]{2,1,0:T(8,128)(2,1)} %param.6, bf16[2,128,128]{2,1,0:T(8,128)(2,1)} %param.7, pred[]{:T(512)S(6)} %eq.114), kind=kLoop, calls=%fused_computation.8 | loop fusion | flops 131072 | bytes 327681 | tf_op jit(solution)/shard_map/jit(_where)/select_n | solution.py:115
  0.9 16.1 %collective-permute-start = (bf16[4,128,128]{2,1,0:T(8,128)(2,1)S(1)}, bf16[4,128,128]{2,1,0:T(8,128)(2,1)S(1)}, u32[]{:S(2)}, u32[]{:S(2)}) collective-permute-start(bf16[4,128,128]{2,1,0:T(8,128)(2,1)S(1)} %fusion.1), channel_id=1, source_target_pairs={{0,1},{1,0},{2,3},{3,2},{4,5},{5,4},{6,7},{7,6},{8,9},{9,8},{10,11... | collective-permute-start | bytes 393224 | tf_op jit(solution)/shard_map/ppermute | solution.py:109
  17.0 1.0 %collective-permute-done = bf16[4,128,128]{2,1,0:T(8,128)(2,1)S(1)} collective-permute-done((bf16[4,128,128]{2,1,0:T(8,128)(2,1)S(1)}, bf16[4,128,128]{2,1,0:T(8,128)(2,1)S(1)}, u32[]{:S(2)}, u32[]{:S(2)}) %collective-permute-start) | collective-permute-done | bytes 131104 | tf_op jit(solution)/shard_map/ppermute | solution.py:109
  18.0 1.7 %constant_dynamic-update-slice_fusion.15 = (bf16[32,128,128]{2,1,0:T(8,128)(2,1)}, bf16[4,128,128]{2,1,0:T(8,128)(2,1)S(1)}, bf16[4,128,128]{2,1,0:T(8,128)(2,1)S(1)}) fusion(bf16[4,128,128]{2,1,0:T(8,128)(2,1)S(1)} %collective-permute-done, bf16[2,128,128]{2,1,0:T(8,128)(2,1)S(1)} %slice.31, bf16[2,128,128]{2,1,0:T(8,128)(2,1)} %param.7, pred[]{:T(512)S(6)} %eq.114, ...), kind=kLoop, calls=%fused_computation.26 | loop fusion | flops 393215 | bytes 786433
  19.7 1.9 %collective-permute-start.1 = (bf16[4,128,128]{2,1,0:T(8,128)(2,1)S(1)}, bf16[4,128,128]{2,1,0:T(8,128)(2,1)S(1)}, u32[]{:S(2)}, u32[]{:S(2)}) collective-permute-start(bf16[4,128,128]{2,1,0:T(8,128)(2,1)S(1)} %get-tuple-element.8), channel_id=1, source_target_pairs={{0,32},{1,17},{16,48},{17,1},{32,64},{33,49},{48,80},{49,33},{64,9... | collective-permute-start | bytes 393224 | tf_op jit(solution)/shard_map/ppermute | solution.py:105
  21.6 7.3 %collective-permute-start.2 = (bf16[4,128,128]{2,1,0:T(8,128)(2,1)S(1)}, bf16[4,128,128]{2,1,0:T(8,128)(2,1)S(1)}, u32[]{:S(2)}, u32[]{:S(2)}) collective-permute-start(bf16[4,128,128]{2,1,0:T(8,128)(2,1)S(1)} %get-tuple-element.26), channel_id=1, source_target_pairs={{0,64},{1,17},{16,80},{17,1},{32,96},{33,49},{48,112},{49,33},{64,... | collective-permute-start | bytes 393224 | tf_op jit(solution)/shard_map/ppermute | solution.py:105
  28.9 0.7 collective-permute-start.3
  29.5 1.2 %collective-permute-done.1 = bf16[4,128,128]{2,1,0:T(8,128)(2,1)S(1)} collective-permute-done((bf16[4,128,128]{2,1,0:T(8,128)(2,1)S(1)}, bf16[4,128,128]{2,1,0:T(8,128)(2,1)S(1)}, u32[]{:S(2)}, u32[]{:S(2)}) %collective-permute-start.1) | collective-permute-done | bytes 131104 | tf_op jit(solution)/shard_map/ppermute | solution.py:105
  30.8 3.8 %collective-permute-done.2 = bf16[4,128,128]{2,1,0:T(8,128)(2,1)S(1)} collective-permute-done((bf16[4,128,128]{2,1,0:T(8,128)(2,1)S(1)}, bf16[4,128,128]{2,1,0:T(8,128)(2,1)S(1)}, u32[]{:S(2)}, u32[]{:S(2)}) %collective-permute-start.2) | collective-permute-done | bytes 131104 | tf_op jit(solution)/shard_map/ppermute | solution.py:105
  34.5 0.0 collective-permute-done.3
  34.6 0.1 pad_maximum_fusion
  34.6 2.5 %collective-permute-start.4 = (bf16[16,128,128]{2,1,0:T(8,128)(2,1)S(1)}, bf16[16,128,128]{2,1,0:T(8,128)(2,1)S(1)}, u32[]{:S(2)}, u32[]{:S(2)}) collective-permute-start(bf16[16,128,128]{2,1,0:T(8,128)(2,1)S(1)} %pad_maximum_fusion), channel_id=1, source_target_pairs={{0,256},{1,5},{2,258},{3,7},{4,260},{5,9},{6,262},{7,11},{8,264},{... | collective-permute-start | bytes 1572872 | tf_op jit(solution)/shard_map/ppermute | solution.py:95
  37.2 4.8 %collective-permute-start.5 = (bf16[16,128,128]{2,1,0:T(8,128)(2,1)S(1)}, bf16[16,128,128]{2,1,0:T(8,128)(2,1)S(1)}, u32[]{:S(2)}, u32[]{:S(2)}) collective-permute-start(bf16[16,128,128]{2,1,0:T(8,128)(2,1)S(1)} %pad_maximum_fusion), channel_id=1, source_target_pairs={{0,768},{1,13},{2,770},{3,15},{4,772},{5,1},{6,774},{7,3},{8,776},... | collective-permute-start | bytes 1572872 | tf_op jit(solution)/shard_map/ppermute | solution.py:95
  42.0 10.0 %collective-permute-done.4 = bf16[16,128,128]{2,1,0:T(8,128)(2,1)S(1)} collective-permute-done((bf16[16,128,128]{2,1,0:T(8,128)(2,1)S(1)}, bf16[16,128,128]{2,1,0:T(8,128)(2,1)S(1)}, u32[]{:S(2)}, u32[]{:S(2)}) %collective-permute-start.4) | collective-permute-done | bytes 524320 | tf_op jit(solution)/shard_map/ppermute | solution.py:95
  52.0 1.1 %constant_dynamic-update-slice_fusion.10 = (bf16[32,128,128]{2,1,0:T(8,128)(2,1)}, bf16[48,128,128]{2,1,0:T(8,128)(2,1)S(1)}) fusion(bf16[16,128,128]{2,1,0:T(8,128)(2,1)S(1)} %collective-permute-done.4), kind=kLoop, calls=%fused_computation.21 | loop fusion | bytes 1572864
  53.1 0.7 constant_dynamic-update-slice_fusion.9
  53.8 0.8 constant_dynamic-update-slice_fusion.14
  54.6 0.8 constant_dynamic-update-slice_fusion.13
  55.4 0.8 constant_dynamic-update-slice_fusion.12
  56.2 0.0 copy-done
  56.2 0.0 collective-permute-done.5
  56.2 1.1 %constant_dynamic-update-slice_fusion.11 = (bf16[32,128,128]{2,1,0:T(8,128)(2,1)}, bf16[48,128,128]{2,1,0:T(8,128)(2,1)S(1)}) fusion(bf16[32,128,128]{2,1,0:T(8,128)(2,1)} %get-tuple-element.15, bf16[16,128,128]{2,1,0:T(8,128)(2,1)S(1)} %collective-permute-done.5, bf16[48,128,128]{2,1,0:T(8,128)(2,1)S(1)} %get-tuple-element.17), kind=kLoop, calls=%fused_computation.22 | loop fusion | bytes 1572864 | tf_op jit(solution)/shard_map/concatenate | solution.py:123
  57.3 3.0 %collective-permute-start.7 = (bf16[32,128,128]{2,1,0:T(8,128)(2,1)}, bf16[32,128,128]{2,1,0:T(8,128)(2,1)S(1)}, u32[]{:S(2)}, u32[]{:S(2)}) collective-permute-start(bf16[32,128,128]{2,1,0:T(8,128)(2,1)} %get-tuple-element.11), channel_id=1, source_target_pairs={{0,896},{1,15},{2,898},{3,1},{4,900},{5,3},{6,902},{7,5},{8,904},{... | collective-permute-start | bytes 3145736 | tf_op jit(solution)/shard_map/ppermute | solution.py:95
  60.3 2.2 %collective-permute-start.6 = (bf16[32,128,128]{2,1,0:T(8,128)(2,1)}, bf16[32,128,128]{2,1,0:T(8,128)(2,1)}, u32[]{:S(2)}, u32[]{:S(2)}) collective-permute-start(bf16[32,128,128]{2,1,0:T(8,128)(2,1)} %get-tuple-element.16), channel_id=1, source_target_pairs={{0,128},{1,3},{2,130},{3,5},{4,132},{5,7},{6,134},{7,9},{8,136},{9... | collective-permute-start | bytes 3145736 | tf_op jit(solution)/shard_map/ppermute | solution.py:95
  62.6 0.0 copy-done.1
  62.6 0.0 copy-done.2
  62.6 0.1 broadcast_in_dim.46
  62.7 0.1 reshape.339
  62.9 1.9 %collective-permute-start.10 = (bf16[48,128,128]{2,1,0:T(8,128)(2,1)S(1)}, bf16[48,128,128]{2,1,0:T(8,128)(2,1)S(1)}, u32[]{:S(2)}, u32[]{:S(2)}) collective-permute-start(bf16[48,128,128]{2,1,0:T(8,128)(2,1)S(1)} %get-tuple-element.12.refs_2_), channel_id=1, source_target_pairs={{0,1},{1,0},{2,3},{3,2},{4,5},{5,4},{6,7},{7,6},{8,9},{9,8},{10,11... | collective-permute-start | bytes 4718600 | tf_op jit(solution)/shard_map/ppermute | solution.py:109
  64.8 0.1 select_reduce_fusion.1
  64.9 1.0 %slice.32 = bf16[8,128,128]{2,1,0:T(8,128)(2,1)S(1)} slice(bf16[16,128,128]{2,1,0:T(8,128)(2,1)} %copy-done), slice={[0:8], [0:128], [0:128]} | slice | bytes 524288 | tf_op jit(solution)/shard_map/slice | solution.py:125
  65.9 3.6 %collective-permute-start.8 = (bf16[8,128,128]{2,1,0:T(8,128)(2,1)S(1)}, bf16[8,128,128]{2,1,0:T(8,128)(2,1)S(1)}, u32[]{:S(2)}, u32[]{:S(2)}) collective-permute-start(bf16[8,128,128]{2,1,0:T(8,128)(2,1)S(1)} %slice.32), channel_id=1, source_target_pairs={{0,256},{1,5},{2,258},{3,7},{4,260},{5,9},{6,262},{7,11},{8,264},{... | collective-permute-start | bytes 786440 | tf_op jit(solution)/shard_map/ppermute | solution.py:95
  69.6 3.8 %collective-permute-start.9 = (bf16[8,128,128]{2,1,0:T(8,128)(2,1)S(1)}, bf16[8,128,128]{2,1,0:T(8,128)(2,1)S(1)}, u32[]{:S(2)}, u32[]{:S(2)}) collective-permute-start(bf16[8,128,128]{2,1,0:T(8,128)(2,1)S(1)} %slice.33), channel_id=1, source_target_pairs={{0,768},{1,13},{2,770},{3,15},{4,772},{5,1},{6,774},{7,3},{8,776},... | collective-permute-start | bytes 786440 | tf_op jit(solution)/shard_map/ppermute | solution.py:95
  73.3 0.1 collective-permute-done.7.refs_4_
  73.4 2.9 %collective-permute-start.12 = (bf16[32,128,128]{2,1,0:T(8,128)(2,1)S(1)}, bf16[32,128,128]{2,1,0:T(8,128)(2,1)S(1)}, u32[]{:S(2)}, u32[]{:S(2)}) collective-permute-start(bf16[32,128,128]{2,1,0:T(8,128)(2,1)S(1)} %collective-permute-done.7.refs_4_), channel_id=1, source_target_pairs={{0,1},{1,0},{2,3},{3,2},{4,5},{5,4},{6,7},{7,6},{8,9},{9,8},{10,11... | collective-permute-start | bytes 3145736 | tf_op jit(solution)/shard_map/ppermute | solution.py:109
  76.3 2.2 %collective-permute-done.6.refs_3_ = bf16[32,128,128]{2,1,0:T(8,128)(2,1)} collective-permute-done((bf16[32,128,128]{2,1,0:T(8,128)(2,1)}, bf16[32,128,128]{2,1,0:T(8,128)(2,1)}, u32[]{:S(2)}, u32[]{:S(2)}) %collective-permute-start.6) | collective-permute-done | bytes 1048608 | tf_op jit(solution)/shard_map/ppermute | solution.py:95
  78.5 2.3 %collective-permute-start.11 = (bf16[32,128,128]{2,1,0:T(8,128)(2,1)}, bf16[32,128,128]{2,1,0:T(8,128)(2,1)S(1)}, u32[]{:S(2)}, u32[]{:S(2)}) collective-permute-start(bf16[32,128,128]{2,1,0:T(8,128)(2,1)} %collective-permute-done.6.refs_3_), channel_id=1, source_target_pairs={{0,1},{1,0},{2,3},{3,2},{4,5},{5,4},{6,7},{7,6},{8,9},{9,8},{10,11... | collective-permute-start | bytes 3145736 | tf_op jit(solution)/shard_map/ppermute | solution.py:109
  80.8 0.1 convert_reduce_fusion.1
  81.0 0.0 collective-permute-done.8
  81.0 0.0 collective-permute-done.9
  81.0 4.1 %collective-permute-start.13 = (bf16[16,128,128]{2,1,0:T(8,128)(2,1)S(1)}, bf16[16,128,128]{2,1,0:T(8,128)(2,1)S(1)}, u32[]{:S(2)}, u32[]{:S(2)}) collective-permute-start(bf16[16,128,128]{2,1,0:T(8,128)(2,1)S(1)} %constant_dynamic-update-slice_fusion.16.refs_5_), channel_id=1, source_target_pairs={{0,1},{1,0},{2,3},{3,2},{4,5},{5,4},{6,7},{7,6},{8,9},{9,8},{10,11... | collective-permute-start | bytes 1572872 | tf_op jit(solution)/shard_map/ppermute | solution.py:109
  85.2 0.1 convert_reduce_fusion
  85.3 0.3 select_reduce_fusion
  85.6 1.1 %collective-permute-done.13.refs_9_ = bf16[16,128,128]{2,1,0:T(8,128)(2,1)S(1)} collective-permute-done((bf16[16,128,128]{2,1,0:T(8,128)(2,1)S(1)}, bf16[16,128,128]{2,1,0:T(8,128)(2,1)S(1)}, u32[]{:S(2)}, u32[]{:S(2)}) %collective-permute-start.13) | collective-permute-done | bytes 524320 | tf_op jit(solution)/shard_map/ppermute | solution.py:109
  86.6 0.0 collective-permute-done.10.refs_6_
  86.6 0.0 collective-permute-done.12.refs_8_
  86.6 0.0 collective-permute-done.11.refs_7_
  86.7 4.5 %block_products.1 = bf16[2,128,128]{2,1,0:T(8,128)(2,1)} custom-call(s32[2,256]{1,0:T(2,128)S(1)} %broadcast_add_fusion.refs_0_, s32[2]{0:T(128)S(1)} %get-tuple-element.9.refs_1_, bf16[48,128,128]{2,1,0:T(8,128)(2,1)S(1)} %get-tuple-element.12.refs_2_, bf16[32,128,128]{2,1,0:T(8,128)(2,1)} %collective-permute-done.6.refs_3_, ...), custom_call_target="tpu_custom_call" | custom-call | flops 536870912 | bytes 6291456 | tf_op jit(solution)/shard_map/block_products/pallas_call | solution.py:138
  (17 shorter events, 0.2 us)
Async XLA Ops:
  0.9 17.1 %collective-permute-start = (bf16[4,128,128]{2,1,0:T(8,128)(2,1)S(1)}, bf16[4,128,128]{2,1,0:T(8,128)(2,1)S(1)}, u32[]{:S(2)}, u32[]{:S(2)}) collective-permute-start(bf16[4,128,128]{2,1,0:T(8,128)(2,1)S(1)} %fusion.1), channel_id=1, source_target_pairs={{0,1},{1,0},{2,3},{3,2},{4,5},{5,4},{6,7},{7,6},{8,9},{9,8},{10,11... | collective-permute-start | bytes 393224 | tf_op jit(solution)/shard_map/ppermute | solution.py:109
  19.7 11.1 %collective-permute-start.1 = (bf16[4,128,128]{2,1,0:T(8,128)(2,1)S(1)}, bf16[4,128,128]{2,1,0:T(8,128)(2,1)S(1)}, u32[]{:S(2)}, u32[]{:S(2)}) collective-permute-start(bf16[4,128,128]{2,1,0:T(8,128)(2,1)S(1)} %get-tuple-element.8), channel_id=1, source_target_pairs={{0,32},{1,17},{16,48},{17,1},{32,64},{33,49},{48,80},{49,33},{64,9... | collective-permute-start | bytes 393224 | tf_op jit(solution)/shard_map/ppermute | solution.py:105
  21.6 13.0 %collective-permute-start.2 = (bf16[4,128,128]{2,1,0:T(8,128)(2,1)S(1)}, bf16[4,128,128]{2,1,0:T(8,128)(2,1)S(1)}, u32[]{:S(2)}, u32[]{:S(2)}) collective-permute-start(bf16[4,128,128]{2,1,0:T(8,128)(2,1)S(1)} %get-tuple-element.26), channel_id=1, source_target_pairs={{0,64},{1,17},{16,80},{17,1},{32,96},{33,49},{48,112},{49,33},{64,... | collective-permute-start | bytes 393224 | tf_op jit(solution)/shard_map/ppermute | solution.py:105
  28.9 5.7 %collective-permute-start.3 = (bf16[4,128,128]{2,1,0:T(8,128)(2,1)S(1)}, bf16[4,128,128]{2,1,0:T(8,128)(2,1)S(1)}, u32[]{:S(2)}, u32[]{:S(2)}) collective-permute-start(bf16[4,128,128]{2,1,0:T(8,128)(2,1)S(1)} %get-tuple-element.26), channel_id=1, source_target_pairs={{0,96},{1,1},{16,112},{17,17},{32,0},{33,33},{48,16},{49,49},{64,3... | collective-permute-start | bytes 393224 | tf_op jit(solution)/shard_map/ppermute | solution.py:105
  34.6 17.4 %collective-permute-start.4 = (bf16[16,128,128]{2,1,0:T(8,128)(2,1)S(1)}, bf16[16,128,128]{2,1,0:T(8,128)(2,1)S(1)}, u32[]{:S(2)}, u32[]{:S(2)}) collective-permute-start(bf16[16,128,128]{2,1,0:T(8,128)(2,1)S(1)} %pad_maximum_fusion), channel_id=1, source_target_pairs={{0,256},{1,5},{2,258},{3,7},{4,260},{5,9},{6,262},{7,11},{8,264},{... | collective-permute-start | bytes 1572872 | tf_op jit(solution)/shard_map/ppermute | solution.py:95
  37.2 19.0 %collective-permute-start.5 = (bf16[16,128,128]{2,1,0:T(8,128)(2,1)S(1)}, bf16[16,128,128]{2,1,0:T(8,128)(2,1)S(1)}, u32[]{:S(2)}, u32[]{:S(2)}) collective-permute-start(bf16[16,128,128]{2,1,0:T(8,128)(2,1)S(1)} %pad_maximum_fusion), channel_id=1, source_target_pairs={{0,768},{1,13},{2,770},{3,15},{4,772},{5,1},{6,774},{7,3},{8,776},... | collective-permute-start | bytes 1572872 | tf_op jit(solution)/shard_map/ppermute | solution.py:95
  52.0 4.1 %copy-start = (bf16[16,128,128]{2,1,0:T(8,128)(2,1)}, bf16[16,128,128]{2,1,0:T(8,128)(2,1)S(1)}, u32[]{:S(2)}) copy-start(bf16[16,128,128]{2,1,0:T(8,128)(2,1)S(1)} %collective-permute-done.4) | copy-start | bytes 1572868
  53.8 8.8 %copy-start.1 = (s32[1,256,3]{1,0,2:T(1,128)S(1)}, s32[1,256,3]{1,0,2:T(1,128)}, u32[]{:S(2)}) copy-start(s32[1,256,3]{1,0,2:T(1,128)} %param.8) | copy-start | bytes 9220
  53.8 8.8 %copy-start.2 = (s32[1,32]{1,0:T(1,128)S(1)}, s32[1,32]{1,0:T(1,128)}, u32[]{:S(2)}) copy-start(s32[1,32]{1,0:T(1,128)} %param.9) | copy-start | bytes 388
  53.8 11.0 %copy-start.3 = (s32[8]{0:T(128)S(1)}, s32[8]{0:T(128)}, u32[]{:S(2)}) copy-start(s32[8]{0:T(128)} %constant.162.clone) | copy-start | bytes 100
  57.3 16.1 %collective-permute-start.7 = (bf16[32,128,128]{2,1,0:T(8,128)(2,1)}, bf16[32,128,128]{2,1,0:T(8,128)(2,1)S(1)}, u32[]{:S(2)}, u32[]{:S(2)}) collective-permute-start(bf16[32,128,128]{2,1,0:T(8,128)(2,1)} %get-tuple-element.11), channel_id=1, source_target_pairs={{0,896},{1,15},{2,898},{3,1},{4,900},{5,3},{6,902},{7,5},{8,904},{... | collective-permute-start | bytes 3145736 | tf_op jit(solution)/shard_map/ppermute | solution.py:95
  60.3 18.2 %collective-permute-start.6 = (bf16[32,128,128]{2,1,0:T(8,128)(2,1)}, bf16[32,128,128]{2,1,0:T(8,128)(2,1)}, u32[]{:S(2)}, u32[]{:S(2)}) collective-permute-start(bf16[32,128,128]{2,1,0:T(8,128)(2,1)} %get-tuple-element.16), channel_id=1, source_target_pairs={{0,128},{1,3},{2,130},{3,5},{4,132},{5,7},{6,134},{7,9},{8,136},{9... | collective-permute-start | bytes 3145736 | tf_op jit(solution)/shard_map/ppermute | solution.py:95
  62.9 23.8 %collective-permute-start.10 = (bf16[48,128,128]{2,1,0:T(8,128)(2,1)S(1)}, bf16[48,128,128]{2,1,0:T(8,128)(2,1)S(1)}, u32[]{:S(2)}, u32[]{:S(2)}) collective-permute-start(bf16[48,128,128]{2,1,0:T(8,128)(2,1)S(1)} %get-tuple-element.12.refs_2_), channel_id=1, source_target_pairs={{0,1},{1,0},{2,3},{3,2},{4,5},{5,4},{6,7},{7,6},{8,9},{9,8},{10,11... | collective-permute-start | bytes 4718600 | tf_op jit(solution)/shard_map/ppermute | solution.py:109
  65.9 15.1 %collective-permute-start.8 = (bf16[8,128,128]{2,1,0:T(8,128)(2,1)S(1)}, bf16[8,128,128]{2,1,0:T(8,128)(2,1)S(1)}, u32[]{:S(2)}, u32[]{:S(2)}) collective-permute-start(bf16[8,128,128]{2,1,0:T(8,128)(2,1)S(1)} %slice.32), channel_id=1, source_target_pairs={{0,256},{1,5},{2,258},{3,7},{4,260},{5,9},{6,262},{7,11},{8,264},{... | collective-permute-start | bytes 786440 | tf_op jit(solution)/shard_map/ppermute | solution.py:95
  69.6 11.4 %collective-permute-start.9 = (bf16[8,128,128]{2,1,0:T(8,128)(2,1)S(1)}, bf16[8,128,128]{2,1,0:T(8,128)(2,1)S(1)}, u32[]{:S(2)}, u32[]{:S(2)}) collective-permute-start(bf16[8,128,128]{2,1,0:T(8,128)(2,1)S(1)} %slice.33), channel_id=1, source_target_pairs={{0,768},{1,13},{2,770},{3,15},{4,772},{5,1},{6,774},{7,3},{8,776},... | collective-permute-start | bytes 786440 | tf_op jit(solution)/shard_map/ppermute | solution.py:95
  73.4 13.2 %collective-permute-start.12 = (bf16[32,128,128]{2,1,0:T(8,128)(2,1)S(1)}, bf16[32,128,128]{2,1,0:T(8,128)(2,1)S(1)}, u32[]{:S(2)}, u32[]{:S(2)}) collective-permute-start(bf16[32,128,128]{2,1,0:T(8,128)(2,1)S(1)} %collective-permute-done.7.refs_4_), channel_id=1, source_target_pairs={{0,1},{1,0},{2,3},{3,2},{4,5},{5,4},{6,7},{7,6},{8,9},{9,8},{10,11... | collective-permute-start | bytes 3145736 | tf_op jit(solution)/shard_map/ppermute | solution.py:109
  78.5 8.1 %collective-permute-start.11 = (bf16[32,128,128]{2,1,0:T(8,128)(2,1)}, bf16[32,128,128]{2,1,0:T(8,128)(2,1)S(1)}, u32[]{:S(2)}, u32[]{:S(2)}) collective-permute-start(bf16[32,128,128]{2,1,0:T(8,128)(2,1)} %collective-permute-done.6.refs_3_), channel_id=1, source_target_pairs={{0,1},{1,0},{2,3},{3,2},{4,5},{5,4},{6,7},{7,6},{8,9},{9,8},{10,11... | collective-permute-start | bytes 3145736 | tf_op jit(solution)/shard_map/ppermute | solution.py:109
  81.0 5.6 %collective-permute-start.13 = (bf16[16,128,128]{2,1,0:T(8,128)(2,1)S(1)}, bf16[16,128,128]{2,1,0:T(8,128)(2,1)S(1)}, u32[]{:S(2)}, u32[]{:S(2)}) collective-permute-start(bf16[16,128,128]{2,1,0:T(8,128)(2,1)S(1)} %constant_dynamic-update-slice_fusion.16.refs_5_), channel_id=1, source_target_pairs={{0,1},{1,0},{2,3},{3,2},{4,5},{5,4},{6,7},{7,6},{8,9},{9,8},{10,11... | collective-permute-start | bytes 1572872 | tf_op jit(solution)/shard_map/ppermute | solution.py:109

commit v5 on v4

--- a/solution.py
+++ b/solution.py
@@ -11,8 +11,8 @@
 NA, NB, NC, NT = 4, 2, 2, 8
 BS = 128
 GROUP = 16
-TILE = 16
-ZERO = 2 * NY * TILE
+TILE = 8
+ZERO = 3 * NY * TILE
 SEATS = (1, 5, 2, 6, 7, 3, 0, 4)
 
 
@@ -33,14 +33,12 @@
     row, col = x * NZL + zl, (zh * NY + y) * NCORE + c
     source = (k - row) % NK
     from_zh, from_y, from_c = source // (NY * NCORE), source // NCORE % NY, source % NCORE
-    near = from_zh == zh
-    part = jnp.where(from_c == 0, jnp.where(near, 0, 1), jnp.where(near, 3, 2))
-    left = (jnp.where(c == 1, 0, NY) + seat_of(from_y - y)) * TILE + part * NA + pairs[:, 0]
+    left = (jnp.where(from_c == c, 0, NY) + from_y) * TILE + pairs[:, 0]
+    left = left + jnp.where(from_zh == zh, 0, NA)
     holder = (k - col) % NK
-    part = (zl - holder % NZL) % NZL
-    right = (jnp.where(c == 0, 0, NY) + seat_of(holder // NZL - x)) * TILE
-    right = right + (part * NCORE + c) * NB + pairs[:, 1]
-    code = left * 512 + right
+    right = (2 * NY + seat_of(holder // NZL - x)) * TILE
+    right = right + (zl - holder % NZL) % NZL * NB + pairs[:, 1]
+    code = left * 256 + right
     target = jnp.arange(NC, dtype=jnp.int32)[:, None]
     mine = live[None] & (pairs[:, 2][None] == target)
     seat = jnp.sum(mine[:, None, :] & (flat[None, None, :] < flat[None, :, None]), axis=-1)
@@ -66,8 +64,8 @@
         first, second = [], []
         for g in range(GROUP):
             code = codes[n, step * GROUP + g]
-            first.append(held[code // 512])
-            second.append(held[code % 512])
+            first.append(held[code // 256])
+            second.append(held[code % 256])
         return jnp.dot(
             jnp.concatenate(first, axis=1),
             jnp.concatenate(second, axis=0),
@@ -85,46 +83,30 @@
     out[1] = total[1].astype(jnp.bfloat16)
 
 
-def along_plane(value, shift):
-    pairs = []
-    for x in range(NX):
-        for y in range(NY):
-            place = (x * NY + y) * NCORE
-            pairs.append((place, ((x + shift) % NX * NY + y) * NCORE))
-            pairs.append((place + 1, (x * NY + (y + shift) % NY) * NCORE + 1))
-    return lax.ppermute(value, ("x", "y", "c"), pairs)
-
-
-def along_z(value, shift, swap):
-    pairs = []
-    for zl in range(NZL):
-        for zh in range(NZH):
-            place = (zl * NZH + zh) * NCORE
-            pairs.append((place, ((zl + shift) % NZL * NZH + zh) * NCORE))
-            pairs.append((place + 1, (zl * NZH + (zh + swap) % NZH) * NCORE + 1))
-    return lax.ppermute(value, ("zl", "zh", "c"), pairs)
-
-
-def to_partner(value):
-    return lax.ppermute(value, "c", rot(NCORE, 1))
-
-
 def per_device(left_blocks, right_blocks, pair_lists, pair_count):
     x, zl, zh, y, c = (lax.axis_index(name) for name in ("x", "zl", "zh", "y", "c"))
 
-    got = to_partner(jnp.where(c == 0, left_blocks, jnp.concatenate([right_blocks] * 2)))
-    rights = jnp.concatenate([right_blocks, got[:NB]])
-    first, second = jnp.where(c == 0, rights, got), jnp.where(c == 0, rights, left_blocks)
-    own = jnp.concatenate(
-        [first, along_z(first, 1, 1), along_z(second, 2, 1), along_z(second, 3, 0)]
-    )
+    own = [right_blocks]
+    own += [lax.ppermute(right_blocks, "zl", rot(NZL, shift)) for shift in range(1, NZL)]
+    own = jnp.concatenate(own)
+    lefts = jnp.concatenate([left_blocks, lax.ppermute(left_blocks, "zh", rot(NZH, 1))])
+    lefts, own = lax.optimization_barrier((lefts, own))
+    spread = jnp.broadcast_to(lefts[None], (NY,) + lefts.shape).reshape(NY * TILE, BS, BS)
+    lefts = lax.all_to_all(spread, "y", 0, 0, tiled=True)
+
     half = TILE // 2
-    behind, ahead = along_plane(own, 2), along_plane(own, -2)
+    behind = lax.ppermute(own, "x", rot(NX, 2))
+    ahead = lax.ppermute(own, "x", rot(NX, -2))
+    behind, ahead = lax.optimization_barrier((behind, ahead))
     near = jnp.concatenate([behind, own, ahead])
-    pieces = [near, along_plane(near[: 2 * TILE], 1), along_plane(near[TILE:], -1)]
-    far = [along_plane(behind[:half], 2), along_plane(ahead[half:], -2)]
-    pieces.append(jnp.concatenate(far))
-    pieces += [to_partner(piece) for piece in pieces]
+    rights = [near]
+    rights.append(lax.ppermute(near[: 2 * TILE], "x", rot(NX, 1)))
+    rights.append(lax.ppermute(near[TILE:], "x", rot(NX, -1)))
+    rights.append(lax.ppermute(behind[:half], "x", rot(NX, 2)))
+    rights.append(lax.ppermute(ahead[half:], "x", rot(NX, -2)))
+
+    lefts, *rights = lax.optimization_barrier((lefts, *rights))
+    pieces = [lefts, lax.ppermute(lefts, "c", rot(NCORE, 1))] + rights
     plan, at = [], 0
     for piece in pieces:
         plan.append((piece.shape[0], at))

time: 92.4 us -> 108 us (1.17)
  starting transfers between devices: 57.2 us -> 64.6 us
  waiting for transfers between devices: 19.3 us -> 24.5 us
  local copies, waits for them, and re-layouts: 6.46 us -> 8.05 us
  other arithmetic: 3.42 us -> 4.96 us
    all_to_all x0 -> x1, starting transfers between devices: none -> 7.58 us  [per_device(): lefts = lax.all_to_all(spread, 'y', 0, 0, tiled=True)]
    all_to_all x0 -> x1, waiting for transfers between devices: none -> 6.95 us  [per_device(): lefts = lax.all_to_all(spread, 'y', 0, 0, tiled=True)]
    concatenate x1 -> x4, other arithmetic: 0.07 us -> 2.93 us  [the longest x2 1.13 us: per_device(): near = jnp.concatenate([behind, own, ahead])]
    broadcast_in_dim x0 -> x1, local copies, waits for them, and re-layouts: none -> 1.84 us  [per_device(): jnp.broadcast_to(lefts[None], (NY,) + lefts.shape)]
    ppermute x14 -> x11, waiting for transfers between devices: 19.3 us -> 17.6 us  [the longest x1 8.06 us: per_device(): ahead = lax.ppermute(own, 'x', rot(NX, -2))]
    unnamed x1 -> x0, other arithmetic: 1.68 us -> none
    concatenate x2 -> x0, local copies, waits for them, and re-layouts: 1.13 us -> none  [the longest x1 1.1 us: per_device(): near = jnp.concatenate([behind, own, ahead])]
    unnamed x15 -> x13, local copies, waits for them, and re-layouts: 4.17 us -> 4 us
  transfers between devices with their start and end apart: 14 -> 12, of which waited for: 7 -> 6; matrix products, arithmetic and copies ran while one was open for 7% -> 6% of each run, Pallas kernels for 0% -> 0%
where the time goes in v5:
time: 108 us; the launch traced here: 107 us
  starting transfers between devices  64.6 us (60%)
  waiting for transfers between devices  24.5 us (23%)
  local copies, waits for them, and re-layouts  8.05 us (7%)
  other arithmetic  4.96 us (5%)
  Pallas kernels  4.9 us (5%)
    ppermute x3, starting transfers between devices, per_device(): lax.ppermute(right_blocks, 'zl', rot(NZL, shift))  15.5 us
    ppermute x1, starting transfers between devices, per_device(): lax.ppermute(left_blocks, 'zh', rot(NZH, 1))  12.5 us
    ppermute x1, waiting for transfers between devices, per_device(): ahead = lax.ppermute(own, 'x', rot(NX, -2))  8.06 us
    ppermute x1, starting transfers between devices, per_device(): rights.append(lax.ppermute(near[TILE:], 'x', rot(NX, -1)))  8.03 us
    all_to_all x1, starting transfers between devices, per_device(): lefts = lax.all_to_all(spread, 'y', 0, 0, tiled=True)  7.58 us
    all_to_all x1, waiting for transfers between devices, per_device(): lefts = lax.all_to_all(spread, 'y', 0, 0, tiled=True)  6.95 us
    ppermute x1, waiting for transfers between devices, per_device(): rights.append(lax.ppermute(ahead[half:], 'x', rot(NX, -2)))  5.64 us
    ppermute x1, starting transfers between devices, per_device(): pieces = [lefts, lax.ppermute(lefts, 'c', rot(NCORE, 1))] + rights  5.6 us
  transfers between devices with their start and end apart: 12, of which 6 were waited for; matrix products, arithmetic and copies ran while one was open for 6% of the time, Pallas kernels for 0%

profile of v5, /device:TPU:1, one launch (start us, length us, event | category | flops | bytes accessed | tf_op | source)
XLA Modules:
  0.0 107.3 jit_solution(8015401121167180815)
XLA Ops:
  0.0 8.4 %collective-permute-start.2 = (bf16[2,128,128]{2,1,0:T(8,128)(2,1)}, bf16[2,128,128]{2,1,0:T(8,128)(2,1)S(1)}, u32[]{:S(2)}, u32[]{:S(2)}) collective-permute-start(bf16[2,128,128]{2,1,0:T(8,128)(2,1)} %param.6), channel_id=1, source_target_pairs={{0,64},{32,96},{64,0},{96,32},{1,65},{33,97},{65,1},{97,33},{2,66}... | collective-permute-start | bytes 196616 | tf_op jit(solution)/shard_map/ppermute | solution.py:90
  8.5 4.9 %collective-permute-start.1 = (bf16[2,128,128]{2,1,0:T(8,128)(2,1)}, bf16[2,128,128]{2,1,0:T(8,128)(2,1)S(1)}, u32[]{:S(2)}, u32[]{:S(2)}) collective-permute-start(bf16[2,128,128]{2,1,0:T(8,128)(2,1)} %param.6), channel_id=1, source_target_pairs={{0,32},{32,64},{64,96},{96,0},{1,33},{33,65},{65,97},{97,1},{2,34}... | collective-permute-start | bytes 196616 | tf_op jit(solution)/shard_map/ppermute | solution.py:90
  13.4 2.2 %collective-permute-start.3 = (bf16[2,128,128]{2,1,0:T(8,128)(2,1)}, bf16[2,128,128]{2,1,0:T(8,128)(2,1)S(1)}, u32[]{:S(2)}, u32[]{:S(2)}) collective-permute-start(bf16[2,128,128]{2,1,0:T(8,128)(2,1)} %param.6), channel_id=1, source_target_pairs={{0,96},{32,0},{64,32},{96,64},{1,97},{33,1},{65,33},{97,65},{2,98}... | collective-permute-start | bytes 196616 | tf_op jit(solution)/shard_map/ppermute | solution.py:90
  15.5 12.5 %collective-permute-start = (bf16[4,128,128]{2,1,0:T(8,128)(2,1)}, bf16[4,128,128]{2,1,0:T(8,128)(2,1)S(1)}, u32[]{:S(2)}, u32[]{:S(2)}) collective-permute-start(bf16[4,128,128]{2,1,0:T(8,128)(2,1)} %param.5), channel_id=1, source_target_pairs={{0,16},{16,0},{1,17},{17,1},{2,18},{18,2},{3,19},{19,3},{4,20},{20... | collective-permute-start | bytes 393224 | tf_op jit(solution)/shard_map/ppermute | solution.py:92
  28.0 0.0 collective-permute-done.2
  28.0 0.0 collective-permute-done.1
  28.1 0.0 collective-permute-done.3
  28.1 0.9 pad_maximum_fusion.4
  28.9 0.0 copy-start.4
  29.0 2.2 %collective-permute-done = bf16[4,128,128]{2,1,0:T(8,128)(2,1)S(1)} collective-permute-done((bf16[4,128,128]{2,1,0:T(8,128)(2,1)}, bf16[4,128,128]{2,1,0:T(8,128)(2,1)S(1)}, u32[]{:S(2)}, u32[]{:S(2)}) %collective-permute-start) | collective-permute-done | bytes 131104 | tf_op jit(solution)/shard_map/ppermute | solution.py:92
  31.2 0.9 pad_maximum_fusion.3
  32.1 1.8 %broadcast_in_dim.51 = bf16[8,8,128,128]{3,2,1,0:T(8,128)(2,1)} broadcast(bf16[8,128,128]{2,1,0:T(8,128)(2,1)S(1)} %pad_maximum_fusion.3), dimensions={1,2,3} | broadcast | bytes 2359296 | tf_op jit(solution)/shard_map/broadcast_in_dim | solution.py:94
  33.9 7.6 %all-to-all-start = ((bf16[64,128,128]{2,1,0:T(8,128)(2,1)}), bf16[64,128,128]{2,1,0:T(8,128)(2,1)S(1)}, u32[]{:S(2)}, u32[]{:S(2)}) async-start(bf16[64,128,128]{2,1,0:T(8,128)(2,1)} %bitcast.8), calls=%async_computation | async-start | bytes 4194304 | tf_op jit(solution)/shard_map/all_to_all | solution.py:95
  41.5 0.0 copy-start.5
  41.5 5.4 %collective-permute-start.5 = (bf16[8,128,128]{2,1,0:T(8,128)(2,1)S(1)}, bf16[8,128,128]{2,1,0:T(8,128)(2,1)S(1)}, u32[]{:S(2)}, u32[]{:S(2)}) collective-permute-start(bf16[8,128,128]{2,1,0:T(8,128)(2,1)S(1)} %pad_maximum_fusion.4), channel_id=1, source_target_pairs={{0,768},{128,896},{256,0},{384,128},{512,256},{640,384},{768,512},... | collective-permute-start | bytes 786440 | tf_op jit(solution)/shard_map/ppermute | solution.py:99
  46.9 1.9 %collective-permute-start.4 = (bf16[8,128,128]{2,1,0:T(8,128)(2,1)S(1)}, bf16[8,128,128]{2,1,0:T(8,128)(2,1)S(1)}, u32[]{:S(2)}, u32[]{:S(2)}) collective-permute-start(bf16[8,128,128]{2,1,0:T(8,128)(2,1)S(1)} %pad_maximum_fusion.4), channel_id=1, source_target_pairs={{0,256},{128,384},{256,512},{384,640},{512,768},{640,896},{768,0},... | collective-permute-start | bytes 786440 | tf_op jit(solution)/shard_map/ppermute | solution.py:98
  48.8 8.1 %collective-permute-done.5 = bf16[8,128,128]{2,1,0:T(8,128)(2,1)S(1)} collective-permute-done((bf16[8,128,128]{2,1,0:T(8,128)(2,1)S(1)}, bf16[8,128,128]{2,1,0:T(8,128)(2,1)S(1)}, u32[]{:S(2)}, u32[]{:S(2)}) %collective-permute-start.5) | collective-permute-done | bytes 262176 | tf_op jit(solution)/shard_map/ppermute | solution.py:99
  56.9 0.3 collective-permute-done.4
  57.1 0.0 copy-done.4
  57.1 0.1 pad_maximum_fusion.2
  57.2 8.0 %collective-permute-start.7 = (bf16[16,128,128]{2,1,0:T(8,128)(2,1)S(1)}, bf16[16,128,128]{2,1,0:T(8,128)(2,1)S(1)}, u32[]{:S(2)}, u32[]{:S(2)}) collective-permute-start(bf16[16,128,128]{2,1,0:T(8,128)(2,1)S(1)} %get-tuple-element.27), channel_id=1, source_target_pairs={{0,896},{128,0},{256,128},{384,256},{512,384},{640,512},{768,640},... | collective-permute-start | bytes 1572872 | tf_op jit(solution)/shard_map/ppermute | solution.py:104
  65.3 1.9 %collective-permute-start.6 = (bf16[16,128,128]{2,1,0:T(8,128)(2,1)S(1)}, bf16[16,128,128]{2,1,0:T(8,128)(2,1)S(1)}, u32[]{:S(2)}, u32[]{:S(2)}) collective-permute-start(bf16[16,128,128]{2,1,0:T(8,128)(2,1)S(1)} %get-tuple-element.28), channel_id=1, source_target_pairs={{0,128},{128,256},{256,384},{384,512},{512,640},{640,768},{768,896... | collective-permute-start | bytes 1572872 | tf_op jit(solution)/shard_map/ppermute | solution.py:103
  67.2 3.5 %collective-permute-start.9 = (bf16[4,128,128]{2,1,0:T(8,128)(2,1)S(1)}, bf16[4,128,128]{2,1,0:T(8,128)(2,1)S(1)}, u32[]{:S(2)}, u32[]{:S(2)}) collective-permute-start(bf16[4,128,128]{2,1,0:T(8,128)(2,1)S(1)} %slice.23), channel_id=1, source_target_pairs={{0,768},{128,896},{256,0},{384,128},{512,256},{640,384},{768,512},... | collective-permute-start | bytes 393224 | tf_op jit(solution)/shard_map/ppermute | solution.py:106
  70.8 2.6 %collective-permute-start.8 = (bf16[4,128,128]{2,1,0:T(8,128)(2,1)S(1)}, bf16[4,128,128]{2,1,0:T(8,128)(2,1)S(1)}, u32[]{:S(2)}, u32[]{:S(2)}) collective-permute-start(bf16[4,128,128]{2,1,0:T(8,128)(2,1)S(1)} %slice.22), channel_id=1, source_target_pairs={{0,256},{128,384},{256,512},{384,640},{512,768},{640,896},{768,0},... | collective-permute-start | bytes 393224 | tf_op jit(solution)/shard_map/ppermute | solution.py:105
  73.4 1.0 pad_maximum_fusion.refs_4_
  74.5 5.6 %collective-permute-done.9.refs_8_ = bf16[4,128,128]{2,1,0:T(8,128)(2,1)S(1)} collective-permute-done((bf16[4,128,128]{2,1,0:T(8,128)(2,1)S(1)}, bf16[4,128,128]{2,1,0:T(8,128)(2,1)S(1)}, u32[]{:S(2)}, u32[]{:S(2)}) %collective-permute-start.9) | collective-permute-done | bytes 131104 | tf_op jit(solution)/shard_map/ppermute | solution.py:106
  80.1 1.4 %collective-permute-done.8.refs_7_ = bf16[4,128,128]{2,1,0:T(8,128)(2,1)S(1)} collective-permute-done((bf16[4,128,128]{2,1,0:T(8,128)(2,1)S(1)}, bf16[4,128,128]{2,1,0:T(8,128)(2,1)S(1)}, u32[]{:S(2)}, u32[]{:S(2)}) %collective-permute-start.8) | collective-permute-done | bytes 131104 | tf_op jit(solution)/shard_map/ppermute | solution.py:105
  81.5 0.7 copy-done.2
  82.2 0.0 collective-permute-done.7.refs_6_
  82.2 0.0 collective-permute-done.6.refs_5_
  82.2 0.8 copy-done
  83.0 7.0 %all-to-all-done.refs_2_ = bf16[64,128,128]{2,1,0:T(8,128)(2,1)S(1)} async-done(((bf16[64,128,128]{2,1,0:T(8,128)(2,1)}), bf16[64,128,128]{2,1,0:T(8,128)(2,1)S(1)}, u32[]{:S(2)}, u32[]{:S(2)}) %all-to-all-start) | async-done | bytes 2097184 | tf_op jit(solution)/shard_map/all_to_all | solution.py:95
  90.0 5.6 %collective-permute-start.10 = (bf16[64,128,128]{2,1,0:T(8,128)(2,1)S(1)}, bf16[64,128,128]{2,1,0:T(8,128)(2,1)}, u32[]{:S(2)}, u32[]{:S(2)}) collective-permute-start(bf16[64,128,128]{2,1,0:T(8,128)(2,1)S(1)} %all-to-all-done.refs_2_), channel_id=1, source_target_pairs={{0,1},{1,0},{2,3},{3,2},{4,5},{5,4},{6,7},{7,6},{8,9},{9,8},{10,11... | collective-permute-start | bytes 6291464 | tf_op jit(solution)/shard_map/ppermute | solution.py:109
  95.6 0.0 copy-done.5
  95.6 0.6 copy.8
  96.2 0.7 broadcast_in_dim.26
  96.9 0.7 reshape.300
  97.6 0.7 select_reduce_fusion.1
  98.4 0.7 fusion.2
  99.0 0.8 fusion.17
  99.8 0.1 convert_reduce_fusion.1
  100.0 0.1 convert_reduce_fusion
  100.2 0.2 select_reduce_fusion
  100.4 0.0 collective-permute-done.10.refs_3_
  100.4 0.0 copy-start.1
  100.4 1.0 copy-done.1
  101.5 0.9 copy-done.3
  102.4 4.9 %block_products.1 = bf16[2,128,128]{2,1,0:T(8,128)(2,1)} custom-call(s32[2,256]{1,0:T(2,128)S(1)} %broadcast_add_fusion.refs_0_, s32[2]{0:T(128)S(1)} %get-tuple-element.25.refs_1_, bf16[64,128,128]{2,1,0:T(8,128)(2,1)S(1)} %all-to-all-done.refs_2_, bf16[64,128,128]{2,1,0:T(8,128)(2,1)} %collective-permute-done.10.refs_3_, ...), custom_call_target="tpu_custom_call" | custom-call | flops 536870912 | bytes 6291456 | tf_op jit(solution)/shard_map/block_products/pallas_call | solution.py:120
  (9 shorter events, 0.1 us)
Async XLA Ops:
  0.0 28.0 %collective-permute-start.2 = (bf16[2,128,128]{2,1,0:T(8,128)(2,1)}, bf16[2,128,128]{2,1,0:T(8,128)(2,1)S(1)}, u32[]{:S(2)}, u32[]{:S(2)}) collective-permute-start(bf16[2,128,128]{2,1,0:T(8,128)(2,1)} %param.6), channel_id=1, source_target_pairs={{0,64},{32,96},{64,0},{96,32},{1,65},{33,97},{65,1},{97,33},{2,66}... | collective-permute-start | bytes 196616 | tf_op jit(solution)/shard_map/ppermute | solution.py:90
  8.5 19.6 %collective-permute-start.1 = (bf16[2,128,128]{2,1,0:T(8,128)(2,1)}, bf16[2,128,128]{2,1,0:T(8,128)(2,1)S(1)}, u32[]{:S(2)}, u32[]{:S(2)}) collective-permute-start(bf16[2,128,128]{2,1,0:T(8,128)(2,1)} %param.6), channel_id=1, source_target_pairs={{0,32},{32,64},{64,96},{96,0},{1,33},{33,65},{65,97},{97,1},{2,34}... | collective-permute-start | bytes 196616 | tf_op jit(solution)/shard_map/ppermute | solution.py:90
  13.4 14.7 %collective-permute-start.3 = (bf16[2,128,128]{2,1,0:T(8,128)(2,1)}, bf16[2,128,128]{2,1,0:T(8,128)(2,1)S(1)}, u32[]{:S(2)}, u32[]{:S(2)}) collective-permute-start(bf16[2,128,128]{2,1,0:T(8,128)(2,1)} %param.6), channel_id=1, source_target_pairs={{0,96},{32,0},{64,32},{96,64},{1,97},{33,1},{65,33},{97,65},{2,98}... | collective-permute-start | bytes 196616 | tf_op jit(solution)/shard_map/ppermute | solution.py:90
  15.5 15.6 %collective-permute-start = (bf16[4,128,128]{2,1,0:T(8,128)(2,1)}, bf16[4,128,128]{2,1,0:T(8,128)(2,1)S(1)}, u32[]{:S(2)}, u32[]{:S(2)}) collective-permute-start(bf16[4,128,128]{2,1,0:T(8,128)(2,1)} %param.5), channel_id=1, source_target_pairs={{0,16},{16,0},{1,17},{17,1},{2,18},{18,2},{3,19},{19,3},{4,20},{20... | collective-permute-start | bytes 393224 | tf_op jit(solution)/shard_map/ppermute | solution.py:92
  28.9 28.2 %copy-start.4 = (bf16[8,128,128]{2,1,0:T(8,128)(2,1)}, bf16[8,128,128]{2,1,0:T(8,128)(2,1)S(1)}, u32[]{:S(2)}) copy-start(bf16[8,128,128]{2,1,0:T(8,128)(2,1)S(1)} %pad_maximum_fusion.4) | copy-start | bytes 786436
  33.9 56.0 %all-to-all-start = ((bf16[64,128,128]{2,1,0:T(8,128)(2,1)}), bf16[64,128,128]{2,1,0:T(8,128)(2,1)S(1)}, u32[]{:S(2)}, u32[]{:S(2)}) async-start(bf16[64,128,128]{2,1,0:T(8,128)(2,1)} %bitcast.8), calls=%async_computation | async-start | bytes 4194304 | tf_op jit(solution)/shard_map/all_to_all | solution.py:95
  41.5 54.1 %copy-start.5 = (s32[1,256,3]{1,0,2:T(1,128)S(1)}, s32[1,256,3]{1,0,2:T(1,128)}, u32[]{:S(2)}) copy-start(s32[1,256,3]{1,0,2:T(1,128)} %param.7) | copy-start | bytes 9220
  41.5 15.4 %collective-permute-start.5 = (bf16[8,128,128]{2,1,0:T(8,128)(2,1)S(1)}, bf16[8,128,128]{2,1,0:T(8,128)(2,1)S(1)}, u32[]{:S(2)}, u32[]{:S(2)}) collective-permute-start(bf16[8,128,128]{2,1,0:T(8,128)(2,1)S(1)} %pad_maximum_fusion.4), channel_id=1, source_target_pairs={{0,768},{128,896},{256,0},{384,128},{512,256},{640,384},{768,512},... | collective-permute-start | bytes 786440 | tf_op jit(solution)/shard_map/ppermute | solution.py:99
  46.9 10.3 %collective-permute-start.4 = (bf16[8,128,128]{2,1,0:T(8,128)(2,1)S(1)}, bf16[8,128,128]{2,1,0:T(8,128)(2,1)S(1)}, u32[]{:S(2)}, u32[]{:S(2)}) collective-permute-start(bf16[8,128,128]{2,1,0:T(8,128)(2,1)S(1)} %pad_maximum_fusion.4), channel_id=1, source_target_pairs={{0,256},{128,384},{256,512},{384,640},{512,768},{640,896},{768,0},... | collective-permute-start | bytes 786440 | tf_op jit(solution)/shard_map/ppermute | solution.py:98
  57.2 25.0 %collective-permute-start.7 = (bf16[16,128,128]{2,1,0:T(8,128)(2,1)S(1)}, bf16[16,128,128]{2,1,0:T(8,128)(2,1)S(1)}, u32[]{:S(2)}, u32[]{:S(2)}) collective-permute-start(bf16[16,128,128]{2,1,0:T(8,128)(2,1)S(1)} %get-tuple-element.27), channel_id=1, source_target_pairs={{0,896},{128,0},{256,128},{384,256},{512,384},{640,512},{768,640},... | collective-permute-start | bytes 1572872 | tf_op jit(solution)/shard_map/ppermute | solution.py:104
  65.3 16.9 %collective-permute-start.6 = (bf16[16,128,128]{2,1,0:T(8,128)(2,1)S(1)}, bf16[16,128,128]{2,1,0:T(8,128)(2,1)S(1)}, u32[]{:S(2)}, u32[]{:S(2)}) collective-permute-start(bf16[16,128,128]{2,1,0:T(8,128)(2,1)S(1)} %get-tuple-element.28), channel_id=1, source_target_pairs={{0,128},{128,256},{256,384},{384,512},{512,640},{640,768},{768,896... | collective-permute-start | bytes 1572872 | tf_op jit(solution)/shard_map/ppermute | solution.py:103
  67.2 12.9 %collective-permute-start.9 = (bf16[4,128,128]{2,1,0:T(8,128)(2,1)S(1)}, bf16[4,128,128]{2,1,0:T(8,128)(2,1)S(1)}, u32[]{:S(2)}, u32[]{:S(2)}) collective-permute-start(bf16[4,128,128]{2,1,0:T(8,128)(2,1)S(1)} %slice.23), channel_id=1, source_target_pairs={{0,768},{128,896},{256,0},{384,128},{512,256},{640,384},{768,512},... | collective-permute-start | bytes 393224 | tf_op jit(solution)/shard_map/ppermute | solution.py:106
  70.8 10.8 %collective-permute-start.8 = (bf16[4,128,128]{2,1,0:T(8,128)(2,1)S(1)}, bf16[4,128,128]{2,1,0:T(8,128)(2,1)S(1)}, u32[]{:S(2)}, u32[]{:S(2)}) collective-permute-start(bf16[4,128,128]{2,1,0:T(8,128)(2,1)S(1)} %slice.22), channel_id=1, source_target_pairs={{0,256},{128,384},{256,512},{384,640},{512,768},{640,896},{768,0},... | collective-permute-start | bytes 393224 | tf_op jit(solution)/shard_map/ppermute | solution.py:105
  81.5 0.7 copy-start.2
  82.2 0.8 copy-start
  90.0 10.5 %collective-permute-start.10 = (bf16[64,128,128]{2,1,0:T(8,128)(2,1)S(1)}, bf16[64,128,128]{2,1,0:T(8,128)(2,1)}, u32[]{:S(2)}, u32[]{:S(2)}) collective-permute-start(bf16[64,128,128]{2,1,0:T(8,128)(2,1)S(1)} %all-to-all-done.refs_2_), channel_id=1, source_target_pairs={{0,1},{1,0},{2,3},{3,2},{4,5},{5,4},{6,7},{7,6},{8,9},{9,8},{10,11... | collective-permute-start | bytes 6291464 | tf_op jit(solution)/shard_map/ppermute | solution.py:109
  100.4 1.0 copy-start.1
  101.5 0.9 copy-start.3

commit v6 on v4

--- a/solution.py
+++ b/solution.py
@@ -13,7 +13,7 @@
 GROUP = 16
 TILE = 16
 ZERO = 2 * NY * TILE
-SEATS = (1, 5, 2, 6, 7, 3, 0, 4)
+SEATS = (0, 2, 4, 6, 7, 5, 3, 1)
 
 
 def rot(size, shift):
@@ -120,10 +120,10 @@
     )
     half = TILE // 2
     behind, ahead = along_plane(own, 2), along_plane(own, -2)
-    near = jnp.concatenate([behind, own, ahead])
-    pieces = [near, along_plane(near[: 2 * TILE], 1), along_plane(near[TILE:], -1)]
+    near = [own, along_plane(own, 1), along_plane(own, -1)]
     far = [along_plane(behind[:half], 2), along_plane(ahead[half:], -2)]
-    pieces.append(jnp.concatenate(far))
+    pieces = [jnp.concatenate(near), jnp.concatenate([behind, ahead])]
+    pieces += [along_plane(behind, 1), along_plane(ahead, -1), jnp.concatenate(far)]
     pieces += [to_partner(piece) for piece in pieces]
     plan, at = [], 0
     for piece in pieces:

time: 92.4 us -> 99.7 us (1.079)
  starting transfers between devices: 57.2 us -> 65.6 us
  local copies, waits for them, and re-layouts: 6.46 us -> 5.26 us
  waiting for transfers between devices: 19.3 us -> 20.4 us
    ppermute x6 -> x8, starting transfers between devices: 20.1 us -> 26.4 us  [along_plane(): return lax.ppermute(value, ('x', 'y', 'c'), pairs)]
    ppermute x3, waiting for transfers between devices: 5 us -> 7.35 us  [along_z(): return lax.ppermute(value, ('zl', 'zh', 'c'), pairs)]
    unnamed x15 -> x11, local copies, waits for them, and re-layouts: 4.17 us -> 1.93 us
    ppermute x5 -> x6, starting transfers between devices: 27.3 us -> 29.3 us  [to_partner(): return lax.ppermute(value, 'c', rot(NCORE, 1))]
    ppermute x6 -> x8, waiting for transfers between devices: 12.3 us -> 11.3 us  [along_plane(): return lax.ppermute(value, ('x', 'y', 'c'), pairs)]
    ppermute x5 -> x6, waiting for transfers between devices: 2.03 us -> 1.69 us  [to_partner(): return lax.ppermute(value, 'c', rot(NCORE, 1))]
  transfers between devices with their start and end apart: 14 -> 17, of which waited for: 7 -> 5; matrix products, arithmetic and copies ran while one was open for 7% -> 6% of each run, Pallas kernels for 0% -> 0%
where the time goes in v6:
time: 99.7 us; the launch traced here: 98.9 us
  starting transfers between devices  65.6 us (66%)
  waiting for transfers between devices  20.4 us (20%)
  local copies, waits for them, and re-layouts  5.26 us (5%)
  Pallas kernels  3.78 us (4%)
  other arithmetic  3.57 us (4%)
    ppermute x6, starting transfers between devices, to_partner(): return lax.ppermute(value, 'c', rot(NCORE, 1))  29.3 us
    ppermute x8, starting transfers between devices, along_plane(): return lax.ppermute(value, ('x', 'y', 'c'), pairs)  26.4 us
    ppermute x8, waiting for transfers between devices, along_plane(): return lax.ppermute(value, ('x', 'y', 'c'), pairs)  11.3 us
    ppermute x3, starting transfers between devices, along_z(): return lax.ppermute(value, ('zl', 'zh', 'c'), pairs)  9.86 us
    ppermute x3, waiting for transfers between devices, along_z(): return lax.ppermute(value, ('zl', 'zh', 'c'), pairs)  7.35 us
    pallas_call x1, Pallas kernels, per_device(): pl.pallas_call(kernel, out_shape=jax.ShapeDtypeStruct((NC, BS, BS), jnp.b...  3.78 us
  transfers between devices with their start and end apart: 17, of which 5 were waited for; matrix products, arithmetic and copies ran while one was open for 6% of the time, Pallas kernels for 0%

profile of v6, /device:TPU:1, one launch (start us, length us, event | category | flops | bytes accessed | tf_op | source)
XLA Modules:
  0.0 98.9 jit_solution(12079584548360088295)
XLA Ops:
  0.0 0.9 fusion.1
  0.9 16.1 %collective-permute-start = (bf16[4,128,128]{2,1,0:T(8,128)(2,1)S(1)}, bf16[4,128,128]{2,1,0:T(8,128)(2,1)S(1)}, u32[]{:S(2)}, u32[]{:S(2)}) collective-permute-start(bf16[4,128,128]{2,1,0:T(8,128)(2,1)S(1)} %fusion.1), channel_id=1, source_target_pairs={{0,1},{1,0},{2,3},{3,2},{4,5},{5,4},{6,7},{7,6},{8,9},{9,8},{10,11... | collective-permute-start | bytes 393224 | tf_op jit(solution)/shard_map/ppermute | solution.py:109
  17.0 0.7 copy.9
  17.7 0.3 collective-permute-done
  18.0 1.0 %constant_dynamic-update-slice_fusion.5 = (bf16[48,128,128]{2,1,0:T(8,128)(2,1)S(1)}, bf16[4,128,128]{2,1,0:T(8,128)(2,1)S(1)}, bf16[4,128,128]{2,1,0:T(8,128)(2,1)S(1)}) fusion(bf16[4,128,128]{2,1,0:T(8,128)(2,1)S(1)} %collective-permute-done, bf16[2,128,128]{2,1,0:T(8,128)(2,1)S(1)} %slice.27, bf16[2,128,128]{2,1,0:T(8,128)(2,1)} %param.7, pred[]{:T(512)S(6)} %eq.114, ...), kind=kLoop, calls=%fused_computation.16 | loop fusion | flops 393215 | bytes 786433
  19.0 0.7 collective-permute-start.3
  19.7 1.9 %collective-permute-start.2 = (bf16[4,128,128]{2,1,0:T(8,128)(2,1)S(1)}, bf16[4,128,128]{2,1,0:T(8,128)(2,1)S(1)}, u32[]{:S(2)}, u32[]{:S(2)}) collective-permute-start(bf16[4,128,128]{2,1,0:T(8,128)(2,1)S(1)} %get-tuple-element.11), channel_id=1, source_target_pairs={{0,64},{1,17},{16,80},{17,1},{32,96},{33,49},{48,112},{49,33},{64,... | collective-permute-start | bytes 393224 | tf_op jit(solution)/shard_map/ppermute | solution.py:105
  21.6 7.3 %collective-permute-start.1 = (bf16[4,128,128]{2,1,0:T(8,128)(2,1)S(1)}, bf16[4,128,128]{2,1,0:T(8,128)(2,1)S(1)}, u32[]{:S(2)}, u32[]{:S(2)}) collective-permute-start(bf16[4,128,128]{2,1,0:T(8,128)(2,1)S(1)} %get-tuple-element.8), channel_id=1, source_target_pairs={{0,32},{1,17},{16,48},{17,1},{32,64},{33,49},{48,80},{49,33},{64,9... | collective-permute-start | bytes 393224 | tf_op jit(solution)/shard_map/ppermute | solution.py:105
  29.0 7.3 %collective-permute-done.1 = bf16[4,128,128]{2,1,0:T(8,128)(2,1)S(1)} collective-permute-done((bf16[4,128,128]{2,1,0:T(8,128)(2,1)S(1)}, bf16[4,128,128]{2,1,0:T(8,128)(2,1)S(1)}, u32[]{:S(2)}, u32[]{:S(2)}) %collective-permute-start.1) | collective-permute-done | bytes 131104 | tf_op jit(solution)/shard_map/ppermute | solution.py:105
  36.3 0.0 collective-permute-done.3
  36.3 0.0 collective-permute-done.2
  36.3 0.9 pad_maximum_fusion
  37.2 2.1 %collective-permute-start.4 = (bf16[16,128,128]{2,1,0:T(8,128)(2,1)}, bf16[16,128,128]{2,1,0:T(8,128)(2,1)S(1)}, u32[]{:S(2)}, u32[]{:S(2)}) collective-permute-start(bf16[16,128,128]{2,1,0:T(8,128)(2,1)} %pad_maximum_fusion), channel_id=1, source_target_pairs={{0,128},{1,3},{2,130},{3,5},{4,132},{5,7},{6,134},{7,9},{8,136},{9... | collective-permute-start | bytes 1572872 | tf_op jit(solution)/shard_map/ppermute | solution.py:95
  39.4 4.5 %collective-permute-start.5 = (bf16[16,128,128]{2,1,0:T(8,128)(2,1)}, bf16[16,128,128]{2,1,0:T(8,128)(2,1)S(1)}, u32[]{:S(2)}, u32[]{:S(2)}) collective-permute-start(bf16[16,128,128]{2,1,0:T(8,128)(2,1)} %pad_maximum_fusion), channel_id=1, source_target_pairs={{0,896},{1,15},{2,898},{3,1},{4,900},{5,3},{6,902},{7,5},{8,904},{... | collective-permute-start | bytes 1572872 | tf_op jit(solution)/shard_map/ppermute | solution.py:95
  43.9 0.1 select_reduce_fusion.1
  44.0 4.0 %collective-permute-start.7 = (bf16[16,128,128]{2,1,0:T(8,128)(2,1)}, bf16[16,128,128]{2,1,0:T(8,128)(2,1)}, u32[]{:S(2)}, u32[]{:S(2)}) collective-permute-start(bf16[16,128,128]{2,1,0:T(8,128)(2,1)} %pad_maximum_fusion), channel_id=1, source_target_pairs={{0,768},{1,13},{2,770},{3,15},{4,772},{5,1},{6,774},{7,3},{8,776},... | collective-permute-start | bytes 1572872 | tf_op jit(solution)/shard_map/ppermute | solution.py:95
  48.0 2.1 %collective-permute-start.6 = (bf16[16,128,128]{2,1,0:T(8,128)(2,1)}, bf16[16,128,128]{2,1,0:T(8,128)(2,1)}, u32[]{:S(2)}, u32[]{:S(2)}) collective-permute-start(bf16[16,128,128]{2,1,0:T(8,128)(2,1)} %pad_maximum_fusion), channel_id=1, source_target_pairs={{0,256},{1,5},{2,258},{3,7},{4,260},{5,9},{6,262},{7,11},{8,264},{... | collective-permute-start | bytes 1572872 | tf_op jit(solution)/shard_map/ppermute | solution.py:95
  50.3 0.1 constant_dynamic-update-slice_fusion.1
  50.3 1.1 %collective-permute-done.5 = bf16[16,128,128]{2,1,0:T(8,128)(2,1)S(1)} collective-permute-done((bf16[16,128,128]{2,1,0:T(8,128)(2,1)}, bf16[16,128,128]{2,1,0:T(8,128)(2,1)S(1)}, u32[]{:S(2)}, u32[]{:S(2)}) %collective-permute-start.5) | collective-permute-done | bytes 524320 | tf_op jit(solution)/shard_map/ppermute | solution.py:95
  51.4 0.1 constant_dynamic-update-slice_fusion.refs_2_
  51.5 2.3 %collective-permute-start.12 = (bf16[48,128,128]{2,1,0:T(8,128)(2,1)S(1)}, bf16[48,128,128]{2,1,0:T(8,128)(2,1)S(1)}, u32[]{:S(2)}, u32[]{:S(2)}) collective-permute-start(bf16[48,128,128]{2,1,0:T(8,128)(2,1)S(1)} %constant_dynamic-update-slice_fusion.refs_2_), channel_id=1, source_target_pairs={{0,1},{1,0},{2,3},{3,2},{4,5},{5,4},{6,7},{7,6},{8,9},{9,8},{10,11... | collective-permute-start | bytes 4718600 | tf_op jit(solution)/shard_map/ppermute | solution.py:109
  53.8 0.1 broadcast_in_dim.46
  53.9 0.1 reshape.339
  54.0 10.2 %collective-permute-done.6 = bf16[16,128,128]{2,1,0:T(8,128)(2,1)} collective-permute-done((bf16[16,128,128]{2,1,0:T(8,128)(2,1)}, bf16[16,128,128]{2,1,0:T(8,128)(2,1)}, u32[]{:S(2)}, u32[]{:S(2)}) %collective-permute-start.6) | collective-permute-done | bytes 524320 | tf_op jit(solution)/shard_map/ppermute | solution.py:95
  64.2 1.0 slice.28
  65.2 1.9 %collective-permute-start.10 = (bf16[8,128,128]{2,1,0:T(8,128)(2,1)S(1)}, bf16[8,128,128]{2,1,0:T(8,128)(2,1)S(1)}, u32[]{:S(2)}, u32[]{:S(2)}) collective-permute-start(bf16[8,128,128]{2,1,0:T(8,128)(2,1)S(1)} %slice.28), channel_id=1, source_target_pairs={{0,256},{1,5},{2,258},{3,7},{4,260},{5,9},{6,262},{7,11},{8,264},{... | collective-permute-start | bytes 786440 | tf_op jit(solution)/shard_map/ppermute | solution.py:95
  67.1 0.0 collective-permute-done.7
  67.1 1.0 slice.29
  68.1 5.5 %collective-permute-start.11 = (bf16[8,128,128]{2,1,0:T(8,128)(2,1)S(1)}, bf16[8,128,128]{2,1,0:T(8,128)(2,1)S(1)}, u32[]{:S(2)}, u32[]{:S(2)}) collective-permute-start(bf16[8,128,128]{2,1,0:T(8,128)(2,1)S(1)} %slice.29), channel_id=1, source_target_pairs={{0,768},{1,13},{2,770},{3,15},{4,772},{5,1},{6,774},{7,3},{8,776},... | collective-permute-start | bytes 786440 | tf_op jit(solution)/shard_map/ppermute | solution.py:95
  73.6 3.1 %collective-permute-start.9 = (bf16[16,128,128]{2,1,0:T(8,128)(2,1)}, bf16[16,128,128]{2,1,0:T(8,128)(2,1)S(1)}, u32[]{:S(2)}, u32[]{:S(2)}) collective-permute-start(bf16[16,128,128]{2,1,0:T(8,128)(2,1)} %collective-permute-done.7), channel_id=1, source_target_pairs={{0,896},{1,15},{2,898},{3,1},{4,900},{5,3},{6,902},{7,5},{8,904},{... | collective-permute-start | bytes 1572872 | tf_op jit(solution)/shard_map/ppermute | solution.py:95
  76.6 3.1 %collective-permute-start.8 = (bf16[16,128,128]{2,1,0:T(8,128)(2,1)}, bf16[16,128,128]{2,1,0:T(8,128)(2,1)S(1)}, u32[]{:S(2)}, u32[]{:S(2)}) collective-permute-start(bf16[16,128,128]{2,1,0:T(8,128)(2,1)} %collective-permute-done.6), channel_id=1, source_target_pairs={{0,128},{1,3},{2,130},{3,5},{4,132},{5,7},{6,134},{7,9},{8,136},{9... | collective-permute-start | bytes 1572872 | tf_op jit(solution)/shard_map/ppermute | solution.py:95
  79.7 1.1 %constant_dynamic-update-slice_fusion.7 = bf16[32,128,128]{2,1,0:T(8,128)(2,1)S(1)} fusion(bf16[16,128,128]{2,1,0:T(8,128)(2,1)} %collective-permute-done.6), kind=kLoop, calls=%fused_computation.18 | loop fusion | bytes 1048576
  80.8 1.1 %constant_dynamic-update-slice_fusion.6.refs_3_ = bf16[32,128,128]{2,1,0:T(8,128)(2,1)S(1)} fusion(bf16[32,128,128]{2,1,0:T(8,128)(2,1)S(1)} %constant_dynamic-update-slice_fusion.7, bf16[16,128,128]{2,1,0:T(8,128)(2,1)} %collective-permute-done.7), kind=kLoop, calls=%fused_computation.17 | loop fusion | bytes 1048576 | tf_op jit(solution)/shard_map/concatenate | solution.py:125
  82.0 0.0 collective-permute-done.10
  82.0 2.7 %collective-permute-start.13 = (bf16[32,128,128]{2,1,0:T(8,128)(2,1)S(1)}, bf16[32,128,128]{2,1,0:T(8,128)(2,1)S(1)}, u32[]{:S(2)}, u32[]{:S(2)}) collective-permute-start(bf16[32,128,128]{2,1,0:T(8,128)(2,1)S(1)} %constant_dynamic-update-slice_fusion.6.refs_3_), channel_id=1, source_target_pairs={{0,1},{1,0},{2,3},{3,2},{4,5},{5,4},{6,7},{7,6},{8,9},{9,8},{10,11... | collective-permute-start | bytes 3145736 | tf_op jit(solution)/shard_map/ppermute | solution.py:109
  84.7 0.1 convert_reduce_fusion.1
  84.8 0.0 collective-permute-done.11
  84.9 1.9 %collective-permute-start.16 = (bf16[16,128,128]{2,1,0:T(8,128)(2,1)S(1)}, bf16[16,128,128]{2,1,0:T(8,128)(2,1)S(1)}, u32[]{:S(2)}, u32[]{:S(2)}) collective-permute-start(bf16[16,128,128]{2,1,0:T(8,128)(2,1)S(1)} %constant_dynamic-update-slice_fusion.8.refs_6_), channel_id=1, source_target_pairs={{0,1},{1,0},{2,3},{3,2},{4,5},{5,4},{6,7},{7,6},{8,9},{9,8},{10,11... | collective-permute-start | bytes 1572872 | tf_op jit(solution)/shard_map/ppermute | solution.py:109
  86.8 4.5 %collective-permute-start.15 = (bf16[16,128,128]{2,1,0:T(8,128)(2,1)S(1)}, bf16[16,128,128]{2,1,0:T(8,128)(2,1)S(1)}, u32[]{:S(2)}, u32[]{:S(2)}) collective-permute-start(bf16[16,128,128]{2,1,0:T(8,128)(2,1)S(1)} %collective-permute-done.9.refs_5_), channel_id=1, source_target_pairs={{0,1},{1,0},{2,3},{3,2},{4,5},{5,4},{6,7},{7,6},{8,9},{9,8},{10,11... | collective-permute-start | bytes 1572872 | tf_op jit(solution)/shard_map/ppermute | solution.py:109
  91.3 0.0 collective-permute-done.8.refs_4_
  91.3 1.9 %collective-permute-start.14 = (bf16[16,128,128]{2,1,0:T(8,128)(2,1)S(1)}, bf16[16,128,128]{2,1,0:T(8,128)(2,1)S(1)}, u32[]{:S(2)}, u32[]{:S(2)}) collective-permute-start(bf16[16,128,128]{2,1,0:T(8,128)(2,1)S(1)} %collective-permute-done.8.refs_4_), channel_id=1, source_target_pairs={{0,1},{1,0},{2,3},{3,2},{4,5},{5,4},{6,7},{7,6},{8,9},{9,8},{10,11... | collective-permute-start | bytes 1572872 | tf_op jit(solution)/shard_map/ppermute | solution.py:109
  93.3 0.1 convert_reduce_fusion
  93.4 0.3 select_reduce_fusion
  93.7 0.0 collective-permute-done.16.refs_11_
  93.7 0.0 collective-permute-done.15.refs_10_
  93.7 1.4 %collective-permute-done.14.refs_9_ = bf16[16,128,128]{2,1,0:T(8,128)(2,1)S(1)} collective-permute-done((bf16[16,128,128]{2,1,0:T(8,128)(2,1)S(1)}, bf16[16,128,128]{2,1,0:T(8,128)(2,1)S(1)}, u32[]{:S(2)}, u32[]{:S(2)}) %collective-permute-start.14) | collective-permute-done | bytes 524320 | tf_op jit(solution)/shard_map/ppermute | solution.py:109
  95.1 0.0 collective-permute-done.13.refs_8_
  95.1 3.8 %block_products.1 = bf16[2,128,128]{2,1,0:T(8,128)(2,1)} custom-call(s32[2,256]{1,0:T(2,128)S(1)} %broadcast_add_fusion.refs_0_, s32[2]{0:T(128)S(1)} %get-tuple-element.9.refs_1_, bf16[48,128,128]{2,1,0:T(8,128)(2,1)S(1)} %constant_dynamic-update-slice_fusion.refs_2_, bf16[32,128,128]{2,1,0:T(8,128)(2,1)S(1)} %constant_dynamic-update-slice_fusion.6.refs_3_, ...), custom_call_target="tpu_custom_call" | custom-call | flops 536870912 | bytes 6291456 | tf_op jit(solution)/shard_map/block_products/pallas_call | solution.py:138
  (20 shorter events, 0.3 us)
Async XLA Ops:
  0.0 43.9 %copy-start.1 = (s32[8]{0:T(128)S(1)}, s32[8]{0:T(128)}, u32[]{:S(2)}) copy-start(s32[8]{0:T(128)} %constant.162.clone) | copy-start | bytes 100
  0.9 17.1 %collective-permute-start = (bf16[4,128,128]{2,1,0:T(8,128)(2,1)S(1)}, bf16[4,128,128]{2,1,0:T(8,128)(2,1)S(1)}, u32[]{:S(2)}, u32[]{:S(2)}) collective-permute-start(bf16[4,128,128]{2,1,0:T(8,128)(2,1)S(1)} %fusion.1), channel_id=1, source_target_pairs={{0,1},{1,0},{2,3},{3,2},{4,5},{5,4},{6,7},{7,6},{8,9},{9,8},{10,11... | collective-permute-start | bytes 393224 | tf_op jit(solution)/shard_map/ppermute | solution.py:109
  19.0 17.3 %collective-permute-start.3 = (bf16[4,128,128]{2,1,0:T(8,128)(2,1)S(1)}, bf16[4,128,128]{2,1,0:T(8,128)(2,1)S(1)}, u32[]{:S(2)}, u32[]{:S(2)}) collective-permute-start(bf16[4,128,128]{2,1,0:T(8,128)(2,1)S(1)} %get-tuple-element.11), channel_id=1, source_target_pairs={{0,96},{1,1},{16,112},{17,17},{32,0},{33,33},{48,16},{49,49},{64,3... | collective-permute-start | bytes 393224 | tf_op jit(solution)/shard_map/ppermute | solution.py:105
  19.7 16.6 %collective-permute-start.2 = (bf16[4,128,128]{2,1,0:T(8,128)(2,1)S(1)}, bf16[4,128,128]{2,1,0:T(8,128)(2,1)S(1)}, u32[]{:S(2)}, u32[]{:S(2)}) collective-permute-start(bf16[4,128,128]{2,1,0:T(8,128)(2,1)S(1)} %get-tuple-element.11), channel_id=1, source_target_pairs={{0,64},{1,17},{16,80},{17,1},{32,96},{33,49},{48,112},{49,33},{64,... | collective-permute-start | bytes 393224 | tf_op jit(solution)/shard_map/ppermute | solution.py:105
  21.6 14.7 %collective-permute-start.1 = (bf16[4,128,128]{2,1,0:T(8,128)(2,1)S(1)}, bf16[4,128,128]{2,1,0:T(8,128)(2,1)S(1)}, u32[]{:S(2)}, u32[]{:S(2)}) collective-permute-start(bf16[4,128,128]{2,1,0:T(8,128)(2,1)S(1)} %get-tuple-element.8), channel_id=1, source_target_pairs={{0,32},{1,17},{16,48},{17,1},{32,64},{33,49},{48,80},{49,33},{64,9... | collective-permute-start | bytes 393224 | tf_op jit(solution)/shard_map/ppermute | solution.py:105
  37.2 16.6 %copy-start = (s32[1,32]{1,0:T(1,128)S(1)}, s32[1,32]{1,0:T(1,128)}, u32[]{:S(2)}) copy-start(s32[1,32]{1,0:T(1,128)} %param.9) | copy-start | bytes 388
  37.2 13.0 %collective-permute-start.4 = (bf16[16,128,128]{2,1,0:T(8,128)(2,1)}, bf16[16,128,128]{2,1,0:T(8,128)(2,1)S(1)}, u32[]{:S(2)}, u32[]{:S(2)}) collective-permute-start(bf16[16,128,128]{2,1,0:T(8,128)(2,1)} %pad_maximum_fusion), channel_id=1, source_target_pairs={{0,128},{1,3},{2,130},{3,5},{4,132},{5,7},{6,134},{7,9},{8,136},{9... | collective-permute-start | bytes 1572872 | tf_op jit(solution)/shard_map/ppermute | solution.py:95
  39.4 12.0 %collective-permute-start.5 = (bf16[16,128,128]{2,1,0:T(8,128)(2,1)}, bf16[16,128,128]{2,1,0:T(8,128)(2,1)S(1)}, u32[]{:S(2)}, u32[]{:S(2)}) collective-permute-start(bf16[16,128,128]{2,1,0:T(8,128)(2,1)} %pad_maximum_fusion), channel_id=1, source_target_pairs={{0,896},{1,15},{2,898},{3,1},{4,900},{5,3},{6,902},{7,5},{8,904},{... | collective-permute-start | bytes 1572872 | tf_op jit(solution)/shard_map/ppermute | solution.py:95
  44.0 23.1 %collective-permute-start.7 = (bf16[16,128,128]{2,1,0:T(8,128)(2,1)}, bf16[16,128,128]{2,1,0:T(8,128)(2,1)}, u32[]{:S(2)}, u32[]{:S(2)}) collective-permute-start(bf16[16,128,128]{2,1,0:T(8,128)(2,1)} %pad_maximum_fusion), channel_id=1, source_target_pairs={{0,768},{1,13},{2,770},{3,15},{4,772},{5,1},{6,774},{7,3},{8,776},... | collective-permute-start | bytes 1572872 | tf_op jit(solution)/shard_map/ppermute | solution.py:95
  48.0 16.2 %collective-permute-start.6 = (bf16[16,128,128]{2,1,0:T(8,128)(2,1)}, bf16[16,128,128]{2,1,0:T(8,128)(2,1)}, u32[]{:S(2)}, u32[]{:S(2)}) collective-permute-start(bf16[16,128,128]{2,1,0:T(8,128)(2,1)} %pad_maximum_fusion), channel_id=1, source_target_pairs={{0,256},{1,5},{2,258},{3,7},{4,260},{5,9},{6,262},{7,11},{8,264},{... | collective-permute-start | bytes 1572872 | tf_op jit(solution)/shard_map/ppermute | solution.py:95
  51.5 43.6 %collective-permute-start.12 = (bf16[48,128,128]{2,1,0:T(8,128)(2,1)S(1)}, bf16[48,128,128]{2,1,0:T(8,128)(2,1)S(1)}, u32[]{:S(2)}, u32[]{:S(2)}) collective-permute-start(bf16[48,128,128]{2,1,0:T(8,128)(2,1)S(1)} %constant_dynamic-update-slice_fusion.refs_2_), channel_id=1, source_target_pairs={{0,1},{1,0},{2,3},{3,2},{4,5},{5,4},{6,7},{7,6},{8,9},{9,8},{10,11... | collective-permute-start | bytes 4718600 | tf_op jit(solution)/shard_map/ppermute | solution.py:109
  65.2 16.8 %collective-permute-start.10 = (bf16[8,128,128]{2,1,0:T(8,128)(2,1)S(1)}, bf16[8,128,128]{2,1,0:T(8,128)(2,1)S(1)}, u32[]{:S(2)}, u32[]{:S(2)}) collective-permute-start(bf16[8,128,128]{2,1,0:T(8,128)(2,1)S(1)} %slice.28), channel_id=1, source_target_pairs={{0,256},{1,5},{2,258},{3,7},{4,260},{5,9},{6,262},{7,11},{8,264},{... | collective-permute-start | bytes 786440 | tf_op jit(solution)/shard_map/ppermute | solution.py:95
  68.1 16.7 %collective-permute-start.11 = (bf16[8,128,128]{2,1,0:T(8,128)(2,1)S(1)}, bf16[8,128,128]{2,1,0:T(8,128)(2,1)S(1)}, u32[]{:S(2)}, u32[]{:S(2)}) collective-permute-start(bf16[8,128,128]{2,1,0:T(8,128)(2,1)S(1)} %slice.29), channel_id=1, source_target_pairs={{0,768},{1,13},{2,770},{3,15},{4,772},{5,1},{6,774},{7,3},{8,776},... | collective-permute-start | bytes 786440 | tf_op jit(solution)/shard_map/ppermute | solution.py:95
  73.6 13.2 %collective-permute-start.9 = (bf16[16,128,128]{2,1,0:T(8,128)(2,1)}, bf16[16,128,128]{2,1,0:T(8,128)(2,1)S(1)}, u32[]{:S(2)}, u32[]{:S(2)}) collective-permute-start(bf16[16,128,128]{2,1,0:T(8,128)(2,1)} %collective-permute-done.7), channel_id=1, source_target_pairs={{0,896},{1,15},{2,898},{3,1},{4,900},{5,3},{6,902},{7,5},{8,904},{... | collective-permute-start | bytes 1572872 | tf_op jit(solution)/shard_map/ppermute | solution.py:95
  76.6 14.6 %collective-permute-start.8 = (bf16[16,128,128]{2,1,0:T(8,128)(2,1)}, bf16[16,128,128]{2,1,0:T(8,128)(2,1)S(1)}, u32[]{:S(2)}, u32[]{:S(2)}) collective-permute-start(bf16[16,128,128]{2,1,0:T(8,128)(2,1)} %collective-permute-done.6), channel_id=1, source_target_pairs={{0,128},{1,3},{2,130},{3,5},{4,132},{5,7},{6,134},{7,9},{8,136},{9... | collective-permute-start | bytes 1572872 | tf_op jit(solution)/shard_map/ppermute | solution.py:95
  82.0 13.1 %collective-permute-start.13 = (bf16[32,128,128]{2,1,0:T(8,128)(2,1)S(1)}, bf16[32,128,128]{2,1,0:T(8,128)(2,1)S(1)}, u32[]{:S(2)}, u32[]{:S(2)}) collective-permute-start(bf16[32,128,128]{2,1,0:T(8,128)(2,1)S(1)} %constant_dynamic-update-slice_fusion.6.refs_3_), channel_id=1, source_target_pairs={{0,1},{1,0},{2,3},{3,2},{4,5},{5,4},{6,7},{7,6},{8,9},{9,8},{10,11... | collective-permute-start | bytes 3145736 | tf_op jit(solution)/shard_map/ppermute | solution.py:109
  84.9 8.8 %collective-permute-start.16 = (bf16[16,128,128]{2,1,0:T(8,128)(2,1)S(1)}, bf16[16,128,128]{2,1,0:T(8,128)(2,1)S(1)}, u32[]{:S(2)}, u32[]{:S(2)}) collective-permute-start(bf16[16,128,128]{2,1,0:T(8,128)(2,1)S(1)} %constant_dynamic-update-slice_fusion.8.refs_6_), channel_id=1, source_target_pairs={{0,1},{1,0},{2,3},{3,2},{4,5},{5,4},{6,7},{7,6},{8,9},{9,8},{10,11... | collective-permute-start | bytes 1572872 | tf_op jit(solution)/shard_map/ppermute | solution.py:109
  86.8 6.9 %collective-permute-start.15 = (bf16[16,128,128]{2,1,0:T(8,128)(2,1)S(1)}, bf16[16,128,128]{2,1,0:T(8,128)(2,1)S(1)}, u32[]{:S(2)}, u32[]{:S(2)}) collective-permute-start(bf16[16,128,128]{2,1,0:T(8,128)(2,1)S(1)} %collective-permute-done.9.refs_5_), channel_id=1, source_target_pairs={{0,1},{1,0},{2,3},{3,2},{4,5},{5,4},{6,7},{7,6},{8,9},{9,8},{10,11... | collective-permute-start | bytes 1572872 | tf_op jit(solution)/shard_map/ppermute | solution.py:109
  91.3 3.8 %collective-permute-start.14 = (bf16[16,128,128]{2,1,0:T(8,128)(2,1)S(1)}, bf16[16,128,128]{2,1,0:T(8,128)(2,1)S(1)}, u32[]{:S(2)}, u32[]{:S(2)}) collective-permute-start(bf16[16,128,128]{2,1,0:T(8,128)(2,1)S(1)} %collective-permute-done.8.refs_4_), channel_id=1, source_target_pairs={{0,1},{1,0},{2,3},{3,2},{4,5},{5,4},{6,7},{7,6},{8,9},{9,8},{10,11... | collective-permute-start | bytes 1572872 | tf_op jit(solution)/shard_map/ppermute | solution.py:109

commit v7 on v6

--- a/solution.py
+++ b/solution.py
@@ -13,7 +13,7 @@
 GROUP = 16
 TILE = 16
 ZERO = 2 * NY * TILE
-SEATS = (0, 2, 4, 6, 7, 5, 3, 1)
+SEATS = (1, 4, 7, 2, 5, 0, 3, 6)
 
 
 def rot(size, shift):
@@ -119,11 +119,8 @@
         [first, along_z(first, 1, 1), along_z(second, 2, 1), along_z(second, 3, 0)]
     )
     half = TILE // 2
-    behind, ahead = along_plane(own, 2), along_plane(own, -2)
-    near = [own, along_plane(own, 1), along_plane(own, -1)]
-    far = [along_plane(behind[:half], 2), along_plane(ahead[half:], -2)]
-    pieces = [jnp.concatenate(near), jnp.concatenate([behind, ahead])]
-    pieces += [along_plane(behind, 1), along_plane(ahead, -1), jnp.concatenate(far)]
+    near = jnp.concatenate([along_plane(own, 3), own, along_plane(own, -3)])
+    pieces = [near, along_plane(near[: 2 * TILE + half], -1), along_plane(near[half:], 1)]
     pieces += [to_partner(piece) for piece in pieces]
     plan, at = [], 0
     for piece in pieces:

time: 99.7 us -> 102 us (1.023)
  waiting for transfers between devices: 20.4 us -> 41.5 us
  starting transfers between devices: 65.6 us -> 48.5 us
  local copies, waits for them, and re-layouts: 5.26 us -> 2.43 us
  Pallas kernels: 3.78 us -> 5.78 us
    ppermute x8 -> x4, waiting for transfers between devices: 11.3 us -> 30.5 us  [along_plane(): return lax.ppermute(value, ('x', 'y', 'c'), pairs)]
    ppermute x8 -> x4, starting transfers between devices: 26.4 us -> 16.9 us  [along_plane(): return lax.ppermute(value, ('x', 'y', 'c'), pairs)]
    ppermute x6 -> x4, starting transfers between devices: 29.3 us -> 21.8 us  [to_partner(): return lax.ppermute(value, 'c', rot(NCORE, 1))]
    pallas_call x1, Pallas kernels: 3.78 us -> 5.78 us  [per_device(): pl.pallas_call(kernel, out_shape=jax.ShapeDtypeStruct((NC, BS, BS), jnp.b...]
    ppermute x6 -> x4, waiting for transfers between devices: 1.69 us -> 3.56 us  [to_partner(): return lax.ppermute(value, 'c', rot(NCORE, 1))]
    unnamed x11 -> x12, local copies, waits for them, and re-layouts: 1.93 us -> 0.14 us
    concatenate x3 -> x1, local copies, waits for them, and re-layouts: 1.23 us -> 0.07 us  [per_device(): near = jnp.concatenate([along_plane(own, 3), own, along_plane(own, -3)])]
    unnamed x1 -> x0, other arithmetic: 1.02 us -> none
  transfers between devices with their start and end apart: 17 -> 11, of which waited for: 5 -> 8; matrix products, arithmetic and copies ran while one was open for 6% -> 1% of each run, Pallas kernels for 0% -> 0%
where the time goes in v7:
time: 102 us; the launch traced here: 101 us
  starting transfers between devices  48.5 us (48%)
  waiting for transfers between devices  41.5 us (41%)
  Pallas kernels  5.78 us (6%)
  other arithmetic  2.71 us (3%)
  local copies, waits for them, and re-layouts  2.43 us (2%)
    ppermute x4, waiting for transfers between devices, along_plane(): return lax.ppermute(value, ('x', 'y', 'c'), pairs)  30.5 us
    ppermute x4, starting transfers between devices, to_partner(): return lax.ppermute(value, 'c', rot(NCORE, 1))  21.8 us
    ppermute x4, starting transfers between devices, along_plane(): return lax.ppermute(value, ('x', 'y', 'c'), pairs)  16.9 us
    ppermute x3, starting transfers between devices, along_z(): return lax.ppermute(value, ('zl', 'zh', 'c'), pairs)  9.86 us
    ppermute x3, waiting for transfers between devices, along_z(): return lax.ppermute(value, ('zl', 'zh', 'c'), pairs)  7.39 us
    pallas_call x1, Pallas kernels, per_device(): pl.pallas_call(kernel, out_shape=jax.ShapeDtypeStruct((NC, BS, BS), jnp.b...  5.78 us
    ppermute x4, waiting for transfers between devices, to_partner(): return lax.ppermute(value, 'c', rot(NCORE, 1))  3.56 us
    slice x1, local copies, waits for them, and re-layouts, per_device(): near[half:]  2.05 us
  transfers between devices with their start and end apart: 11, of which 8 were waited for; matrix products, arithmetic and copies ran while one was open for 1% of the time, Pallas kernels for 0%

profile of v7, /device:TPU:1, one launch (start us, length us, event | category | flops | bytes accessed | tf_op | source)
XLA Modules:
  0.0 101.2 jit_solution(15281045947967134029)
XLA Ops:
  0.0 0.9 fusion.1
  0.9 16.1 %collective-permute-start = (bf16[4,128,128]{2,1,0:T(8,128)(2,1)S(1)}, bf16[4,128,128]{2,1,0:T(8,128)(2,1)S(1)}, u32[]{:S(2)}, u32[]{:S(2)}) collective-permute-start(bf16[4,128,128]{2,1,0:T(8,128)(2,1)S(1)} %fusion.1), channel_id=1, source_target_pairs={{0,1},{1,0},{2,3},{3,2},{4,5},{5,4},{6,7},{7,6},{8,9},{9,8},{10,11... | collective-permute-start | bytes 393224 | tf_op jit(solution)/shard_map/ppermute | solution.py:109
  17.0 1.0 collective-permute-done
  18.0 1.0 broadcast_select_fusion.1
  19.0 0.7 collective-permute-start.3
  19.6 1.9 %collective-permute-start.2 = (bf16[4,128,128]{2,1,0:T(8,128)(2,1)S(1)}, bf16[4,128,128]{2,1,0:T(8,128)(2,1)S(1)}, u32[]{:S(2)}, u32[]{:S(2)}) collective-permute-start(bf16[4,128,128]{2,1,0:T(8,128)(2,1)S(1)} %get-tuple-element.12), channel_id=1, source_target_pairs={{0,64},{1,17},{16,80},{17,1},{32,96},{33,49},{48,112},{49,33},{64,... | collective-permute-start | bytes 393224 | tf_op jit(solution)/shard_map/ppermute | solution.py:105
  21.6 7.3 %collective-permute-start.1 = (bf16[4,128,128]{2,1,0:T(8,128)(2,1)S(1)}, bf16[4,128,128]{2,1,0:T(8,128)(2,1)S(1)}, u32[]{:S(2)}, u32[]{:S(2)}) collective-permute-start(bf16[4,128,128]{2,1,0:T(8,128)(2,1)S(1)} %get-tuple-element.11), channel_id=1, source_target_pairs={{0,32},{1,17},{16,48},{17,1},{32,64},{33,49},{48,80},{49,33},{64,9... | collective-permute-start | bytes 393224 | tf_op jit(solution)/shard_map/ppermute | solution.py:105
  28.9 0.0 collective-permute-done.3
  28.9 4.7 %collective-permute-done.2 = bf16[4,128,128]{2,1,0:T(8,128)(2,1)S(1)} collective-permute-done((bf16[4,128,128]{2,1,0:T(8,128)(2,1)S(1)}, bf16[4,128,128]{2,1,0:T(8,128)(2,1)S(1)}, u32[]{:S(2)}, u32[]{:S(2)}) %collective-permute-start.2) | collective-permute-done | bytes 131104 | tf_op jit(solution)/shard_map/ppermute | solution.py:105
  33.5 2.7 %collective-permute-done.1 = bf16[4,128,128]{2,1,0:T(8,128)(2,1)S(1)} collective-permute-done((bf16[4,128,128]{2,1,0:T(8,128)(2,1)S(1)}, bf16[4,128,128]{2,1,0:T(8,128)(2,1)S(1)}, u32[]{:S(2)}, u32[]{:S(2)}) %collective-permute-start.1) | collective-permute-done | bytes 131104 | tf_op jit(solution)/shard_map/ppermute | solution.py:105
  36.3 0.1 pad_maximum_fusion
  36.3 4.3 %collective-permute-start.4 = (bf16[16,128,128]{2,1,0:T(8,128)(2,1)S(1)}, bf16[16,128,128]{2,1,0:T(8,128)(2,1)S(1)}, u32[]{:S(2)}, u32[]{:S(2)}) collective-permute-start(bf16[16,128,128]{2,1,0:T(8,128)(2,1)S(1)} %pad_maximum_fusion), channel_id=1, source_target_pairs={{0,384},{1,7},{2,386},{3,9},{4,388},{5,11},{6,390},{7,13},{8,392},... | collective-permute-start | bytes 1572872 | tf_op jit(solution)/shard_map/ppermute | solution.py:95
  40.6 4.0 %collective-permute-start.5 = (bf16[16,128,128]{2,1,0:T(8,128)(2,1)S(1)}, bf16[16,128,128]{2,1,0:T(8,128)(2,1)S(1)}, u32[]{:S(2)}, u32[]{:S(2)}) collective-permute-start(bf16[16,128,128]{2,1,0:T(8,128)(2,1)S(1)} %pad_maximum_fusion), channel_id=1, source_target_pairs={{0,640},{1,11},{2,642},{3,13},{4,644},{5,15},{6,646},{7,1},{8,648}... | collective-permute-start | bytes 1572872 | tf_op jit(solution)/shard_map/ppermute | solution.py:95
  44.6 15.4 %collective-permute-done.4 = bf16[16,128,128]{2,1,0:T(8,128)(2,1)S(1)} collective-permute-done((bf16[16,128,128]{2,1,0:T(8,128)(2,1)S(1)}, bf16[16,128,128]{2,1,0:T(8,128)(2,1)S(1)}, u32[]{:S(2)}, u32[]{:S(2)}) %collective-permute-start.4) | collective-permute-done | bytes 524320 | tf_op jit(solution)/shard_map/ppermute | solution.py:95
  60.1 2.5 %collective-permute-done.5 = bf16[16,128,128]{2,1,0:T(8,128)(2,1)S(1)} collective-permute-done((bf16[16,128,128]{2,1,0:T(8,128)(2,1)S(1)}, bf16[16,128,128]{2,1,0:T(8,128)(2,1)S(1)}, u32[]{:S(2)}, u32[]{:S(2)}) %collective-permute-start.5) | collective-permute-done | bytes 524320 | tf_op jit(solution)/shard_map/ppermute | solution.py:95
  62.7 0.1 constant_dynamic-update-slice_fusion.refs_2_
  62.8 0.0 copy-start.1
  62.8 0.0 copy-start.2
  62.8 0.0 copy-start
  62.8 2.1 %fusion.18 = (bf16[40,128,128]{2,1,0:T(8,128)(2,1)}, bf16[40,128,128]{2,1,0:T(8,128)(2,1)}) fusion(bf16[48,128,128]{2,1,0:T(8,128)(2,1)S(1)} %constant_dynamic-update-slice_fusion.refs_2_), kind=kLoop, calls=%fused_computation.82 | loop fusion | bytes 5242880 | tf_op jit(solution)/shard_map/slice | solution.py:123
  64.9 6.6 %collective-permute-start.7 = (bf16[40,128,128]{2,1,0:T(8,128)(2,1)}, bf16[40,128,128]{2,1,0:T(8,128)(2,1)}, u32[]{:S(2)}, u32[]{:S(2)}) collective-permute-start(bf16[40,128,128]{2,1,0:T(8,128)(2,1)} %get-tuple-element.9), channel_id=1, source_target_pairs={{0,128},{1,3},{2,130},{3,5},{4,132},{5,7},{6,134},{7,9},{8,136},{9... | collective-permute-start | bytes 3932168 | tf_op jit(solution)/shard_map/ppermute | solution.py:95
  71.5 1.9 %collective-permute-start.6 = (bf16[40,128,128]{2,1,0:T(8,128)(2,1)}, bf16[40,128,128]{2,1,0:T(8,128)(2,1)}, u32[]{:S(2)}, u32[]{:S(2)}) collective-permute-start(bf16[40,128,128]{2,1,0:T(8,128)(2,1)} %get-tuple-element.10), channel_id=1, source_target_pairs={{0,896},{1,15},{2,898},{3,1},{4,900},{5,3},{6,902},{7,5},{8,904},{... | collective-permute-start | bytes 3932168 | tf_op jit(solution)/shard_map/ppermute | solution.py:95
  73.5 0.0 copy-done.1
  73.5 0.1 broadcast_in_dim.46
  73.5 0.1 reshape.339
  73.7 1.9 %collective-permute-start.8 = (bf16[48,128,128]{2,1,0:T(8,128)(2,1)S(1)}, bf16[48,128,128]{2,1,0:T(8,128)(2,1)S(1)}, u32[]{:S(2)}, u32[]{:S(2)}) collective-permute-start(bf16[48,128,128]{2,1,0:T(8,128)(2,1)S(1)} %constant_dynamic-update-slice_fusion.refs_2_), channel_id=1, source_target_pairs={{0,1},{1,0},{2,3},{3,2},{4,5},{5,4},{6,7},{7,6},{8,9},{9,8},{10,11... | collective-permute-start | bytes 4718600 | tf_op jit(solution)/shard_map/ppermute | solution.py:109
  75.6 10.7 %collective-permute-done.7.refs_4_ = bf16[40,128,128]{2,1,0:T(8,128)(2,1)} collective-permute-done((bf16[40,128,128]{2,1,0:T(8,128)(2,1)}, bf16[40,128,128]{2,1,0:T(8,128)(2,1)}, u32[]{:S(2)}, u32[]{:S(2)}) %collective-permute-start.7) | collective-permute-done | bytes 1310752 | tf_op jit(solution)/shard_map/ppermute | solution.py:95
  86.4 1.9 %collective-permute-start.10 = (bf16[40,128,128]{2,1,0:T(8,128)(2,1)}, bf16[40,128,128]{2,1,0:T(8,128)(2,1)}, u32[]{:S(2)}, u32[]{:S(2)}) collective-permute-start(bf16[40,128,128]{2,1,0:T(8,128)(2,1)} %collective-permute-done.7.refs_4_), channel_id=1, source_target_pairs={{0,1},{1,0},{2,3},{3,2},{4,5},{5,4},{6,7},{7,6},{8,9},{9,8},{10,11... | collective-permute-start | bytes 3932168 | tf_op jit(solution)/shard_map/ppermute | solution.py:109
  88.3 1.9 %collective-permute-done.6.refs_3_ = bf16[40,128,128]{2,1,0:T(8,128)(2,1)} collective-permute-done((bf16[40,128,128]{2,1,0:T(8,128)(2,1)}, bf16[40,128,128]{2,1,0:T(8,128)(2,1)}, u32[]{:S(2)}, u32[]{:S(2)}) %collective-permute-start.6) | collective-permute-done | bytes 1310752 | tf_op jit(solution)/shard_map/ppermute | solution.py:95
  90.2 1.9 %collective-permute-start.9 = (bf16[40,128,128]{2,1,0:T(8,128)(2,1)}, bf16[40,128,128]{2,1,0:T(8,128)(2,1)}, u32[]{:S(2)}, u32[]{:S(2)}) collective-permute-start(bf16[40,128,128]{2,1,0:T(8,128)(2,1)} %collective-permute-done.6.refs_3_), channel_id=1, source_target_pairs={{0,1},{1,0},{2,3},{3,2},{4,5},{5,4},{6,7},{7,6},{8,9},{9,8},{10,11... | collective-permute-start | bytes 3932168 | tf_op jit(solution)/shard_map/ppermute | solution.py:109
  92.1 0.0 copy-done.2
  92.1 0.1 select_reduce_fusion.1
  92.2 0.0 copy-done
  92.2 0.1 convert_reduce_fusion.1
  92.4 0.1 convert_reduce_fusion
  92.6 0.3 select_reduce_fusion
  92.8 0.0 collective-permute-done.8.refs_5_
  92.8 0.0 collective-permute-done.10.refs_7_
  92.8 2.6 %collective-permute-done.9.refs_6_ = bf16[40,128,128]{2,1,0:T(8,128)(2,1)} collective-permute-done((bf16[40,128,128]{2,1,0:T(8,128)(2,1)}, bf16[40,128,128]{2,1,0:T(8,128)(2,1)}, u32[]{:S(2)}, u32[]{:S(2)}) %collective-permute-start.9) | collective-permute-done | bytes 1310752 | tf_op jit(solution)/shard_map/ppermute | solution.py:109
  95.4 5.8 %block_products.1 = bf16[2,128,128]{2,1,0:T(8,128)(2,1)} custom-call(s32[2,256]{1,0:T(2,128)S(1)} %broadcast_add_fusion.refs_0_, s32[2]{0:T(128)S(1)} %get-tuple-element.7.refs_1_, bf16[48,128,128]{2,1,0:T(8,128)(2,1)S(1)} %constant_dynamic-update-slice_fusion.refs_2_, bf16[40,128,128]{2,1,0:T(8,128)(2,1)} %collective-permute-done.6.refs_3_, ...), custom_call_target="tpu_custom_call" | custom-call | flops 536870912 | bytes 6291456 | tf_op jit(solution)/shard_map/block_products/pallas_call | solution.py:135
  (14 shorter events, 0.3 us)
Async XLA Ops:
  0.9 17.1 %collective-permute-start = (bf16[4,128,128]{2,1,0:T(8,128)(2,1)S(1)}, bf16[4,128,128]{2,1,0:T(8,128)(2,1)S(1)}, u32[]{:S(2)}, u32[]{:S(2)}) collective-permute-start(bf16[4,128,128]{2,1,0:T(8,128)(2,1)S(1)} %fusion.1), channel_id=1, source_target_pairs={{0,1},{1,0},{2,3},{3,2},{4,5},{5,4},{6,7},{7,6},{8,9},{9,8},{10,11... | collective-permute-start | bytes 393224 | tf_op jit(solution)/shard_map/ppermute | solution.py:109
  19.0 9.9 %collective-permute-start.3 = (bf16[4,128,128]{2,1,0:T(8,128)(2,1)S(1)}, bf16[4,128,128]{2,1,0:T(8,128)(2,1)S(1)}, u32[]{:S(2)}, u32[]{:S(2)}) collective-permute-start(bf16[4,128,128]{2,1,0:T(8,128)(2,1)S(1)} %get-tuple-element.12), channel_id=1, source_target_pairs={{0,96},{1,1},{16,112},{17,17},{32,0},{33,33},{48,16},{49,49},{64,3... | collective-permute-start | bytes 393224 | tf_op jit(solution)/shard_map/ppermute | solution.py:105
  19.6 13.9 %collective-permute-start.2 = (bf16[4,128,128]{2,1,0:T(8,128)(2,1)S(1)}, bf16[4,128,128]{2,1,0:T(8,128)(2,1)S(1)}, u32[]{:S(2)}, u32[]{:S(2)}) collective-permute-start(bf16[4,128,128]{2,1,0:T(8,128)(2,1)S(1)} %get-tuple-element.12), channel_id=1, source_target_pairs={{0,64},{1,17},{16,80},{17,1},{32,96},{33,49},{48,112},{49,33},{64,... | collective-permute-start | bytes 393224 | tf_op jit(solution)/shard_map/ppermute | solution.py:105
  21.6 14.7 %collective-permute-start.1 = (bf16[4,128,128]{2,1,0:T(8,128)(2,1)S(1)}, bf16[4,128,128]{2,1,0:T(8,128)(2,1)S(1)}, u32[]{:S(2)}, u32[]{:S(2)}) collective-permute-start(bf16[4,128,128]{2,1,0:T(8,128)(2,1)S(1)} %get-tuple-element.11), channel_id=1, source_target_pairs={{0,32},{1,17},{16,48},{17,1},{32,64},{33,49},{48,80},{49,33},{64,9... | collective-permute-start | bytes 393224 | tf_op jit(solution)/shard_map/ppermute | solution.py:105
  36.3 23.7 %collective-permute-start.4 = (bf16[16,128,128]{2,1,0:T(8,128)(2,1)S(1)}, bf16[16,128,128]{2,1,0:T(8,128)(2,1)S(1)}, u32[]{:S(2)}, u32[]{:S(2)}) collective-permute-start(bf16[16,128,128]{2,1,0:T(8,128)(2,1)S(1)} %pad_maximum_fusion), channel_id=1, source_target_pairs={{0,384},{1,7},{2,386},{3,9},{4,388},{5,11},{6,390},{7,13},{8,392},... | collective-permute-start | bytes 1572872 | tf_op jit(solution)/shard_map/ppermute | solution.py:95
  40.6 22.1 %collective-permute-start.5 = (bf16[16,128,128]{2,1,0:T(8,128)(2,1)S(1)}, bf16[16,128,128]{2,1,0:T(8,128)(2,1)S(1)}, u32[]{:S(2)}, u32[]{:S(2)}) collective-permute-start(bf16[16,128,128]{2,1,0:T(8,128)(2,1)S(1)} %pad_maximum_fusion), channel_id=1, source_target_pairs={{0,640},{1,11},{2,642},{3,13},{4,644},{5,15},{6,646},{7,1},{8,648}... | collective-permute-start | bytes 1572872 | tf_op jit(solution)/shard_map/ppermute | solution.py:95
  62.8 10.7 %copy-start.1 = (s32[1,32]{1,0:T(1,128)S(1)}, s32[1,32]{1,0:T(1,128)}, u32[]{:S(2)}) copy-start(s32[1,32]{1,0:T(1,128)} %param.9) | copy-start | bytes 388
  62.8 29.3 %copy-start.2 = (s32[8]{0:T(128)S(1)}, s32[8]{0:T(128)}, u32[]{:S(2)}) copy-start(s32[8]{0:T(128)} %constant.162.clone) | copy-start | bytes 100
  62.8 29.4 %copy-start = (s32[1,256,3]{1,0,2:T(1,128)S(1)}, s32[1,256,3]{1,0,2:T(1,128)}, u32[]{:S(2)}) copy-start(s32[1,256,3]{1,0,2:T(1,128)} %param.8) | copy-start | bytes 9220
  64.9 21.5 %collective-permute-start.7 = (bf16[40,128,128]{2,1,0:T(8,128)(2,1)}, bf16[40,128,128]{2,1,0:T(8,128)(2,1)}, u32[]{:S(2)}, u32[]{:S(2)}) collective-permute-start(bf16[40,128,128]{2,1,0:T(8,128)(2,1)} %get-tuple-element.9), channel_id=1, source_target_pairs={{0,128},{1,3},{2,130},{3,5},{4,132},{5,7},{6,134},{7,9},{8,136},{9... | collective-permute-start | bytes 3932168 | tf_op jit(solution)/shard_map/ppermute | solution.py:95
  71.5 18.7 %collective-permute-start.6 = (bf16[40,128,128]{2,1,0:T(8,128)(2,1)}, bf16[40,128,128]{2,1,0:T(8,128)(2,1)}, u32[]{:S(2)}, u32[]{:S(2)}) collective-permute-start(bf16[40,128,128]{2,1,0:T(8,128)(2,1)} %get-tuple-element.10), channel_id=1, source_target_pairs={{0,896},{1,15},{2,898},{3,1},{4,900},{5,3},{6,902},{7,5},{8,904},{... | collective-permute-start | bytes 3932168 | tf_op jit(solution)/shard_map/ppermute | solution.py:95
  73.7 19.1 %collective-permute-start.8 = (bf16[48,128,128]{2,1,0:T(8,128)(2,1)S(1)}, bf16[48,128,128]{2,1,0:T(8,128)(2,1)S(1)}, u32[]{:S(2)}, u32[]{:S(2)}) collective-permute-start(bf16[48,128,128]{2,1,0:T(8,128)(2,1)S(1)} %constant_dynamic-update-slice_fusion.refs_2_), channel_id=1, source_target_pairs={{0,1},{1,0},{2,3},{3,2},{4,5},{5,4},{6,7},{7,6},{8,9},{9,8},{10,11... | collective-permute-start | bytes 4718600 | tf_op jit(solution)/shard_map/ppermute | solution.py:109
  86.4 6.5 %collective-permute-start.10 = (bf16[40,128,128]{2,1,0:T(8,128)(2,1)}, bf16[40,128,128]{2,1,0:T(8,128)(2,1)}, u32[]{:S(2)}, u32[]{:S(2)}) collective-permute-start(bf16[40,128,128]{2,1,0:T(8,128)(2,1)} %collective-permute-done.7.refs_4_), channel_id=1, source_target_pairs={{0,1},{1,0},{2,3},{3,2},{4,5},{5,4},{6,7},{7,6},{8,9},{9,8},{10,11... | collective-permute-start | bytes 3932168 | tf_op jit(solution)/shard_map/ppermute | solution.py:109
  90.2 5.3 %collective-permute-start.9 = (bf16[40,128,128]{2,1,0:T(8,128)(2,1)}, bf16[40,128,128]{2,1,0:T(8,128)(2,1)}, u32[]{:S(2)}, u32[]{:S(2)}) collective-permute-start(bf16[40,128,128]{2,1,0:T(8,128)(2,1)} %collective-permute-done.6.refs_3_), channel_id=1, source_target_pairs={{0,1},{1,0},{2,3},{3,2},{4,5},{5,4},{6,7},{7,6},{8,9},{9,8},{10,11... | collective-permute-start | bytes 3932168 | tf_op jit(solution)/shard_map/ppermute | solution.py:109

commit v8 on v5

--- a/solution.py
+++ b/solution.py
@@ -25,16 +25,14 @@
     return jnp.sum(jnp.where(hit, jnp.array(SEATS, jnp.int32), 0), axis=1)
 
 
-def slot_lists(pair_lists, pair_count, x, zl, zh, y, c):
+def slot_lists(pair_lists, pair_count, x, zl, col, c):
     pairs = pair_lists.reshape(NK * NT, 3)
     flat = jnp.arange(NK * NT, dtype=jnp.int32)
     k = flat // NT
     live = flat % NT < jnp.repeat(pair_count.reshape(NK), NT)
-    row, col = x * NZL + zl, (zh * NY + y) * NCORE + c
+    row = x * NZL + zl
     source = (k - row) % NK
-    from_zh, from_y, from_c = source // (NY * NCORE), source // NCORE % NY, source % NCORE
-    left = (jnp.where(from_c == c, 0, NY) + from_y) * TILE + pairs[:, 0]
-    left = left + jnp.where(from_zh == zh, 0, NA)
+    left = jnp.where(source % NCORE == c, 0, NY * TILE) + source // NCORE * NA + pairs[:, 0]
     holder = (k - col) % NK
     right = (2 * NY + seat_of(holder // NZL - x)) * TILE
     right = right + (zl - holder % NZL) % NZL * NB + pairs[:, 1]
@@ -85,19 +83,21 @@
 
 def per_device(left_blocks, right_blocks, pair_lists, pair_count):
     x, zl, zh, y, c = (lax.axis_index(name) for name in ("x", "zl", "zh", "y", "c"))
+    col = (zh * NY + y) * NCORE + c
+    codes, counts = slot_lists(pair_lists, pair_count, x, zl, col, c)
 
     own = [right_blocks]
     own += [lax.ppermute(right_blocks, "zl", rot(NZL, shift)) for shift in range(1, NZL)]
+    left_blocks, *own = lax.optimization_barrier((left_blocks, *own))
+    spread = jnp.broadcast_to(left_blocks[None], (NZH * NY,) + left_blocks.shape)
+    lefts = spread.reshape(NZH * NY * NA, BS, BS)
+    lefts = lax.all_to_all(lefts, ("zh", "y"), 0, 0, tiled=True)
+
     own = jnp.concatenate(own)
-    lefts = jnp.concatenate([left_blocks, lax.ppermute(left_blocks, "zh", rot(NZH, 1))])
-    lefts, own = lax.optimization_barrier((lefts, own))
-    spread = jnp.broadcast_to(lefts[None], (NY,) + lefts.shape).reshape(NY * TILE, BS, BS)
-    lefts = lax.all_to_all(spread, "y", 0, 0, tiled=True)
-
     half = TILE // 2
     behind = lax.ppermute(own, "x", rot(NX, 2))
     ahead = lax.ppermute(own, "x", rot(NX, -2))
-    behind, ahead = lax.optimization_barrier((behind, ahead))
+    behind, ahead, codes, counts = lax.optimization_barrier((behind, ahead, codes, counts))
     near = jnp.concatenate([behind, own, ahead])
     rights = [near]
     rights.append(lax.ppermute(near[: 2 * TILE], "x", rot(NX, 1)))
@@ -111,8 +111,6 @@
     for piece in pieces:
         plan.append((piece.shape[0], at))
         at += piece.shape[0]
-
-    codes, counts = slot_lists(pair_lists, pair_count, x, zl, zh, y, c)
 
     def kernel(*refs):
         product_kernel(plan, *refs)

time: 108 us -> 112 us (1.037)
  the two profiles are of different devices: /device:TPU:1 before, /device:TPU:55 now
where the time goes in v8:
time: 112 us
  starting transfers between devices  58.4 us (52%)
  waiting for transfers between devices  41.8 us (37%)
  local copies, waits for them, and re-layouts  6.79 us (6%)
  Pallas kernels  3.93 us (4%)
    all_to_all x1, waiting for transfers between devices, per_device(): lefts = lax.all_to_all(lefts, ('zh', 'y'), 0, 0, tiled=True)  18.8 us
    all_to_all x1, starting transfers between devices, per_device(): lefts = lax.all_to_all(lefts, ('zh', 'y'), 0, 0, tiled=True)  16.5 us
    ppermute x3, starting transfers between devices, per_device(): lax.ppermute(right_blocks, 'zl', rot(NZL, shift))  14.7 us
    ppermute x1, waiting for transfers between devices, per_device(): behind = lax.ppermute(own, 'x', rot(NX, 2))  8.03 us
    ppermute x1, waiting for transfers between devices, per_device(): rights.append(lax.ppermute(ahead[half:], 'x', rot(NX, -2)))  6.04 us
    ppermute x1, starting transfers between devices, per_device(): pieces = [lefts, lax.ppermute(lefts, 'c', rot(NCORE, 1))] + rights  5.98 us
    ppermute x1, starting transfers between devices, per_device(): rights.append(lax.ppermute(behind[:half], 'x', rot(NX, 2)))  5.47 us
    ppermute x1, starting transfers between devices, per_device(): behind = lax.ppermute(own, 'x', rot(NX, 2))  5.26 us
  transfers between devices with their start and end apart: 11, of which 6 were waited for; matrix products, arithmetic and copies ran while one was open for 1% of the time, Pallas kernels for 0%

profile of v8, /device:TPU:55, one launch (start us, length us, event | category | flops | bytes accessed | tf_op | source)
XLA Modules:
  0.0 111.9 jit_solution(13837573257486518301)
XLA Ops:
  0.0 7.6 %collective-permute-start.1 = (bf16[2,128,128]{2,1,0:T(8,128)(2,1)}, bf16[2,128,128]{2,1,0:T(8,128)(2,1)S(1)}, u32[]{:S(2)}, u32[]{:S(2)}) collective-permute-start(bf16[2,128,128]{2,1,0:T(8,128)(2,1)} %param.6), channel_id=1, source_target_pairs={{0,64},{32,96},{64,0},{96,32},{1,65},{33,97},{65,1},{97,33},{2,66}... | collective-permute-start | bytes 196616 | tf_op jit(solution)/shard_map/ppermute | solution.py:90
  7.6 4.9 %collective-permute-start = (bf16[2,128,128]{2,1,0:T(8,128)(2,1)}, bf16[2,128,128]{2,1,0:T(8,128)(2,1)S(1)}, u32[]{:S(2)}, u32[]{:S(2)}) collective-permute-start(bf16[2,128,128]{2,1,0:T(8,128)(2,1)} %param.6), channel_id=1, source_target_pairs={{0,32},{32,64},{64,96},{96,0},{1,33},{33,65},{65,97},{97,1},{2,34}... | collective-permute-start | bytes 196616 | tf_op jit(solution)/shard_map/ppermute | solution.py:90
  12.5 2.2 %collective-permute-start.2 = (bf16[2,128,128]{2,1,0:T(8,128)(2,1)}, bf16[2,128,128]{2,1,0:T(8,128)(2,1)S(1)}, u32[]{:S(2)}, u32[]{:S(2)}) collective-permute-start(bf16[2,128,128]{2,1,0:T(8,128)(2,1)} %param.6), channel_id=1, source_target_pairs={{0,96},{32,0},{64,32},{96,64},{1,97},{33,1},{65,33},{97,65},{2,98}... | collective-permute-start | bytes 196616 | tf_op jit(solution)/shard_map/ppermute | solution.py:90
  14.7 0.0 collective-permute-done.1
  14.7 0.0 collective-permute-done
  14.7 3.0 %collective-permute-done.2 = bf16[2,128,128]{2,1,0:T(8,128)(2,1)S(1)} collective-permute-done((bf16[2,128,128]{2,1,0:T(8,128)(2,1)}, bf16[2,128,128]{2,1,0:T(8,128)(2,1)S(1)}, u32[]{:S(2)}, u32[]{:S(2)}) %collective-permute-start.2) | collective-permute-done | bytes 65568 | tf_op jit(solution)/shard_map/ppermute | solution.py:90
  17.8 2.7 %broadcast_in_dim.52 = bf16[16,4,128,128]{3,2,1,0:T(8,128)(2,1)} broadcast(bf16[4,128,128]{2,1,0:T(8,128)(2,1)} %param.5), dimensions={1,2,3} | broadcast | bytes 2228224 | tf_op jit(solution)/shard_map/broadcast_in_dim | solution.py:92
  20.5 0.0 copy-start.5
  20.5 0.0 copy-start.6
  20.5 0.0 copy-start.7
  20.5 0.0 copy-start.4
  20.5 16.5 %all-to-all-start = ((bf16[64,128,128]{2,1,0:T(8,128)(2,1)}), bf16[64,128,128]{2,1,0:T(8,128)(2,1)S(1)}, u32[]{:S(2)}, u32[]{:S(2)}) async-start(bf16[64,128,128]{2,1,0:T(8,128)(2,1)} %bitcast.8), calls=%async_computation | async-start | bytes 4194304 | tf_op jit(solution)/shard_map/all_to_all | solution.py:94
  37.0 0.0 copy-done.5
  37.0 0.0 copy-done.6
  37.0 0.1 broadcast_in_dim.30
  37.1 0.1 reshape.276
  37.2 0.0 copy-done.7
  37.3 0.1 select_reduce_fusion.1
  37.4 0.1 convert_reduce_fusion.1
  37.5 0.1 convert_reduce_fusion
  37.7 0.0 copy-done.4
  37.8 2.1 %collective-permute-start.4 = (bf16[8,128,128]{2,1,0:T(8,128)(2,1)S(1)}, bf16[8,128,128]{2,1,0:T(8,128)(2,1)S(1)}, u32[]{:S(2)}, u32[]{:S(2)}) collective-permute-start(bf16[8,128,128]{2,1,0:T(8,128)(2,1)S(1)} %constant_dynamic-update-slice_fusion), channel_id=1, source_target_pairs={{0,768},{128,896},{256,0},{384,128},{512,256},{640,384},{768,512},... | collective-permute-start | bytes 786440 | tf_op jit(solution)/shard_map/ppermute | solution.py:99
  39.9 5.3 %collective-permute-start.3 = (bf16[8,128,128]{2,1,0:T(8,128)(2,1)S(1)}, bf16[8,128,128]{2,1,0:T(8,128)(2,1)S(1)}, u32[]{:S(2)}, u32[]{:S(2)}) collective-permute-start(bf16[8,128,128]{2,1,0:T(8,128)(2,1)S(1)} %constant_dynamic-update-slice_fusion), channel_id=1, source_target_pairs={{0,256},{128,384},{256,512},{384,640},{512,768},{640,896},{768,0},... | collective-permute-start | bytes 786440 | tf_op jit(solution)/shard_map/ppermute | solution.py:98
  45.2 0.2 select_reduce_fusion
  45.5 2.1 %collective-permute-done.4 = bf16[8,128,128]{2,1,0:T(8,128)(2,1)S(1)} collective-permute-done((bf16[8,128,128]{2,1,0:T(8,128)(2,1)S(1)}, bf16[8,128,128]{2,1,0:T(8,128)(2,1)S(1)}, u32[]{:S(2)}, u32[]{:S(2)}) %collective-permute-start.4) | collective-permute-done | bytes 262176 | tf_op jit(solution)/shard_map/ppermute | solution.py:99
  47.5 8.0 %collective-permute-done.3 = bf16[8,128,128]{2,1,0:T(8,128)(2,1)S(1)} collective-permute-done((bf16[8,128,128]{2,1,0:T(8,128)(2,1)S(1)}, bf16[8,128,128]{2,1,0:T(8,128)(2,1)S(1)}, u32[]{:S(2)}, u32[]{:S(2)}) %collective-permute-start.3) | collective-permute-done | bytes 262176 | tf_op jit(solution)/shard_map/ppermute | solution.py:98
  55.6 0.1 constant_dynamic-update-slice_fusion.14
  55.8 0.1 constant_dynamic-update-slice_fusion.15
  56.0 1.9 %collective-permute-start.6 = (bf16[16,128,128]{2,1,0:T(8,128)(2,1)S(1)}, bf16[16,128,128]{2,1,0:T(8,128)(2,1)S(1)}, u32[]{:S(2)}, u32[]{:S(2)}) collective-permute-start(bf16[16,128,128]{2,1,0:T(8,128)(2,1)S(1)} %get-tuple-element.37), channel_id=1, source_target_pairs={{0,896},{128,0},{256,128},{384,256},{512,384},{640,512},{768,640},... | collective-permute-start | bytes 1572872 | tf_op jit(solution)/shard_map/ppermute | solution.py:104
  57.9 4.6 %collective-permute-start.5 = (bf16[16,128,128]{2,1,0:T(8,128)(2,1)S(1)}, bf16[16,128,128]{2,1,0:T(8,128)(2,1)S(1)}, u32[]{:S(2)}, u32[]{:S(2)}) collective-permute-start(bf16[16,128,128]{2,1,0:T(8,128)(2,1)S(1)} %get-tuple-element.42), channel_id=1, source_target_pairs={{0,128},{128,256},{256,384},{384,512},{512,640},{640,768},{768,896... | collective-permute-start | bytes 1572872 | tf_op jit(solution)/shard_map/ppermute | solution.py:103
  62.5 1.9 %collective-permute-start.8 = (bf16[4,128,128]{2,1,0:T(8,128)(2,1)S(1)}, bf16[4,128,128]{2,1,0:T(8,128)(2,1)S(1)}, u32[]{:S(2)}, u32[]{:S(2)}) collective-permute-start(bf16[4,128,128]{2,1,0:T(8,128)(2,1)S(1)} %slice.23), channel_id=1, source_target_pairs={{0,768},{128,896},{256,0},{384,128},{512,256},{640,384},{768,512},... | collective-permute-start | bytes 393224 | tf_op jit(solution)/shard_map/ppermute | solution.py:106
  64.4 5.5 %collective-permute-start.7 = (bf16[4,128,128]{2,1,0:T(8,128)(2,1)S(1)}, bf16[4,128,128]{2,1,0:T(8,128)(2,1)S(1)}, u32[]{:S(2)}, u32[]{:S(2)}) collective-permute-start(bf16[4,128,128]{2,1,0:T(8,128)(2,1)S(1)} %slice.22), channel_id=1, source_target_pairs={{0,256},{128,384},{256,512},{384,640},{512,768},{640,896},{768,0},... | collective-permute-start | bytes 393224 | tf_op jit(solution)/shard_map/ppermute | solution.py:105
  69.9 6.0 %collective-permute-done.8.refs_8_ = bf16[4,128,128]{2,1,0:T(8,128)(2,1)S(1)} collective-permute-done((bf16[4,128,128]{2,1,0:T(8,128)(2,1)S(1)}, bf16[4,128,128]{2,1,0:T(8,128)(2,1)S(1)}, u32[]{:S(2)}, u32[]{:S(2)}) %collective-permute-start.8) | collective-permute-done | bytes 131104 | tf_op jit(solution)/shard_map/ppermute | solution.py:106
  76.0 0.0 collective-permute-done.7.refs_7_
  76.0 0.0 copy-start.2
  76.0 0.6 copy-done.2
  76.6 0.0 collective-permute-done.6.refs_6_
  76.6 0.0 collective-permute-done.5.refs_5_
  76.6 0.0 copy-start
  76.6 0.8 copy-done
  77.4 18.8 %all-to-all-done.refs_2_ = bf16[64,128,128]{2,1,0:T(8,128)(2,1)S(1)} async-done(((bf16[64,128,128]{2,1,0:T(8,128)(2,1)}), bf16[64,128,128]{2,1,0:T(8,128)(2,1)S(1)}, u32[]{:S(2)}, u32[]{:S(2)}) %all-to-all-start) | async-done | bytes 2097184 | tf_op jit(solution)/shard_map/all_to_all | solution.py:94
  96.3 6.0 %collective-permute-start.9 = (bf16[64,128,128]{2,1,0:T(8,128)(2,1)S(1)}, bf16[64,128,128]{2,1,0:T(8,128)(2,1)S(1)}, u32[]{:S(2)}, u32[]{:S(2)}) collective-permute-start(bf16[64,128,128]{2,1,0:T(8,128)(2,1)S(1)} %all-to-all-done.refs_2_), channel_id=1, source_target_pairs={{0,1},{1,0},{2,3},{3,2},{4,5},{5,4},{6,7},{7,6},{8,9},{9,8},{10,11... | collective-permute-start | bytes 6291464 | tf_op jit(solution)/shard_map/ppermute | solution.py:109
  102.3 3.8 %collective-permute-done.9.refs_3_ = bf16[64,128,128]{2,1,0:T(8,128)(2,1)S(1)} collective-permute-done((bf16[64,128,128]{2,1,0:T(8,128)(2,1)S(1)}, bf16[64,128,128]{2,1,0:T(8,128)(2,1)S(1)}, u32[]{:S(2)}, u32[]{:S(2)}) %collective-permute-start.9) | collective-permute-done | bytes 2097184 | tf_op jit(solution)/shard_map/ppermute | solution.py:109
  106.0 0.0 copy-start.1
  106.0 1.0 copy-done.1
  107.1 0.0 copy-start.3
  107.1 0.9 copy-done.3
  108.0 3.9 %block_products.1 = bf16[2,128,128]{2,1,0:T(8,128)(2,1)} custom-call(s32[2,256]{1,0:T(2,128)S(1)} %broadcast_add_fusion.refs_0_, s32[2]{0:T(128)S(1)} %get-tuple-element.25.refs_1_, bf16[64,128,128]{2,1,0:T(8,128)(2,1)S(1)} %all-to-all-done.refs_2_, bf16[64,128,128]{2,1,0:T(8,128)(2,1)S(1)} %collective-permute-done.9.refs_3_, ...), custom_call_target="tpu_custom_call" | custom-call | flops 536870912 | bytes 6291456 | tf_op jit(solution)/shard_map/block_products/pallas_call | solution.py:118
  (17 shorter events, 0.4 us)
Async XLA Ops:
  0.0 14.7 %collective-permute-start.1 = (bf16[2,128,128]{2,1,0:T(8,128)(2,1)}, bf16[2,128,128]{2,1,0:T(8,128)(2,1)S(1)}, u32[]{:S(2)}, u32[]{:S(2)}) collective-permute-start(bf16[2,128,128]{2,1,0:T(8,128)(2,1)} %param.6), channel_id=1, source_target_pairs={{0,64},{32,96},{64,0},{96,32},{1,65},{33,97},{65,1},{97,33},{2,66}... | collective-permute-start | bytes 196616 | tf_op jit(solution)/shard_map/ppermute | solution.py:90
  7.6 7.1 %collective-permute-start = (bf16[2,128,128]{2,1,0:T(8,128)(2,1)}, bf16[2,128,128]{2,1,0:T(8,128)(2,1)S(1)}, u32[]{:S(2)}, u32[]{:S(2)}) collective-permute-start(bf16[2,128,128]{2,1,0:T(8,128)(2,1)} %param.6), channel_id=1, source_target_pairs={{0,32},{32,64},{64,96},{96,0},{1,33},{33,65},{65,97},{97,1},{2,34}... | collective-permute-start | bytes 196616 | tf_op jit(solution)/shard_map/ppermute | solution.py:90
  12.5 5.2 %collective-permute-start.2 = (bf16[2,128,128]{2,1,0:T(8,128)(2,1)}, bf16[2,128,128]{2,1,0:T(8,128)(2,1)S(1)}, u32[]{:S(2)}, u32[]{:S(2)}) collective-permute-start(bf16[2,128,128]{2,1,0:T(8,128)(2,1)} %param.6), channel_id=1, source_target_pairs={{0,96},{32,0},{64,32},{96,64},{1,97},{33,1},{65,33},{97,65},{2,98}... | collective-permute-start | bytes 196616 | tf_op jit(solution)/shard_map/ppermute | solution.py:90
  20.5 16.5 %copy-start.5 = (s32[1,256,3]{1,0,2:T(1,128)S(1)}, s32[1,256,3]{1,0,2:T(1,128)}, u32[]{:S(2)}) copy-start(s32[1,256,3]{1,0,2:T(1,128)} %param.7) | copy-start | bytes 9220
  20.5 16.5 %copy-start.6 = (s32[1,32]{1,0:T(1,128)S(1)}, s32[1,32]{1,0:T(1,128)}, u32[]{:S(2)}) copy-start(s32[1,32]{1,0:T(1,128)} %param.8) | copy-start | bytes 388
  20.5 16.7 %copy-start.7 = (s32[8]{0:T(128)S(1)}, s32[8]{0:T(128)}, u32[]{:S(2)}) copy-start(s32[8]{0:T(128)} %constant.138.clone) | copy-start | bytes 100
  20.5 17.2 %copy-start.4 = (bf16[2,128,128]{2,1,0:T(8,128)(2,1)S(1)}, bf16[2,128,128]{2,1,0:T(8,128)(2,1)}, u32[]{:S(2)}) copy-start(bf16[2,128,128]{2,1,0:T(8,128)(2,1)} %param.6) | copy-start | bytes 196612
  20.5 75.8 %all-to-all-start = ((bf16[64,128,128]{2,1,0:T(8,128)(2,1)}), bf16[64,128,128]{2,1,0:T(8,128)(2,1)S(1)}, u32[]{:S(2)}, u32[]{:S(2)}) async-start(bf16[64,128,128]{2,1,0:T(8,128)(2,1)} %bitcast.8), calls=%async_computation | async-start | bytes 4194304 | tf_op jit(solution)/shard_map/all_to_all | solution.py:94
  37.8 9.7 %collective-permute-start.4 = (bf16[8,128,128]{2,1,0:T(8,128)(2,1)S(1)}, bf16[8,128,128]{2,1,0:T(8,128)(2,1)S(1)}, u32[]{:S(2)}, u32[]{:S(2)}) collective-permute-start(bf16[8,128,128]{2,1,0:T(8,128)(2,1)S(1)} %constant_dynamic-update-slice_fusion), channel_id=1, source_target_pairs={{0,768},{128,896},{256,0},{384,128},{512,256},{640,384},{768,512},... | collective-permute-start | bytes 786440 | tf_op jit(solution)/shard_map/ppermute | solution.py:99
  39.9 15.6 %collective-permute-start.3 = (bf16[8,128,128]{2,1,0:T(8,128)(2,1)S(1)}, bf16[8,128,128]{2,1,0:T(8,128)(2,1)S(1)}, u32[]{:S(2)}, u32[]{:S(2)}) collective-permute-start(bf16[8,128,128]{2,1,0:T(8,128)(2,1)S(1)} %constant_dynamic-update-slice_fusion), channel_id=1, source_target_pairs={{0,256},{128,384},{256,512},{384,640},{512,768},{640,896},{768,0},... | collective-permute-start | bytes 786440 | tf_op jit(solution)/shard_map/ppermute | solution.py:98
  56.0 20.6 %collective-permute-start.6 = (bf16[16,128,128]{2,1,0:T(8,128)(2,1)S(1)}, bf16[16,128,128]{2,1,0:T(8,128)(2,1)S(1)}, u32[]{:S(2)}, u32[]{:S(2)}) collective-permute-start(bf16[16,128,128]{2,1,0:T(8,128)(2,1)S(1)} %get-tuple-element.37), channel_id=1, source_target_pairs={{0,896},{128,0},{256,128},{384,256},{512,384},{640,512},{768,640},... | collective-permute-start | bytes 1572872 | tf_op jit(solution)/shard_map/ppermute | solution.py:104
  57.9 18.7 %collective-permute-start.5 = (bf16[16,128,128]{2,1,0:T(8,128)(2,1)S(1)}, bf16[16,128,128]{2,1,0:T(8,128)(2,1)S(1)}, u32[]{:S(2)}, u32[]{:S(2)}) collective-permute-start(bf16[16,128,128]{2,1,0:T(8,128)(2,1)S(1)} %get-tuple-element.42), channel_id=1, source_target_pairs={{0,128},{128,256},{256,384},{384,512},{512,640},{640,768},{768,896... | collective-permute-start | bytes 1572872 | tf_op jit(solution)/shard_map/ppermute | solution.py:103
  62.5 13.4 %collective-permute-start.8 = (bf16[4,128,128]{2,1,0:T(8,128)(2,1)S(1)}, bf16[4,128,128]{2,1,0:T(8,128)(2,1)S(1)}, u32[]{:S(2)}, u32[]{:S(2)}) collective-permute-start(bf16[4,128,128]{2,1,0:T(8,128)(2,1)S(1)} %slice.23), channel_id=1, source_target_pairs={{0,768},{128,896},{256,0},{384,128},{512,256},{640,384},{768,512},... | collective-permute-start | bytes 393224 | tf_op jit(solution)/shard_map/ppermute | solution.py:106
  64.4 11.5 %collective-permute-start.7 = (bf16[4,128,128]{2,1,0:T(8,128)(2,1)S(1)}, bf16[4,128,128]{2,1,0:T(8,128)(2,1)S(1)}, u32[]{:S(2)}, u32[]{:S(2)}) collective-permute-start(bf16[4,128,128]{2,1,0:T(8,128)(2,1)S(1)} %slice.22), channel_id=1, source_target_pairs={{0,256},{128,384},{256,512},{384,640},{512,768},{640,896},{768,0},... | collective-permute-start | bytes 393224 | tf_op jit(solution)/shard_map/ppermute | solution.py:105
  76.0 0.6 copy-start.2
  76.6 0.8 copy-start
  96.3 9.8 %collective-permute-start.9 = (bf16[64,128,128]{2,1,0:T(8,128)(2,1)S(1)}, bf16[64,128,128]{2,1,0:T(8,128)(2,1)S(1)}, u32[]{:S(2)}, u32[]{:S(2)}) collective-permute-start(bf16[64,128,128]{2,1,0:T(8,128)(2,1)S(1)} %all-to-all-done.refs_2_), channel_id=1, source_target_pairs={{0,1},{1,0},{2,3},{3,2},{4,5},{5,4},{6,7},{7,6},{8,9},{9,8},{10,11... | collective-permute-start | bytes 6291464 | tf_op jit(solution)/shard_map/ppermute | solution.py:109
  106.0 1.0 copy-start.1
  107.1 0.9 copy-start.3

commit v9 on v7

--- a/solution.py
+++ b/solution.py
@@ -13,16 +13,10 @@
 GROUP = 16
 TILE = 16
 ZERO = 2 * NY * TILE
-SEATS = (1, 4, 7, 2, 5, 0, 3, 6)
 
 
 def rot(size, shift):
     return [(s, (s + shift) % size) for s in range(size)]
-
-
-def seat_of(distance):
-    hit = distance[:, None] % NY == jnp.arange(NY, dtype=jnp.int32)
-    return jnp.sum(jnp.where(hit, jnp.array(SEATS, jnp.int32), 0), axis=1)
 
 
 def slot_lists(pair_lists, pair_count, x, zl, zh, y, c):
@@ -35,10 +29,10 @@
     from_zh, from_y, from_c = source // (NY * NCORE), source // NCORE % NY, source % NCORE
     near = from_zh == zh
     part = jnp.where(from_c == 0, jnp.where(near, 0, 1), jnp.where(near, 3, 2))
-    left = (jnp.where(c == 1, 0, NY) + seat_of(from_y - y)) * TILE + part * NA + pairs[:, 0]
+    left = (jnp.where(c == 1, 0, NY) + (from_y - y) * (1 - y % 2 * 2) % NY) * TILE + part * NA + pairs[:, 0]
     holder = (k - col) % NK
-    part = (zl - holder % NZL) % NZL
-    right = (jnp.where(c == 0, 0, NY) + seat_of(holder // NZL - x)) * TILE
+    part = zl ^ holder % NZL
+    right = (jnp.where(c == 0, 0, NY) + (holder // NZL - x) * (1 - x % 2 * 2) % NX) * TILE
     right = right + (part * NCORE + c) * NB + pairs[:, 1]
     code = left * 512 + right
     target = jnp.arange(NC, dtype=jnp.int32)[:, None]
@@ -85,22 +79,22 @@
     out[1] = total[1].astype(jnp.bfloat16)
 
 
-def along_plane(value, shift):
+def along_plane(value, kind):
     pairs = []
     for x in range(NX):
         for y in range(NY):
             place = (x * NY + y) * NCORE
-            pairs.append((place, ((x + shift) % NX * NY + y) * NCORE))
-            pairs.append((place + 1, (x * NY + (y + shift) % NY) * NCORE + 1))
+            pairs.append((place, ((((x + kind) ^ 1) - kind) % NX * NY + y) * NCORE))
+            pairs.append((place + 1, (x * NY + (((y + kind) ^ 1) - kind) % NY) * NCORE + 1))
     return lax.ppermute(value, ("x", "y", "c"), pairs)
 
 
-def along_z(value, shift, swap):
+def along_z(value, flip, swap):
     pairs = []
     for zl in range(NZL):
         for zh in range(NZH):
             place = (zl * NZH + zh) * NCORE
-            pairs.append((place, ((zl + shift) % NZL * NZH + zh) * NCORE))
+            pairs.append((place, ((zl ^ flip) * NZH + zh) * NCORE))
             pairs.append((place + 1, (zl * NZH + (zh + swap) % NZH) * NCORE + 1))
     return lax.ppermute(value, ("zl", "zh", "c"), pairs)
 
@@ -119,13 +113,16 @@
         [first, along_z(first, 1, 1), along_z(second, 2, 1), along_z(second, 3, 0)]
     )
     half = TILE // 2
-    near = jnp.concatenate([along_plane(own, 3), own, along_plane(own, -3)])
-    pieces = [near, along_plane(near[: 2 * TILE + half], -1), along_plane(near[half:], 1)]
+    pieces, plan = [own], [(TILE, 0)]
+    one = two = own
+    for distance in range(1, NY // 2):
+        one, two = along_plane(two, 0), along_plane(one, 1)
+        pieces += [one, two]
+        plan += [(TILE, distance * TILE), (TILE, (NY - distance) * TILE)]
+    pieces += [along_plane(two[:half], 0), along_plane(one[half:], 1)]
+    plan += [(half, NY // 2 * TILE), (half, NY // 2 * TILE + half)]
     pieces += [to_partner(piece) for piece in pieces]
-    plan, at = [], 0
-    for piece in pieces:
-        plan.append((piece.shape[0], at))
-        at += piece.shape[0]
+    plan += [(size, NY * TILE + at) for size, at in plan]
 
     codes, counts = slot_lists(pair_lists, pair_count, x, zl, zh, y, c)
 

time: 102 us -> 100 us (0.980)
  starting transfers between devices: 48.5 us -> 74.3 us
  waiting for transfers between devices: 41.5 us -> 17.6 us
  local copies, waits for them, and re-layouts: 2.43 us -> 0.87 us
  Pallas kernels: 5.78 us -> 4.64 us
  other arithmetic: 2.71 us -> 1.66 us
    ppermute x4 -> x8, waiting for transfers between devices: 30.5 us -> 10.4 us  [along_plane(): return lax.ppermute(value, ('x', 'y', 'c'), pairs)]
    ppermute x4 -> x10, starting transfers between devices: 21.8 us -> 41.5 us  [to_partner(): return lax.ppermute(value, 'c', rot(NCORE, 1))]
    ppermute x4 -> x8, starting transfers between devices: 16.9 us -> 22.9 us  [along_plane(): return lax.ppermute(value, ('x', 'y', 'c'), pairs)]
    slice x1 -> x2, local copies, waits for them, and re-layouts: 2.05 us -> 0.04 us  [per_device(): pieces += [along_plane(two[:half], 0), along_plane(one[half:], 1)]]
    ppermute x3, waiting for transfers between devices: 7.39 us -> 5.43 us  [along_z(): return lax.ppermute(value, ('zl', 'zh', 'c'), pairs)]
    ppermute x4 -> x10, waiting for transfers between devices: 3.56 us -> 1.84 us  [to_partner(): return lax.ppermute(value, 'c', rot(NCORE, 1))]
    pallas_call x1, Pallas kernels: 5.78 us -> 4.64 us  [per_device(): pl.pallas_call(kernel, out_shape=jax.ShapeDtypeStruct((NC, BS, BS), jnp.b...]
  transfers between devices with their start and end apart: 11 -> 21, of which waited for: 8 -> 7; matrix products, arithmetic and copies ran while one was open for 1% -> 1% of each run, Pallas kernels for 0% -> 0%
where the time goes in v9:
time: 100 us; the launch traced here: 99.5 us
  starting transfers between devices  74.3 us (74%)
  waiting for transfers between devices  17.6 us (18%)
  Pallas kernels  4.64 us (5%)
  other arithmetic  1.66 us (2%)
    ppermute x10, starting transfers between devices, to_partner(): return lax.ppermute(value, 'c', rot(NCORE, 1))  41.5 us
    ppermute x8, starting transfers between devices, along_plane(): return lax.ppermute(value, ('x', 'y', 'c'), pairs)  22.9 us
    ppermute x8, waiting for transfers between devices, along_plane(): return lax.ppermute(value, ('x', 'y', 'c'), pairs)  10.4 us
    ppermute x3, starting transfers between devices, along_z(): return lax.ppermute(value, ('zl', 'zh', 'c'), pairs)  9.86 us
    ppermute x3, waiting for transfers between devices, along_z(): return lax.ppermute(value, ('zl', 'zh', 'c'), pairs)  5.43 us
    pallas_call x1, Pallas kernels, per_device(): pl.pallas_call(kernel, out_shape=jax.ShapeDtypeStruct((NC, BS, BS), jnp.b...  4.64 us
  transfers between devices with their start and end apart: 21, of which 7 were waited for; matrix products, arithmetic and copies ran while one was open for 1% of the time, Pallas kernels for 0%

profile of v9, /device:TPU:1, one launch (start us, length us, event | category | flops | bytes accessed | tf_op | source)
XLA Modules:
  0.0 99.5 jit_solution(14241143472820282691)
XLA Ops:
  0.0 1.0 fusion.1
  1.0 0.0 copy-start
  1.0 16.2 %collective-permute-start = (bf16[4,128,128]{2,1,0:T(8,128)(2,1)S(1)}, bf16[4,128,128]{2,1,0:T(8,128)(2,1)S(1)}, u32[]{:S(2)}, u32[]{:S(2)}) collective-permute-start(bf16[4,128,128]{2,1,0:T(8,128)(2,1)S(1)} %fusion.1), channel_id=1, source_target_pairs={{0,1},{1,0},{2,3},{3,2},{4,5},{5,4},{6,7},{7,6},{8,9},{9,8},{10,11... | collective-permute-start | bytes 393224 | tf_op jit(solution)/shard_map/ppermute | solution.py:103
  17.2 1.0 collective-permute-done
  18.2 1.9 %collective-permute-start.1 = (bf16[4,128,128]{2,1,0:T(8,128)(2,1)S(1)}, bf16[4,128,128]{2,1,0:T(8,128)(2,1)S(1)}, u32[]{:S(2)}, u32[]{:S(2)}) collective-permute-start(bf16[4,128,128]{2,1,0:T(8,128)(2,1)S(1)} %get-tuple-element.7), channel_id=1, source_target_pairs={{0,32},{1,17},{16,48},{17,1},{32,0},{33,49},{48,16},{49,33},{64,96... | collective-permute-start | bytes 393224 | tf_op jit(solution)/shard_map/ppermute | solution.py:99
  20.2 0.0 copy-start.2
  20.2 0.7 collective-permute-start.3
  20.9 7.3 %collective-permute-start.2 = (bf16[4,128,128]{2,1,0:T(8,128)(2,1)S(1)}, bf16[4,128,128]{2,1,0:T(8,128)(2,1)S(1)}, u32[]{:S(2)}, u32[]{:S(2)}) collective-permute-start(bf16[4,128,128]{2,1,0:T(8,128)(2,1)S(1)} %get-tuple-element.8), channel_id=1, source_target_pairs={{0,64},{1,17},{16,80},{17,1},{32,96},{33,49},{48,112},{49,33},{64,... | collective-permute-start | bytes 393224 | tf_op jit(solution)/shard_map/ppermute | solution.py:99
  28.1 1.2 %collective-permute-done.1 = bf16[4,128,128]{2,1,0:T(8,128)(2,1)S(1)} collective-permute-done((bf16[4,128,128]{2,1,0:T(8,128)(2,1)S(1)}, bf16[4,128,128]{2,1,0:T(8,128)(2,1)S(1)}, u32[]{:S(2)}, u32[]{:S(2)}) %collective-permute-start.1) | collective-permute-done | bytes 131104 | tf_op jit(solution)/shard_map/ppermute | solution.py:99
  29.3 0.0 collective-permute-done.3
  29.3 4.3 %collective-permute-done.2 = bf16[4,128,128]{2,1,0:T(8,128)(2,1)S(1)} collective-permute-done((bf16[4,128,128]{2,1,0:T(8,128)(2,1)S(1)}, bf16[4,128,128]{2,1,0:T(8,128)(2,1)S(1)}, u32[]{:S(2)}, u32[]{:S(2)}) %collective-permute-start.2) | collective-permute-done | bytes 131104 | tf_op jit(solution)/shard_map/ppermute | solution.py:99
  33.6 0.1 pad_maximum_fusion.refs_2_
  33.6 5.7 %collective-permute-start.5 = (bf16[16,128,128]{2,1,0:T(8,128)(2,1)S(1)}, bf16[16,128,128]{2,1,0:T(8,128)(2,1)S(1)}, u32[]{:S(2)}, u32[]{:S(2)}) collective-permute-start(bf16[16,128,128]{2,1,0:T(8,128)(2,1)S(1)} %pad_maximum_fusion.refs_2_), channel_id=1, source_target_pairs={{0,896},{1,15},{2,898},{3,5},{4,900},{5,3},{6,902},{7,9},{8,904},{... | collective-permute-start | bytes 1572872 | tf_op jit(solution)/shard_map/ppermute | solution.py:89
  39.3 1.9 %collective-permute-start.4 = (bf16[16,128,128]{2,1,0:T(8,128)(2,1)S(1)}, bf16[16,128,128]{2,1,0:T(8,128)(2,1)S(1)}, u32[]{:S(2)}, u32[]{:S(2)}) collective-permute-start(bf16[16,128,128]{2,1,0:T(8,128)(2,1)S(1)} %pad_maximum_fusion.refs_2_), channel_id=1, source_target_pairs={{0,128},{1,3},{2,130},{3,1},{4,132},{5,7},{6,134},{7,5},{8,136},{9... | collective-permute-start | bytes 1572872 | tf_op jit(solution)/shard_map/ppermute | solution.py:89
  41.2 4.9 %collective-permute-done.5.refs_4_ = bf16[16,128,128]{2,1,0:T(8,128)(2,1)S(1)} collective-permute-done((bf16[16,128,128]{2,1,0:T(8,128)(2,1)S(1)}, bf16[16,128,128]{2,1,0:T(8,128)(2,1)S(1)}, u32[]{:S(2)}, u32[]{:S(2)}) %collective-permute-start.5) | collective-permute-done | bytes 524320 | tf_op jit(solution)/shard_map/ppermute | solution.py:89
  46.2 1.9 %collective-permute-start.6 = (bf16[16,128,128]{2,1,0:T(8,128)(2,1)S(1)}, bf16[16,128,128]{2,1,0:T(8,128)(2,1)S(1)}, u32[]{:S(2)}, u32[]{:S(2)}) collective-permute-start(bf16[16,128,128]{2,1,0:T(8,128)(2,1)S(1)} %collective-permute-done.5.refs_4_), channel_id=1, source_target_pairs={{0,128},{1,3},{2,130},{3,1},{4,132},{5,7},{6,134},{7,5},{8,136},{9... | collective-permute-start | bytes 1572872 | tf_op jit(solution)/shard_map/ppermute | solution.py:89
  48.1 1.5 %collective-permute-done.4.refs_3_ = bf16[16,128,128]{2,1,0:T(8,128)(2,1)S(1)} collective-permute-done((bf16[16,128,128]{2,1,0:T(8,128)(2,1)S(1)}, bf16[16,128,128]{2,1,0:T(8,128)(2,1)S(1)}, u32[]{:S(2)}, u32[]{:S(2)}) %collective-permute-start.4) | collective-permute-done | bytes 524320 | tf_op jit(solution)/shard_map/ppermute | solution.py:89
  49.5 2.9 %collective-permute-start.7 = (bf16[16,128,128]{2,1,0:T(8,128)(2,1)S(1)}, bf16[16,128,128]{2,1,0:T(8,128)(2,1)}, u32[]{:S(2)}, u32[]{:S(2)}) collective-permute-start(bf16[16,128,128]{2,1,0:T(8,128)(2,1)S(1)} %collective-permute-done.4.refs_3_), channel_id=1, source_target_pairs={{0,896},{1,15},{2,898},{3,5},{4,900},{5,3},{6,902},{7,9},{8,904},{... | collective-permute-start | bytes 1572872 | tf_op jit(solution)/shard_map/ppermute | solution.py:89
  52.4 4.0 %collective-permute-done.6.refs_5_ = bf16[16,128,128]{2,1,0:T(8,128)(2,1)S(1)} collective-permute-done((bf16[16,128,128]{2,1,0:T(8,128)(2,1)S(1)}, bf16[16,128,128]{2,1,0:T(8,128)(2,1)S(1)}, u32[]{:S(2)}, u32[]{:S(2)}) %collective-permute-start.6) | collective-permute-done | bytes 524320 | tf_op jit(solution)/shard_map/ppermute | solution.py:89
  56.4 4.4 %collective-permute-start.9 = (bf16[16,128,128]{2,1,0:T(8,128)(2,1)S(1)}, bf16[16,128,128]{2,1,0:T(8,128)(2,1)S(1)}, u32[]{:S(2)}, u32[]{:S(2)}) collective-permute-start(bf16[16,128,128]{2,1,0:T(8,128)(2,1)S(1)} %collective-permute-done.6.refs_5_), channel_id=1, source_target_pairs={{0,896},{1,15},{2,898},{3,5},{4,900},{5,3},{6,902},{7,9},{8,904},{... | collective-permute-start | bytes 1572872 | tf_op jit(solution)/shard_map/ppermute | solution.py:89
  60.8 3.5 %collective-permute-start.12 = (bf16[16,128,128]{2,1,0:T(8,128)(2,1)S(1)}, bf16[16,128,128]{2,1,0:T(8,128)(2,1)}, u32[]{:S(2)}, u32[]{:S(2)}) collective-permute-start(bf16[16,128,128]{2,1,0:T(8,128)(2,1)S(1)} %pad_maximum_fusion.refs_2_), channel_id=1, source_target_pairs={{0,1},{1,0},{2,3},{3,2},{4,5},{5,4},{6,7},{7,6},{8,9},{9,8},{10,11... | collective-permute-start | bytes 1572872 | tf_op jit(solution)/shard_map/ppermute | solution.py:103
  64.3 0.0 collective-permute-done.7.refs_6_
  64.3 1.9 %collective-permute-start.8 = (bf16[16,128,128]{2,1,0:T(8,128)(2,1)}, bf16[16,128,128]{2,1,0:T(8,128)(2,1)S(1)}, u32[]{:S(2)}, u32[]{:S(2)}) collective-permute-start(bf16[16,128,128]{2,1,0:T(8,128)(2,1)} %collective-permute-done.7.refs_6_), channel_id=1, source_target_pairs={{0,128},{1,3},{2,130},{3,1},{4,132},{5,7},{6,134},{7,5},{8,136},{9... | collective-permute-start | bytes 1572872 | tf_op jit(solution)/shard_map/ppermute | solution.py:89
  66.3 0.0 copy-start.3
  66.3 0.6 copy-done.3
  66.9 0.1 broadcast_in_dim.16
  67.0 0.1 reshape.270
  67.1 2.3 %collective-permute-start.14 = (bf16[16,128,128]{2,1,0:T(8,128)(2,1)S(1)}, bf16[16,128,128]{2,1,0:T(8,128)(2,1)}, u32[]{:S(2)}, u32[]{:S(2)}) collective-permute-start(bf16[16,128,128]{2,1,0:T(8,128)(2,1)S(1)} %collective-permute-done.5.refs_4_), channel_id=1, source_target_pairs={{0,1},{1,0},{2,3},{3,2},{4,5},{5,4},{6,7},{7,6},{8,9},{9,8},{10,11... | collective-permute-start | bytes 1572872 | tf_op jit(solution)/shard_map/ppermute | solution.py:103
  69.4 2.1 %collective-permute-start.13 = (bf16[16,128,128]{2,1,0:T(8,128)(2,1)S(1)}, bf16[16,128,128]{2,1,0:T(8,128)(2,1)}, u32[]{:S(2)}, u32[]{:S(2)}) collective-permute-start(bf16[16,128,128]{2,1,0:T(8,128)(2,1)S(1)} %collective-permute-done.4.refs_3_), channel_id=1, source_target_pairs={{0,1},{1,0},{2,3},{3,2},{4,5},{5,4},{6,7},{7,6},{8,9},{9,8},{10,11... | collective-permute-start | bytes 1572872 | tf_op jit(solution)/shard_map/ppermute | solution.py:103
  71.4 0.0 collective-permute-done.9.refs_8_
  71.5 3.2 %collective-permute-start.15 = (bf16[16,128,128]{2,1,0:T(8,128)(2,1)S(1)}, bf16[16,128,128]{2,1,0:T(8,128)(2,1)}, u32[]{:S(2)}, u32[]{:S(2)}) collective-permute-start(bf16[16,128,128]{2,1,0:T(8,128)(2,1)S(1)} %collective-permute-done.6.refs_5_), channel_id=1, source_target_pairs={{0,1},{1,0},{2,3},{3,2},{4,5},{5,4},{6,7},{7,6},{8,9},{9,8},{10,11... | collective-permute-start | bytes 1572872 | tf_op jit(solution)/shard_map/ppermute | solution.py:103
  74.8 0.0 collective-permute-done.8.refs_7_
  74.8 2.1 %collective-permute-start.10 = (bf16[8,128,128]{2,1,0:T(8,128)(2,1)S(1)}, bf16[8,128,128]{2,1,0:T(8,128)(2,1)S(1)}, u32[]{:S(2)}, u32[]{:S(2)}) collective-permute-start(bf16[8,128,128]{2,1,0:T(8,128)(2,1)S(1)} %slice.28), channel_id=1, source_target_pairs={{0,128},{1,3},{2,130},{3,1},{4,132},{5,7},{6,134},{7,5},{8,136},{9... | collective-permute-start | bytes 786440 | tf_op jit(solution)/shard_map/ppermute | solution.py:89
  76.9 2.2 %collective-permute-start.11 = (bf16[8,128,128]{2,1,0:T(8,128)(2,1)S(1)}, bf16[8,128,128]{2,1,0:T(8,128)(2,1)S(1)}, u32[]{:S(2)}, u32[]{:S(2)}) collective-permute-start(bf16[8,128,128]{2,1,0:T(8,128)(2,1)S(1)} %slice.29), channel_id=1, source_target_pairs={{0,896},{1,15},{2,898},{3,5},{4,900},{5,3},{6,902},{7,9},{8,904},{... | collective-permute-start | bytes 786440 | tf_op jit(solution)/shard_map/ppermute | solution.py:89
  79.1 0.1 convert_reduce_fusion.1
  79.3 5.5 %collective-permute-start.16 = (bf16[16,128,128]{2,1,0:T(8,128)(2,1)}, bf16[16,128,128]{2,1,0:T(8,128)(2,1)S(1)}, u32[]{:S(2)}, u32[]{:S(2)}) collective-permute-start(bf16[16,128,128]{2,1,0:T(8,128)(2,1)} %collective-permute-done.7.refs_6_), channel_id=1, source_target_pairs={{0,1},{1,0},{2,3},{3,2},{4,5},{5,4},{6,7},{7,6},{8,9},{9,8},{10,11... | collective-permute-start | bytes 1572872 | tf_op jit(solution)/shard_map/ppermute | solution.py:103
  84.8 0.0 collective-permute-done.13.refs_12_
  84.8 1.9 %collective-permute-start.18 = (bf16[16,128,128]{2,1,0:T(8,128)(2,1)S(1)}, bf16[16,128,128]{2,1,0:T(8,128)(2,1)S(1)}, u32[]{:S(2)}, u32[]{:S(2)}) collective-permute-start(bf16[16,128,128]{2,1,0:T(8,128)(2,1)S(1)} %collective-permute-done.9.refs_8_), channel_id=1, source_target_pairs={{0,1},{1,0},{2,3},{3,2},{4,5},{5,4},{6,7},{7,6},{8,9},{9,8},{10,11... | collective-permute-start | bytes 1572872 | tf_op jit(solution)/shard_map/ppermute | solution.py:103
  86.7 0.0 collective-permute-done.15.refs_14_
  86.7 2.4 %collective-permute-start.17 = (bf16[16,128,128]{2,1,0:T(8,128)(2,1)S(1)}, bf16[16,128,128]{2,1,0:T(8,128)(2,1)S(1)}, u32[]{:S(2)}, u32[]{:S(2)}) collective-permute-start(bf16[16,128,128]{2,1,0:T(8,128)(2,1)S(1)} %collective-permute-done.8.refs_7_), channel_id=1, source_target_pairs={{0,1},{1,0},{2,3},{3,2},{4,5},{5,4},{6,7},{7,6},{8,9},{9,8},{10,11... | collective-permute-start | bytes 1572872 | tf_op jit(solution)/shard_map/ppermute | solution.py:103
  89.2 0.1 convert_reduce_fusion
  89.3 1.9 %collective-permute-start.19 = (bf16[8,128,128]{2,1,0:T(8,128)(2,1)S(1)}, bf16[8,128,128]{2,1,0:T(8,128)(2,1)S(1)}, u32[]{:S(2)}, u32[]{:S(2)}) collective-permute-start(bf16[8,128,128]{2,1,0:T(8,128)(2,1)S(1)} %collective-permute-done.10.refs_9_), channel_id=1, source_target_pairs={{0,1},{1,0},{2,3},{3,2},{4,5},{5,4},{6,7},{7,6},{8,9},{9,8},{10,11... | collective-permute-start | bytes 786440 | tf_op jit(solution)/shard_map/ppermute | solution.py:103
  91.3 0.0 collective-permute-done.11.refs_10_
  91.3 2.4 %collective-permute-start.20 = (bf16[8,128,128]{2,1,0:T(8,128)(2,1)S(1)}, bf16[8,128,128]{2,1,0:T(8,128)(2,1)S(1)}, u32[]{:S(2)}, u32[]{:S(2)}) collective-permute-start(bf16[8,128,128]{2,1,0:T(8,128)(2,1)S(1)} %collective-permute-done.11.refs_10_), channel_id=1, source_target_pairs={{0,1},{1,0},{2,3},{3,2},{4,5},{5,4},{6,7},{7,6},{8,9},{9,8},{10,11... | collective-permute-start | bytes 786440 | tf_op jit(solution)/shard_map/ppermute | solution.py:103
  93.7 0.2 select_reduce_fusion
  94.0 0.0 collective-permute-done.16.refs_15_
  94.0 0.9 collective-permute-done.20.refs_19_
  94.8 4.6 %block_products.1 = bf16[2,128,128]{2,1,0:T(8,128)(2,1)} custom-call(s32[2,256]{1,0:T(2,128)S(1)} %broadcast_add_fusion.refs_0_, s32[2]{0:T(128)S(1)} %get-tuple-element.5.refs_1_, bf16[16,128,128]{2,1,0:T(8,128)(2,1)S(1)} %pad_maximum_fusion.refs_2_, bf16[16,128,128]{2,1,0:T(8,128)(2,1)S(1)} %collective-permute-done.4.refs_3_, ...), custom_call_target="tpu_custom_call" | custom-call | flops 536870912 | bytes 6291456 | tf_op jit(solution)/shard_map/block_products/pallas_call | solution.py:132
  (20 shorter events, 0.2 us)
Async XLA Ops:
  0.0 18.2 %copy-start.1 = (bf16[2,128,128]{2,1,0:T(8,128)(2,1)S(1)}, bf16[2,128,128]{2,1,0:T(8,128)(2,1)}, u32[]{:S(2)}) copy-start(bf16[2,128,128]{2,1,0:T(8,128)(2,1)} %param.5) | copy-start | bytes 196612
  1.0 17.2 %copy-start = (bf16[4,128,128]{2,1,0:T(8,128)(2,1)S(1)}, bf16[4,128,128]{2,1,0:T(8,128)(2,1)}, u32[]{:S(2)}) copy-start(bf16[4,128,128]{2,1,0:T(8,128)(2,1)} %param.4) | copy-start | bytes 393220
  1.0 17.2 %collective-permute-start = (bf16[4,128,128]{2,1,0:T(8,128)(2,1)S(1)}, bf16[4,128,128]{2,1,0:T(8,128)(2,1)S(1)}, u32[]{:S(2)}, u32[]{:S(2)}) collective-permute-start(bf16[4,128,128]{2,1,0:T(8,128)(2,1)S(1)} %fusion.1), channel_id=1, source_target_pairs={{0,1},{1,0},{2,3},{3,2},{4,5},{5,4},{6,7},{7,6},{8,9},{9,8},{10,11... | collective-permute-start | bytes 393224 | tf_op jit(solution)/shard_map/ppermute | solution.py:103
  18.2 11.0 %collective-permute-start.1 = (bf16[4,128,128]{2,1,0:T(8,128)(2,1)S(1)}, bf16[4,128,128]{2,1,0:T(8,128)(2,1)S(1)}, u32[]{:S(2)}, u32[]{:S(2)}) collective-permute-start(bf16[4,128,128]{2,1,0:T(8,128)(2,1)S(1)} %get-tuple-element.7), channel_id=1, source_target_pairs={{0,32},{1,17},{16,48},{17,1},{32,0},{33,49},{48,16},{49,33},{64,96... | collective-permute-start | bytes 393224 | tf_op jit(solution)/shard_map/ppermute | solution.py:99
  20.2 40.6 %copy-start.2 = (s32[1,256,3]{1,0,2:T(1,128)S(1)}, s32[1,256,3]{1,0,2:T(1,128)}, u32[]{:S(2)}) copy-start(s32[1,256,3]{1,0,2:T(1,128)} %param.6) | copy-start | bytes 9220
  20.2 9.1 %collective-permute-start.3 = (bf16[4,128,128]{2,1,0:T(8,128)(2,1)S(1)}, bf16[4,128,128]{2,1,0:T(8,128)(2,1)S(1)}, u32[]{:S(2)}, u32[]{:S(2)}) collective-permute-start(bf16[4,128,128]{2,1,0:T(8,128)(2,1)S(1)} %get-tuple-element.8), channel_id=1, source_target_pairs={{0,96},{1,1},{16,112},{17,17},{32,64},{33,33},{48,80},{49,49},{64,... | collective-permute-start | bytes 393224 | tf_op jit(solution)/shard_map/ppermute | solution.py:99
  20.9 12.7 %collective-permute-start.2 = (bf16[4,128,128]{2,1,0:T(8,128)(2,1)S(1)}, bf16[4,128,128]{2,1,0:T(8,128)(2,1)S(1)}, u32[]{:S(2)}, u32[]{:S(2)}) collective-permute-start(bf16[4,128,128]{2,1,0:T(8,128)(2,1)S(1)} %get-tuple-element.8), channel_id=1, source_target_pairs={{0,64},{1,17},{16,80},{17,1},{32,96},{33,49},{48,112},{49,33},{64,... | collective-permute-start | bytes 393224 | tf_op jit(solution)/shard_map/ppermute | solution.py:99
  33.6 12.5 %collective-permute-start.5 = (bf16[16,128,128]{2,1,0:T(8,128)(2,1)S(1)}, bf16[16,128,128]{2,1,0:T(8,128)(2,1)S(1)}, u32[]{:S(2)}, u32[]{:S(2)}) collective-permute-start(bf16[16,128,128]{2,1,0:T(8,128)(2,1)S(1)} %pad_maximum_fusion.refs_2_), channel_id=1, source_target_pairs={{0,896},{1,15},{2,898},{3,5},{4,900},{5,3},{6,902},{7,9},{8,904},{... | collective-permute-start | bytes 1572872 | tf_op jit(solution)/shard_map/ppermute | solution.py:89
  39.3 10.2 %collective-permute-start.4 = (bf16[16,128,128]{2,1,0:T(8,128)(2,1)S(1)}, bf16[16,128,128]{2,1,0:T(8,128)(2,1)S(1)}, u32[]{:S(2)}, u32[]{:S(2)}) collective-permute-start(bf16[16,128,128]{2,1,0:T(8,128)(2,1)S(1)} %pad_maximum_fusion.refs_2_), channel_id=1, source_target_pairs={{0,128},{1,3},{2,130},{3,1},{4,132},{5,7},{6,134},{7,5},{8,136},{9... | collective-permute-start | bytes 1572872 | tf_op jit(solution)/shard_map/ppermute | solution.py:89
  46.2 10.2 %collective-permute-start.6 = (bf16[16,128,128]{2,1,0:T(8,128)(2,1)S(1)}, bf16[16,128,128]{2,1,0:T(8,128)(2,1)S(1)}, u32[]{:S(2)}, u32[]{:S(2)}) collective-permute-start(bf16[16,128,128]{2,1,0:T(8,128)(2,1)S(1)} %collective-permute-done.5.refs_4_), channel_id=1, source_target_pairs={{0,128},{1,3},{2,130},{3,1},{4,132},{5,7},{6,134},{7,5},{8,136},{9... | collective-permute-start | bytes 1572872 | tf_op jit(solution)/shard_map/ppermute | solution.py:89
  49.5 14.8 %collective-permute-start.7 = (bf16[16,128,128]{2,1,0:T(8,128)(2,1)S(1)}, bf16[16,128,128]{2,1,0:T(8,128)(2,1)}, u32[]{:S(2)}, u32[]{:S(2)}) collective-permute-start(bf16[16,128,128]{2,1,0:T(8,128)(2,1)S(1)} %collective-permute-done.4.refs_3_), channel_id=1, source_target_pairs={{0,896},{1,15},{2,898},{3,5},{4,900},{5,3},{6,902},{7,9},{8,904},{... | collective-permute-start | bytes 1572872 | tf_op jit(solution)/shard_map/ppermute | solution.py:89
  56.4 15.1 %collective-permute-start.9 = (bf16[16,128,128]{2,1,0:T(8,128)(2,1)S(1)}, bf16[16,128,128]{2,1,0:T(8,128)(2,1)S(1)}, u32[]{:S(2)}, u32[]{:S(2)}) collective-permute-start(bf16[16,128,128]{2,1,0:T(8,128)(2,1)S(1)} %collective-permute-done.6.refs_5_), channel_id=1, source_target_pairs={{0,896},{1,15},{2,898},{3,5},{4,900},{5,3},{6,902},{7,9},{8,904},{... | collective-permute-start | bytes 1572872 | tf_op jit(solution)/shard_map/ppermute | solution.py:89
  60.8 16.1 %collective-permute-start.12 = (bf16[16,128,128]{2,1,0:T(8,128)(2,1)S(1)}, bf16[16,128,128]{2,1,0:T(8,128)(2,1)}, u32[]{:S(2)}, u32[]{:S(2)}) collective-permute-start(bf16[16,128,128]{2,1,0:T(8,128)(2,1)S(1)} %pad_maximum_fusion.refs_2_), channel_id=1, source_target_pairs={{0,1},{1,0},{2,3},{3,2},{4,5},{5,4},{6,7},{7,6},{8,9},{9,8},{10,11... | collective-permute-start | bytes 1572872 | tf_op jit(solution)/shard_map/ppermute | solution.py:103
  64.3 10.4 %collective-permute-start.8 = (bf16[16,128,128]{2,1,0:T(8,128)(2,1)}, bf16[16,128,128]{2,1,0:T(8,128)(2,1)S(1)}, u32[]{:S(2)}, u32[]{:S(2)}) collective-permute-start(bf16[16,128,128]{2,1,0:T(8,128)(2,1)} %collective-permute-done.7.refs_6_), channel_id=1, source_target_pairs={{0,128},{1,3},{2,130},{3,1},{4,132},{5,7},{6,134},{7,5},{8,136},{9... | collective-permute-start | bytes 1572872 | tf_op jit(solution)/shard_map/ppermute | solution.py:89
  66.3 0.7 copy-start.3
  67.1 12.2 %collective-permute-start.14 = (bf16[16,128,128]{2,1,0:T(8,128)(2,1)S(1)}, bf16[16,128,128]{2,1,0:T(8,128)(2,1)}, u32[]{:S(2)}, u32[]{:S(2)}) collective-permute-start(bf16[16,128,128]{2,1,0:T(8,128)(2,1)S(1)} %collective-permute-done.5.refs_4_), channel_id=1, source_target_pairs={{0,1},{1,0},{2,3},{3,2},{4,5},{5,4},{6,7},{7,6},{8,9},{9,8},{10,11... | collective-permute-start | bytes 1572872 | tf_op jit(solution)/shard_map/ppermute | solution.py:103
  69.4 15.4 %collective-permute-start.13 = (bf16[16,128,128]{2,1,0:T(8,128)(2,1)S(1)}, bf16[16,128,128]{2,1,0:T(8,128)(2,1)}, u32[]{:S(2)}, u32[]{:S(2)}) collective-permute-start(bf16[16,128,128]{2,1,0:T(8,128)(2,1)S(1)} %collective-permute-done.4.refs_3_), channel_id=1, source_target_pairs={{0,1},{1,0},{2,3},{3,2},{4,5},{5,4},{6,7},{7,6},{8,9},{9,8},{10,11... | collective-permute-start | bytes 1572872 | tf_op jit(solution)/shard_map/ppermute | solution.py:103
  71.5 15.3 %collective-permute-start.15 = (bf16[16,128,128]{2,1,0:T(8,128)(2,1)S(1)}, bf16[16,128,128]{2,1,0:T(8,128)(2,1)}, u32[]{:S(2)}, u32[]{:S(2)}) collective-permute-start(bf16[16,128,128]{2,1,0:T(8,128)(2,1)S(1)} %collective-permute-done.6.refs_5_), channel_id=1, source_target_pairs={{0,1},{1,0},{2,3},{3,2},{4,5},{5,4},{6,7},{7,6},{8,9},{9,8},{10,11... | collective-permute-start | bytes 1572872 | tf_op jit(solution)/shard_map/ppermute | solution.py:103
  74.8 14.5 %collective-permute-start.10 = (bf16[8,128,128]{2,1,0:T(8,128)(2,1)S(1)}, bf16[8,128,128]{2,1,0:T(8,128)(2,1)S(1)}, u32[]{:S(2)}, u32[]{:S(2)}) collective-permute-start(bf16[8,128,128]{2,1,0:T(8,128)(2,1)S(1)} %slice.28), channel_id=1, source_target_pairs={{0,128},{1,3},{2,130},{3,1},{4,132},{5,7},{6,134},{7,5},{8,136},{9... | collective-permute-start | bytes 786440 | tf_op jit(solution)/shard_map/ppermute | solution.py:89
  76.9 14.3 %collective-permute-start.11 = (bf16[8,128,128]{2,1,0:T(8,128)(2,1)S(1)}, bf16[8,128,128]{2,1,0:T(8,128)(2,1)S(1)}, u32[]{:S(2)}, u32[]{:S(2)}) collective-permute-start(bf16[8,128,128]{2,1,0:T(8,128)(2,1)S(1)} %slice.29), channel_id=1, source_target_pairs={{0,896},{1,15},{2,898},{3,5},{4,900},{5,3},{6,902},{7,9},{8,904},{... | collective-permute-start | bytes 786440 | tf_op jit(solution)/shard_map/ppermute | solution.py:89
  79.3 14.7 %collective-permute-start.16 = (bf16[16,128,128]{2,1,0:T(8,128)(2,1)}, bf16[16,128,128]{2,1,0:T(8,128)(2,1)S(1)}, u32[]{:S(2)}, u32[]{:S(2)}) collective-permute-start(bf16[16,128,128]{2,1,0:T(8,128)(2,1)} %collective-permute-done.7.refs_6_), channel_id=1, source_target_pairs={{0,1},{1,0},{2,3},{3,2},{4,5},{5,4},{6,7},{7,6},{8,9},{9,8},{10,11... | collective-permute-start | bytes 1572872 | tf_op jit(solution)/shard_map/ppermute | solution.py:103
  84.8 10.0 %collective-permute-start.18 = (bf16[16,128,128]{2,1,0:T(8,128)(2,1)S(1)}, bf16[16,128,128]{2,1,0:T(8,128)(2,1)S(1)}, u32[]{:S(2)}, u32[]{:S(2)}) collective-permute-start(bf16[16,128,128]{2,1,0:T(8,128)(2,1)S(1)} %collective-permute-done.9.refs_8_), channel_id=1, source_target_pairs={{0,1},{1,0},{2,3},{3,2},{4,5},{5,4},{6,7},{7,6},{8,9},{9,8},{10,11... | collective-permute-start | bytes 1572872 | tf_op jit(solution)/shard_map/ppermute | solution.py:103
  86.7 8.1 %collective-permute-start.17 = (bf16[16,128,128]{2,1,0:T(8,128)(2,1)S(1)}, bf16[16,128,128]{2,1,0:T(8,128)(2,1)S(1)}, u32[]{:S(2)}, u32[]{:S(2)}) collective-permute-start(bf16[16,128,128]{2,1,0:T(8,128)(2,1)S(1)} %collective-permute-done.8.refs_7_), channel_id=1, source_target_pairs={{0,1},{1,0},{2,3},{3,2},{4,5},{5,4},{6,7},{7,6},{8,9},{9,8},{10,11... | collective-permute-start | bytes 1572872 | tf_op jit(solution)/shard_map/ppermute | solution.py:103
  89.3 4.6 %collective-permute-start.19 = (bf16[8,128,128]{2,1,0:T(8,128)(2,1)S(1)}, bf16[8,128,128]{2,1,0:T(8,128)(2,1)S(1)}, u32[]{:S(2)}, u32[]{:S(2)}) collective-permute-start(bf16[8,128,128]{2,1,0:T(8,128)(2,1)S(1)} %collective-permute-done.10.refs_9_), channel_id=1, source_target_pairs={{0,1},{1,0},{2,3},{3,2},{4,5},{5,4},{6,7},{7,6},{8,9},{9,8},{10,11... | collective-permute-start | bytes 786440 | tf_op jit(solution)/shard_map/ppermute | solution.py:103
  91.3 3.6 %collective-permute-start.20 = (bf16[8,128,128]{2,1,0:T(8,128)(2,1)S(1)}, bf16[8,128,128]{2,1,0:T(8,128)(2,1)S(1)}, u32[]{:S(2)}, u32[]{:S(2)}) collective-permute-start(bf16[8,128,128]{2,1,0:T(8,128)(2,1)S(1)} %collective-permute-done.11.refs_10_), channel_id=1, source_target_pairs={{0,1},{1,0},{2,3},{3,2},{4,5},{5,4},{6,7},{7,6},{8,9},{9,8},{10,11... | collective-permute-start | bytes 786440 | tf_op jit(solution)/shard_map/ppermute | solution.py:103

commit v10 on v5

--- a/solution.py
+++ b/solution.py
@@ -13,7 +13,7 @@
 GROUP = 16
 TILE = 8
 ZERO = 3 * NY * TILE
-SEATS = (1, 5, 2, 6, 7, 3, 0, 4)
+SEATS = (0, 1, 3, 5, 7, 6, 4, 2)
 
 
 def rot(size, shift):
@@ -33,11 +33,11 @@
     row, col = x * NZL + zl, (zh * NY + y) * NCORE + c
     source = (k - row) % NK
     from_zh, from_y, from_c = source // (NY * NCORE), source // NCORE % NY, source % NCORE
-    left = (jnp.where(from_c == c, 0, NY) + from_y) * TILE + pairs[:, 0]
+    left = (jnp.where(from_c == c, 0, NY) + seat_of((from_y - y) * (1 - y % 2 * 2))) * TILE + pairs[:, 0]
     left = left + jnp.where(from_zh == zh, 0, NA)
     holder = (k - col) % NK
-    right = (2 * NY + seat_of(holder // NZL - x)) * TILE
-    right = right + (zl - holder % NZL) % NZL * NB + pairs[:, 1]
+    right = (2 * NY + seat_of((holder // NZL - x) * (1 - x % 2 * 2))) * TILE
+    right = right + (zl ^ holder % NZL) * NB + pairs[:, 1]
     code = left * 256 + right
     target = jnp.arange(NC, dtype=jnp.int32)[:, None]
     mine = live[None] & (pairs[:, 2][None] == target)
@@ -83,30 +83,33 @@
     out[1] = total[1].astype(jnp.bfloat16)
 
 
+def swaps(size, kind):
+    return [(s, (((s + kind) ^ 1) - kind) % size) for s in range(size)]
+
+
+def ring(own, axis):
+    pieces = [own]
+    one = two = own
+    for _ in range(1, NY // 2):
+        one, two = lax.ppermute(two, axis, swaps(NY, 0)), lax.ppermute(one, axis, swaps(NY, 1))
+        pieces += [one, two]
+    half = TILE // 2
+    pieces.append(lax.ppermute(two[:half], axis, swaps(NY, 0)))
+    pieces.append(lax.ppermute(one[half:], axis, swaps(NY, 1)))
+    return pieces
+
+
 def per_device(left_blocks, right_blocks, pair_lists, pair_count):
     x, zl, zh, y, c = (lax.axis_index(name) for name in ("x", "zl", "zh", "y", "c"))
 
     own = [right_blocks]
-    own += [lax.ppermute(right_blocks, "zl", rot(NZL, shift)) for shift in range(1, NZL)]
-    own = jnp.concatenate(own)
-    lefts = jnp.concatenate([left_blocks, lax.ppermute(left_blocks, "zh", rot(NZH, 1))])
-    lefts, own = lax.optimization_barrier((lefts, own))
-    spread = jnp.broadcast_to(lefts[None], (NY,) + lefts.shape).reshape(NY * TILE, BS, BS)
-    lefts = lax.all_to_all(spread, "y", 0, 0, tiled=True)
-
-    half = TILE // 2
-    behind = lax.ppermute(own, "x", rot(NX, 2))
-    ahead = lax.ppermute(own, "x", rot(NX, -2))
-    behind, ahead = lax.optimization_barrier((behind, ahead))
-    near = jnp.concatenate([behind, own, ahead])
-    rights = [near]
-    rights.append(lax.ppermute(near[: 2 * TILE], "x", rot(NX, 1)))
-    rights.append(lax.ppermute(near[TILE:], "x", rot(NX, -1)))
-    rights.append(lax.ppermute(behind[:half], "x", rot(NX, 2)))
-    rights.append(lax.ppermute(ahead[half:], "x", rot(NX, -2)))
-
-    lefts, *rights = lax.optimization_barrier((lefts, *rights))
-    pieces = [lefts, lax.ppermute(lefts, "c", rot(NCORE, 1))] + rights
+    for flip in range(1, NZL):
+        own.append(lax.ppermute(right_blocks, "zl", [(s, s ^ flip) for s in range(NZL)]))
+    rights = ring(jnp.concatenate(own), "x")
+    other = lax.ppermute(left_blocks, "zh", rot(NZH, 1))
+    lefts = ring(jnp.concatenate([left_blocks, other]), "y")
+    lefts = [jnp.concatenate(part) for part in (lefts[:3], lefts[3:5], lefts[5:])]
+    pieces = lefts + [lax.ppermute(part, "c", rot(NCORE, 1)) for part in lefts] + rights
     plan, at = [], 0
     for piece in pieces:
         plan.append((piece.shape[0], at))

time: 108 us -> 109 us (level)
  starting transfers between devices: 64.6 us -> 88 us
  waiting for transfers between devices: 24.5 us -> 10.6 us
  local copies, waits for them, and re-layouts: 8.05 us -> 3.43 us
  other arithmetic: 4.96 us -> 0.71 us
    ppermute x11 -> x23, starting transfers between devices: 57 us -> 88 us  [the longest x6 24.1 us: ring(): lax.ppermute(one, axis, swaps(NY, 1))]
    all_to_all x1 -> x0, starting transfers between devices: 7.58 us -> none  [per_device(): lefts = lax.all_to_all(spread, 'y', 0, 0, tiled=True)]
    ppermute x11 -> x23, waiting for transfers between devices: 17.6 us -> 10.6 us  [the longest x2 8.24 us: ring(): pieces.append(lax.ppermute(one[half:], axis, swaps(NY, 1)))]
    all_to_all x1 -> x0, waiting for transfers between devices: 6.95 us -> none  [per_device(): lefts = lax.all_to_all(spread, 'y', 0, 0, tiled=True)]
    concatenate x4 -> x0, other arithmetic: 2.93 us -> none  [the longest x2 1.13 us: per_device(): near = jnp.concatenate([behind, own, ahead])]
    broadcast_in_dim x1 -> x0, local copies, waits for them, and re-layouts: 1.84 us -> none  [per_device(): jnp.broadcast_to(lefts[None], (NY,) + lefts.shape)]
    unnamed x13 -> x18, local copies, waits for them, and re-layouts: 4 us -> 3.07 us
  transfers between devices with their start and end apart: 12 -> 23, of which waited for: 6 -> 5; matrix products, arithmetic and copies ran while one was open for 6% -> 2% of each run, Pallas kernels for 0% -> 0%
where the time goes in v10:
time: 109 us; the launch traced here: 107 us
  starting transfers between devices  88 us (81%)
  waiting for transfers between devices  10.6 us (10%)
  Pallas kernels  4.03 us (4%)
  local copies, waits for them, and re-layouts  3.43 us (3%)
    ppermute x6, starting transfers between devices, ring(): lax.ppermute(one, axis, swaps(NY, 1))  24.1 us
    ppermute x3, starting transfers between devices, per_device(): lax.ppermute(right_blocks, 'zl', [(s, s ^ flip) for s in range(NZL)])  15.3 us
    ppermute x6, starting transfers between devices, ring(): lax.ppermute(two, axis, swaps(NY, 0))  14.4 us
    ppermute x1, starting transfers between devices, per_device(): other = lax.ppermute(left_blocks, 'zh', rot(NZH, 1))  11.6 us
    ppermute x3, starting transfers between devices, per_device(): lax.ppermute(part, 'c', rot(NCORE, 1))  11.1 us
    ppermute x2, waiting for transfers between devices, ring(): pieces.append(lax.ppermute(one[half:], axis, swaps(NY, 1)))  8.24 us
    ppermute x2, starting transfers between devices, ring(): pieces.append(lax.ppermute(two[:half], axis, swaps(NY, 0)))  7 us
    ppermute x2, starting transfers between devices, ring(): pieces.append(lax.ppermute(one[half:], axis, swaps(NY, 1)))  4.57 us
  transfers between devices with their start and end apart: 23, of which 5 were waited for; matrix products, arithmetic and copies ran while one was open for 2% of the time, Pallas kernels for 0%

profile of v10, /device:TPU:1, one launch (start us, length us, event | category | flops | bytes accessed | tf_op | source)
XLA Modules:
  0.0 107.3 jit_solution(7554313423322385581)
XLA Ops:
  0.0 8.4 %collective-permute-start.13 = (bf16[2,128,128]{2,1,0:T(8,128)(2,1)}, bf16[2,128,128]{2,1,0:T(8,128)(2,1)S(1)}, u32[]{:S(2)}, u32[]{:S(2)}) collective-permute-start(bf16[2,128,128]{2,1,0:T(8,128)(2,1)} %param.7), channel_id=1, source_target_pairs={{0,64},{32,96},{64,0},{96,32},{1,65},{33,97},{65,1},{97,33},{2,66}... | collective-permute-start | bytes 196616 | tf_op jit(solution)/shard_map/ppermute | solution.py:107
  8.5 4.9 %collective-permute-start.12 = (bf16[2,128,128]{2,1,0:T(8,128)(2,1)}, bf16[2,128,128]{2,1,0:T(8,128)(2,1)S(1)}, u32[]{:S(2)}, u32[]{:S(2)}) collective-permute-start(bf16[2,128,128]{2,1,0:T(8,128)(2,1)} %param.7), channel_id=1, source_target_pairs={{0,32},{32,0},{64,96},{96,64},{1,33},{33,1},{65,97},{97,65},{2,34}... | collective-permute-start | bytes 196616 | tf_op jit(solution)/shard_map/ppermute | solution.py:107
  13.4 1.9 %collective-permute-start.14 = (bf16[2,128,128]{2,1,0:T(8,128)(2,1)}, bf16[2,128,128]{2,1,0:T(8,128)(2,1)S(1)}, u32[]{:S(2)}, u32[]{:S(2)}) collective-permute-start(bf16[2,128,128]{2,1,0:T(8,128)(2,1)} %param.7), channel_id=1, source_target_pairs={{0,96},{32,64},{64,32},{96,0},{1,97},{33,65},{65,33},{97,1},{2,98}... | collective-permute-start | bytes 196616 | tf_op jit(solution)/shard_map/ppermute | solution.py:107
  15.3 11.6 %collective-permute-start = (bf16[4,128,128]{2,1,0:T(8,128)(2,1)}, bf16[4,128,128]{2,1,0:T(8,128)(2,1)S(1)}, u32[]{:S(2)}, u32[]{:S(2)}) collective-permute-start(bf16[4,128,128]{2,1,0:T(8,128)(2,1)} %param.6), channel_id=1, source_target_pairs={{0,16},{16,0},{1,17},{17,1},{2,18},{18,2},{3,19},{19,3},{4,20},{20... | collective-permute-start | bytes 393224 | tf_op jit(solution)/shard_map/ppermute | solution.py:109
  26.9 0.9 constant_dynamic-update-slice_fusion.15
  27.8 0.7 copy-done.1
  28.5 0.7 copy-done.2
  29.1 0.1 broadcast_in_dim.46
  29.2 0.1 reshape.326
  29.4 0.3 collective-permute-done
  29.7 0.1 constant_dynamic-update-slice_fusion
  29.8 6.3 %collective-permute-start.2 = (bf16[8,128,128]{2,1,0:T(8,128)(2,1)S(1)}, bf16[8,128,128]{2,1,0:T(8,128)(2,1)S(1)}, u32[]{:S(2)}, u32[]{:S(2)}) collective-permute-start(bf16[8,128,128]{2,1,0:T(8,128)(2,1)S(1)} %get-tuple-element.9), channel_id=1, source_target_pairs={{0,14},{2,4},{4,2},{6,8},{8,6},{10,12},{12,10},{14,0},{1,15},{3,5}... | collective-permute-start | bytes 786440 | tf_op jit(solution)/shard_map/ppermute | solution.py:94
  36.1 1.9 %collective-permute-start.1 = (bf16[8,128,128]{2,1,0:T(8,128)(2,1)S(1)}, bf16[8,128,128]{2,1,0:T(8,128)(2,1)S(1)}, u32[]{:S(2)}, u32[]{:S(2)}) collective-permute-start(bf16[8,128,128]{2,1,0:T(8,128)(2,1)S(1)} %get-tuple-element.9), channel_id=1, source_target_pairs={{0,2},{2,0},{4,6},{6,4},{8,10},{10,8},{12,14},{14,12},{1,3},{3,1},... | collective-permute-start | bytes 786440 | tf_op jit(solution)/shard_map/ppermute | solution.py:94
  38.0 0.0 collective-permute-done.12
  38.1 0.0 collective-permute-done.13
  38.1 0.0 collective-permute-done.14
  38.1 4.5 %collective-permute-start.16 = (bf16[8,128,128]{2,1,0:T(8,128)(2,1)S(1)}, bf16[8,128,128]{2,1,0:T(8,128)(2,1)S(1)}, u32[]{:S(2)}, u32[]{:S(2)}) collective-permute-start(bf16[8,128,128]{2,1,0:T(8,128)(2,1)S(1)} %constant_dynamic-update-slice_fusion.12.refs_8_), channel_id=1, source_target_pairs={{0,896},{128,256},{256,128},{384,512},{512,384},{640,768},{768,640... | collective-permute-start | bytes 786440 | tf_op jit(solution)/shard_map/ppermute | solution.py:94
  42.6 1.9 %collective-permute-start.15 = (bf16[8,128,128]{2,1,0:T(8,128)(2,1)S(1)}, bf16[8,128,128]{2,1,0:T(8,128)(2,1)S(1)}, u32[]{:S(2)}, u32[]{:S(2)}) collective-permute-start(bf16[8,128,128]{2,1,0:T(8,128)(2,1)S(1)} %constant_dynamic-update-slice_fusion.12.refs_8_), channel_id=1, source_target_pairs={{0,128},{128,0},{256,384},{384,256},{512,640},{640,512},{768,896},... | collective-permute-start | bytes 786440 | tf_op jit(solution)/shard_map/ppermute | solution.py:94
  44.5 0.0 collective-permute-done.2
  44.6 3.4 %collective-permute-start.3 = (bf16[8,128,128]{2,1,0:T(8,128)(2,1)S(1)}, bf16[8,128,128]{2,1,0:T(8,128)(2,1)S(1)}, u32[]{:S(2)}, u32[]{:S(2)}) collective-permute-start(bf16[8,128,128]{2,1,0:T(8,128)(2,1)S(1)} %collective-permute-done.2), channel_id=1, source_target_pairs={{0,2},{2,0},{4,6},{6,4},{8,10},{10,8},{12,14},{14,12},{1,3},{3,1},... | collective-permute-start | bytes 786440 | tf_op jit(solution)/shard_map/ppermute | solution.py:94
  47.9 2.4 %collective-permute-start.4 = (bf16[8,128,128]{2,1,0:T(8,128)(2,1)S(1)}, bf16[8,128,128]{2,1,0:T(8,128)(2,1)S(1)}, u32[]{:S(2)}, u32[]{:S(2)}) collective-permute-start(bf16[8,128,128]{2,1,0:T(8,128)(2,1)S(1)} %collective-permute-done.1), channel_id=1, source_target_pairs={{0,14},{2,4},{4,2},{6,8},{8,6},{10,12},{12,10},{14,0},{1,15},{3,5}... | collective-permute-start | bytes 786440 | tf_op jit(solution)/shard_map/ppermute | solution.py:94
  50.3 0.0 copy-start.3
  50.3 0.6 copy-done.3
  51.0 0.1 select_reduce_fusion.2
  51.1 0.0 collective-permute-done.16.refs_10_
  51.1 3.4 %collective-permute-start.17 = (bf16[8,128,128]{2,1,0:T(8,128)(2,1)S(1)}, bf16[8,128,128]{2,1,0:T(8,128)(2,1)S(1)}, u32[]{:S(2)}, u32[]{:S(2)}) collective-permute-start(bf16[8,128,128]{2,1,0:T(8,128)(2,1)S(1)} %collective-permute-done.16.refs_10_), channel_id=1, source_target_pairs={{0,128},{128,0},{256,384},{384,256},{512,640},{640,512},{768,896},... | collective-permute-start | bytes 786440 | tf_op jit(solution)/shard_map/ppermute | solution.py:94
  54.5 0.0 collective-permute-done.15.refs_9_
  54.5 2.8 %collective-permute-start.18 = (bf16[8,128,128]{2,1,0:T(8,128)(2,1)S(1)}, bf16[8,128,128]{2,1,0:T(8,128)(2,1)S(1)}, u32[]{:S(2)}, u32[]{:S(2)}) collective-permute-start(bf16[8,128,128]{2,1,0:T(8,128)(2,1)S(1)} %collective-permute-done.15.refs_9_), channel_id=1, source_target_pairs={{0,896},{128,256},{256,128},{384,512},{512,384},{640,768},{768,640... | collective-permute-start | bytes 786440 | tf_op jit(solution)/shard_map/ppermute | solution.py:94
  57.2 0.0 collective-permute-done.3
  57.3 4.1 %collective-permute-start.6 = (bf16[8,128,128]{2,1,0:T(8,128)(2,1)S(1)}, bf16[8,128,128]{2,1,0:T(8,128)(2,1)S(1)}, u32[]{:S(2)}, u32[]{:S(2)}) collective-permute-start(bf16[8,128,128]{2,1,0:T(8,128)(2,1)S(1)} %collective-permute-done.3), channel_id=1, source_target_pairs={{0,14},{2,4},{4,2},{6,8},{8,6},{10,12},{12,10},{14,0},{1,15},{3,5}... | collective-permute-start | bytes 786440 | tf_op jit(solution)/shard_map/ppermute | solution.py:94
  61.4 1.9 %collective-permute-start.5 = (bf16[8,128,128]{2,1,0:T(8,128)(2,1)S(1)}, bf16[8,128,128]{2,1,0:T(8,128)(2,1)S(1)}, u32[]{:S(2)}, u32[]{:S(2)}) collective-permute-start(bf16[8,128,128]{2,1,0:T(8,128)(2,1)S(1)} %collective-permute-done.4), channel_id=1, source_target_pairs={{0,2},{2,0},{4,6},{6,4},{8,10},{10,8},{12,14},{14,12},{1,3},{3,1},... | collective-permute-start | bytes 786440 | tf_op jit(solution)/shard_map/ppermute | solution.py:94
  63.3 0.1 convert_reduce_fusion.1
  63.5 5.8 %collective-permute-start.9 = (bf16[24,128,128]{2,1,0:T(8,128)(2,1)S(1)}, bf16[24,128,128]{2,1,0:T(8,128)(2,1)S(1)}, u32[]{:S(2)}, u32[]{:S(2)}) collective-permute-start(bf16[24,128,128]{2,1,0:T(8,128)(2,1)S(1)} %constant_dynamic-update-slice_fusion.2.refs_2_), channel_id=1, source_target_pairs={{0,1},{1,0},{2,3},{3,2},{4,5},{5,4},{6,7},{7,6},{8,9},{9,8},{10,11... | collective-permute-start | bytes 2359304 | tf_op jit(solution)/shard_map/ppermute | solution.py:112
  69.4 4.0 %collective-permute-start.20 = (bf16[8,128,128]{2,1,0:T(8,128)(2,1)S(1)}, bf16[8,128,128]{2,1,0:T(8,128)(2,1)S(1)}, u32[]{:S(2)}, u32[]{:S(2)}) collective-permute-start(bf16[8,128,128]{2,1,0:T(8,128)(2,1)S(1)} %collective-permute-done.17.refs_11_), channel_id=1, source_target_pairs={{0,896},{128,256},{256,128},{384,512},{512,384},{640,768},{768,640... | collective-permute-start | bytes 786440 | tf_op jit(solution)/shard_map/ppermute | solution.py:94
  73.4 1.9 %collective-permute-start.19 = (bf16[8,128,128]{2,1,0:T(8,128)(2,1)S(1)}, bf16[8,128,128]{2,1,0:T(8,128)(2,1)S(1)}, u32[]{:S(2)}, u32[]{:S(2)}) collective-permute-start(bf16[8,128,128]{2,1,0:T(8,128)(2,1)S(1)} %collective-permute-done.18.refs_12_), channel_id=1, source_target_pairs={{0,128},{128,0},{256,384},{384,256},{512,640},{640,512},{768,896},... | collective-permute-start | bytes 786440 | tf_op jit(solution)/shard_map/ppermute | solution.py:94
  75.4 3.6 %collective-permute-start.7 = (bf16[4,128,128]{2,1,0:T(8,128)(2,1)S(1)}, bf16[4,128,128]{2,1,0:T(8,128)(2,1)S(1)}, u32[]{:S(2)}, u32[]{:S(2)}) collective-permute-start(bf16[4,128,128]{2,1,0:T(8,128)(2,1)S(1)} %slice.31), channel_id=1, source_target_pairs={{0,2},{2,0},{4,6},{6,4},{8,10},{10,8},{12,14},{14,12},{1,3},{3,1},... | collective-permute-start | bytes 393224 | tf_op jit(solution)/shard_map/ppermute | solution.py:97
  79.1 2.1 %collective-permute-start.8 = (bf16[4,128,128]{2,1,0:T(8,128)(2,1)S(1)}, bf16[4,128,128]{2,1,0:T(8,128)(2,1)S(1)}, u32[]{:S(2)}, u32[]{:S(2)}) collective-permute-start(bf16[4,128,128]{2,1,0:T(8,128)(2,1)S(1)} %slice.32), channel_id=1, source_target_pairs={{0,14},{2,4},{4,2},{6,8},{8,6},{10,12},{12,10},{14,0},{1,15},{3,5}... | collective-permute-start | bytes 393224 | tf_op jit(solution)/shard_map/ppermute | solution.py:98
  81.2 1.4 %collective-permute-done.7 = bf16[4,128,128]{2,1,0:T(8,128)(2,1)S(1)} collective-permute-done((bf16[4,128,128]{2,1,0:T(8,128)(2,1)S(1)}, bf16[4,128,128]{2,1,0:T(8,128)(2,1)S(1)}, u32[]{:S(2)}, u32[]{:S(2)}) %collective-permute-start.7) | collective-permute-done | bytes 131104 | tf_op jit(solution)/shard_map/ppermute | solution.py:97
  82.7 4.0 %collective-permute-done.8 = bf16[4,128,128]{2,1,0:T(8,128)(2,1)S(1)} collective-permute-done((bf16[4,128,128]{2,1,0:T(8,128)(2,1)S(1)}, bf16[4,128,128]{2,1,0:T(8,128)(2,1)S(1)}, u32[]{:S(2)}, u32[]{:S(2)}) %collective-permute-start.8) | collective-permute-done | bytes 131104 | tf_op jit(solution)/shard_map/ppermute | solution.py:98
  86.7 3.3 %collective-permute-start.11 = (bf16[24,128,128]{2,1,0:T(8,128)(2,1)S(1)}, bf16[24,128,128]{2,1,0:T(8,128)(2,1)S(1)}, u32[]{:S(2)}, u32[]{:S(2)}) collective-permute-start(bf16[24,128,128]{2,1,0:T(8,128)(2,1)S(1)} %constant_dynamic-update-slice_fusion.8.refs_4_), channel_id=1, source_target_pairs={{0,1},{1,0},{2,3},{3,2},{4,5},{5,4},{6,7},{7,6},{8,9},{9,8},{10,11... | collective-permute-start | bytes 2359304 | tf_op jit(solution)/shard_map/ppermute | solution.py:112
  90.1 1.9 %collective-permute-start.10 = (bf16[16,128,128]{2,1,0:T(8,128)(2,1)S(1)}, bf16[16,128,128]{2,1,0:T(8,128)(2,1)S(1)}, u32[]{:S(2)}, u32[]{:S(2)}) collective-permute-start(bf16[16,128,128]{2,1,0:T(8,128)(2,1)S(1)} %constant_dynamic-update-slice_fusion.6.refs_3_), channel_id=1, source_target_pairs={{0,1},{1,0},{2,3},{3,2},{4,5},{5,4},{6,7},{7,6},{8,9},{9,8},{10,11... | collective-permute-start | bytes 1572872 | tf_op jit(solution)/shard_map/ppermute | solution.py:112
  92.1 0.1 convert_reduce_fusion
  92.2 0.3 select_reduce_fusion
  92.5 3.4 %collective-permute-start.21 = (bf16[4,128,128]{2,1,0:T(8,128)(2,1)S(1)}, bf16[4,128,128]{2,1,0:T(8,128)(2,1)S(1)}, u32[]{:S(2)}, u32[]{:S(2)}) collective-permute-start(bf16[4,128,128]{2,1,0:T(8,128)(2,1)S(1)} %slice.33), channel_id=1, source_target_pairs={{0,128},{128,0},{256,384},{384,256},{512,640},{640,512},{768,896},... | collective-permute-start | bytes 393224 | tf_op jit(solution)/shard_map/ppermute | solution.py:97
  95.9 2.5 %collective-permute-start.22 = (bf16[4,128,128]{2,1,0:T(8,128)(2,1)S(1)}, bf16[4,128,128]{2,1,0:T(8,128)(2,1)S(1)}, u32[]{:S(2)}, u32[]{:S(2)}) collective-permute-start(bf16[4,128,128]{2,1,0:T(8,128)(2,1)S(1)} %slice.34), channel_id=1, source_target_pairs={{0,896},{128,256},{256,128},{384,512},{512,384},{640,768},{768,640... | collective-permute-start | bytes 393224 | tf_op jit(solution)/shard_map/ppermute | solution.py:98
  98.4 0.6 collective-permute-done.21.refs_15_
  98.9 4.3 %collective-permute-done.22.refs_16_ = bf16[4,128,128]{2,1,0:T(8,128)(2,1)S(1)} collective-permute-done((bf16[4,128,128]{2,1,0:T(8,128)(2,1)S(1)}, bf16[4,128,128]{2,1,0:T(8,128)(2,1)S(1)}, u32[]{:S(2)}, u32[]{:S(2)}) %collective-permute-start.22) | collective-permute-done | bytes 131104 | tf_op jit(solution)/shard_map/ppermute | solution.py:98
  103.3 4.0 %block_products.1 = bf16[2,128,128]{2,1,0:T(8,128)(2,1)} custom-call(s32[2,256]{1,0:T(2,128)S(1)} %broadcast_add_fusion.refs_0_, s32[2]{0:T(128)S(1)} %get-tuple-element.7.refs_1_, bf16[24,128,128]{2,1,0:T(8,128)(2,1)S(1)} %constant_dynamic-update-slice_fusion.2.refs_2_, bf16[16,128,128]{2,1,0:T(8,128)(2,1)S(1)} %constant_dynamic-update-slice_fusion.6.refs_3_, ...), custom_call_target="tpu_custom_call" | custom-call | flops 536870912 | bytes 6291456 | tf_op jit(solution)/shard_map/block_products/pallas_call | solution.py:123
  (38 shorter events, 0.5 us)
Async XLA Ops:
  0.0 38.1 %collective-permute-start.13 = (bf16[2,128,128]{2,1,0:T(8,128)(2,1)}, bf16[2,128,128]{2,1,0:T(8,128)(2,1)S(1)}, u32[]{:S(2)}, u32[]{:S(2)}) collective-permute-start(bf16[2,128,128]{2,1,0:T(8,128)(2,1)} %param.7), channel_id=1, source_target_pairs={{0,64},{32,96},{64,0},{96,32},{1,65},{33,97},{65,1},{97,33},{2,66}... | collective-permute-start | bytes 196616 | tf_op jit(solution)/shard_map/ppermute | solution.py:107
  8.5 29.6 %collective-permute-start.12 = (bf16[2,128,128]{2,1,0:T(8,128)(2,1)}, bf16[2,128,128]{2,1,0:T(8,128)(2,1)S(1)}, u32[]{:S(2)}, u32[]{:S(2)}) collective-permute-start(bf16[2,128,128]{2,1,0:T(8,128)(2,1)} %param.7), channel_id=1, source_target_pairs={{0,32},{32,0},{64,96},{96,64},{1,33},{33,1},{65,97},{97,65},{2,34}... | collective-permute-start | bytes 196616 | tf_op jit(solution)/shard_map/ppermute | solution.py:107
  13.4 24.7 %collective-permute-start.14 = (bf16[2,128,128]{2,1,0:T(8,128)(2,1)}, bf16[2,128,128]{2,1,0:T(8,128)(2,1)S(1)}, u32[]{:S(2)}, u32[]{:S(2)}) collective-permute-start(bf16[2,128,128]{2,1,0:T(8,128)(2,1)} %param.7), channel_id=1, source_target_pairs={{0,96},{32,64},{64,32},{96,0},{1,97},{33,65},{65,33},{97,1},{2,98}... | collective-permute-start | bytes 196616 | tf_op jit(solution)/shard_map/ppermute | solution.py:107
  15.3 14.4 %collective-permute-start = (bf16[4,128,128]{2,1,0:T(8,128)(2,1)}, bf16[4,128,128]{2,1,0:T(8,128)(2,1)S(1)}, u32[]{:S(2)}, u32[]{:S(2)}) collective-permute-start(bf16[4,128,128]{2,1,0:T(8,128)(2,1)} %param.6), channel_id=1, source_target_pairs={{0,16},{16,0},{1,17},{17,1},{2,18},{18,2},{3,19},{19,3},{4,20},{20... | collective-permute-start | bytes 393224 | tf_op jit(solution)/shard_map/ppermute | solution.py:109
  26.9 2.5 %copy-start = (bf16[4,128,128]{2,1,0:T(8,128)(2,1)S(1)}, bf16[4,128,128]{2,1,0:T(8,128)(2,1)}, u32[]{:S(2)}) copy-start(bf16[4,128,128]{2,1,0:T(8,128)(2,1)} %param.6) | copy-start | bytes 393220
  27.8 0.7 copy-start.1
  28.5 0.7 copy-start.2
  29.8 14.8 %collective-permute-start.2 = (bf16[8,128,128]{2,1,0:T(8,128)(2,1)S(1)}, bf16[8,128,128]{2,1,0:T(8,128)(2,1)S(1)}, u32[]{:S(2)}, u32[]{:S(2)}) collective-permute-start(bf16[8,128,128]{2,1,0:T(8,128)(2,1)S(1)} %get-tuple-element.9), channel_id=1, source_target_pairs={{0,14},{2,4},{4,2},{6,8},{8,6},{10,12},{12,10},{14,0},{1,15},{3,5}... | collective-permute-start | bytes 786440 | tf_op jit(solution)/shard_map/ppermute | solution.py:94
  36.1 11.8 %collective-permute-start.1 = (bf16[8,128,128]{2,1,0:T(8,128)(2,1)S(1)}, bf16[8,128,128]{2,1,0:T(8,128)(2,1)S(1)}, u32[]{:S(2)}, u32[]{:S(2)}) collective-permute-start(bf16[8,128,128]{2,1,0:T(8,128)(2,1)S(1)} %get-tuple-element.9), channel_id=1, source_target_pairs={{0,2},{2,0},{4,6},{6,4},{8,10},{10,8},{12,14},{14,12},{1,3},{3,1},... | collective-permute-start | bytes 786440 | tf_op jit(solution)/shard_map/ppermute | solution.py:94
  38.1 13.0 %collective-permute-start.16 = (bf16[8,128,128]{2,1,0:T(8,128)(2,1)S(1)}, bf16[8,128,128]{2,1,0:T(8,128)(2,1)S(1)}, u32[]{:S(2)}, u32[]{:S(2)}) collective-permute-start(bf16[8,128,128]{2,1,0:T(8,128)(2,1)S(1)} %constant_dynamic-update-slice_fusion.12.refs_8_), channel_id=1, source_target_pairs={{0,896},{128,256},{256,128},{384,512},{512,384},{640,768},{768,640... | collective-permute-start | bytes 786440 | tf_op jit(solution)/shard_map/ppermute | solution.py:94
  42.6 11.8 %collective-permute-start.15 = (bf16[8,128,128]{2,1,0:T(8,128)(2,1)S(1)}, bf16[8,128,128]{2,1,0:T(8,128)(2,1)S(1)}, u32[]{:S(2)}, u32[]{:S(2)}) collective-permute-start(bf16[8,128,128]{2,1,0:T(8,128)(2,1)S(1)} %constant_dynamic-update-slice_fusion.12.refs_8_), channel_id=1, source_target_pairs={{0,128},{128,0},{256,384},{384,256},{512,640},{640,512},{768,896},... | collective-permute-start | bytes 786440 | tf_op jit(solution)/shard_map/ppermute | solution.py:94
  44.6 12.7 %collective-permute-start.3 = (bf16[8,128,128]{2,1,0:T(8,128)(2,1)S(1)}, bf16[8,128,128]{2,1,0:T(8,128)(2,1)S(1)}, u32[]{:S(2)}, u32[]{:S(2)}) collective-permute-start(bf16[8,128,128]{2,1,0:T(8,128)(2,1)S(1)} %collective-permute-done.2), channel_id=1, source_target_pairs={{0,2},{2,0},{4,6},{6,4},{8,10},{10,8},{12,14},{14,12},{1,3},{3,1},... | collective-permute-start | bytes 786440 | tf_op jit(solution)/shard_map/ppermute | solution.py:94
  47.9 13.5 %collective-permute-start.4 = (bf16[8,128,128]{2,1,0:T(8,128)(2,1)S(1)}, bf16[8,128,128]{2,1,0:T(8,128)(2,1)S(1)}, u32[]{:S(2)}, u32[]{:S(2)}) collective-permute-start(bf16[8,128,128]{2,1,0:T(8,128)(2,1)S(1)} %collective-permute-done.1), channel_id=1, source_target_pairs={{0,14},{2,4},{4,2},{6,8},{8,6},{10,12},{12,10},{14,0},{1,15},{3,5}... | collective-permute-start | bytes 786440 | tf_op jit(solution)/shard_map/ppermute | solution.py:94
  50.3 0.7 copy-start.3
  51.1 18.3 %collective-permute-start.17 = (bf16[8,128,128]{2,1,0:T(8,128)(2,1)S(1)}, bf16[8,128,128]{2,1,0:T(8,128)(2,1)S(1)}, u32[]{:S(2)}, u32[]{:S(2)}) collective-permute-start(bf16[8,128,128]{2,1,0:T(8,128)(2,1)S(1)} %collective-permute-done.16.refs_10_), channel_id=1, source_target_pairs={{0,128},{128,0},{256,384},{384,256},{512,640},{640,512},{768,896},... | collective-permute-start | bytes 786440 | tf_op jit(solution)/shard_map/ppermute | solution.py:94
  54.5 18.9 %collective-permute-start.18 = (bf16[8,128,128]{2,1,0:T(8,128)(2,1)S(1)}, bf16[8,128,128]{2,1,0:T(8,128)(2,1)S(1)}, u32[]{:S(2)}, u32[]{:S(2)}) collective-permute-start(bf16[8,128,128]{2,1,0:T(8,128)(2,1)S(1)} %collective-permute-done.15.refs_9_), channel_id=1, source_target_pairs={{0,896},{128,256},{256,128},{384,512},{512,384},{640,768},{768,640... | collective-permute-start | bytes 786440 | tf_op jit(solution)/shard_map/ppermute | solution.py:94
  57.3 18.1 %collective-permute-start.6 = (bf16[8,128,128]{2,1,0:T(8,128)(2,1)S(1)}, bf16[8,128,128]{2,1,0:T(8,128)(2,1)S(1)}, u32[]{:S(2)}, u32[]{:S(2)}) collective-permute-start(bf16[8,128,128]{2,1,0:T(8,128)(2,1)S(1)} %collective-permute-done.3), channel_id=1, source_target_pairs={{0,14},{2,4},{4,2},{6,8},{8,6},{10,12},{12,10},{14,0},{1,15},{3,5}... | collective-permute-start | bytes 786440 | tf_op jit(solution)/shard_map/ppermute | solution.py:94
  61.4 17.6 %collective-permute-start.5 = (bf16[8,128,128]{2,1,0:T(8,128)(2,1)S(1)}, bf16[8,128,128]{2,1,0:T(8,128)(2,1)S(1)}, u32[]{:S(2)}, u32[]{:S(2)}) collective-permute-start(bf16[8,128,128]{2,1,0:T(8,128)(2,1)S(1)} %collective-permute-done.4), channel_id=1, source_target_pairs={{0,2},{2,0},{4,6},{6,4},{8,10},{10,8},{12,14},{14,12},{1,3},{3,1},... | collective-permute-start | bytes 786440 | tf_op jit(solution)/shard_map/ppermute | solution.py:94
  63.5 39.7 %collective-permute-start.9 = (bf16[24,128,128]{2,1,0:T(8,128)(2,1)S(1)}, bf16[24,128,128]{2,1,0:T(8,128)(2,1)S(1)}, u32[]{:S(2)}, u32[]{:S(2)}) collective-permute-start(bf16[24,128,128]{2,1,0:T(8,128)(2,1)S(1)} %constant_dynamic-update-slice_fusion.2.refs_2_), channel_id=1, source_target_pairs={{0,1},{1,0},{2,3},{3,2},{4,5},{5,4},{6,7},{7,6},{8,9},{9,8},{10,11... | collective-permute-start | bytes 2359304 | tf_op jit(solution)/shard_map/ppermute | solution.py:112
  69.4 23.1 %collective-permute-start.20 = (bf16[8,128,128]{2,1,0:T(8,128)(2,1)S(1)}, bf16[8,128,128]{2,1,0:T(8,128)(2,1)S(1)}, u32[]{:S(2)}, u32[]{:S(2)}) collective-permute-start(bf16[8,128,128]{2,1,0:T(8,128)(2,1)S(1)} %collective-permute-done.17.refs_11_), channel_id=1, source_target_pairs={{0,896},{128,256},{256,128},{384,512},{512,384},{640,768},{768,640... | collective-permute-start | bytes 786440 | tf_op jit(solution)/shard_map/ppermute | solution.py:94
  73.4 22.4 %collective-permute-start.19 = (bf16[8,128,128]{2,1,0:T(8,128)(2,1)S(1)}, bf16[8,128,128]{2,1,0:T(8,128)(2,1)S(1)}, u32[]{:S(2)}, u32[]{:S(2)}) collective-permute-start(bf16[8,128,128]{2,1,0:T(8,128)(2,1)S(1)} %collective-permute-done.18.refs_12_), channel_id=1, source_target_pairs={{0,128},{128,0},{256,384},{384,256},{512,640},{640,512},{768,896},... | collective-permute-start | bytes 786440 | tf_op jit(solution)/shard_map/ppermute | solution.py:94
  75.4 7.3 %collective-permute-start.7 = (bf16[4,128,128]{2,1,0:T(8,128)(2,1)S(1)}, bf16[4,128,128]{2,1,0:T(8,128)(2,1)S(1)}, u32[]{:S(2)}, u32[]{:S(2)}) collective-permute-start(bf16[4,128,128]{2,1,0:T(8,128)(2,1)S(1)} %slice.31), channel_id=1, source_target_pairs={{0,2},{2,0},{4,6},{6,4},{8,10},{10,8},{12,14},{14,12},{1,3},{3,1},... | collective-permute-start | bytes 393224 | tf_op jit(solution)/shard_map/ppermute | solution.py:97
  79.1 7.6 %collective-permute-start.8 = (bf16[4,128,128]{2,1,0:T(8,128)(2,1)S(1)}, bf16[4,128,128]{2,1,0:T(8,128)(2,1)S(1)}, u32[]{:S(2)}, u32[]{:S(2)}) collective-permute-start(bf16[4,128,128]{2,1,0:T(8,128)(2,1)S(1)} %slice.32), channel_id=1, source_target_pairs={{0,14},{2,4},{4,2},{6,8},{8,6},{10,12},{12,10},{14,0},{1,15},{3,5}... | collective-permute-start | bytes 393224 | tf_op jit(solution)/shard_map/ppermute | solution.py:98
  86.7 16.6 %collective-permute-start.11 = (bf16[24,128,128]{2,1,0:T(8,128)(2,1)S(1)}, bf16[24,128,128]{2,1,0:T(8,128)(2,1)S(1)}, u32[]{:S(2)}, u32[]{:S(2)}) collective-permute-start(bf16[24,128,128]{2,1,0:T(8,128)(2,1)S(1)} %constant_dynamic-update-slice_fusion.8.refs_4_), channel_id=1, source_target_pairs={{0,1},{1,0},{2,3},{3,2},{4,5},{5,4},{6,7},{7,6},{8,9},{9,8},{10,11... | collective-permute-start | bytes 2359304 | tf_op jit(solution)/shard_map/ppermute | solution.py:112
  90.1 13.2 %collective-permute-start.10 = (bf16[16,128,128]{2,1,0:T(8,128)(2,1)S(1)}, bf16[16,128,128]{2,1,0:T(8,128)(2,1)S(1)}, u32[]{:S(2)}, u32[]{:S(2)}) collective-permute-start(bf16[16,128,128]{2,1,0:T(8,128)(2,1)S(1)} %constant_dynamic-update-slice_fusion.6.refs_3_), channel_id=1, source_target_pairs={{0,1},{1,0},{2,3},{3,2},{4,5},{5,4},{6,7},{7,6},{8,9},{9,8},{10,11... | collective-permute-start | bytes 1572872 | tf_op jit(solution)/shard_map/ppermute | solution.py:112
  92.5 6.5 %collective-permute-start.21 = (bf16[4,128,128]{2,1,0:T(8,128)(2,1)S(1)}, bf16[4,128,128]{2,1,0:T(8,128)(2,1)S(1)}, u32[]{:S(2)}, u32[]{:S(2)}) collective-permute-start(bf16[4,128,128]{2,1,0:T(8,128)(2,1)S(1)} %slice.33), channel_id=1, source_target_pairs={{0,128},{128,0},{256,384},{384,256},{512,640},{640,512},{768,896},... | collective-permute-start | bytes 393224 | tf_op jit(solution)/shard_map/ppermute | solution.py:97
  95.9 7.3 %collective-permute-start.22 = (bf16[4,128,128]{2,1,0:T(8,128)(2,1)S(1)}, bf16[4,128,128]{2,1,0:T(8,128)(2,1)S(1)}, u32[]{:S(2)}, u32[]{:S(2)}) collective-permute-start(bf16[4,128,128]{2,1,0:T(8,128)(2,1)S(1)} %slice.34), channel_id=1, source_target_pairs={{0,896},{128,256},{256,128},{384,512},{512,384},{640,768},{768,640... | collective-permute-start | bytes 393224 | tf_op jit(solution)/shard_map/ppermute | solution.py:98

commit v11 on v7

--- a/solution.py
+++ b/solution.py
@@ -13,15 +13,17 @@
 GROUP = 16
 TILE = 16
 ZERO = 2 * NY * TILE
-SEATS = (1, 4, 7, 2, 5, 0, 3, 6)
+SEATS = (1, 3, 0, 4, 7, 6, 2, 5)
 
 
 def rot(size, shift):
     return [(s, (s + shift) % size) for s in range(size)]
 
 
-def seat_of(distance):
-    hit = distance[:, None] % NY == jnp.arange(NY, dtype=jnp.int32)
+def seat_of(distance, place):
+    odd, even = 1 - place % 2 * 2, 1 - place // 2 % 2 * 2
+    distance = distance * jnp.where(distance % 2 == 1, odd, even) % NY
+    hit = distance[:, None] == jnp.arange(NY, dtype=jnp.int32)
     return jnp.sum(jnp.where(hit, jnp.array(SEATS, jnp.int32), 0), axis=1)
 
 
@@ -35,10 +37,10 @@
     from_zh, from_y, from_c = source // (NY * NCORE), source // NCORE % NY, source % NCORE
     near = from_zh == zh
     part = jnp.where(from_c == 0, jnp.where(near, 0, 1), jnp.where(near, 3, 2))
-    left = (jnp.where(c == 1, 0, NY) + seat_of(from_y - y)) * TILE + part * NA + pairs[:, 0]
+    left = (jnp.where(c == 1, 0, NY) + seat_of(from_y - y, y)) * TILE + part * NA + pairs[:, 0]
     holder = (k - col) % NK
-    part = (zl - holder % NZL) % NZL
-    right = (jnp.where(c == 0, 0, NY) + seat_of(holder // NZL - x)) * TILE
+    part = zl ^ holder % NZL
+    right = (jnp.where(c == 0, 0, NY) + seat_of(holder // NZL - x, x)) * TILE
     right = right + (part * NCORE + c) * NB + pairs[:, 1]
     code = left * 512 + right
     target = jnp.arange(NC, dtype=jnp.int32)[:, None]
@@ -85,22 +87,23 @@
     out[1] = total[1].astype(jnp.bfloat16)
 
 
-def along_plane(value, shift):
-    pairs = []
+def along_plane(value, reach, kind):
+    pairs, shift = [], kind * reach
     for x in range(NX):
         for y in range(NY):
             place = (x * NY + y) * NCORE
-            pairs.append((place, ((x + shift) % NX * NY + y) * NCORE))
-            pairs.append((place + 1, (x * NY + (y + shift) % NY) * NCORE + 1))
+            pairs.append((place, ((((x + shift) ^ reach) - shift) % NX * NY + y) * NCORE))
+            to_y = (((y + shift) ^ reach) - shift) % NY
+            pairs.append((place + 1, (x * NY + to_y) * NCORE + 1))
     return lax.ppermute(value, ("x", "y", "c"), pairs)
 
 
-def along_z(value, shift, swap):
+def along_z(value, flip, swap):
     pairs = []
     for zl in range(NZL):
         for zh in range(NZH):
             place = (zl * NZH + zh) * NCORE
-            pairs.append((place, ((zl + shift) % NZL * NZH + zh) * NCORE))
+            pairs.append((place, ((zl ^ flip) * NZH + zh) * NCORE))
             pairs.append((place + 1, (zl * NZH + (zh + swap) % NZH) * NCORE + 1))
     return lax.ppermute(value, ("zl", "zh", "c"), pairs)
 
@@ -119,8 +122,14 @@
         [first, along_z(first, 1, 1), along_z(second, 2, 1), along_z(second, 3, 0)]
     )
     half = TILE // 2
-    near = jnp.concatenate([along_plane(own, 3), own, along_plane(own, -3)])
-    pieces = [near, along_plane(near[: 2 * TILE + half], -1), along_plane(near[half:], 1)]
+    one, two = along_plane(own, 2, 0), along_plane(own, 2, 1)
+    place = jnp.where(c == 0, x, y)
+    alike = place % 2 == place // 2 % 2
+    pieces = [jnp.concatenate([one, own, two])]
+    pieces.append(along_plane(jnp.concatenate([own, jnp.where(alike, two, one)]), 1, 0))
+    pieces.append(along_plane(jnp.concatenate([own, jnp.where(alike, one, two)]), 1, 1))
+    far = [along_plane(two[:half], 2, 0), along_plane(one[half:], 2, 1)]
+    pieces.append(jnp.concatenate(far))
     pieces += [to_partner(piece) for piece in pieces]
     plan, at = [], 0
     for piece in pieces:

time: 102 us -> 95.6 us (0.937)
  waiting for transfers between devices: 41.5 us -> 17.4 us
  starting transfers between devices: 48.5 us -> 63.4 us
  other arithmetic: 2.71 us -> 5.97 us
  Pallas kernels: 5.78 us -> 4.59 us
    ppermute x4 -> x6, waiting for transfers between devices: 30.5 us -> 10.4 us  [along_plane(): return lax.ppermute(value, ('x', 'y', 'c'), pairs)]
    ppermute x4 -> x6, starting transfers between devices: 16.9 us -> 24.7 us  [along_plane(): return lax.ppermute(value, ('x', 'y', 'c'), pairs)]
    ppermute x4 -> x5, starting transfers between devices: 21.8 us -> 28.8 us  [to_partner(): return lax.ppermute(value, 'c', rot(NCORE, 1))]
    concatenate x0 -> x2, other arithmetic: none -> 3.2 us  [the longest x1 2.12 us: per_device(): jnp.concatenate([own, jnp.where(alike, one, two)])]
    ppermute x3, waiting for transfers between devices: 7.39 us -> 4.96 us  [along_z(): return lax.ppermute(value, ('zl', 'zh', 'c'), pairs)]
    ppermute x4 -> x5, waiting for transfers between devices: 3.56 us -> 2.03 us  [to_partner(): return lax.ppermute(value, 'c', rot(NCORE, 1))]
    pallas_call x1, Pallas kernels: 5.78 us -> 4.59 us  [per_device(): pl.pallas_call(kernel, out_shape=jax.ShapeDtypeStruct((NC, BS, BS), jnp.b...]
    slice x1 -> x2, local copies, waits for them, and re-layouts: 2.05 us -> 0.99 us  [per_device(): far = [along_plane(two[:half], 2, 0), along_plane(one[half:], 2, 1)]]
  transfers between devices with their start and end apart: 11 -> 14, of which waited for: 8 -> 6; matrix products, arithmetic and copies ran while one was open for 1% -> 6% of each run, Pallas kernels for 0% -> 0%
where the time goes in v11:
time: 95.6 us; the launch traced here: 94.3 us
  starting transfers between devices  63.4 us (66%)
  waiting for transfers between devices  17.4 us (18%)
  other arithmetic  5.97 us (6%)
  Pallas kernels  4.59 us (5%)
  local copies, waits for them, and re-layouts  2.38 us (2%)
    ppermute x5, starting transfers between devices, to_partner(): return lax.ppermute(value, 'c', rot(NCORE, 1))  28.8 us
    ppermute x6, starting transfers between devices, along_plane(): return lax.ppermute(value, ('x', 'y', 'c'), pairs)  24.7 us
    ppermute x6, waiting for transfers between devices, along_plane(): return lax.ppermute(value, ('x', 'y', 'c'), pairs)  10.4 us
    ppermute x3, starting transfers between devices, along_z(): return lax.ppermute(value, ('zl', 'zh', 'c'), pairs)  9.86 us
    ppermute x3, waiting for transfers between devices, along_z(): return lax.ppermute(value, ('zl', 'zh', 'c'), pairs)  4.96 us
    pallas_call x1, Pallas kernels, per_device(): pl.pallas_call(kernel, out_shape=jax.ShapeDtypeStruct((NC, BS, BS), jnp.b...  4.59 us
    concatenate x1, other arithmetic, per_device(): jnp.concatenate([own, jnp.where(alike, one, two)])  2.12 us
    ppermute x5, waiting for transfers between devices, to_partner(): return lax.ppermute(value, 'c', rot(NCORE, 1))  2.03 us
  transfers between devices with their start and end apart: 14, of which 6 were waited for; matrix products, arithmetic and copies ran while one was open for 6% of the time, Pallas kernels for 0%

profile of v11, /device:TPU:1, one launch (start us, length us, event | category | flops | bytes accessed | tf_op | source)
XLA Modules:
  0.0 94.3 jit_solution(738754100366940671)
XLA Ops:
  0.0 0.9 fusion.1
  0.9 16.1 %collective-permute-start = (bf16[4,128,128]{2,1,0:T(8,128)(2,1)S(1)}, bf16[4,128,128]{2,1,0:T(8,128)(2,1)S(1)}, u32[]{:S(2)}, u32[]{:S(2)}) collective-permute-start(bf16[4,128,128]{2,1,0:T(8,128)(2,1)S(1)} %fusion.1), channel_id=1, source_target_pairs={{0,1},{1,0},{2,3},{3,2},{4,5},{5,4},{6,7},{7,6},{8,9},{9,8},{10,11... | collective-permute-start | bytes 393224 | tf_op jit(solution)/shard_map/ppermute | solution.py:112
  17.0 1.0 %collective-permute-done = bf16[4,128,128]{2,1,0:T(8,128)(2,1)S(1)} collective-permute-done((bf16[4,128,128]{2,1,0:T(8,128)(2,1)S(1)}, bf16[4,128,128]{2,1,0:T(8,128)(2,1)S(1)}, u32[]{:S(2)}, u32[]{:S(2)}) %collective-permute-start) | collective-permute-done | bytes 131104 | tf_op jit(solution)/shard_map/ppermute | solution.py:112
  18.0 1.0 %constant_dynamic-update-slice_fusion.9 = (bf16[32,128,128]{2,1,0:T(8,128)(2,1)S(1)}, bf16[4,128,128]{2,1,0:T(8,128)(2,1)S(1)}, bf16[4,128,128]{2,1,0:T(8,128)(2,1)S(1)}) fusion(bf16[4,128,128]{2,1,0:T(8,128)(2,1)S(1)} %collective-permute-done, bf16[2,128,128]{2,1,0:T(8,128)(2,1)S(1)} %slice.27, bf16[2,128,128]{2,1,0:T(8,128)(2,1)} %param.7, pred[]{:T(512)S(6)} %eq.140, ...), kind=kLoop, calls=%fused_computation.22 | loop fusion | flops 393215 | bytes 786433
  19.0 1.9 %collective-permute-start.1 = (bf16[4,128,128]{2,1,0:T(8,128)(2,1)S(1)}, bf16[4,128,128]{2,1,0:T(8,128)(2,1)S(1)}, u32[]{:S(2)}, u32[]{:S(2)}) collective-permute-start(bf16[4,128,128]{2,1,0:T(8,128)(2,1)S(1)} %get-tuple-element.8), channel_id=1, source_target_pairs={{0,32},{1,17},{16,48},{17,1},{32,0},{33,49},{48,16},{49,33},{64,96... | collective-permute-start | bytes 393224 | tf_op jit(solution)/shard_map/ppermute | solution.py:108
  21.0 7.3 %collective-permute-start.2 = (bf16[4,128,128]{2,1,0:T(8,128)(2,1)S(1)}, bf16[4,128,128]{2,1,0:T(8,128)(2,1)S(1)}, u32[]{:S(2)}, u32[]{:S(2)}) collective-permute-start(bf16[4,128,128]{2,1,0:T(8,128)(2,1)S(1)} %get-tuple-element.15), channel_id=1, source_target_pairs={{0,64},{1,17},{16,80},{17,1},{32,96},{33,49},{48,112},{49,33},{64,... | collective-permute-start | bytes 393224 | tf_op jit(solution)/shard_map/ppermute | solution.py:108
  28.2 0.7 collective-permute-start.3
  28.9 1.3 %collective-permute-done.1 = bf16[4,128,128]{2,1,0:T(8,128)(2,1)S(1)} collective-permute-done((bf16[4,128,128]{2,1,0:T(8,128)(2,1)S(1)}, bf16[4,128,128]{2,1,0:T(8,128)(2,1)S(1)}, u32[]{:S(2)}, u32[]{:S(2)}) %collective-permute-start.1) | collective-permute-done | bytes 131104 | tf_op jit(solution)/shard_map/ppermute | solution.py:108
  30.2 3.7 %collective-permute-done.2 = bf16[4,128,128]{2,1,0:T(8,128)(2,1)S(1)} collective-permute-done((bf16[4,128,128]{2,1,0:T(8,128)(2,1)S(1)}, bf16[4,128,128]{2,1,0:T(8,128)(2,1)S(1)}, u32[]{:S(2)}, u32[]{:S(2)}) %collective-permute-start.2) | collective-permute-done | bytes 131104 | tf_op jit(solution)/shard_map/ppermute | solution.py:108
  33.9 0.0 collective-permute-done.3
  33.9 0.1 pad_maximum_fusion
  33.9 2.8 %collective-permute-start.4 = (bf16[16,128,128]{2,1,0:T(8,128)(2,1)S(1)}, bf16[16,128,128]{2,1,0:T(8,128)(2,1)S(1)}, u32[]{:S(2)}, u32[]{:S(2)}) collective-permute-start(bf16[16,128,128]{2,1,0:T(8,128)(2,1)S(1)} %pad_maximum_fusion), channel_id=1, source_target_pairs={{0,256},{1,5},{2,258},{3,7},{4,260},{5,1},{6,262},{7,3},{8,264},{9... | collective-permute-start | bytes 1572872 | tf_op jit(solution)/shard_map/ppermute | solution.py:98
  36.7 5.7 %collective-permute-start.5 = (bf16[16,128,128]{2,1,0:T(8,128)(2,1)S(1)}, bf16[16,128,128]{2,1,0:T(8,128)(2,1)S(1)}, u32[]{:S(2)}, u32[]{:S(2)}) collective-permute-start(bf16[16,128,128]{2,1,0:T(8,128)(2,1)S(1)} %pad_maximum_fusion), channel_id=1, source_target_pairs={{0,768},{1,13},{2,770},{3,15},{4,772},{5,9},{6,774},{7,11},{8,776}... | collective-permute-start | bytes 1572872 | tf_op jit(solution)/shard_map/ppermute | solution.py:98
  42.5 0.0 copy-start.1
  42.5 1.0 %copy.18 = bf16[32,128,128]{2,1,0:T(8,128)(2,1)} copy(bf16[32,128,128]{2,1,0:T(8,128)(2,1)S(1)} %constant_dynamic-update-slice_fusion.6) | data formatting | bytes 2097152
  43.5 6.8 %collective-permute-done.4 = bf16[16,128,128]{2,1,0:T(8,128)(2,1)S(1)} collective-permute-done((bf16[16,128,128]{2,1,0:T(8,128)(2,1)S(1)}, bf16[16,128,128]{2,1,0:T(8,128)(2,1)S(1)}, u32[]{:S(2)}, u32[]{:S(2)}) %collective-permute-start.4) | collective-permute-done | bytes 524320 | tf_op jit(solution)/shard_map/ppermute | solution.py:98
  50.4 0.0 copy-done.1
  50.4 3.6 %collective-permute-done.5 = bf16[16,128,128]{2,1,0:T(8,128)(2,1)S(1)} collective-permute-done((bf16[16,128,128]{2,1,0:T(8,128)(2,1)S(1)}, bf16[16,128,128]{2,1,0:T(8,128)(2,1)S(1)}, u32[]{:S(2)}, u32[]{:S(2)}) %collective-permute-start.5) | collective-permute-done | bytes 524320 | tf_op jit(solution)/shard_map/ppermute | solution.py:98
  53.9 1.1 %select_dynamic-update-slice_fusion.1 = (bf16[32,128,128]{2,1,0:T(8,128)(2,1)}, bf16[48,128,128]{2,1,0:T(8,128)(2,1)S(1)}) fusion(bf16[32,128,128]{2,1,0:T(8,128)(2,1)} %copy-done.1, bf16[16,128,128]{2,1,0:T(8,128)(2,1)S(1)} %collective-permute-done.5, bf16[16,128,128]{2,1,0:T(8,128)(2,1)S(1)} %collective-permute-done.4, pred[]{:T(512)S(6)} %eq.145), kind=kLoop, calls=%fused_computation.2 | loop fusion | flops 262143 | bytes 2097153 | tf_op jit(solution)/shard_map/concatenate | solution.py:129
  55.0 0.0 copy-done
  55.0 0.0 copy-start.3
  55.0 0.0 copy-start.4
  55.1 3.7 %collective-permute-start.6 = (bf16[32,128,128]{2,1,0:T(8,128)(2,1)}, bf16[32,128,128]{2,1,0:T(8,128)(2,1)S(1)}, u32[]{:S(2)}, u32[]{:S(2)}) collective-permute-start(bf16[32,128,128]{2,1,0:T(8,128)(2,1)} %get-tuple-element.13), channel_id=1, source_target_pairs={{0,128},{1,3},{2,130},{3,1},{4,132},{5,7},{6,134},{7,5},{8,136},{9... | collective-permute-start | bytes 3145736 | tf_op jit(solution)/shard_map/ppermute | solution.py:98
  58.9 2.1 %select_dynamic-update-slice_fusion = (bf16[32,128,128]{2,1,0:T(8,128)(2,1)}, bf16[48,128,128]{2,1,0:T(8,128)(2,1)S(1)}) fusion(bf16[32,128,128]{2,1,0:T(8,128)(2,1)} %copy.18, bf16[16,128,128]{2,1,0:T(8,128)(2,1)S(1)} %collective-permute-done.4, bf16[16,128,128]{2,1,0:T(8,128)(2,1)} %copy-done, pred[]{:T(512)S(6)} %eq.145, ...), kind=kLoop, calls=%fused_computation.1 | loop fusion | flops 262144 | bytes 2097153 | tf_op jit(solution)/shard_map/concatenate | solution.py:130
  61.0 3.5 %collective-permute-start.7 = (bf16[32,128,128]{2,1,0:T(8,128)(2,1)}, bf16[32,128,128]{2,1,0:T(8,128)(2,1)}, u32[]{:S(2)}, u32[]{:S(2)}) collective-permute-start(bf16[32,128,128]{2,1,0:T(8,128)(2,1)} %get-tuple-element.11), channel_id=1, source_target_pairs={{0,896},{1,15},{2,898},{3,5},{4,900},{5,3},{6,902},{7,9},{8,904},{... | collective-permute-start | bytes 3145736 | tf_op jit(solution)/shard_map/ppermute | solution.py:98
  64.6 0.0 copy-done.2
  64.7 0.1 broadcast_in_dim.60
  64.7 0.1 reshape.344
  64.9 1.9 %collective-permute-start.10 = (bf16[48,128,128]{2,1,0:T(8,128)(2,1)S(1)}, bf16[48,128,128]{2,1,0:T(8,128)(2,1)S(1)}, u32[]{:S(2)}, u32[]{:S(2)}) collective-permute-start(bf16[48,128,128]{2,1,0:T(8,128)(2,1)S(1)} %get-tuple-element.12.refs_2_), channel_id=1, source_target_pairs={{0,1},{1,0},{2,3},{3,2},{4,5},{5,4},{6,7},{7,6},{8,9},{9,8},{10,11... | collective-permute-start | bytes 4718600 | tf_op jit(solution)/shard_map/ppermute | solution.py:112
  66.9 0.1 select_reduce_fusion.2
  67.0 1.0 %slice.28 = bf16[8,128,128]{2,1,0:T(8,128)(2,1)S(1)} slice(bf16[16,128,128]{2,1,0:T(8,128)(2,1)} %copy-done), slice={[0:8], [0:128], [0:128]} | slice | bytes 524288 | tf_op jit(solution)/shard_map/slice | solution.py:131
  68.0 3.4 %collective-permute-start.8 = (bf16[8,128,128]{2,1,0:T(8,128)(2,1)S(1)}, bf16[8,128,128]{2,1,0:T(8,128)(2,1)S(1)}, u32[]{:S(2)}, u32[]{:S(2)}) collective-permute-start(bf16[8,128,128]{2,1,0:T(8,128)(2,1)S(1)} %slice.28), channel_id=1, source_target_pairs={{0,256},{1,5},{2,258},{3,7},{4,260},{5,1},{6,262},{7,3},{8,264},{9... | collective-permute-start | bytes 786440 | tf_op jit(solution)/shard_map/ppermute | solution.py:98
  71.4 5.7 %collective-permute-start.9 = (bf16[8,128,128]{2,1,0:T(8,128)(2,1)S(1)}, bf16[8,128,128]{2,1,0:T(8,128)(2,1)S(1)}, u32[]{:S(2)}, u32[]{:S(2)}) collective-permute-start(bf16[8,128,128]{2,1,0:T(8,128)(2,1)S(1)} %slice.29), channel_id=1, source_target_pairs={{0,768},{1,13},{2,770},{3,15},{4,772},{5,9},{6,774},{7,11},{8,776}... | collective-permute-start | bytes 786440 | tf_op jit(solution)/shard_map/ppermute | solution.py:98
  77.1 0.0 collective-permute-done.6.refs_3_
  77.1 4.3 %collective-permute-start.11 = (bf16[32,128,128]{2,1,0:T(8,128)(2,1)S(1)}, bf16[32,128,128]{2,1,0:T(8,128)(2,1)S(1)}, u32[]{:S(2)}, u32[]{:S(2)}) collective-permute-start(bf16[32,128,128]{2,1,0:T(8,128)(2,1)S(1)} %collective-permute-done.6.refs_3_), channel_id=1, source_target_pairs={{0,1},{1,0},{2,3},{3,2},{4,5},{5,4},{6,7},{7,6},{8,9},{9,8},{10,11... | collective-permute-start | bytes 3145736 | tf_op jit(solution)/shard_map/ppermute | solution.py:112
  81.3 0.0 collective-permute-done.7.refs_4_
  81.4 1.9 %collective-permute-start.12 = (bf16[32,128,128]{2,1,0:T(8,128)(2,1)}, bf16[32,128,128]{2,1,0:T(8,128)(2,1)S(1)}, u32[]{:S(2)}, u32[]{:S(2)}) collective-permute-start(bf16[32,128,128]{2,1,0:T(8,128)(2,1)} %collective-permute-done.7.refs_4_), channel_id=1, source_target_pairs={{0,1},{1,0},{2,3},{3,2},{4,5},{5,4},{6,7},{7,6},{8,9},{9,8},{10,11... | collective-permute-start | bytes 3145736 | tf_op jit(solution)/shard_map/ppermute | solution.py:112
  83.3 0.1 convert_reduce_fusion.1
  83.4 0.0 collective-permute-done.8
  83.4 0.0 collective-permute-done.9
  83.5 4.6 %collective-permute-start.13 = (bf16[16,128,128]{2,1,0:T(8,128)(2,1)S(1)}, bf16[16,128,128]{2,1,0:T(8,128)(2,1)S(1)}, u32[]{:S(2)}, u32[]{:S(2)}) collective-permute-start(bf16[16,128,128]{2,1,0:T(8,128)(2,1)S(1)} %constant_dynamic-update-slice_fusion.14.refs_5_), channel_id=1, source_target_pairs={{0,1},{1,0},{2,3},{3,2},{4,5},{5,4},{6,7},{7,6},{8,9},{9,8},{10,11... | collective-permute-start | bytes 1572872 | tf_op jit(solution)/shard_map/ppermute | solution.py:112
  88.2 0.1 convert_reduce_fusion
  88.3 0.3 select_reduce_fusion
  88.6 1.1 %collective-permute-done.13.refs_9_ = bf16[16,128,128]{2,1,0:T(8,128)(2,1)S(1)} collective-permute-done((bf16[16,128,128]{2,1,0:T(8,128)(2,1)S(1)}, bf16[16,128,128]{2,1,0:T(8,128)(2,1)S(1)}, u32[]{:S(2)}, u32[]{:S(2)}) %collective-permute-start.13) | collective-permute-done | bytes 524320 | tf_op jit(solution)/shard_map/ppermute | solution.py:112
  89.7 0.0 collective-permute-done.10.refs_6_
  89.7 0.0 collective-permute-done.11.refs_7_
  89.7 0.0 collective-permute-done.12.refs_8_
  89.7 4.6 %block_products.1 = bf16[2,128,128]{2,1,0:T(8,128)(2,1)} custom-call(s32[2,256]{1,0:T(2,128)S(1)} %broadcast_add_fusion.refs_0_, s32[2]{0:T(128)S(1)} %get-tuple-element.9.refs_1_, bf16[48,128,128]{2,1,0:T(8,128)(2,1)S(1)} %get-tuple-element.12.refs_2_, bf16[32,128,128]{2,1,0:T(8,128)(2,1)S(1)} %collective-permute-done.6.refs_3_, ...), custom_call_target="tpu_custom_call" | custom-call | flops 536870912 | bytes 6291456 | tf_op jit(solution)/shard_map/block_products/pallas_call | solution.py:144
  (23 shorter events, 0.4 us)
Async XLA Ops:
  0.9 17.1 %collective-permute-start = (bf16[4,128,128]{2,1,0:T(8,128)(2,1)S(1)}, bf16[4,128,128]{2,1,0:T(8,128)(2,1)S(1)}, u32[]{:S(2)}, u32[]{:S(2)}) collective-permute-start(bf16[4,128,128]{2,1,0:T(8,128)(2,1)S(1)} %fusion.1), channel_id=1, source_target_pairs={{0,1},{1,0},{2,3},{3,2},{4,5},{5,4},{6,7},{7,6},{8,9},{9,8},{10,11... | collective-permute-start | bytes 393224 | tf_op jit(solution)/shard_map/ppermute | solution.py:112
  19.0 11.2 %collective-permute-start.1 = (bf16[4,128,128]{2,1,0:T(8,128)(2,1)S(1)}, bf16[4,128,128]{2,1,0:T(8,128)(2,1)S(1)}, u32[]{:S(2)}, u32[]{:S(2)}) collective-permute-start(bf16[4,128,128]{2,1,0:T(8,128)(2,1)S(1)} %get-tuple-element.8), channel_id=1, source_target_pairs={{0,32},{1,17},{16,48},{17,1},{32,0},{33,49},{48,16},{49,33},{64,96... | collective-permute-start | bytes 393224 | tf_op jit(solution)/shard_map/ppermute | solution.py:108
  21.0 12.9 %collective-permute-start.2 = (bf16[4,128,128]{2,1,0:T(8,128)(2,1)S(1)}, bf16[4,128,128]{2,1,0:T(8,128)(2,1)S(1)}, u32[]{:S(2)}, u32[]{:S(2)}) collective-permute-start(bf16[4,128,128]{2,1,0:T(8,128)(2,1)S(1)} %get-tuple-element.15), channel_id=1, source_target_pairs={{0,64},{1,17},{16,80},{17,1},{32,96},{33,49},{48,112},{49,33},{64,... | collective-permute-start | bytes 393224 | tf_op jit(solution)/shard_map/ppermute | solution.py:108
  28.2 5.6 %collective-permute-start.3 = (bf16[4,128,128]{2,1,0:T(8,128)(2,1)S(1)}, bf16[4,128,128]{2,1,0:T(8,128)(2,1)S(1)}, u32[]{:S(2)}, u32[]{:S(2)}) collective-permute-start(bf16[4,128,128]{2,1,0:T(8,128)(2,1)S(1)} %get-tuple-element.15), channel_id=1, source_target_pairs={{0,96},{1,1},{16,112},{17,17},{32,64},{33,33},{48,80},{49,49},{64,... | collective-permute-start | bytes 393224 | tf_op jit(solution)/shard_map/ppermute | solution.py:108
  33.9 16.4 %collective-permute-start.4 = (bf16[16,128,128]{2,1,0:T(8,128)(2,1)S(1)}, bf16[16,128,128]{2,1,0:T(8,128)(2,1)S(1)}, u32[]{:S(2)}, u32[]{:S(2)}) collective-permute-start(bf16[16,128,128]{2,1,0:T(8,128)(2,1)S(1)} %pad_maximum_fusion), channel_id=1, source_target_pairs={{0,256},{1,5},{2,258},{3,7},{4,260},{5,1},{6,262},{7,3},{8,264},{9... | collective-permute-start | bytes 1572872 | tf_op jit(solution)/shard_map/ppermute | solution.py:98
  36.7 17.2 %collective-permute-start.5 = (bf16[16,128,128]{2,1,0:T(8,128)(2,1)S(1)}, bf16[16,128,128]{2,1,0:T(8,128)(2,1)S(1)}, u32[]{:S(2)}, u32[]{:S(2)}) collective-permute-start(bf16[16,128,128]{2,1,0:T(8,128)(2,1)S(1)} %pad_maximum_fusion), channel_id=1, source_target_pairs={{0,768},{1,13},{2,770},{3,15},{4,772},{5,9},{6,774},{7,11},{8,776}... | collective-permute-start | bytes 1572872 | tf_op jit(solution)/shard_map/ppermute | solution.py:98
  42.5 7.9 %copy-start.1 = (bf16[32,128,128]{2,1,0:T(8,128)(2,1)}, bf16[32,128,128]{2,1,0:T(8,128)(2,1)S(1)}, u32[]{:S(2)}) copy-start(bf16[32,128,128]{2,1,0:T(8,128)(2,1)S(1)} %constant_dynamic-update-slice_fusion.6) | copy-start | bytes 3145732
  53.9 1.1 %copy-start = (bf16[16,128,128]{2,1,0:T(8,128)(2,1)}, bf16[16,128,128]{2,1,0:T(8,128)(2,1)S(1)}, u32[]{:S(2)}) copy-start(bf16[16,128,128]{2,1,0:T(8,128)(2,1)S(1)} %collective-permute-done.5) | copy-start | bytes 1572868
  55.0 9.6 %copy-start.2 = (s32[1,256,3]{1,0,2:T(1,128)S(1)}, s32[1,256,3]{1,0,2:T(1,128)}, u32[]{:S(2)}) copy-start(s32[1,256,3]{1,0,2:T(1,128)} %param.8) | copy-start | bytes 9220
  55.0 9.6 %copy-start.3 = (s32[1,32]{1,0:T(1,128)S(1)}, s32[1,32]{1,0:T(1,128)}, u32[]{:S(2)}) copy-start(s32[1,32]{1,0:T(1,128)} %param.9) | copy-start | bytes 388
  55.0 11.8 %copy-start.4 = (s32[8]{0:T(128)S(1)}, s32[8]{0:T(128)}, u32[]{:S(2)}) copy-start(s32[8]{0:T(128)} %constant.214.clone) | copy-start | bytes 100
  55.1 22.0 %collective-permute-start.6 = (bf16[32,128,128]{2,1,0:T(8,128)(2,1)}, bf16[32,128,128]{2,1,0:T(8,128)(2,1)S(1)}, u32[]{:S(2)}, u32[]{:S(2)}) collective-permute-start(bf16[32,128,128]{2,1,0:T(8,128)(2,1)} %get-tuple-element.13), channel_id=1, source_target_pairs={{0,128},{1,3},{2,130},{3,1},{4,132},{5,7},{6,134},{7,5},{8,136},{9... | collective-permute-start | bytes 3145736 | tf_op jit(solution)/shard_map/ppermute | solution.py:98
  61.0 20.3 %collective-permute-start.7 = (bf16[32,128,128]{2,1,0:T(8,128)(2,1)}, bf16[32,128,128]{2,1,0:T(8,128)(2,1)}, u32[]{:S(2)}, u32[]{:S(2)}) collective-permute-start(bf16[32,128,128]{2,1,0:T(8,128)(2,1)} %get-tuple-element.11), channel_id=1, source_target_pairs={{0,896},{1,15},{2,898},{3,5},{4,900},{5,3},{6,902},{7,9},{8,904},{... | collective-permute-start | bytes 3145736 | tf_op jit(solution)/shard_map/ppermute | solution.py:98
  64.9 24.7 %collective-permute-start.10 = (bf16[48,128,128]{2,1,0:T(8,128)(2,1)S(1)}, bf16[48,128,128]{2,1,0:T(8,128)(2,1)S(1)}, u32[]{:S(2)}, u32[]{:S(2)}) collective-permute-start(bf16[48,128,128]{2,1,0:T(8,128)(2,1)S(1)} %get-tuple-element.12.refs_2_), channel_id=1, source_target_pairs={{0,1},{1,0},{2,3},{3,2},{4,5},{5,4},{6,7},{7,6},{8,9},{9,8},{10,11... | collective-permute-start | bytes 4718600 | tf_op jit(solution)/shard_map/ppermute | solution.py:112
  68.0 15.4 %collective-permute-start.8 = (bf16[8,128,128]{2,1,0:T(8,128)(2,1)S(1)}, bf16[8,128,128]{2,1,0:T(8,128)(2,1)S(1)}, u32[]{:S(2)}, u32[]{:S(2)}) collective-permute-start(bf16[8,128,128]{2,1,0:T(8,128)(2,1)S(1)} %slice.28), channel_id=1, source_target_pairs={{0,256},{1,5},{2,258},{3,7},{4,260},{5,1},{6,262},{7,3},{8,264},{9... | collective-permute-start | bytes 786440 | tf_op jit(solution)/shard_map/ppermute | solution.py:98
  71.4 12.0 %collective-permute-start.9 = (bf16[8,128,128]{2,1,0:T(8,128)(2,1)S(1)}, bf16[8,128,128]{2,1,0:T(8,128)(2,1)S(1)}, u32[]{:S(2)}, u32[]{:S(2)}) collective-permute-start(bf16[8,128,128]{2,1,0:T(8,128)(2,1)S(1)} %slice.29), channel_id=1, source_target_pairs={{0,768},{1,13},{2,770},{3,15},{4,772},{5,9},{6,774},{7,11},{8,776}... | collective-permute-start | bytes 786440 | tf_op jit(solution)/shard_map/ppermute | solution.py:98
  77.1 12.6 %collective-permute-start.11 = (bf16[32,128,128]{2,1,0:T(8,128)(2,1)S(1)}, bf16[32,128,128]{2,1,0:T(8,128)(2,1)S(1)}, u32[]{:S(2)}, u32[]{:S(2)}) collective-permute-start(bf16[32,128,128]{2,1,0:T(8,128)(2,1)S(1)} %collective-permute-done.6.refs_3_), channel_id=1, source_target_pairs={{0,1},{1,0},{2,3},{3,2},{4,5},{5,4},{6,7},{7,6},{8,9},{9,8},{10,11... | collective-permute-start | bytes 3145736 | tf_op jit(solution)/shard_map/ppermute | solution.py:112
  81.4 8.3 %collective-permute-start.12 = (bf16[32,128,128]{2,1,0:T(8,128)(2,1)}, bf16[32,128,128]{2,1,0:T(8,128)(2,1)S(1)}, u32[]{:S(2)}, u32[]{:S(2)}) collective-permute-start(bf16[32,128,128]{2,1,0:T(8,128)(2,1)} %collective-permute-done.7.refs_4_), channel_id=1, source_target_pairs={{0,1},{1,0},{2,3},{3,2},{4,5},{5,4},{6,7},{7,6},{8,9},{9,8},{10,11... | collective-permute-start | bytes 3145736 | tf_op jit(solution)/shard_map/ppermute | solution.py:112
  83.5 6.2 %collective-permute-start.13 = (bf16[16,128,128]{2,1,0:T(8,128)(2,1)S(1)}, bf16[16,128,128]{2,1,0:T(8,128)(2,1)S(1)}, u32[]{:S(2)}, u32[]{:S(2)}) collective-permute-start(bf16[16,128,128]{2,1,0:T(8,128)(2,1)S(1)} %constant_dynamic-update-slice_fusion.14.refs_5_), channel_id=1, source_target_pairs={{0,1},{1,0},{2,3},{3,2},{4,5},{5,4},{6,7},{7,6},{8,9},{9,8},{10,11... | collective-permute-start | bytes 1572872 | tf_op jit(solution)/shard_map/ppermute | solution.py:112

commit v12 on v4

--- a/solution.py
+++ b/solution.py
@@ -118,6 +118,7 @@
     own = jnp.concatenate(
         [first, along_z(first, 1, 1), along_z(second, 2, 1), along_z(second, 3, 0)]
     )
+    own = lax.optimization_barrier(own)
     half = TILE // 2
     behind, ahead = along_plane(own, 2), along_plane(own, -2)
     near = jnp.concatenate([behind, own, ahead])

time: 92.4 us -> 91 us (0.985)
  the two profiles are of different devices: /device:TPU:1 before, /device:TPU:6 now
where the time goes in v12:
time: 91 us; the launch traced here: 90.5 us
  starting transfers between devices  57.5 us (63%)
  waiting for transfers between devices  24.2 us (27%)
  Pallas kernels  5.18 us (6%)
  other arithmetic  3.01 us (3%)
    ppermute x6, starting transfers between devices, along_plane(): return lax.ppermute(value, ('x', 'y', 'c'), pairs)  22.2 us
    ppermute x5, starting transfers between devices, to_partner(): return lax.ppermute(value, 'c', rot(NCORE, 1))  20.2 us
    ppermute x3, starting transfers between devices, along_z(): return lax.ppermute(value, ('zl', 'zh', 'c'), pairs)  15 us
    ppermute x6, waiting for transfers between devices, along_plane(): return lax.ppermute(value, ('x', 'y', 'c'), pairs)  13.3 us
    ppermute x3, waiting for transfers between devices, along_z(): return lax.ppermute(value, ('zl', 'zh', 'c'), pairs)  8.16 us
    pallas_call x1, Pallas kernels, per_device(): pl.pallas_call(kernel, out_shape=jax.ShapeDtypeStruct((NC, BS, BS), jnp.b...  5.18 us
    ppermute x5, waiting for transfers between devices, to_partner(): return lax.ppermute(value, 'c', rot(NCORE, 1))  2.74 us
  transfers between devices with their start and end apart: 14, of which 7 were waited for; matrix products, arithmetic and copies ran while one was open for 1% of the time, Pallas kernels for 0%

profile of v12, /device:TPU:6, one launch (start us, length us, event | category | flops | bytes accessed | tf_op | source)
XLA Modules:
  0.0 90.5 jit_solution(8965916194373060167)
XLA Ops:
  0.0 0.0 copy-start
  0.0 0.0 copy-start.1
  0.0 1.0 %fusion.1 = bf16[4,128,128]{2,1,0:T(8,128)(2,1)S(1)} fusion(bf16[4,128,128]{2,1,0:T(8,128)(2,1)} %param.6, bf16[2,128,128]{2,1,0:T(8,128)(2,1)} %param.7, pred[]{:T(512)S(6)} %eq.114), kind=kLoop, calls=%fused_computation.11 | loop fusion | flops 131072 | bytes 327681 | tf_op jit(solution)/shard_map/jit(_where)/select_n | solution.py:115
  1.0 1.9 %collective-permute-start = (bf16[4,128,128]{2,1,0:T(8,128)(2,1)S(1)}, bf16[4,128,128]{2,1,0:T(8,128)(2,1)S(1)}, u32[]{:S(2)}, u32[]{:S(2)}) collective-permute-start(bf16[4,128,128]{2,1,0:T(8,128)(2,1)S(1)} %fusion.1), channel_id=1, source_target_pairs={{0,1},{1,0},{2,3},{3,2},{4,5},{5,4},{6,7},{7,6},{8,9},{9,8},{10,11... | collective-permute-start | bytes 393224 | tf_op jit(solution)/shard_map/ppermute | solution.py:109
  2.9 1.3 %collective-permute-done = bf16[4,128,128]{2,1,0:T(8,128)(2,1)S(1)} collective-permute-done((bf16[4,128,128]{2,1,0:T(8,128)(2,1)S(1)}, bf16[4,128,128]{2,1,0:T(8,128)(2,1)S(1)}, u32[]{:S(2)}, u32[]{:S(2)}) %collective-permute-start) | collective-permute-done | bytes 131104 | tf_op jit(solution)/shard_map/ppermute | solution.py:109
  4.2 0.9 broadcast_select_fusion.1
  5.1 5.2 %collective-permute-start.1 = (bf16[4,128,128]{2,1,0:T(8,128)(2,1)S(1)}, bf16[4,128,128]{2,1,0:T(8,128)(2,1)S(1)}, u32[]{:S(2)}, u32[]{:S(2)}) collective-permute-start(bf16[4,128,128]{2,1,0:T(8,128)(2,1)S(1)} %get-tuple-element.11), channel_id=1, source_target_pairs={{0,32},{1,17},{16,48},{17,1},{32,64},{33,49},{48,80},{49,33},{64,9... | collective-permute-start | bytes 393224 | tf_op jit(solution)/shard_map/ppermute | solution.py:105
  10.3 7.4 %collective-permute-start.3 = (bf16[4,128,128]{2,1,0:T(8,128)(2,1)S(1)}, bf16[4,128,128]{2,1,0:T(8,128)(2,1)S(1)}, u32[]{:S(2)}, u32[]{:S(2)}) collective-permute-start(bf16[4,128,128]{2,1,0:T(8,128)(2,1)S(1)} %get-tuple-element.12), channel_id=1, source_target_pairs={{0,96},{1,1},{16,112},{17,17},{32,0},{33,33},{48,16},{49,49},{64,3... | collective-permute-start | bytes 393224 | tf_op jit(solution)/shard_map/ppermute | solution.py:105
  17.7 2.5 %collective-permute-start.2 = (bf16[4,128,128]{2,1,0:T(8,128)(2,1)S(1)}, bf16[4,128,128]{2,1,0:T(8,128)(2,1)S(1)}, u32[]{:S(2)}, u32[]{:S(2)}) collective-permute-start(bf16[4,128,128]{2,1,0:T(8,128)(2,1)S(1)} %get-tuple-element.12), channel_id=1, source_target_pairs={{0,64},{1,17},{16,80},{17,1},{32,96},{33,49},{48,112},{49,33},{64,... | collective-permute-start | bytes 393224 | tf_op jit(solution)/shard_map/ppermute | solution.py:105
  20.2 0.0 collective-permute-done.1
  20.2 0.1 collective-permute-done.3
  20.2 8.1 %collective-permute-done.2 = bf16[4,128,128]{2,1,0:T(8,128)(2,1)S(1)} collective-permute-done((bf16[4,128,128]{2,1,0:T(8,128)(2,1)S(1)}, bf16[4,128,128]{2,1,0:T(8,128)(2,1)S(1)}, u32[]{:S(2)}, u32[]{:S(2)}) %collective-permute-start.2) | collective-permute-done | bytes 131104 | tf_op jit(solution)/shard_map/ppermute | solution.py:105
  28.3 0.1 pad_maximum_fusion.3
  28.4 2.4 %collective-permute-start.5 = (bf16[16,128,128]{2,1,0:T(8,128)(2,1)S(1)}, bf16[16,128,128]{2,1,0:T(8,128)(2,1)S(1)}, u32[]{:S(2)}, u32[]{:S(2)}) collective-permute-start(bf16[16,128,128]{2,1,0:T(8,128)(2,1)S(1)} %pad_maximum_fusion.3), channel_id=1, source_target_pairs={{0,768},{1,13},{2,770},{3,15},{4,772},{5,1},{6,774},{7,3},{8,776},... | collective-permute-start | bytes 1572872 | tf_op jit(solution)/shard_map/ppermute | solution.py:95
  30.8 5.5 %collective-permute-start.4 = (bf16[16,128,128]{2,1,0:T(8,128)(2,1)S(1)}, bf16[16,128,128]{2,1,0:T(8,128)(2,1)S(1)}, u32[]{:S(2)}, u32[]{:S(2)}) collective-permute-start(bf16[16,128,128]{2,1,0:T(8,128)(2,1)S(1)} %pad_maximum_fusion.3), channel_id=1, source_target_pairs={{0,256},{1,5},{2,258},{3,7},{4,260},{5,9},{6,262},{7,11},{8,264},{... | collective-permute-start | bytes 1572872 | tf_op jit(solution)/shard_map/ppermute | solution.py:95
  36.4 0.0 copy-done
  36.4 0.0 copy-done.1
  36.4 0.1 broadcast_in_dim.46
  36.5 0.1 reshape.339
  36.6 5.1 %collective-permute-done.5 = bf16[16,128,128]{2,1,0:T(8,128)(2,1)S(1)} collective-permute-done((bf16[16,128,128]{2,1,0:T(8,128)(2,1)S(1)}, bf16[16,128,128]{2,1,0:T(8,128)(2,1)S(1)}, u32[]{:S(2)}, u32[]{:S(2)}) %collective-permute-start.5) | collective-permute-done | bytes 524320 | tf_op jit(solution)/shard_map/ppermute | solution.py:95
  41.7 7.0 %collective-permute-done.4 = bf16[16,128,128]{2,1,0:T(8,128)(2,1)S(1)} collective-permute-done((bf16[16,128,128]{2,1,0:T(8,128)(2,1)S(1)}, bf16[16,128,128]{2,1,0:T(8,128)(2,1)S(1)}, u32[]{:S(2)}, u32[]{:S(2)}) %collective-permute-start.4) | collective-permute-done | bytes 524320 | tf_op jit(solution)/shard_map/ppermute | solution.py:95
  48.7 0.2 pad_maximum_fusion.2
  48.9 5.6 %collective-permute-start.7 = (bf16[32,128,128]{2,1,0:T(8,128)(2,1)S(1)}, bf16[32,128,128]{2,1,0:T(8,128)(2,1)S(1)}, u32[]{:S(2)}, u32[]{:S(2)}) collective-permute-start(bf16[32,128,128]{2,1,0:T(8,128)(2,1)S(1)} %get-tuple-element.9), channel_id=1, source_target_pairs={{0,896},{1,15},{2,898},{3,1},{4,900},{5,3},{6,902},{7,5},{8,904},{... | collective-permute-start | bytes 3145736 | tf_op jit(solution)/shard_map/ppermute | solution.py:95
  54.6 1.9 %collective-permute-start.6 = (bf16[32,128,128]{2,1,0:T(8,128)(2,1)S(1)}, bf16[32,128,128]{2,1,0:T(8,128)(2,1)S(1)}, u32[]{:S(2)}, u32[]{:S(2)}) collective-permute-start(bf16[32,128,128]{2,1,0:T(8,128)(2,1)S(1)} %get-tuple-element.10), channel_id=1, source_target_pairs={{0,128},{1,3},{2,130},{3,5},{4,132},{5,7},{6,134},{7,9},{8,136},{9... | collective-permute-start | bytes 3145736 | tf_op jit(solution)/shard_map/ppermute | solution.py:95
  56.5 0.0 copy-start.2
  56.5 0.2 pad_maximum_fusion.refs_2_
  56.7 6.7 %collective-permute-start.10 = (bf16[48,128,128]{2,1,0:T(8,128)(2,1)S(1)}, bf16[48,128,128]{2,1,0:T(8,128)(2,1)S(1)}, u32[]{:S(2)}, u32[]{:S(2)}) collective-permute-start(bf16[48,128,128]{2,1,0:T(8,128)(2,1)S(1)} %pad_maximum_fusion.refs_2_), channel_id=1, source_target_pairs={{0,1},{1,0},{2,3},{3,2},{4,5},{5,4},{6,7},{7,6},{8,9},{9,8},{10,11... | collective-permute-start | bytes 4718600 | tf_op jit(solution)/shard_map/ppermute | solution.py:109
  63.4 0.0 copy-done.2
  63.4 0.1 select_reduce_fusion.1
  63.6 4.6 %collective-permute-start.8 = (bf16[8,128,128]{2,1,0:T(8,128)(2,1)S(1)}, bf16[8,128,128]{2,1,0:T(8,128)(2,1)S(1)}, u32[]{:S(2)}, u32[]{:S(2)}) collective-permute-start(bf16[8,128,128]{2,1,0:T(8,128)(2,1)S(1)} %slice.32), channel_id=1, source_target_pairs={{0,256},{1,5},{2,258},{3,7},{4,260},{5,9},{6,262},{7,11},{8,264},{... | collective-permute-start | bytes 786440 | tf_op jit(solution)/shard_map/ppermute | solution.py:95
  68.3 2.1 %collective-permute-start.9 = (bf16[8,128,128]{2,1,0:T(8,128)(2,1)S(1)}, bf16[8,128,128]{2,1,0:T(8,128)(2,1)S(1)}, u32[]{:S(2)}, u32[]{:S(2)}) collective-permute-start(bf16[8,128,128]{2,1,0:T(8,128)(2,1)S(1)} %slice.33), channel_id=1, source_target_pairs={{0,768},{1,13},{2,770},{3,15},{4,772},{5,1},{6,774},{7,3},{8,776},... | collective-permute-start | bytes 786440 | tf_op jit(solution)/shard_map/ppermute | solution.py:95
  70.4 0.0 collective-permute-done.7.refs_4_
  70.4 3.3 %collective-permute-start.12 = (bf16[32,128,128]{2,1,0:T(8,128)(2,1)S(1)}, bf16[32,128,128]{2,1,0:T(8,128)(2,1)S(1)}, u32[]{:S(2)}, u32[]{:S(2)}) collective-permute-start(bf16[32,128,128]{2,1,0:T(8,128)(2,1)S(1)} %collective-permute-done.7.refs_4_), channel_id=1, source_target_pairs={{0,1},{1,0},{2,3},{3,2},{4,5},{5,4},{6,7},{7,6},{8,9},{9,8},{10,11... | collective-permute-start | bytes 3145736 | tf_op jit(solution)/shard_map/ppermute | solution.py:109
  73.7 0.0 collective-permute-done.6.refs_3_
  73.7 6.4 %collective-permute-start.11 = (bf16[32,128,128]{2,1,0:T(8,128)(2,1)S(1)}, bf16[32,128,128]{2,1,0:T(8,128)(2,1)S(1)}, u32[]{:S(2)}, u32[]{:S(2)}) collective-permute-start(bf16[32,128,128]{2,1,0:T(8,128)(2,1)S(1)} %collective-permute-done.6.refs_3_), channel_id=1, source_target_pairs={{0,1},{1,0},{2,3},{3,2},{4,5},{5,4},{6,7},{7,6},{8,9},{9,8},{10,11... | collective-permute-start | bytes 3145736 | tf_op jit(solution)/shard_map/ppermute | solution.py:109
  80.1 0.1 convert_reduce_fusion.1
  80.2 0.0 collective-permute-done.8
  80.3 1.1 %collective-permute-done.9 = bf16[8,128,128]{2,1,0:T(8,128)(2,1)S(1)} collective-permute-done((bf16[8,128,128]{2,1,0:T(8,128)(2,1)S(1)}, bf16[8,128,128]{2,1,0:T(8,128)(2,1)S(1)}, u32[]{:S(2)}, u32[]{:S(2)}) %collective-permute-start.9) | collective-permute-done | bytes 262176 | tf_op jit(solution)/shard_map/ppermute | solution.py:95
  81.5 1.9 %collective-permute-start.13 = (bf16[16,128,128]{2,1,0:T(8,128)(2,1)S(1)}, bf16[16,128,128]{2,1,0:T(8,128)(2,1)S(1)}, u32[]{:S(2)}, u32[]{:S(2)}) collective-permute-start(bf16[16,128,128]{2,1,0:T(8,128)(2,1)S(1)} %constant_dynamic-update-slice_fusion.refs_5_), channel_id=1, source_target_pairs={{0,1},{1,0},{2,3},{3,2},{4,5},{5,4},{6,7},{7,6},{8,9},{9,8},{10,11... | collective-permute-start | bytes 1572872 | tf_op jit(solution)/shard_map/ppermute | solution.py:109
  83.4 0.1 convert_reduce_fusion
  83.6 0.3 select_reduce_fusion
  83.8 1.4 %collective-permute-done.13.refs_9_ = bf16[16,128,128]{2,1,0:T(8,128)(2,1)S(1)} collective-permute-done((bf16[16,128,128]{2,1,0:T(8,128)(2,1)S(1)}, bf16[16,128,128]{2,1,0:T(8,128)(2,1)S(1)}, u32[]{:S(2)}, u32[]{:S(2)}) %collective-permute-start.13) | collective-permute-done | bytes 524320 | tf_op jit(solution)/shard_map/ppermute | solution.py:109
  85.3 0.0 collective-permute-done.10.refs_6_
  85.3 0.0 collective-permute-done.12.refs_8_
  85.3 0.0 collective-permute-done.11.refs_7_
  85.3 5.2 %block_products.1 = bf16[2,128,128]{2,1,0:T(8,128)(2,1)} custom-call(s32[2,256]{1,0:T(2,128)S(1)} %broadcast_add_fusion.refs_0_, s32[2]{0:T(128)S(1)} %get-tuple-element.7.refs_1_, bf16[48,128,128]{2,1,0:T(8,128)(2,1)S(1)} %pad_maximum_fusion.refs_2_, bf16[32,128,128]{2,1,0:T(8,128)(2,1)S(1)} %collective-permute-done.6.refs_3_, ...), custom_call_target="tpu_custom_call" | custom-call | flops 536870912 | bytes 6291456 | tf_op jit(solution)/shard_map/block_products/pallas_call | solution.py:139
  (13 shorter events, 0.2 us)
Async XLA Ops:
  0.0 36.4 %copy-start = (s32[1,256,3]{1,0,2:T(1,128)S(1)}, s32[1,256,3]{1,0,2:T(1,128)}, u32[]{:S(2)}) copy-start(s32[1,256,3]{1,0,2:T(1,128)} %param.8) | copy-start | bytes 9220
  0.0 36.4 %copy-start.1 = (s32[1,32]{1,0:T(1,128)S(1)}, s32[1,32]{1,0:T(1,128)}, u32[]{:S(2)}) copy-start(s32[1,32]{1,0:T(1,128)} %param.9) | copy-start | bytes 388
  1.0 3.2 %collective-permute-start = (bf16[4,128,128]{2,1,0:T(8,128)(2,1)S(1)}, bf16[4,128,128]{2,1,0:T(8,128)(2,1)S(1)}, u32[]{:S(2)}, u32[]{:S(2)}) collective-permute-start(bf16[4,128,128]{2,1,0:T(8,128)(2,1)S(1)} %fusion.1), channel_id=1, source_target_pairs={{0,1},{1,0},{2,3},{3,2},{4,5},{5,4},{6,7},{7,6},{8,9},{9,8},{10,11... | collective-permute-start | bytes 393224 | tf_op jit(solution)/shard_map/ppermute | solution.py:109
  5.1 15.0 %collective-permute-start.1 = (bf16[4,128,128]{2,1,0:T(8,128)(2,1)S(1)}, bf16[4,128,128]{2,1,0:T(8,128)(2,1)S(1)}, u32[]{:S(2)}, u32[]{:S(2)}) collective-permute-start(bf16[4,128,128]{2,1,0:T(8,128)(2,1)S(1)} %get-tuple-element.11), channel_id=1, source_target_pairs={{0,32},{1,17},{16,48},{17,1},{32,64},{33,49},{48,80},{49,33},{64,9... | collective-permute-start | bytes 393224 | tf_op jit(solution)/shard_map/ppermute | solution.py:105
  10.3 9.9 %collective-permute-start.3 = (bf16[4,128,128]{2,1,0:T(8,128)(2,1)S(1)}, bf16[4,128,128]{2,1,0:T(8,128)(2,1)S(1)}, u32[]{:S(2)}, u32[]{:S(2)}) collective-permute-start(bf16[4,128,128]{2,1,0:T(8,128)(2,1)S(1)} %get-tuple-element.12), channel_id=1, source_target_pairs={{0,96},{1,1},{16,112},{17,17},{32,0},{33,33},{48,16},{49,49},{64,3... | collective-permute-start | bytes 393224 | tf_op jit(solution)/shard_map/ppermute | solution.py:105
  17.7 10.7 %collective-permute-start.2 = (bf16[4,128,128]{2,1,0:T(8,128)(2,1)S(1)}, bf16[4,128,128]{2,1,0:T(8,128)(2,1)S(1)}, u32[]{:S(2)}, u32[]{:S(2)}) collective-permute-start(bf16[4,128,128]{2,1,0:T(8,128)(2,1)S(1)} %get-tuple-element.12), channel_id=1, source_target_pairs={{0,64},{1,17},{16,80},{17,1},{32,96},{33,49},{48,112},{49,33},{64,... | collective-permute-start | bytes 393224 | tf_op jit(solution)/shard_map/ppermute | solution.py:105
  28.4 13.3 %collective-permute-start.5 = (bf16[16,128,128]{2,1,0:T(8,128)(2,1)S(1)}, bf16[16,128,128]{2,1,0:T(8,128)(2,1)S(1)}, u32[]{:S(2)}, u32[]{:S(2)}) collective-permute-start(bf16[16,128,128]{2,1,0:T(8,128)(2,1)S(1)} %pad_maximum_fusion.3), channel_id=1, source_target_pairs={{0,768},{1,13},{2,770},{3,15},{4,772},{5,1},{6,774},{7,3},{8,776},... | collective-permute-start | bytes 1572872 | tf_op jit(solution)/shard_map/ppermute | solution.py:95
  30.8 17.9 %collective-permute-start.4 = (bf16[16,128,128]{2,1,0:T(8,128)(2,1)S(1)}, bf16[16,128,128]{2,1,0:T(8,128)(2,1)S(1)}, u32[]{:S(2)}, u32[]{:S(2)}) collective-permute-start(bf16[16,128,128]{2,1,0:T(8,128)(2,1)S(1)} %pad_maximum_fusion.3), channel_id=1, source_target_pairs={{0,256},{1,5},{2,258},{3,7},{4,260},{5,9},{6,262},{7,11},{8,264},{... | collective-permute-start | bytes 1572872 | tf_op jit(solution)/shard_map/ppermute | solution.py:95
  48.9 21.5 %collective-permute-start.7 = (bf16[32,128,128]{2,1,0:T(8,128)(2,1)S(1)}, bf16[32,128,128]{2,1,0:T(8,128)(2,1)S(1)}, u32[]{:S(2)}, u32[]{:S(2)}) collective-permute-start(bf16[32,128,128]{2,1,0:T(8,128)(2,1)S(1)} %get-tuple-element.9), channel_id=1, source_target_pairs={{0,896},{1,15},{2,898},{3,1},{4,900},{5,3},{6,902},{7,5},{8,904},{... | collective-permute-start | bytes 3145736 | tf_op jit(solution)/shard_map/ppermute | solution.py:95
  54.6 19.2 %collective-permute-start.6 = (bf16[32,128,128]{2,1,0:T(8,128)(2,1)S(1)}, bf16[32,128,128]{2,1,0:T(8,128)(2,1)S(1)}, u32[]{:S(2)}, u32[]{:S(2)}) collective-permute-start(bf16[32,128,128]{2,1,0:T(8,128)(2,1)S(1)} %get-tuple-element.10), channel_id=1, source_target_pairs={{0,128},{1,3},{2,130},{3,5},{4,132},{5,7},{6,134},{7,9},{8,136},{9... | collective-permute-start | bytes 3145736 | tf_op jit(solution)/shard_map/ppermute | solution.py:95
  56.5 6.9 %copy-start.2 = (s32[8]{0:T(128)S(1)}, s32[8]{0:T(128)}, u32[]{:S(2)}) copy-start(s32[8]{0:T(128)} %constant.162.clone) | copy-start | bytes 100
  56.7 28.5 %collective-permute-start.10 = (bf16[48,128,128]{2,1,0:T(8,128)(2,1)S(1)}, bf16[48,128,128]{2,1,0:T(8,128)(2,1)S(1)}, u32[]{:S(2)}, u32[]{:S(2)}) collective-permute-start(bf16[48,128,128]{2,1,0:T(8,128)(2,1)S(1)} %pad_maximum_fusion.refs_2_), channel_id=1, source_target_pairs={{0,1},{1,0},{2,3},{3,2},{4,5},{5,4},{6,7},{7,6},{8,9},{9,8},{10,11... | collective-permute-start | bytes 4718600 | tf_op jit(solution)/shard_map/ppermute | solution.py:109
  63.6 16.7 %collective-permute-start.8 = (bf16[8,128,128]{2,1,0:T(8,128)(2,1)S(1)}, bf16[8,128,128]{2,1,0:T(8,128)(2,1)S(1)}, u32[]{:S(2)}, u32[]{:S(2)}) collective-permute-start(bf16[8,128,128]{2,1,0:T(8,128)(2,1)S(1)} %slice.32), channel_id=1, source_target_pairs={{0,256},{1,5},{2,258},{3,7},{4,260},{5,9},{6,262},{7,11},{8,264},{... | collective-permute-start | bytes 786440 | tf_op jit(solution)/shard_map/ppermute | solution.py:95
  68.3 13.2 %collective-permute-start.9 = (bf16[8,128,128]{2,1,0:T(8,128)(2,1)S(1)}, bf16[8,128,128]{2,1,0:T(8,128)(2,1)S(1)}, u32[]{:S(2)}, u32[]{:S(2)}) collective-permute-start(bf16[8,128,128]{2,1,0:T(8,128)(2,1)S(1)} %slice.33), channel_id=1, source_target_pairs={{0,768},{1,13},{2,770},{3,15},{4,772},{5,1},{6,774},{7,3},{8,776},... | collective-permute-start | bytes 786440 | tf_op jit(solution)/shard_map/ppermute | solution.py:95
  70.4 14.9 %collective-permute-start.12 = (bf16[32,128,128]{2,1,0:T(8,128)(2,1)S(1)}, bf16[32,128,128]{2,1,0:T(8,128)(2,1)S(1)}, u32[]{:S(2)}, u32[]{:S(2)}) collective-permute-start(bf16[32,128,128]{2,1,0:T(8,128)(2,1)S(1)} %collective-permute-done.7.refs_4_), channel_id=1, source_target_pairs={{0,1},{1,0},{2,3},{3,2},{4,5},{5,4},{6,7},{7,6},{8,9},{9,8},{10,11... | collective-permute-start | bytes 3145736 | tf_op jit(solution)/shard_map/ppermute | solution.py:109
  73.7 11.6 %collective-permute-start.11 = (bf16[32,128,128]{2,1,0:T(8,128)(2,1)S(1)}, bf16[32,128,128]{2,1,0:T(8,128)(2,1)S(1)}, u32[]{:S(2)}, u32[]{:S(2)}) collective-permute-start(bf16[32,128,128]{2,1,0:T(8,128)(2,1)S(1)} %collective-permute-done.6.refs_3_), channel_id=1, source_target_pairs={{0,1},{1,0},{2,3},{3,2},{4,5},{5,4},{6,7},{7,6},{8,9},{9,8},{10,11... | collective-permute-start | bytes 3145736 | tf_op jit(solution)/shard_map/ppermute | solution.py:109
  81.5 3.8 %collective-permute-start.13 = (bf16[16,128,128]{2,1,0:T(8,128)(2,1)S(1)}, bf16[16,128,128]{2,1,0:T(8,128)(2,1)S(1)}, u32[]{:S(2)}, u32[]{:S(2)}) collective-permute-start(bf16[16,128,128]{2,1,0:T(8,128)(2,1)S(1)} %constant_dynamic-update-slice_fusion.refs_5_), channel_id=1, source_target_pairs={{0,1},{1,0},{2,3},{3,2},{4,5},{5,4},{6,7},{7,6},{8,9},{9,8},{10,11... | collective-permute-start | bytes 1572872 | tf_op jit(solution)/shard_map/ppermute | solution.py:109

commit v13 on v12

--- a/solution.py
+++ b/solution.py
@@ -34,10 +34,11 @@
     source = (k - row) % NK
     from_zh, from_y, from_c = source // (NY * NCORE), source // NCORE % NY, source % NCORE
     near = from_zh == zh
-    part = jnp.where(from_c == 0, jnp.where(near, 0, 1), jnp.where(near, 3, 2))
+    part = jnp.where(from_c == 0, jnp.where(near, 0, 1), jnp.where(near, 2, 3))
     left = (jnp.where(c == 1, 0, NY) + seat_of(from_y - y)) * TILE + part * NA + pairs[:, 0]
     holder = (k - col) % NK
     part = (zl - holder % NZL) % NZL
+    part = part ^ part // 2
     right = (jnp.where(c == 0, 0, NY) + seat_of(holder // NZL - x)) * TILE
     right = right + (part * NCORE + c) * NB + pairs[:, 1]
     code = left * 512 + right
@@ -116,7 +117,7 @@
     rights = jnp.concatenate([right_blocks, got[:NB]])
     first, second = jnp.where(c == 0, rights, got), jnp.where(c == 0, rights, left_blocks)
     own = jnp.concatenate(
-        [first, along_z(first, 1, 1), along_z(second, 2, 1), along_z(second, 3, 0)]
+        [first, along_z(first, 1, 1), along_z(second, 3, 0), along_z(second, 2, 1)]
     )
     own = lax.optimization_barrier(own)
     half = TILE // 2

time: 91 us -> 89.3 us (0.981)
  the two profiles are of different devices: /device:TPU:6 before, /device:TPU:1 now
where the time goes in v13:
time: 89.3 us; the launch traced here: 88 us
  starting transfers between devices  56.3 us (63%)
  waiting for transfers between devices  24.3 us (27%)
  Pallas kernels  3.76 us (4%)
  other arithmetic  3.07 us (3%)
    ppermute x5, starting transfers between devices, to_partner(): return lax.ppermute(value, 'c', rot(NCORE, 1))  25.1 us
    ppermute x6, starting transfers between devices, along_plane(): return lax.ppermute(value, ('x', 'y', 'c'), pairs)  21.4 us
    ppermute x6, waiting for transfers between devices, along_plane(): return lax.ppermute(value, ('x', 'y', 'c'), pairs)  17.2 us
    ppermute x3, starting transfers between devices, along_z(): return lax.ppermute(value, ('zl', 'zh', 'c'), pairs)  9.86 us
    ppermute x3, waiting for transfers between devices, along_z(): return lax.ppermute(value, ('zl', 'zh', 'c'), pairs)  5 us
    pallas_call x1, Pallas kernels, per_device(): pl.pallas_call(kernel, out_shape=jax.ShapeDtypeStruct((NC, BS, BS), jnp.b...  3.76 us
    ppermute x5, waiting for transfers between devices, to_partner(): return lax.ppermute(value, 'c', rot(NCORE, 1))  2.03 us
  transfers between devices with their start and end apart: 14, of which 8 were waited for; matrix products, arithmetic and copies ran while one was open for 1% of the time, Pallas kernels for 0%

profile of v13, /device:TPU:1, one launch (start us, length us, event | category | flops | bytes accessed | tf_op | source)
XLA Modules:
  0.0 88.0 jit_solution(9997866369358217328)
XLA Ops:
  0.0 0.0 copy-start
  0.0 0.0 copy-start.1
  0.0 0.9 %fusion.1 = bf16[4,128,128]{2,1,0:T(8,128)(2,1)S(1)} fusion(bf16[4,128,128]{2,1,0:T(8,128)(2,1)} %param.6, bf16[2,128,128]{2,1,0:T(8,128)(2,1)} %param.7, pred[]{:T(512)S(6)} %eq.114), kind=kLoop, calls=%fused_computation.11 | loop fusion | flops 131072 | bytes 327681 | tf_op jit(solution)/shard_map/jit(_where)/select_n | solution.py:116
  0.9 16.1 %collective-permute-start = (bf16[4,128,128]{2,1,0:T(8,128)(2,1)S(1)}, bf16[4,128,128]{2,1,0:T(8,128)(2,1)S(1)}, u32[]{:S(2)}, u32[]{:S(2)}) collective-permute-start(bf16[4,128,128]{2,1,0:T(8,128)(2,1)S(1)} %fusion.1), channel_id=1, source_target_pairs={{0,1},{1,0},{2,3},{3,2},{4,5},{5,4},{6,7},{7,6},{8,9},{9,8},{10,11... | collective-permute-start | bytes 393224 | tf_op jit(solution)/shard_map/ppermute | solution.py:110
  17.1 1.0 %collective-permute-done = bf16[4,128,128]{2,1,0:T(8,128)(2,1)S(1)} collective-permute-done((bf16[4,128,128]{2,1,0:T(8,128)(2,1)S(1)}, bf16[4,128,128]{2,1,0:T(8,128)(2,1)S(1)}, u32[]{:S(2)}, u32[]{:S(2)}) %collective-permute-start) | collective-permute-done | bytes 131104 | tf_op jit(solution)/shard_map/ppermute | solution.py:110
  18.0 1.0 %broadcast_select_fusion.1 = (bf16[4,128,128]{2,1,0:T(8,128)(2,1)S(1)}, bf16[4,128,128]{2,1,0:T(8,128)(2,1)S(1)}) fusion(bf16[4,128,128]{2,1,0:T(8,128)(2,1)S(1)} %collective-permute-done, pred[]{:T(512)S(6)} %eq.114, bf16[2,128,128]{2,1,0:T(8,128)(2,1)S(1)} %slice.31, bf16[2,128,128]{2,1,0:T(8,128)(2,1)} %param.7, bf16[4,128,128]{2,1,0:T(8,128)(2,1)} %param.6), kind=kLoop, calls=%fused_computation.13 | loop fusion | flops 196608 | bytes 655361 | tf_op jit(solution)/shard_map/jit(_where)/select_n | solution.py:118
  19.0 1.9 %collective-permute-start.1 = (bf16[4,128,128]{2,1,0:T(8,128)(2,1)S(1)}, bf16[4,128,128]{2,1,0:T(8,128)(2,1)S(1)}, u32[]{:S(2)}, u32[]{:S(2)}) collective-permute-start(bf16[4,128,128]{2,1,0:T(8,128)(2,1)S(1)} %get-tuple-element.11), channel_id=1, source_target_pairs={{0,32},{1,17},{16,48},{17,1},{32,64},{33,49},{48,80},{49,33},{64,9... | collective-permute-start | bytes 393224 | tf_op jit(solution)/shard_map/ppermute | solution.py:106
  20.9 7.3 %collective-permute-start.3 = (bf16[4,128,128]{2,1,0:T(8,128)(2,1)S(1)}, bf16[4,128,128]{2,1,0:T(8,128)(2,1)S(1)}, u32[]{:S(2)}, u32[]{:S(2)}) collective-permute-start(bf16[4,128,128]{2,1,0:T(8,128)(2,1)S(1)} %get-tuple-element.12), channel_id=1, source_target_pairs={{0,64},{1,17},{16,80},{17,1},{32,96},{33,49},{48,112},{49,33},{64,... | collective-permute-start | bytes 393224 | tf_op jit(solution)/shard_map/ppermute | solution.py:106
  28.2 0.7 collective-permute-start.2
  28.9 1.2 %collective-permute-done.1 = bf16[4,128,128]{2,1,0:T(8,128)(2,1)S(1)} collective-permute-done((bf16[4,128,128]{2,1,0:T(8,128)(2,1)S(1)}, bf16[4,128,128]{2,1,0:T(8,128)(2,1)S(1)}, u32[]{:S(2)}, u32[]{:S(2)}) %collective-permute-start.1) | collective-permute-done | bytes 131104 | tf_op jit(solution)/shard_map/ppermute | solution.py:106
  30.1 3.8 %collective-permute-done.3 = bf16[4,128,128]{2,1,0:T(8,128)(2,1)S(1)} collective-permute-done((bf16[4,128,128]{2,1,0:T(8,128)(2,1)S(1)}, bf16[4,128,128]{2,1,0:T(8,128)(2,1)S(1)}, u32[]{:S(2)}, u32[]{:S(2)}) %collective-permute-start.3) | collective-permute-done | bytes 131104 | tf_op jit(solution)/shard_map/ppermute | solution.py:106
  33.9 0.0 collective-permute-done.2
  33.9 0.1 pad_maximum_fusion.3
  34.0 4.7 %collective-permute-start.5 = (bf16[16,128,128]{2,1,0:T(8,128)(2,1)S(1)}, bf16[16,128,128]{2,1,0:T(8,128)(2,1)S(1)}, u32[]{:S(2)}, u32[]{:S(2)}) collective-permute-start(bf16[16,128,128]{2,1,0:T(8,128)(2,1)S(1)} %pad_maximum_fusion.3), channel_id=1, source_target_pairs={{0,768},{1,13},{2,770},{3,15},{4,772},{5,1},{6,774},{7,3},{8,776},... | collective-permute-start | bytes 1572872 | tf_op jit(solution)/shard_map/ppermute | solution.py:96
  38.6 1.9 %collective-permute-start.4 = (bf16[16,128,128]{2,1,0:T(8,128)(2,1)S(1)}, bf16[16,128,128]{2,1,0:T(8,128)(2,1)S(1)}, u32[]{:S(2)}, u32[]{:S(2)}) collective-permute-start(bf16[16,128,128]{2,1,0:T(8,128)(2,1)S(1)} %pad_maximum_fusion.3), channel_id=1, source_target_pairs={{0,256},{1,5},{2,258},{3,7},{4,260},{5,9},{6,262},{7,11},{8,264},{... | collective-permute-start | bytes 1572872 | tf_op jit(solution)/shard_map/ppermute | solution.py:96
  40.6 0.0 copy-done
  40.6 0.0 copy-done.1
  40.6 0.1 broadcast_in_dim.46
  40.7 0.1 reshape.355
  40.8 9.3 %collective-permute-done.5 = bf16[16,128,128]{2,1,0:T(8,128)(2,1)S(1)} collective-permute-done((bf16[16,128,128]{2,1,0:T(8,128)(2,1)S(1)}, bf16[16,128,128]{2,1,0:T(8,128)(2,1)S(1)}, u32[]{:S(2)}, u32[]{:S(2)}) %collective-permute-start.5) | collective-permute-done | bytes 524320 | tf_op jit(solution)/shard_map/ppermute | solution.py:96
  50.2 3.1 %collective-permute-done.4 = bf16[16,128,128]{2,1,0:T(8,128)(2,1)S(1)} collective-permute-done((bf16[16,128,128]{2,1,0:T(8,128)(2,1)S(1)}, bf16[16,128,128]{2,1,0:T(8,128)(2,1)S(1)}, u32[]{:S(2)}, u32[]{:S(2)}) %collective-permute-start.4) | collective-permute-done | bytes 524320 | tf_op jit(solution)/shard_map/ppermute | solution.py:96
  53.2 0.2 pad_maximum_fusion.2
  53.4 4.7 %collective-permute-start.7 = (bf16[32,128,128]{2,1,0:T(8,128)(2,1)S(1)}, bf16[32,128,128]{2,1,0:T(8,128)(2,1)S(1)}, u32[]{:S(2)}, u32[]{:S(2)}) collective-permute-start(bf16[32,128,128]{2,1,0:T(8,128)(2,1)S(1)} %get-tuple-element.9), channel_id=1, source_target_pairs={{0,896},{1,15},{2,898},{3,1},{4,900},{5,3},{6,902},{7,5},{8,904},{... | collective-permute-start | bytes 3145736 | tf_op jit(solution)/shard_map/ppermute | solution.py:96
  58.2 2.6 %collective-permute-start.6 = (bf16[32,128,128]{2,1,0:T(8,128)(2,1)S(1)}, bf16[32,128,128]{2,1,0:T(8,128)(2,1)S(1)}, u32[]{:S(2)}, u32[]{:S(2)}) collective-permute-start(bf16[32,128,128]{2,1,0:T(8,128)(2,1)S(1)} %get-tuple-element.10), channel_id=1, source_target_pairs={{0,128},{1,3},{2,130},{3,5},{4,132},{5,7},{6,134},{7,9},{8,136},{9... | collective-permute-start | bytes 3145736 | tf_op jit(solution)/shard_map/ppermute | solution.py:96
  60.9 0.0 copy-start.2
  60.9 0.2 pad_maximum_fusion.refs_2_
  61.1 1.9 %collective-permute-start.10 = (bf16[48,128,128]{2,1,0:T(8,128)(2,1)S(1)}, bf16[48,128,128]{2,1,0:T(8,128)(2,1)S(1)}, u32[]{:S(2)}, u32[]{:S(2)}) collective-permute-start(bf16[48,128,128]{2,1,0:T(8,128)(2,1)S(1)} %pad_maximum_fusion.refs_2_), channel_id=1, source_target_pairs={{0,1},{1,0},{2,3},{3,2},{4,5},{5,4},{6,7},{7,6},{8,9},{9,8},{10,11... | collective-permute-start | bytes 4718600 | tf_op jit(solution)/shard_map/ppermute | solution.py:110
  63.0 0.0 copy-done.2
  63.0 0.1 select_reduce_fusion.2
  63.2 3.1 %collective-permute-start.8 = (bf16[8,128,128]{2,1,0:T(8,128)(2,1)S(1)}, bf16[8,128,128]{2,1,0:T(8,128)(2,1)S(1)}, u32[]{:S(2)}, u32[]{:S(2)}) collective-permute-start(bf16[8,128,128]{2,1,0:T(8,128)(2,1)S(1)} %slice.32), channel_id=1, source_target_pairs={{0,256},{1,5},{2,258},{3,7},{4,260},{5,9},{6,262},{7,11},{8,264},{... | collective-permute-start | bytes 786440 | tf_op jit(solution)/shard_map/ppermute | solution.py:96
  66.3 4.3 %collective-permute-start.9 = (bf16[8,128,128]{2,1,0:T(8,128)(2,1)S(1)}, bf16[8,128,128]{2,1,0:T(8,128)(2,1)S(1)}, u32[]{:S(2)}, u32[]{:S(2)}) collective-permute-start(bf16[8,128,128]{2,1,0:T(8,128)(2,1)S(1)} %slice.33), channel_id=1, source_target_pairs={{0,768},{1,13},{2,770},{3,15},{4,772},{5,1},{6,774},{7,3},{8,776},... | collective-permute-start | bytes 786440 | tf_op jit(solution)/shard_map/ppermute | solution.py:96
  70.6 0.8 collective-permute-done.7.refs_4_
  71.4 2.2 %collective-permute-start.12 = (bf16[32,128,128]{2,1,0:T(8,128)(2,1)S(1)}, bf16[32,128,128]{2,1,0:T(8,128)(2,1)S(1)}, u32[]{:S(2)}, u32[]{:S(2)}) collective-permute-start(bf16[32,128,128]{2,1,0:T(8,128)(2,1)S(1)} %collective-permute-done.7.refs_4_), channel_id=1, source_target_pairs={{0,1},{1,0},{2,3},{3,2},{4,5},{5,4},{6,7},{7,6},{8,9},{9,8},{10,11... | collective-permute-start | bytes 3145736 | tf_op jit(solution)/shard_map/ppermute | solution.py:110
  73.6 4.0 %collective-permute-done.6.refs_3_ = bf16[32,128,128]{2,1,0:T(8,128)(2,1)S(1)} collective-permute-done((bf16[32,128,128]{2,1,0:T(8,128)(2,1)S(1)}, bf16[32,128,128]{2,1,0:T(8,128)(2,1)S(1)}, u32[]{:S(2)}, u32[]{:S(2)}) %collective-permute-start.6) | collective-permute-done | bytes 1048608 | tf_op jit(solution)/shard_map/ppermute | solution.py:96
  77.6 1.9 %collective-permute-start.11 = (bf16[32,128,128]{2,1,0:T(8,128)(2,1)S(1)}, bf16[32,128,128]{2,1,0:T(8,128)(2,1)S(1)}, u32[]{:S(2)}, u32[]{:S(2)}) collective-permute-start(bf16[32,128,128]{2,1,0:T(8,128)(2,1)S(1)} %collective-permute-done.6.refs_3_), channel_id=1, source_target_pairs={{0,1},{1,0},{2,3},{3,2},{4,5},{5,4},{6,7},{7,6},{8,9},{9,8},{10,11... | collective-permute-start | bytes 3145736 | tf_op jit(solution)/shard_map/ppermute | solution.py:110
  79.5 0.1 convert_reduce_fusion.1
  79.7 0.0 collective-permute-done.8
  79.7 0.0 collective-permute-done.9
  79.7 2.9 %collective-permute-start.13 = (bf16[16,128,128]{2,1,0:T(8,128)(2,1)S(1)}, bf16[16,128,128]{2,1,0:T(8,128)(2,1)S(1)}, u32[]{:S(2)}, u32[]{:S(2)}) collective-permute-start(bf16[16,128,128]{2,1,0:T(8,128)(2,1)S(1)} %constant_dynamic-update-slice_fusion.refs_5_), channel_id=1, source_target_pairs={{0,1},{1,0},{2,3},{3,2},{4,5},{5,4},{6,7},{7,6},{8,9},{9,8},{10,11... | collective-permute-start | bytes 1572872 | tf_op jit(solution)/shard_map/ppermute | solution.py:110
  82.7 0.1 convert_reduce_fusion
  82.9 0.3 select_reduce_fusion
  83.1 1.1 %collective-permute-done.13.refs_9_ = bf16[16,128,128]{2,1,0:T(8,128)(2,1)S(1)} collective-permute-done((bf16[16,128,128]{2,1,0:T(8,128)(2,1)S(1)}, bf16[16,128,128]{2,1,0:T(8,128)(2,1)S(1)}, u32[]{:S(2)}, u32[]{:S(2)}) %collective-permute-start.13) | collective-permute-done | bytes 524320 | tf_op jit(solution)/shard_map/ppermute | solution.py:110
  84.2 0.0 collective-permute-done.10.refs_6_
  84.2 0.0 collective-permute-done.12.refs_8_
  84.2 0.0 collective-permute-done.11.refs_7_
  84.2 3.8 %block_products.1 = bf16[2,128,128]{2,1,0:T(8,128)(2,1)} custom-call(s32[2,256]{1,0:T(2,128)S(1)} %broadcast_add_fusion.refs_0_, s32[2]{0:T(128)S(1)} %get-tuple-element.7.refs_1_, bf16[48,128,128]{2,1,0:T(8,128)(2,1)S(1)} %pad_maximum_fusion.refs_2_, bf16[32,128,128]{2,1,0:T(8,128)(2,1)S(1)} %collective-permute-done.6.refs_3_, ...), custom_call_target="tpu_custom_call" | custom-call | flops 536870912 | bytes 6291456 | tf_op jit(solution)/shard_map/block_products/pallas_call | solution.py:140
  (13 shorter events, 0.2 us)
Async XLA Ops:
  0.0 40.6 %copy-start = (s32[1,256,3]{1,0,2:T(1,128)S(1)}, s32[1,256,3]{1,0,2:T(1,128)}, u32[]{:S(2)}) copy-start(s32[1,256,3]{1,0,2:T(1,128)} %param.8) | copy-start | bytes 9220
  0.0 40.6 %copy-start.1 = (s32[1,32]{1,0:T(1,128)S(1)}, s32[1,32]{1,0:T(1,128)}, u32[]{:S(2)}) copy-start(s32[1,32]{1,0:T(1,128)} %param.9) | copy-start | bytes 388
  0.9 17.1 %collective-permute-start = (bf16[4,128,128]{2,1,0:T(8,128)(2,1)S(1)}, bf16[4,128,128]{2,1,0:T(8,128)(2,1)S(1)}, u32[]{:S(2)}, u32[]{:S(2)}) collective-permute-start(bf16[4,128,128]{2,1,0:T(8,128)(2,1)S(1)} %fusion.1), channel_id=1, source_target_pairs={{0,1},{1,0},{2,3},{3,2},{4,5},{5,4},{6,7},{7,6},{8,9},{9,8},{10,11... | collective-permute-start | bytes 393224 | tf_op jit(solution)/shard_map/ppermute | solution.py:110
  19.0 11.1 %collective-permute-start.1 = (bf16[4,128,128]{2,1,0:T(8,128)(2,1)S(1)}, bf16[4,128,128]{2,1,0:T(8,128)(2,1)S(1)}, u32[]{:S(2)}, u32[]{:S(2)}) collective-permute-start(bf16[4,128,128]{2,1,0:T(8,128)(2,1)S(1)} %get-tuple-element.11), channel_id=1, source_target_pairs={{0,32},{1,17},{16,48},{17,1},{32,64},{33,49},{48,80},{49,33},{64,9... | collective-permute-start | bytes 393224 | tf_op jit(solution)/shard_map/ppermute | solution.py:106
  20.9 13.0 %collective-permute-start.3 = (bf16[4,128,128]{2,1,0:T(8,128)(2,1)S(1)}, bf16[4,128,128]{2,1,0:T(8,128)(2,1)S(1)}, u32[]{:S(2)}, u32[]{:S(2)}) collective-permute-start(bf16[4,128,128]{2,1,0:T(8,128)(2,1)S(1)} %get-tuple-element.12), channel_id=1, source_target_pairs={{0,64},{1,17},{16,80},{17,1},{32,96},{33,49},{48,112},{49,33},{64,... | collective-permute-start | bytes 393224 | tf_op jit(solution)/shard_map/ppermute | solution.py:106
  28.2 5.7 %collective-permute-start.2 = (bf16[4,128,128]{2,1,0:T(8,128)(2,1)S(1)}, bf16[4,128,128]{2,1,0:T(8,128)(2,1)S(1)}, u32[]{:S(2)}, u32[]{:S(2)}) collective-permute-start(bf16[4,128,128]{2,1,0:T(8,128)(2,1)S(1)} %get-tuple-element.12), channel_id=1, source_target_pairs={{0,96},{1,1},{16,112},{17,17},{32,0},{33,33},{48,16},{49,49},{64,3... | collective-permute-start | bytes 393224 | tf_op jit(solution)/shard_map/ppermute | solution.py:106
  34.0 16.2 %collective-permute-start.5 = (bf16[16,128,128]{2,1,0:T(8,128)(2,1)S(1)}, bf16[16,128,128]{2,1,0:T(8,128)(2,1)S(1)}, u32[]{:S(2)}, u32[]{:S(2)}) collective-permute-start(bf16[16,128,128]{2,1,0:T(8,128)(2,1)S(1)} %pad_maximum_fusion.3), channel_id=1, source_target_pairs={{0,768},{1,13},{2,770},{3,15},{4,772},{5,1},{6,774},{7,3},{8,776},... | collective-permute-start | bytes 1572872 | tf_op jit(solution)/shard_map/ppermute | solution.py:96
  38.6 14.6 %collective-permute-start.4 = (bf16[16,128,128]{2,1,0:T(8,128)(2,1)S(1)}, bf16[16,128,128]{2,1,0:T(8,128)(2,1)S(1)}, u32[]{:S(2)}, u32[]{:S(2)}) collective-permute-start(bf16[16,128,128]{2,1,0:T(8,128)(2,1)S(1)} %pad_maximum_fusion.3), channel_id=1, source_target_pairs={{0,256},{1,5},{2,258},{3,7},{4,260},{5,9},{6,262},{7,11},{8,264},{... | collective-permute-start | bytes 1572872 | tf_op jit(solution)/shard_map/ppermute | solution.py:96
  53.4 17.9 %collective-permute-start.7 = (bf16[32,128,128]{2,1,0:T(8,128)(2,1)S(1)}, bf16[32,128,128]{2,1,0:T(8,128)(2,1)S(1)}, u32[]{:S(2)}, u32[]{:S(2)}) collective-permute-start(bf16[32,128,128]{2,1,0:T(8,128)(2,1)S(1)} %get-tuple-element.9), channel_id=1, source_target_pairs={{0,896},{1,15},{2,898},{3,1},{4,900},{5,3},{6,902},{7,5},{8,904},{... | collective-permute-start | bytes 3145736 | tf_op jit(solution)/shard_map/ppermute | solution.py:96
  58.2 19.4 %collective-permute-start.6 = (bf16[32,128,128]{2,1,0:T(8,128)(2,1)S(1)}, bf16[32,128,128]{2,1,0:T(8,128)(2,1)S(1)}, u32[]{:S(2)}, u32[]{:S(2)}) collective-permute-start(bf16[32,128,128]{2,1,0:T(8,128)(2,1)S(1)} %get-tuple-element.10), channel_id=1, source_target_pairs={{0,128},{1,3},{2,130},{3,5},{4,132},{5,7},{6,134},{7,9},{8,136},{9... | collective-permute-start | bytes 3145736 | tf_op jit(solution)/shard_map/ppermute | solution.py:96
  60.9 2.1 %copy-start.2 = (s32[8]{0:T(128)S(1)}, s32[8]{0:T(128)}, u32[]{:S(2)}) copy-start(s32[8]{0:T(128)} %constant.169.clone) | copy-start | bytes 100
  61.1 23.1 %collective-permute-start.10 = (bf16[48,128,128]{2,1,0:T(8,128)(2,1)S(1)}, bf16[48,128,128]{2,1,0:T(8,128)(2,1)S(1)}, u32[]{:S(2)}, u32[]{:S(2)}) collective-permute-start(bf16[48,128,128]{2,1,0:T(8,128)(2,1)S(1)} %pad_maximum_fusion.refs_2_), channel_id=1, source_target_pairs={{0,1},{1,0},{2,3},{3,2},{4,5},{5,4},{6,7},{7,6},{8,9},{9,8},{10,11... | collective-permute-start | bytes 4718600 | tf_op jit(solution)/shard_map/ppermute | solution.py:110
  63.2 16.5 %collective-permute-start.8 = (bf16[8,128,128]{2,1,0:T(8,128)(2,1)S(1)}, bf16[8,128,128]{2,1,0:T(8,128)(2,1)S(1)}, u32[]{:S(2)}, u32[]{:S(2)}) collective-permute-start(bf16[8,128,128]{2,1,0:T(8,128)(2,1)S(1)} %slice.32), channel_id=1, source_target_pairs={{0,256},{1,5},{2,258},{3,7},{4,260},{5,9},{6,262},{7,11},{8,264},{... | collective-permute-start | bytes 786440 | tf_op jit(solution)/shard_map/ppermute | solution.py:96
  66.3 13.4 %collective-permute-start.9 = (bf16[8,128,128]{2,1,0:T(8,128)(2,1)S(1)}, bf16[8,128,128]{2,1,0:T(8,128)(2,1)S(1)}, u32[]{:S(2)}, u32[]{:S(2)}) collective-permute-start(bf16[8,128,128]{2,1,0:T(8,128)(2,1)S(1)} %slice.33), channel_id=1, source_target_pairs={{0,768},{1,13},{2,770},{3,15},{4,772},{5,1},{6,774},{7,3},{8,776},... | collective-permute-start | bytes 786440 | tf_op jit(solution)/shard_map/ppermute | solution.py:96
  71.4 12.8 %collective-permute-start.12 = (bf16[32,128,128]{2,1,0:T(8,128)(2,1)S(1)}, bf16[32,128,128]{2,1,0:T(8,128)(2,1)S(1)}, u32[]{:S(2)}, u32[]{:S(2)}) collective-permute-start(bf16[32,128,128]{2,1,0:T(8,128)(2,1)S(1)} %collective-permute-done.7.refs_4_), channel_id=1, source_target_pairs={{0,1},{1,0},{2,3},{3,2},{4,5},{5,4},{6,7},{7,6},{8,9},{9,8},{10,11... | collective-permute-start | bytes 3145736 | tf_op jit(solution)/shard_map/ppermute | solution.py:110
  77.6 6.6 %collective-permute-start.11 = (bf16[32,128,128]{2,1,0:T(8,128)(2,1)S(1)}, bf16[32,128,128]{2,1,0:T(8,128)(2,1)S(1)}, u32[]{:S(2)}, u32[]{:S(2)}) collective-permute-start(bf16[32,128,128]{2,1,0:T(8,128)(2,1)S(1)} %collective-permute-done.6.refs_3_), channel_id=1, source_target_pairs={{0,1},{1,0},{2,3},{3,2},{4,5},{5,4},{6,7},{7,6},{8,9},{9,8},{10,11... | collective-permute-start | bytes 3145736 | tf_op jit(solution)/shard_map/ppermute | solution.py:110
  79.7 4.4 %collective-permute-start.13 = (bf16[16,128,128]{2,1,0:T(8,128)(2,1)S(1)}, bf16[16,128,128]{2,1,0:T(8,128)(2,1)S(1)}, u32[]{:S(2)}, u32[]{:S(2)}) collective-permute-start(bf16[16,128,128]{2,1,0:T(8,128)(2,1)S(1)} %constant_dynamic-update-slice_fusion.refs_5_), channel_id=1, source_target_pairs={{0,1},{1,0},{2,3},{3,2},{4,5},{5,4},{6,7},{7,6},{8,9},{9,8},{10,11... | collective-permute-start | bytes 1572872 | tf_op jit(solution)/shard_map/ppermute | solution.py:110

commit v14 on v13

--- a/solution.py
+++ b/solution.py
@@ -13,7 +13,7 @@
 GROUP = 16
 TILE = 16
 ZERO = 2 * NY * TILE
-SEATS = (1, 5, 2, 6, 7, 3, 0, 4)
+SEATS = (0, 5, 2, 6, 7, 3, 1, 4)
 
 
 def rot(size, shift):
@@ -123,7 +123,8 @@
     half = TILE // 2
     behind, ahead = along_plane(own, 2), along_plane(own, -2)
     near = jnp.concatenate([behind, own, ahead])
-    pieces = [near, along_plane(near[: 2 * TILE], 1), along_plane(near[TILE:], -1)]
+    pieces = [own, jnp.concatenate([behind, ahead])]
+    pieces += [along_plane(near[: 2 * TILE], 1), along_plane(near[TILE:], -1)]
     far = [along_plane(behind[:half], 2), along_plane(ahead[half:], -2)]
     pieces.append(jnp.concatenate(far))
     pieces += [to_partner(piece) for piece in pieces]

time: 89.3 us -> 90.9 us (1.018)
  local copies, waits for them, and re-layouts: 0.28 us -> 2.27 us
  waiting for transfers between devices: 24.3 us -> 22.4 us
  starting transfers between devices: 56.3 us -> 58.1 us
    ppermute x5 -> x6, starting transfers between devices: 25.1 us -> 28.2 us  [to_partner(): return lax.ppermute(value, 'c', rot(NCORE, 1))]
    ppermute x6, waiting for transfers between devices: 17.2 us -> 15.1 us  [along_plane(): return lax.ppermute(value, ('x', 'y', 'c'), pairs)]
    unnamed x8 -> x17, local copies, waits for them, and re-layouts: 0.04 us -> 1.96 us
    ppermute x6, starting transfers between devices: 21.4 us -> 20.1 us  [along_plane(): return lax.ppermute(value, ('x', 'y', 'c'), pairs)]
    concatenate x2 -> x1, other arithmetic: 0.35 us -> 1.52 us  [per_device(): near = jnp.concatenate([behind, own, ahead])]
    select_n x1, other arithmetic: 0.97 us -> 0.03 us  [per_device(): jnp.where(c == 0, rights, got)]
    ppermute x5 -> x6, waiting for transfers between devices: 2.03 us -> 2.39 us  [to_partner(): return lax.ppermute(value, 'c', rot(NCORE, 1))]
  transfers between devices with their start and end apart: 14 -> 15, of which waited for: 8 -> 8; matrix products, arithmetic and copies ran while one was open for 1% -> 1% of each run, Pallas kernels for 0% -> 0%
where the time goes in v14:
time: 90.9 us; the launch traced here: 89.8 us
  starting transfers between devices  58.1 us (64%)
  waiting for transfers between devices  22.4 us (25%)
  other arithmetic  3.33 us (4%)
  Pallas kernels  3.31 us (4%)
  local copies, waits for them, and re-layouts  2.27 us (2%)
    ppermute x6, starting transfers between devices, to_partner(): return lax.ppermute(value, 'c', rot(NCORE, 1))  28.2 us
    ppermute x6, starting transfers between devices, along_plane(): return lax.ppermute(value, ('x', 'y', 'c'), pairs)  20.1 us
    ppermute x6, waiting for transfers between devices, along_plane(): return lax.ppermute(value, ('x', 'y', 'c'), pairs)  15.1 us
    ppermute x3, starting transfers between devices, along_z(): return lax.ppermute(value, ('zl', 'zh', 'c'), pairs)  9.86 us
    ppermute x3, waiting for transfers between devices, along_z(): return lax.ppermute(value, ('zl', 'zh', 'c'), pairs)  4.95 us
    pallas_call x1, Pallas kernels, per_device(): pl.pallas_call(kernel, out_shape=jax.ShapeDtypeStruct((NC, BS, BS), jnp.b...  3.31 us
    ppermute x6, waiting for transfers between devices, to_partner(): return lax.ppermute(value, 'c', rot(NCORE, 1))  2.39 us
    unnamed x17, local copies, waits for them, and re-layouts  1.96 us
  transfers between devices with their start and end apart: 15, of which 8 were waited for; matrix products, arithmetic and copies ran while one was open for 1% of the time, Pallas kernels for 0%

profile of v14, /device:TPU:1, one launch (start us, length us, event | category | flops | bytes accessed | tf_op | source)
XLA Modules:
  0.0 89.8 jit_solution(17541559269084902957)
XLA Ops:
  0.0 1.0 %fusion.1 = bf16[4,128,128]{2,1,0:T(8,128)(2,1)S(1)} fusion(bf16[4,128,128]{2,1,0:T(8,128)(2,1)} %param.6, bf16[2,128,128]{2,1,0:T(8,128)(2,1)} %param.7, pred[]{:T(512)S(6)} %eq.114), kind=kLoop, calls=%fused_computation.10 | loop fusion | flops 131072 | bytes 327681 | tf_op jit(solution)/shard_map/jit(_where)/select_n | solution.py:116
  1.0 0.0 copy-start.2
  1.0 16.2 %collective-permute-start = (bf16[4,128,128]{2,1,0:T(8,128)(2,1)S(1)}, bf16[4,128,128]{2,1,0:T(8,128)(2,1)S(1)}, u32[]{:S(2)}, u32[]{:S(2)}) collective-permute-start(bf16[4,128,128]{2,1,0:T(8,128)(2,1)S(1)} %fusion.1), channel_id=1, source_target_pairs={{0,1},{1,0},{2,3},{3,2},{4,5},{5,4},{6,7},{7,6},{8,9},{9,8},{10,11... | collective-permute-start | bytes 393224 | tf_op jit(solution)/shard_map/ppermute | solution.py:110
  17.2 1.0 %collective-permute-done = bf16[4,128,128]{2,1,0:T(8,128)(2,1)S(1)} collective-permute-done((bf16[4,128,128]{2,1,0:T(8,128)(2,1)S(1)}, bf16[4,128,128]{2,1,0:T(8,128)(2,1)S(1)}, u32[]{:S(2)}, u32[]{:S(2)}) %collective-permute-start) | collective-permute-done | bytes 131104 | tf_op jit(solution)/shard_map/ppermute | solution.py:110
  18.2 0.0 copy-done.3
  18.2 0.0 copy-done.2
  18.2 1.9 %collective-permute-start.1 = (bf16[4,128,128]{2,1,0:T(8,128)(2,1)S(1)}, bf16[4,128,128]{2,1,0:T(8,128)(2,1)S(1)}, u32[]{:S(2)}, u32[]{:S(2)}) collective-permute-start(bf16[4,128,128]{2,1,0:T(8,128)(2,1)S(1)} %get-tuple-element.11), channel_id=1, source_target_pairs={{0,32},{1,17},{16,48},{17,1},{32,64},{33,49},{48,80},{49,33},{64,9... | collective-permute-start | bytes 393224 | tf_op jit(solution)/shard_map/ppermute | solution.py:106
  20.2 7.3 %collective-permute-start.3 = (bf16[4,128,128]{2,1,0:T(8,128)(2,1)S(1)}, bf16[4,128,128]{2,1,0:T(8,128)(2,1)S(1)}, u32[]{:S(2)}, u32[]{:S(2)}) collective-permute-start(bf16[4,128,128]{2,1,0:T(8,128)(2,1)S(1)} %get-tuple-element.12), channel_id=1, source_target_pairs={{0,64},{1,17},{16,80},{17,1},{32,96},{33,49},{48,112},{49,33},{64,... | collective-permute-start | bytes 393224 | tf_op jit(solution)/shard_map/ppermute | solution.py:106
  27.4 0.7 collective-permute-start.2
  28.1 1.2 %collective-permute-done.1 = bf16[4,128,128]{2,1,0:T(8,128)(2,1)S(1)} collective-permute-done((bf16[4,128,128]{2,1,0:T(8,128)(2,1)S(1)}, bf16[4,128,128]{2,1,0:T(8,128)(2,1)S(1)}, u32[]{:S(2)}, u32[]{:S(2)}) %collective-permute-start.1) | collective-permute-done | bytes 131104 | tf_op jit(solution)/shard_map/ppermute | solution.py:106
  29.4 3.7 %collective-permute-done.3 = bf16[4,128,128]{2,1,0:T(8,128)(2,1)S(1)} collective-permute-done((bf16[4,128,128]{2,1,0:T(8,128)(2,1)S(1)}, bf16[4,128,128]{2,1,0:T(8,128)(2,1)S(1)}, u32[]{:S(2)}, u32[]{:S(2)}) %collective-permute-start.3) | collective-permute-done | bytes 131104 | tf_op jit(solution)/shard_map/ppermute | solution.py:106
  33.1 0.0 collective-permute-done.2
  33.1 0.1 pad_maximum_fusion.2.refs_2_
  33.1 4.6 %collective-permute-start.5 = (bf16[16,128,128]{2,1,0:T(8,128)(2,1)S(1)}, bf16[16,128,128]{2,1,0:T(8,128)(2,1)S(1)}, u32[]{:S(2)}, u32[]{:S(2)}) collective-permute-start(bf16[16,128,128]{2,1,0:T(8,128)(2,1)S(1)} %pad_maximum_fusion.2.refs_2_), channel_id=1, source_target_pairs={{0,768},{1,13},{2,770},{3,15},{4,772},{5,1},{6,774},{7,3},{8,776},... | collective-permute-start | bytes 1572872 | tf_op jit(solution)/shard_map/ppermute | solution.py:96
  37.8 1.9 %collective-permute-start.4 = (bf16[16,128,128]{2,1,0:T(8,128)(2,1)S(1)}, bf16[16,128,128]{2,1,0:T(8,128)(2,1)S(1)}, u32[]{:S(2)}, u32[]{:S(2)}) collective-permute-start(bf16[16,128,128]{2,1,0:T(8,128)(2,1)S(1)} %pad_maximum_fusion.2.refs_2_), channel_id=1, source_target_pairs={{0,256},{1,5},{2,258},{3,7},{4,260},{5,9},{6,262},{7,11},{8,264},{... | collective-permute-start | bytes 1572872 | tf_op jit(solution)/shard_map/ppermute | solution.py:96
  39.7 9.5 %collective-permute-done.5 = bf16[16,128,128]{2,1,0:T(8,128)(2,1)S(1)} collective-permute-done((bf16[16,128,128]{2,1,0:T(8,128)(2,1)S(1)}, bf16[16,128,128]{2,1,0:T(8,128)(2,1)S(1)}, u32[]{:S(2)}, u32[]{:S(2)}) %collective-permute-start.5) | collective-permute-done | bytes 524320 | tf_op jit(solution)/shard_map/ppermute | solution.py:96
  49.3 3.1 %collective-permute-done.4 = bf16[16,128,128]{2,1,0:T(8,128)(2,1)S(1)} collective-permute-done((bf16[16,128,128]{2,1,0:T(8,128)(2,1)S(1)}, bf16[16,128,128]{2,1,0:T(8,128)(2,1)S(1)}, u32[]{:S(2)}, u32[]{:S(2)}) %collective-permute-start.4) | collective-permute-done | bytes 524320 | tf_op jit(solution)/shard_map/ppermute | solution.py:96
  52.4 1.5 %pad_maximum_fusion.1 = (bf16[32,128,128]{2,1,0:T(8,128)(2,1)}, bf16[32,128,128]{2,1,0:T(8,128)(2,1)}) fusion(bf16[16,128,128]{2,1,0:T(8,128)(2,1)S(1)} %collective-permute-done.5, bf16[16,128,128]{2,1,0:T(8,128)(2,1)S(1)} %pad_maximum_fusion.2.refs_2_, bf16[16,128,128]{2,1,0:T(8,128)(2,1)S(1)} %collective-permute-done.4), kind=kLoop, calls=%fused_computation.1 | loop fusion | flops 1048576 | bytes 3670016 | tf_op jit(solution)/shard_map/concatenate | solution.py:125
  53.9 0.0 copy-done
  53.9 4.7 %collective-permute-start.7 = (bf16[32,128,128]{2,1,0:T(8,128)(2,1)}, bf16[32,128,128]{2,1,0:T(8,128)(2,1)S(1)}, u32[]{:S(2)}, u32[]{:S(2)}) collective-permute-start(bf16[32,128,128]{2,1,0:T(8,128)(2,1)} %get-tuple-element.9), channel_id=1, source_target_pairs={{0,896},{1,15},{2,898},{3,1},{4,900},{5,3},{6,902},{7,5},{8,904},{... | collective-permute-start | bytes 3145736 | tf_op jit(solution)/shard_map/ppermute | solution.py:96
  58.6 2.6 %collective-permute-start.6 = (bf16[32,128,128]{2,1,0:T(8,128)(2,1)}, bf16[32,128,128]{2,1,0:T(8,128)(2,1)S(1)}, u32[]{:S(2)}, u32[]{:S(2)}) collective-permute-start(bf16[32,128,128]{2,1,0:T(8,128)(2,1)} %get-tuple-element.10), channel_id=1, source_target_pairs={{0,128},{1,3},{2,130},{3,5},{4,132},{5,7},{6,134},{7,9},{8,136},{9... | collective-permute-start | bytes 3145736 | tf_op jit(solution)/shard_map/ppermute | solution.py:96
  61.3 0.7 copy-done.4
  62.0 0.7 copy-done.5
  62.7 0.1 broadcast_in_dim.46
  62.7 0.1 reshape.355
  62.8 0.6 copy-done.6
  63.4 0.1 select_reduce_fusion.2
  63.6 3.1 %collective-permute-start.9 = (bf16[8,128,128]{2,1,0:T(8,128)(2,1)S(1)}, bf16[8,128,128]{2,1,0:T(8,128)(2,1)S(1)}, u32[]{:S(2)}, u32[]{:S(2)}) collective-permute-start(bf16[8,128,128]{2,1,0:T(8,128)(2,1)S(1)} %slice.33), channel_id=1, source_target_pairs={{0,768},{1,13},{2,770},{3,15},{4,772},{5,1},{6,774},{7,3},{8,776},... | collective-permute-start | bytes 786440 | tf_op jit(solution)/shard_map/ppermute | solution.py:96
  66.7 3.1 %collective-permute-start.8 = (bf16[8,128,128]{2,1,0:T(8,128)(2,1)S(1)}, bf16[8,128,128]{2,1,0:T(8,128)(2,1)S(1)}, u32[]{:S(2)}, u32[]{:S(2)}) collective-permute-start(bf16[8,128,128]{2,1,0:T(8,128)(2,1)S(1)} %slice.32), channel_id=1, source_target_pairs={{0,256},{1,5},{2,258},{3,7},{4,260},{5,9},{6,262},{7,11},{8,264},{... | collective-permute-start | bytes 786440 | tf_op jit(solution)/shard_map/ppermute | solution.py:96
  69.8 0.1 constant_dynamic-update-slice_fusion.refs_3_
  69.9 1.9 %collective-permute-start.11 = (bf16[32,128,128]{2,1,0:T(8,128)(2,1)S(1)}, bf16[32,128,128]{2,1,0:T(8,128)(2,1)S(1)}, u32[]{:S(2)}, u32[]{:S(2)}) collective-permute-start(bf16[32,128,128]{2,1,0:T(8,128)(2,1)S(1)} %constant_dynamic-update-slice_fusion.refs_3_), channel_id=1, source_target_pairs={{0,1},{1,0},{2,3},{3,2},{4,5},{5,4},{6,7},{7,6},{8,9},{9,8},{10,11... | collective-permute-start | bytes 3145736 | tf_op jit(solution)/shard_map/ppermute | solution.py:110
  71.8 0.2 collective-permute-done.7.refs_5_
  72.0 3.8 %collective-permute-start.13 = (bf16[32,128,128]{2,1,0:T(8,128)(2,1)S(1)}, bf16[32,128,128]{2,1,0:T(8,128)(2,1)S(1)}, u32[]{:S(2)}, u32[]{:S(2)}) collective-permute-start(bf16[32,128,128]{2,1,0:T(8,128)(2,1)S(1)} %collective-permute-done.7.refs_5_), channel_id=1, source_target_pairs={{0,1},{1,0},{2,3},{3,2},{4,5},{5,4},{6,7},{7,6},{8,9},{9,8},{10,11... | collective-permute-start | bytes 3145736 | tf_op jit(solution)/shard_map/ppermute | solution.py:110
  75.9 2.3 %collective-permute-done.6.refs_4_ = bf16[32,128,128]{2,1,0:T(8,128)(2,1)S(1)} collective-permute-done((bf16[32,128,128]{2,1,0:T(8,128)(2,1)}, bf16[32,128,128]{2,1,0:T(8,128)(2,1)S(1)}, u32[]{:S(2)}, u32[]{:S(2)}) %collective-permute-start.6) | collective-permute-done | bytes 1048608 | tf_op jit(solution)/shard_map/ppermute | solution.py:96
  78.1 1.9 %collective-permute-start.12 = (bf16[32,128,128]{2,1,0:T(8,128)(2,1)S(1)}, bf16[32,128,128]{2,1,0:T(8,128)(2,1)S(1)}, u32[]{:S(2)}, u32[]{:S(2)}) collective-permute-start(bf16[32,128,128]{2,1,0:T(8,128)(2,1)S(1)} %collective-permute-done.6.refs_4_), channel_id=1, source_target_pairs={{0,1},{1,0},{2,3},{3,2},{4,5},{5,4},{6,7},{7,6},{8,9},{9,8},{10,11... | collective-permute-start | bytes 3145736 | tf_op jit(solution)/shard_map/ppermute | solution.py:110
  80.1 0.1 convert_reduce_fusion.1
  80.2 0.0 collective-permute-done.8
  80.2 2.4 %collective-permute-start.10 = (bf16[16,128,128]{2,1,0:T(8,128)(2,1)S(1)}, bf16[16,128,128]{2,1,0:T(8,128)(2,1)S(1)}, u32[]{:S(2)}, u32[]{:S(2)}) collective-permute-start(bf16[16,128,128]{2,1,0:T(8,128)(2,1)S(1)} %pad_maximum_fusion.2.refs_2_), channel_id=1, source_target_pairs={{0,1},{1,0},{2,3},{3,2},{4,5},{5,4},{6,7},{7,6},{8,9},{9,8},{10,11... | collective-permute-start | bytes 1572872 | tf_op jit(solution)/shard_map/ppermute | solution.py:110
  82.6 0.0 collective-permute-done.9
  82.7 1.9 %collective-permute-start.14 = (bf16[16,128,128]{2,1,0:T(8,128)(2,1)S(1)}, bf16[16,128,128]{2,1,0:T(8,128)(2,1)S(1)}, u32[]{:S(2)}, u32[]{:S(2)}) collective-permute-start(bf16[16,128,128]{2,1,0:T(8,128)(2,1)S(1)} %constant_dynamic-update-slice_fusion.2.refs_6_), channel_id=1, source_target_pairs={{0,1},{1,0},{2,3},{3,2},{4,5},{5,4},{6,7},{7,6},{8,9},{9,8},{10,11... | collective-permute-start | bytes 1572872 | tf_op jit(solution)/shard_map/ppermute | solution.py:110
  84.6 0.1 convert_reduce_fusion
  84.8 0.3 select_reduce_fusion
  85.1 0.0 collective-permute-done.10.refs_7_
  85.1 1.4 %collective-permute-done.14.refs_11_ = bf16[16,128,128]{2,1,0:T(8,128)(2,1)S(1)} collective-permute-done((bf16[16,128,128]{2,1,0:T(8,128)(2,1)S(1)}, bf16[16,128,128]{2,1,0:T(8,128)(2,1)S(1)}, u32[]{:S(2)}, u32[]{:S(2)}) %collective-permute-start.14) | collective-permute-done | bytes 524320 | tf_op jit(solution)/shard_map/ppermute | solution.py:110
  86.5 0.0 collective-permute-done.11.refs_8_
  86.5 0.0 collective-permute-done.13.refs_10_
  86.5 0.0 collective-permute-done.12.refs_9_
  86.5 3.3 %block_products.1 = bf16[2,128,128]{2,1,0:T(8,128)(2,1)} custom-call(s32[2,256]{1,0:T(2,128)S(1)} %broadcast_add_fusion.refs_0_, s32[2]{0:T(128)S(1)} %get-tuple-element.7.refs_1_, bf16[16,128,128]{2,1,0:T(8,128)(2,1)S(1)} %pad_maximum_fusion.2.refs_2_, bf16[32,128,128]{2,1,0:T(8,128)(2,1)S(1)} %constant_dynamic-update-slice_fusion.refs_3_, ...), custom_call_target="tpu_custom_call" | custom-call | flops 536870912 | bytes 6291456 | tf_op jit(solution)/shard_map/block_products/pallas_call | solution.py:141
  (22 shorter events, 0.3 us)
Async XLA Ops:
  0.0 18.2 %copy-start.3 = (bf16[2,128,128]{2,1,0:T(8,128)(2,1)S(1)}, bf16[2,128,128]{2,1,0:T(8,128)(2,1)}, u32[]{:S(2)}) copy-start(bf16[2,128,128]{2,1,0:T(8,128)(2,1)} %param.7) | copy-start | bytes 196612
  1.0 17.2 %copy-start.2 = (bf16[4,128,128]{2,1,0:T(8,128)(2,1)S(1)}, bf16[4,128,128]{2,1,0:T(8,128)(2,1)}, u32[]{:S(2)}) copy-start(bf16[4,128,128]{2,1,0:T(8,128)(2,1)} %param.6) | copy-start | bytes 393220
  1.0 17.2 %collective-permute-start = (bf16[4,128,128]{2,1,0:T(8,128)(2,1)S(1)}, bf16[4,128,128]{2,1,0:T(8,128)(2,1)S(1)}, u32[]{:S(2)}, u32[]{:S(2)}) collective-permute-start(bf16[4,128,128]{2,1,0:T(8,128)(2,1)S(1)} %fusion.1), channel_id=1, source_target_pairs={{0,1},{1,0},{2,3},{3,2},{4,5},{5,4},{6,7},{7,6},{8,9},{9,8},{10,11... | collective-permute-start | bytes 393224 | tf_op jit(solution)/shard_map/ppermute | solution.py:110
  18.2 11.1 %collective-permute-start.1 = (bf16[4,128,128]{2,1,0:T(8,128)(2,1)S(1)}, bf16[4,128,128]{2,1,0:T(8,128)(2,1)S(1)}, u32[]{:S(2)}, u32[]{:S(2)}) collective-permute-start(bf16[4,128,128]{2,1,0:T(8,128)(2,1)S(1)} %get-tuple-element.11), channel_id=1, source_target_pairs={{0,32},{1,17},{16,48},{17,1},{32,64},{33,49},{48,80},{49,33},{64,9... | collective-permute-start | bytes 393224 | tf_op jit(solution)/shard_map/ppermute | solution.py:106
  20.2 12.9 %collective-permute-start.3 = (bf16[4,128,128]{2,1,0:T(8,128)(2,1)S(1)}, bf16[4,128,128]{2,1,0:T(8,128)(2,1)S(1)}, u32[]{:S(2)}, u32[]{:S(2)}) collective-permute-start(bf16[4,128,128]{2,1,0:T(8,128)(2,1)S(1)} %get-tuple-element.12), channel_id=1, source_target_pairs={{0,64},{1,17},{16,80},{17,1},{32,96},{33,49},{48,112},{49,33},{64,... | collective-permute-start | bytes 393224 | tf_op jit(solution)/shard_map/ppermute | solution.py:106
  27.4 5.6 %collective-permute-start.2 = (bf16[4,128,128]{2,1,0:T(8,128)(2,1)S(1)}, bf16[4,128,128]{2,1,0:T(8,128)(2,1)S(1)}, u32[]{:S(2)}, u32[]{:S(2)}) collective-permute-start(bf16[4,128,128]{2,1,0:T(8,128)(2,1)S(1)} %get-tuple-element.12), channel_id=1, source_target_pairs={{0,96},{1,1},{16,112},{17,17},{32,0},{33,33},{48,16},{49,49},{64,3... | collective-permute-start | bytes 393224 | tf_op jit(solution)/shard_map/ppermute | solution.py:106
  33.1 16.1 %collective-permute-start.5 = (bf16[16,128,128]{2,1,0:T(8,128)(2,1)S(1)}, bf16[16,128,128]{2,1,0:T(8,128)(2,1)S(1)}, u32[]{:S(2)}, u32[]{:S(2)}) collective-permute-start(bf16[16,128,128]{2,1,0:T(8,128)(2,1)S(1)} %pad_maximum_fusion.2.refs_2_), channel_id=1, source_target_pairs={{0,768},{1,13},{2,770},{3,15},{4,772},{5,1},{6,774},{7,3},{8,776},... | collective-permute-start | bytes 1572872 | tf_op jit(solution)/shard_map/ppermute | solution.py:96
  37.8 14.6 %collective-permute-start.4 = (bf16[16,128,128]{2,1,0:T(8,128)(2,1)S(1)}, bf16[16,128,128]{2,1,0:T(8,128)(2,1)S(1)}, u32[]{:S(2)}, u32[]{:S(2)}) collective-permute-start(bf16[16,128,128]{2,1,0:T(8,128)(2,1)S(1)} %pad_maximum_fusion.2.refs_2_), channel_id=1, source_target_pairs={{0,256},{1,5},{2,258},{3,7},{4,260},{5,9},{6,262},{7,11},{8,264},{... | collective-permute-start | bytes 1572872 | tf_op jit(solution)/shard_map/ppermute | solution.py:96
  52.4 1.5 %copy-start = (bf16[16,128,128]{2,1,0:T(8,128)(2,1)}, bf16[16,128,128]{2,1,0:T(8,128)(2,1)S(1)}, u32[]{:S(2)}) copy-start(bf16[16,128,128]{2,1,0:T(8,128)(2,1)S(1)} %collective-permute-done.4) | copy-start | bytes 1572868
  53.9 18.1 %collective-permute-start.7 = (bf16[32,128,128]{2,1,0:T(8,128)(2,1)}, bf16[32,128,128]{2,1,0:T(8,128)(2,1)S(1)}, u32[]{:S(2)}, u32[]{:S(2)}) collective-permute-start(bf16[32,128,128]{2,1,0:T(8,128)(2,1)} %get-tuple-element.9), channel_id=1, source_target_pairs={{0,896},{1,15},{2,898},{3,1},{4,900},{5,3},{6,902},{7,5},{8,904},{... | collective-permute-start | bytes 3145736 | tf_op jit(solution)/shard_map/ppermute | solution.py:96
  58.6 19.5 %collective-permute-start.6 = (bf16[32,128,128]{2,1,0:T(8,128)(2,1)}, bf16[32,128,128]{2,1,0:T(8,128)(2,1)S(1)}, u32[]{:S(2)}, u32[]{:S(2)}) collective-permute-start(bf16[32,128,128]{2,1,0:T(8,128)(2,1)} %get-tuple-element.10), channel_id=1, source_target_pairs={{0,128},{1,3},{2,130},{3,5},{4,132},{5,7},{6,134},{7,9},{8,136},{9... | collective-permute-start | bytes 3145736 | tf_op jit(solution)/shard_map/ppermute | solution.py:96
  61.3 0.7 copy-start.4
  62.0 0.7 copy-start.5
  62.7 0.7 copy-start.6
  63.4 3.3 %copy-start.1 = (bf16[16,128,128]{2,1,0:T(8,128)(2,1)S(1)}, bf16[16,128,128]{2,1,0:T(8,128)(2,1)}, u32[]{:S(2)}) copy-start(bf16[16,128,128]{2,1,0:T(8,128)(2,1)} %copy-done) | copy-start | bytes 1572868
  63.6 19.1 %collective-permute-start.9 = (bf16[8,128,128]{2,1,0:T(8,128)(2,1)S(1)}, bf16[8,128,128]{2,1,0:T(8,128)(2,1)S(1)}, u32[]{:S(2)}, u32[]{:S(2)}) collective-permute-start(bf16[8,128,128]{2,1,0:T(8,128)(2,1)S(1)} %slice.33), channel_id=1, source_target_pairs={{0,768},{1,13},{2,770},{3,15},{4,772},{5,1},{6,774},{7,3},{8,776},... | collective-permute-start | bytes 786440 | tf_op jit(solution)/shard_map/ppermute | solution.py:96
  66.7 13.5 %collective-permute-start.8 = (bf16[8,128,128]{2,1,0:T(8,128)(2,1)S(1)}, bf16[8,128,128]{2,1,0:T(8,128)(2,1)S(1)}, u32[]{:S(2)}, u32[]{:S(2)}) collective-permute-start(bf16[8,128,128]{2,1,0:T(8,128)(2,1)S(1)} %slice.32), channel_id=1, source_target_pairs={{0,256},{1,5},{2,258},{3,7},{4,260},{5,9},{6,262},{7,11},{8,264},{... | collective-permute-start | bytes 786440 | tf_op jit(solution)/shard_map/ppermute | solution.py:96
  69.9 16.6 %collective-permute-start.11 = (bf16[32,128,128]{2,1,0:T(8,128)(2,1)S(1)}, bf16[32,128,128]{2,1,0:T(8,128)(2,1)S(1)}, u32[]{:S(2)}, u32[]{:S(2)}) collective-permute-start(bf16[32,128,128]{2,1,0:T(8,128)(2,1)S(1)} %constant_dynamic-update-slice_fusion.refs_3_), channel_id=1, source_target_pairs={{0,1},{1,0},{2,3},{3,2},{4,5},{5,4},{6,7},{7,6},{8,9},{9,8},{10,11... | collective-permute-start | bytes 3145736 | tf_op jit(solution)/shard_map/ppermute | solution.py:110
  72.0 14.5 %collective-permute-start.13 = (bf16[32,128,128]{2,1,0:T(8,128)(2,1)S(1)}, bf16[32,128,128]{2,1,0:T(8,128)(2,1)S(1)}, u32[]{:S(2)}, u32[]{:S(2)}) collective-permute-start(bf16[32,128,128]{2,1,0:T(8,128)(2,1)S(1)} %collective-permute-done.7.refs_5_), channel_id=1, source_target_pairs={{0,1},{1,0},{2,3},{3,2},{4,5},{5,4},{6,7},{7,6},{8,9},{9,8},{10,11... | collective-permute-start | bytes 3145736 | tf_op jit(solution)/shard_map/ppermute | solution.py:110
  78.1 8.3 %collective-permute-start.12 = (bf16[32,128,128]{2,1,0:T(8,128)(2,1)S(1)}, bf16[32,128,128]{2,1,0:T(8,128)(2,1)S(1)}, u32[]{:S(2)}, u32[]{:S(2)}) collective-permute-start(bf16[32,128,128]{2,1,0:T(8,128)(2,1)S(1)} %collective-permute-done.6.refs_4_), channel_id=1, source_target_pairs={{0,1},{1,0},{2,3},{3,2},{4,5},{5,4},{6,7},{7,6},{8,9},{9,8},{10,11... | collective-permute-start | bytes 3145736 | tf_op jit(solution)/shard_map/ppermute | solution.py:110
  80.2 4.9 %collective-permute-start.10 = (bf16[16,128,128]{2,1,0:T(8,128)(2,1)S(1)}, bf16[16,128,128]{2,1,0:T(8,128)(2,1)S(1)}, u32[]{:S(2)}, u32[]{:S(2)}) collective-permute-start(bf16[16,128,128]{2,1,0:T(8,128)(2,1)S(1)} %pad_maximum_fusion.2.refs_2_), channel_id=1, source_target_pairs={{0,1},{1,0},{2,3},{3,2},{4,5},{5,4},{6,7},{7,6},{8,9},{9,8},{10,11... | collective-permute-start | bytes 1572872 | tf_op jit(solution)/shard_map/ppermute | solution.py:110
  82.7 3.8 %collective-permute-start.14 = (bf16[16,128,128]{2,1,0:T(8,128)(2,1)S(1)}, bf16[16,128,128]{2,1,0:T(8,128)(2,1)S(1)}, u32[]{:S(2)}, u32[]{:S(2)}) collective-permute-start(bf16[16,128,128]{2,1,0:T(8,128)(2,1)S(1)} %constant_dynamic-update-slice_fusion.2.refs_6_), channel_id=1, source_target_pairs={{0,1},{1,0},{2,3},{3,2},{4,5},{5,4},{6,7},{7,6},{8,9},{9,8},{10,11... | collective-permute-start | bytes 1572872 | tf_op jit(solution)/shard_map/ppermute | solution.py:110
